TPU v7x, 32 devices: a whole 2x2x4 slice. The times are simulated.
32 devices in a mesh: pole: 2 (over y), row: 16 (over z, x, core).
Axes of the slice: x: 2, y: 2, z: 4, core: 2. Of those that a mesh axis runs over, the one named last changes fastest.
Arguments:
- anc_blocks: float32 [32, 384, 96], P(('pole', 'row')), parts along dimension 0, may hold values from -1 to 18, as said below
- anc_links: float32 [1536, 8, 256], P(('pole', 'row')), parts along dimension 0, may hold values from -0.21875 to 0.21875
- parent_links: float32 [14, 256, 256], P('pole'), parts along dimension 0, may hold values from -0.375 to 0.375
- pivot_inverse: float32 [16, 256, 256], P('pole'), parts along dimension 0, may hold values from -1 to 18, as said below
- pattern: int32 [8, 6], replicated, may hold values 0 or 1
Outputs:
- anc_panels: float32 [1536, 8, 256], P(('pole', 'row')), parts along dimension 0
- parent_blocks: float32 [14, 256, 256], P('pole'), parts along dimension 0
- diagonal_blocks: float32 [16, 256, 256], P('pole'), parts along dimension 0
There are 2 independent parts, one for each index of `pole`. A program takes and returns all parts, laid end to end along the dimension named above; an argument that names none is the same for every part. Nothing has to cross between parts.
Inputs may be any that keep to these rules, and one draw needn't show every extreme that they name: `anc_blocks`: the matrix S that the blocks form is symmetric and positive definite. `pivot_inverse`: each block is symmetric and positive definite.
All inputs are finite; a program needn't handle non-finite values.
Results may differ from a plain program's by a relative error of at most 0.0001.
Values sent between devices are 32-bit elements; how exact they have to be, the bound alone decides.
No kernel may reach another device: no remote copies, remote signals or barrier semaphores. Data moves between devices by JAX's collectives and lax.ppermute only.
A program may use at most 128 MiB of HBM per device.

v0:
```python
import jax
import jax.numpy as jnp
from jax import lax
from jax.sharding import PartitionSpec as P

PCOL = 8
TILE = 128


def from_partner(value, axis, bit):
    mask = 2**bit
    pairs = [(source, source ^ mask) for source in range(lax.axis_size(axis))]
    return lax.ppermute(value, axis, pairs)


def product(left, right):
    return jnp.dot(left, right, precision=lax.Precision.HIGHEST, preferred_element_type=jnp.float32)


def inner_product(left, right):
    return lax.dot_general(
        left,
        right,
        (((0,), (0,)), ((), ())),
        precision=lax.Precision.HIGHEST,
        preferred_element_type=jnp.float32,
    )


def gather_high(segment, my_index, low_bits, total_bits):
    for bit_number in range(low_bits, total_bits):
        partner = from_partner(segment, "row", bit_number)
        upper_half = my_index >> bit_number & 1
        rows_now = segment.shape[0]
        segment = lax.dynamic_update_slice_in_dim(
            jnp.concatenate([partner, partner], 0), segment, upper_half * rows_now, 0
        )
    return segment


def reduce_low(partial_value, my_index, low_bits):
    for bit_number in reversed(range(low_bits)):
        half_rows = partial_value.shape[0] // 2
        upper_half = my_index >> bit_number & 1
        retained = lax.dynamic_slice_in_dim(partial_value, upper_half * half_rows, half_rows, 0)
        outgoing = lax.dynamic_slice_in_dim(
            partial_value, (1 - upper_half) * half_rows, half_rows, 0
        )
        partial_value = retained + from_partner(outgoing, "row", bit_number)
    return partial_value


def collect(segment, my_index, low_bits, total_bits):
    return gather_high(segment, my_index, low_bits, total_bits)


def apply_block(local_block, gathered, my_index, low_bits):
    partial_value = product(local_block, gathered)
    return reduce_low(partial_value, my_index, low_bits)


def on_device(anc_blocks, anc_links, parent_links, pivot_inverse, pattern):
    my_index = lax.axis_index("row")
    total_bits = lax.axis_size("row").bit_length() - 1
    low_bits = PCOL.bit_length() - 1
    rows_here = anc_links.shape[0]
    node_count = anc_links.shape[1]
    local_block = anc_blocks[0]
    tile_index = (my_index * rows_here + jnp.arange(rows_here, dtype=jnp.int32)) // TILE
    onehot = (tile_index[:, None] == jnp.arange(pattern.shape[1], dtype=jnp.int32)[None, :]).astype(
        jnp.float32
    )
    row_keep = jnp.dot(onehot, pattern.T.astype(jnp.float32), preferred_element_type=jnp.float32)
    masked = anc_links * row_keep[:, :, None]
    panels = []
    parents = []
    diagonals = []
    for super_node in range(node_count):
        link_panel = masked[:, super_node]
        gathered = collect(link_panel, my_index, low_bits, total_bits)
        image_rows = apply_block(local_block, gathered, my_index, low_bits)
        if super_node > 0:
            parent_link = parent_links[super_node - 1]
            cross_total = lax.psum(inner_product(panels[-1], link_panel), "row")
            inverse_panel = -(image_rows + product(panels[-1], parent_link))
            parent_block = -(cross_total + product(diagonals[-1], parent_link))
        else:
            inverse_panel = -image_rows
        quad_term = inner_product(link_panel, inverse_panel)
        quad_total = lax.psum(quad_term, "row")
        diagonal = pivot_inverse[super_node] - quad_total
        if super_node > 0:
            diagonal = diagonal - inner_product(parent_link, parent_block)
            parents.append(parent_block)
        panels.append(inverse_panel)
        diagonals.append(diagonal)
    return (jnp.stack(panels, axis=1), jnp.stack(parents), jnp.stack(diagonals))


def solution(mesh):
    return jax.shard_map(
        on_device,
        mesh=mesh,
        in_specs=(
            P(("pole", "row"), None, None),
            P(("pole", "row"), None, None),
            P("pole", None, None),
            P("pole", None, None),
            P(),
        ),
        out_specs=(P(("pole", "row"), None, None), P("pole", None, None), P("pole", None, None)),
        check_vma=False,
    )
```

profile of v0, /device:TPU:0, one launch (start us, length us, event | category | flops | bytes accessed | tf_op | source)
XLA Modules:
  0.0 253.6 jit_solution(15291808671186897176)
XLA Ops:
  9.3 4.1 %collective-permute-start.28 = (f32[48,256]{1,0:T(8,128)S(1)}, f32[48,256]{1,0:T(8,128)S(1)}, u32[]{:S(2)}, u32[]{:S(2)}) collective-permute-start(f32[48,256]{1,0:T(8,128)S(1)} %get-tuple-element.32), channel_id=1, source_target_pairs={{0,8},{1,9},{2,10},{3,11},{4,12},{5,13},{6,14},{7,15},{8,0},{9,1},... | collective-permute-start | bytes 147464 | tf_op jit(solution)/shard_map/ppermute | solution.py:13
  13.5 2.8 %collective-permute-start.20 = (f32[48,256]{1,0:T(8,128)S(1)}, f32[48,256]{1,0:T(8,128)S(1)}, u32[]{:S(2)}, u32[]{:S(2)}) collective-permute-start(f32[48,256]{1,0:T(8,128)S(1)} %get-tuple-element.34), channel_id=1, source_target_pairs={{0,8},{1,9},{2,10},{3,11},{4,12},{5,13},{6,14},{7,15},{8,0},{9,1},... | collective-permute-start | bytes 147464 | tf_op jit(solution)/shard_map/ppermute | solution.py:13
  16.4 2.8 %collective-permute-start.12 = (f32[48,256]{1,0:T(8,128)S(1)}, f32[48,256]{1,0:T(8,128)S(1)}, u32[]{:S(2)}, u32[]{:S(2)}) collective-permute-start(f32[48,256]{1,0:T(8,128)S(1)} %get-tuple-element.36), channel_id=1, source_target_pairs={{0,8},{1,9},{2,10},{3,11},{4,12},{5,13},{6,14},{7,15},{8,0},{9,1},... | collective-permute-start | bytes 147464 | tf_op jit(solution)/shard_map/ppermute | solution.py:13
  19.4 2.5 collective-permute-done.24
  22.3 2.2 collective-permute-done.20
  25.6 1.6 collective-permute-done.12
  27.1 1.6 collective-permute-done.8
  28.7 1.3 collective-permute-done.4
  31.3 2.4 collective-permute-start.29
  35.1 2.1 collective-permute-start.21
  38.6 2.1 collective-permute-start.13
  43.2 3.3 %collective-permute-done.25 = f32[192,256]{0,1:T(8,128)S(1)} collective-permute-done((f32[192,256]{0,1:T(8,128)S(1)}, f32[192,256]{0,1:T(8,128)S(1)}, u32[]{:S(2)}, u32[]{:S(2)}) %collective-permute-start.25) | collective-permute-done | bytes 196640 | tf_op jit(solution)/shard_map/ppermute | solution.py:13
  46.5 2.0 collective-permute-start.5
  48.7 3.5 %collective-permute-done.21 = f32[192,256]{0,1:T(8,128)S(1)} collective-permute-done((f32[192,256]{0,1:T(8,128)S(1)}, f32[192,256]{0,1:T(8,128)S(1)}, u32[]{:S(2)}, u32[]{:S(2)}) %collective-permute-start.21) | collective-permute-done | bytes 196640 | tf_op jit(solution)/shard_map/ppermute | solution.py:13
  52.1 2.0 collective-permute-start.1
  54.5 3.2 %collective-permute-done.17 = f32[192,256]{0,1:T(8,128)S(1)} collective-permute-done((f32[192,256]{0,1:T(8,128)S(1)}, f32[192,256]{0,1:T(8,128)S(1)}, u32[]{:S(2)}, u32[]{:S(2)}) %collective-permute-start.17) | collective-permute-done | bytes 196640 | tf_op jit(solution)/shard_map/ppermute | solution.py:13
  57.7 1.5 collective-permute-start.30
  59.4 4.0 %collective-permute-done.13 = f32[192,256]{0,1:T(8,128)S(1)} collective-permute-done((f32[192,256]{0,1:T(8,128)S(1)}, f32[192,256]{0,1:T(8,128)S(1)}, u32[]{:S(2)}, u32[]{:S(2)}) %collective-permute-start.13) | collective-permute-done | bytes 196640 | tf_op jit(solution)/shard_map/ppermute | solution.py:13
  63.4 1.5 collective-permute-start.26
  65.2 3.8 %collective-permute-done.9 = f32[192,256]{0,1:T(8,128)S(1)} collective-permute-done((f32[192,256]{0,1:T(8,128)S(1)}, f32[192,256]{0,1:T(8,128)S(1)}, u32[]{:S(2)}, u32[]{:S(2)}) %collective-permute-start.9) | collective-permute-done | bytes 196640 | tf_op jit(solution)/shard_map/ppermute | solution.py:13
  69.0 1.5 collective-permute-start.22
  70.6 4.0 %collective-permute-done.5 = f32[192,256]{0,1:T(8,128)S(1)} collective-permute-done((f32[192,256]{0,1:T(8,128)S(1)}, f32[192,256]{0,1:T(8,128)S(1)}, u32[]{:S(2)}, u32[]{:S(2)}) %collective-permute-start.5) | collective-permute-done | bytes 196640 | tf_op jit(solution)/shard_map/ppermute | solution.py:13
  74.6 1.5 collective-permute-start.18
  76.5 1.8 collective-permute-done.1
  78.3 1.5 collective-permute-start.14
  80.9 1.6 collective-permute-start.6
  85.0 2.6 %collective-permute-done.10 = f32[96,256]{0,1:T(8,128)S(1)} collective-permute-done((f32[96,256]{0,1:T(8,128)S(1)}, f32[96,256]{0,1:T(8,128)S(1)}, u32[]{:S(2)}, u32[]{:S(2)}) %collective-permute-start.10) | collective-permute-done | bytes 98336 | tf_op jit(solution)/shard_map/ppermute | solution.py:13
  87.8 3.0 %collective-permute-done.2 = f32[96,256]{0,1:T(8,128)S(1)} collective-permute-done((f32[96,256]{0,1:T(8,128)S(1)}, f32[96,256]{0,1:T(8,128)S(1)}, u32[]{:S(2)}, u32[]{:S(2)}) %collective-permute-start.2) | collective-permute-done | bytes 98336 | tf_op jit(solution)/shard_map/ppermute | solution.py:13
  117.0 1.5 stack.86
  118.5 116.2 %all-reduce.3.cloned.1.call-done = (f32[256,256]{1,0:T(8,128)}, f32[256,256]{1,0:T(8,128)}, f32[256,256]{1,0:T(8,128)}, f32[256,256]{1,0:T(8,128)}, f32[256,256]...) async-done(((f32[256,256]{1,0:T(8,128)}, ...) | async-done | bytes 3932176 | tf_op jit(solution)/shard_map/psum | solution.py:84
  236.0 1.5 bitcast_dynamic-update-slice_fusion.13
  237.6 1.6 bitcast_dynamic-update-slice_fusion.5
  (179 shorter events, 50.0 us)
Async XLA Ops:
  7.2 227.6 %all-reduce.3.cloned.1.call-start = ((), (), s32[]{:S(2)}) async-start(), calls=%async_computation | async-start | bytes 7864320 | tf_op jit(solution)/shard_map/psum | solution.py:84
  9.3 10.0 %collective-permute-start.28 = (f32[48,256]{1,0:T(8,128)S(1)}, f32[48,256]{1,0:T(8,128)S(1)}, u32[]{:S(2)}, u32[]{:S(2)}) collective-permute-start(f32[48,256]{1,0:T(8,128)S(1)} %get-tuple-element.32), channel_id=1, source_target_pairs={{0,8},{1,9},{2,10},{3,11},{4,12},{5,13},{6,14},{7,15},{8,0},{9,1},... | collective-permute-start | bytes 147464 | tf_op jit(solution)/shard_map/ppermute | solution.py:13
  13.4 8.4 %collective-permute-start.24 = (f32[48,256]{1,0:T(8,128)S(1)}, f32[48,256]{1,0:T(8,128)S(1)}, u32[]{:S(2)}, u32[]{:S(2)}) collective-permute-start(f32[48,256]{1,0:T(8,128)S(1)} %get-tuple-element.33), channel_id=1, source_target_pairs={{0,8},{1,9},{2,10},{3,11},{4,12},{5,13},{6,14},{7,15},{8,0},{9,1},... | collective-permute-start | bytes 147464 | tf_op jit(solution)/shard_map/ppermute | solution.py:13
  13.5 11.0 %collective-permute-start.20 = (f32[48,256]{1,0:T(8,128)S(1)}, f32[48,256]{1,0:T(8,128)S(1)}, u32[]{:S(2)}, u32[]{:S(2)}) collective-permute-start(f32[48,256]{1,0:T(8,128)S(1)} %get-tuple-element.34), channel_id=1, source_target_pairs={{0,8},{1,9},{2,10},{3,11},{4,12},{5,13},{6,14},{7,15},{8,0},{9,1},... | collective-permute-start | bytes 147464 | tf_op jit(solution)/shard_map/ppermute | solution.py:13
  16.4 9.2 %collective-permute-start.16 = (f32[48,256]{1,0:T(8,128)S(1)}, f32[48,256]{1,0:T(8,128)S(1)}, u32[]{:S(2)}, u32[]{:S(2)}) collective-permute-start(f32[48,256]{1,0:T(8,128)S(1)} %get-tuple-element.35), channel_id=1, source_target_pairs={{0,8},{1,9},{2,10},{3,11},{4,12},{5,13},{6,14},{7,15},{8,0},{9,1},... | collective-permute-start | bytes 147464 | tf_op jit(solution)/shard_map/ppermute | solution.py:13
  16.4 10.7 %collective-permute-start.12 = (f32[48,256]{1,0:T(8,128)S(1)}, f32[48,256]{1,0:T(8,128)S(1)}, u32[]{:S(2)}, u32[]{:S(2)}) collective-permute-start(f32[48,256]{1,0:T(8,128)S(1)} %get-tuple-element.36), channel_id=1, source_target_pairs={{0,8},{1,9},{2,10},{3,11},{4,12},{5,13},{6,14},{7,15},{8,0},{9,1},... | collective-permute-start | bytes 147464 | tf_op jit(solution)/shard_map/ppermute | solution.py:13
  19.3 9.4 %collective-permute-start.8 = (f32[48,256]{1,0:T(8,128)S(1)}, f32[48,256]{1,0:T(8,128)S(1)}, u32[]{:S(2)}, u32[]{:S(2)}) collective-permute-start(f32[48,256]{1,0:T(8,128)S(1)} %get-tuple-element.37), channel_id=1, source_target_pairs={{0,8},{1,9},{2,10},{3,11},{4,12},{5,13},{6,14},{7,15},{8,0},{9,1},... | collective-permute-start | bytes 147464 | tf_op jit(solution)/shard_map/ppermute | solution.py:13
  21.9 8.1 %collective-permute-start.4 = (f32[48,256]{1,0:T(8,128)S(1)}, f32[48,256]{1,0:T(8,128)S(1)}, u32[]{:S(2)}, u32[]{:S(2)}) collective-permute-start(f32[48,256]{1,0:T(8,128)S(1)} %get-tuple-element.38), channel_id=1, source_target_pairs={{0,8},{1,9},{2,10},{3,11},{4,12},{5,13},{6,14},{7,15},{8,0},{9,1},... | collective-permute-start | bytes 147464 | tf_op jit(solution)/shard_map/ppermute | solution.py:13
  24.5 6.1 %collective-permute-start = (f32[48,256]{1,0:T(8,128)S(1)}, f32[48,256]{1,0:T(8,128)S(1)}, u32[]{:S(2)}, u32[]{:S(2)}) collective-permute-start(f32[48,256]{1,0:T(8,128)S(1)} %get-tuple-element.39), channel_id=1, source_target_pairs={{0,8},{1,9},{2,10},{3,11},{4,12},{5,13},{6,14},{7,15},{8,0},{9,1},... | collective-permute-start | bytes 147464 | tf_op jit(solution)/shard_map/ppermute | solution.py:13
  31.3 11.5 %collective-permute-start.29 = (f32[192,256]{0,1:T(8,128)S(1)}, f32[192,256]{0,1:T(8,128)S(1)}, u32[]{:S(2)}, u32[]{:S(2)}) collective-permute-start(f32[192,256]{0,1:T(8,128)S(1)} %dynamic-slice_bitcast_fusion), channel_id=1, source_target_pairs={{0,4},{1,5},{2,6},{3,7},{4,0},{5,1},{6,2},{7,3},{8,12},{9,13},{10,... | collective-permute-start | bytes 589832 | tf_op jit(solution)/shard_map/ppermute | solution.py:13
  34.4 12.2 %collective-permute-start.25 = (f32[192,256]{0,1:T(8,128)S(1)}, f32[192,256]{0,1:T(8,128)S(1)}, u32[]{:S(2)}, u32[]{:S(2)}) collective-permute-start(f32[192,256]{0,1:T(8,128)S(1)} %dynamic-slice_bitcast_fusion.1), channel_id=1, source_target_pairs={{0,4},{1,5},{2,6},{3,7},{4,0},{5,1},{6,2},{7,3},{8,12},{9,13},{10,... | collective-permute-start | bytes 589832 | tf_op jit(solution)/shard_map/ppermute | solution.py:13
  35.1 17.0 %collective-permute-start.21 = (f32[192,256]{0,1:T(8,128)S(1)}, f32[192,256]{0,1:T(8,128)S(1)}, u32[]{:S(2)}, u32[]{:S(2)}) collective-permute-start(f32[192,256]{0,1:T(8,128)S(1)} %dynamic-slice_bitcast_fusion.2), channel_id=1, source_target_pairs={{0,4},{1,5},{2,6},{3,7},{4,0},{5,1},{6,2},{7,3},{8,12},{9,13},{10,... | collective-permute-start | bytes 589832 | tf_op jit(solution)/shard_map/ppermute | solution.py:13
  37.9 19.9 %collective-permute-start.17 = (f32[192,256]{0,1:T(8,128)S(1)}, f32[192,256]{0,1:T(8,128)S(1)}, u32[]{:S(2)}, u32[]{:S(2)}) collective-permute-start(f32[192,256]{0,1:T(8,128)S(1)} %dynamic-slice_bitcast_fusion.3), channel_id=1, source_target_pairs={{0,4},{1,5},{2,6},{3,7},{4,0},{5,1},{6,2},{7,3},{8,12},{9,13},{10,... | collective-permute-start | bytes 589832 | tf_op jit(solution)/shard_map/ppermute | solution.py:13
  38.6 24.7 %collective-permute-start.13 = (f32[192,256]{0,1:T(8,128)S(1)}, f32[192,256]{0,1:T(8,128)S(1)}, u32[]{:S(2)}, u32[]{:S(2)}) collective-permute-start(f32[192,256]{0,1:T(8,128)S(1)} %dynamic-slice_bitcast_fusion.4), channel_id=1, source_target_pairs={{0,4},{1,5},{2,6},{3,7},{4,0},{5,1},{6,2},{7,3},{8,12},{9,13},{10,... | collective-permute-start | bytes 589832 | tf_op jit(solution)/shard_map/ppermute | solution.py:13
  42.8 26.2 %collective-permute-start.9 = (f32[192,256]{0,1:T(8,128)S(1)}, f32[192,256]{0,1:T(8,128)S(1)}, u32[]{:S(2)}, u32[]{:S(2)}) collective-permute-start(f32[192,256]{0,1:T(8,128)S(1)} %dynamic-slice_bitcast_fusion.5), channel_id=1, source_target_pairs={{0,4},{1,5},{2,6},{3,7},{4,0},{5,1},{6,2},{7,3},{8,12},{9,13},{10,... | collective-permute-start | bytes 589832 | tf_op jit(solution)/shard_map/ppermute | solution.py:13
  46.5 28.1 %collective-permute-start.5 = (f32[192,256]{0,1:T(8,128)S(1)}, f32[192,256]{0,1:T(8,128)S(1)}, u32[]{:S(2)}, u32[]{:S(2)}) collective-permute-start(f32[192,256]{0,1:T(8,128)S(1)} %dynamic-slice_bitcast_fusion.6), channel_id=1, source_target_pairs={{0,4},{1,5},{2,6},{3,7},{4,0},{5,1},{6,2},{7,3},{8,12},{9,13},{10,... | collective-permute-start | bytes 589832 | tf_op jit(solution)/shard_map/ppermute | solution.py:13
  52.1 26.2 %collective-permute-start.1 = (f32[192,256]{0,1:T(8,128)S(1)}, f32[192,256]{0,1:T(8,128)S(1)}, u32[]{:S(2)}, u32[]{:S(2)}) collective-permute-start(f32[192,256]{0,1:T(8,128)S(1)} %dynamic-slice_bitcast_fusion.7), channel_id=1, source_target_pairs={{0,4},{1,5},{2,6},{3,7},{4,0},{5,1},{6,2},{7,3},{8,12},{9,13},{10,... | collective-permute-start | bytes 589832 | tf_op jit(solution)/shard_map/ppermute | solution.py:13
  57.7 22.3 %collective-permute-start.30 = (f32[96,256]{0,1:T(8,128)S(1)}, f32[96,256]{0,1:T(8,128)S(1)}, u32[]{:S(2)}, u32[]{:S(2)}) collective-permute-start(f32[96,256]{0,1:T(8,128)S(1)} %constant_dynamic-slice_fusion.1), channel_id=1, source_target_pairs={{0,2},{1,3},{2,0},{3,1},{4,6},{5,7},{6,4},{7,5},{8,10},{9,11},{10,... | collective-permute-start | bytes 294920 | tf_op jit(solution)/shard_map/ppermute | solution.py:13
  63.4 17.5 %collective-permute-start.26 = (f32[96,256]{0,1:T(8,128)S(1)}, f32[96,256]{0,1:T(8,128)S(1)}, u32[]{:S(2)}, u32[]{:S(2)}) collective-permute-start(f32[96,256]{0,1:T(8,128)S(1)} %constant_dynamic-slice_fusion.3), channel_id=1, source_target_pairs={{0,2},{1,3},{2,0},{3,1},{4,6},{5,7},{6,4},{7,5},{8,10},{9,11},{10,... | collective-permute-start | bytes 294920 | tf_op jit(solution)/shard_map/ppermute | solution.py:13
  69.0 13.7 %collective-permute-start.22 = (f32[96,256]{0,1:T(8,128)S(1)}, f32[96,256]{0,1:T(8,128)S(1)}, u32[]{:S(2)}, u32[]{:S(2)}) collective-permute-start(f32[96,256]{0,1:T(8,128)S(1)} %constant_dynamic-slice_fusion.5), channel_id=1, source_target_pairs={{0,2},{1,3},{2,0},{3,1},{4,6},{5,7},{6,4},{7,5},{8,10},{9,11},{10,... | collective-permute-start | bytes 294920 | tf_op jit(solution)/shard_map/ppermute | solution.py:13
  74.6 8.9 %collective-permute-start.18 = (f32[96,256]{0,1:T(8,128)S(1)}, f32[96,256]{0,1:T(8,128)S(1)}, u32[]{:S(2)}, u32[]{:S(2)}) collective-permute-start(f32[96,256]{0,1:T(8,128)S(1)} %constant_dynamic-slice_fusion.7), channel_id=1, source_target_pairs={{0,2},{1,3},{2,0},{3,1},{4,6},{5,7},{6,4},{7,5},{8,10},{9,11},{10,... | collective-permute-start | bytes 294920 | tf_op jit(solution)/shard_map/ppermute | solution.py:13
  78.3 6.4 %collective-permute-start.14 = (f32[96,256]{0,1:T(8,128)S(1)}, f32[96,256]{0,1:T(8,128)S(1)}, u32[]{:S(2)}, u32[]{:S(2)}) collective-permute-start(f32[96,256]{0,1:T(8,128)S(1)} %constant_dynamic-slice_fusion.9), channel_id=1, source_target_pairs={{0,2},{1,3},{2,0},{3,1},{4,6},{5,7},{6,4},{7,5},{8,10},{9,11},{10,... | collective-permute-start | bytes 294920 | tf_op jit(solution)/shard_map/ppermute | solution.py:13
  80.1 7.5 %collective-permute-start.10 = (f32[96,256]{0,1:T(8,128)S(1)}, f32[96,256]{0,1:T(8,128)S(1)}, u32[]{:S(2)}, u32[]{:S(2)}) collective-permute-start(f32[96,256]{0,1:T(8,128)S(1)} %constant_dynamic-slice_fusion.11), channel_id=1, source_target_pairs={{0,2},{1,3},{2,0},{3,1},{4,6},{5,7},{6,4},{7,5},{8,10},{9,11},{10,... | collective-permute-start | bytes 294920 | tf_op jit(solution)/shard_map/ppermute | solution.py:13
  80.9 10.1 %collective-permute-start.6 = (f32[96,256]{0,1:T(8,128)S(1)}, f32[96,256]{0,1:T(8,128)S(1)}, u32[]{:S(2)}, u32[]{:S(2)}) collective-permute-start(f32[96,256]{0,1:T(8,128)S(1)} %constant_dynamic-slice_fusion.13), channel_id=1, source_target_pairs={{0,2},{1,3},{2,0},{3,1},{4,6},{5,7},{6,4},{7,5},{8,10},{9,11},{10,... | collective-permute-start | bytes 294920 | tf_op jit(solution)/shard_map/ppermute | solution.py:13
  82.7 8.1 %collective-permute-start.2 = (f32[96,256]{0,1:T(8,128)S(1)}, f32[96,256]{0,1:T(8,128)S(1)}, u32[]{:S(2)}, u32[]{:S(2)}) collective-permute-start(f32[96,256]{0,1:T(8,128)S(1)} %constant_dynamic-slice_fusion.15), channel_id=1, source_target_pairs={{0,2},{1,3},{2,0},{3,1},{4,6},{5,7},{6,4},{7,5},{8,10},{9,11},{10,... | collective-permute-start | bytes 294920 | tf_op jit(solution)/shard_map/ppermute | solution.py:13
  83.5 31.0 %collective-permute-start.31 = (f32[48,256]{0,1:T(8,128)S(1)}, f32[48,256]{0,1:T(8,128)S(1)}, u32[]{:S(2)}, u32[]{:S(2)}) collective-permute-start(f32[48,256]{0,1:T(8,128)S(1)} %constant_dynamic-slice_fusion), channel_id=1, source_target_pairs={{0,1},{1,0},{2,3},{3,2},{4,5},{5,4},{6,7},{7,6},{8,9},{9,8},{10,11... | collective-permute-start | bytes 147464 | tf_op jit(solution)/shard_map/ppermute | solution.py:13
  84.7 13.9 %collective-permute-start.27 = (f32[48,256]{0,1:T(8,128)S(1)}, f32[48,256]{0,1:T(8,128)S(1)}, u32[]{:S(2)}, u32[]{:S(2)}) collective-permute-start(f32[48,256]{0,1:T(8,128)S(1)} %constant_dynamic-slice_fusion.2), channel_id=1, source_target_pairs={{0,1},{1,0},{2,3},{3,2},{4,5},{5,4},{6,7},{7,6},{8,9},{9,8},{10,11... | collective-permute-start | bytes 147464 | tf_op jit(solution)/shard_map/ppermute | solution.py:13
  87.5 10.3 %collective-permute-start.23 = (f32[48,256]{0,1:T(8,128)S(1)}, f32[48,256]{0,1:T(8,128)S(1)}, u32[]{:S(2)}, u32[]{:S(2)}) collective-permute-start(f32[48,256]{0,1:T(8,128)S(1)} %constant_dynamic-slice_fusion.4), channel_id=1, source_target_pairs={{0,1},{1,0},{2,3},{3,2},{4,5},{5,4},{6,7},{7,6},{8,9},{9,8},{10,11... | collective-permute-start | bytes 147464 | tf_op jit(solution)/shard_map/ppermute | solution.py:13
  90.8 6.4 %collective-permute-start.19 = (f32[48,256]{0,1:T(8,128)S(1)}, f32[48,256]{0,1:T(8,128)S(1)}, u32[]{:S(2)}, u32[]{:S(2)}) collective-permute-start(f32[48,256]{0,1:T(8,128)S(1)} %constant_dynamic-slice_fusion.6), channel_id=1, source_target_pairs={{0,1},{1,0},{2,3},{3,2},{4,5},{5,4},{6,7},{7,6},{8,9},{9,8},{10,11... | collective-permute-start | bytes 147464 | tf_op jit(solution)/shard_map/ppermute | solution.py:13
  91.0 1.6 collective-permute-start.3
  92.6 1.3 collective-permute-start.7
  93.9 1.3 collective-permute-start.11
  (19 other events, 59.6 us)
Sparse Core Ops, SparseCore 0:
  116.4 118.2 all-reduce.2
where the time goes:
time: 254 us
  waiting for transfers between devices  159 us (63%)
  matrix products  34.9 us (14%)
  starting transfers between devices  33.7 us (13%)
  between operations  15 us (6%)
  local copies, waits for them, and re-layouts  6.31 us (2%)
  other arithmetic  4.45 us (2%)
    psum x1, waiting for transfers between devices, on_device(): cross_total = lax.psum(inner_product(panels[-1], link_panel), 'row')  116 us
    ppermute x32, waiting for transfers between devices, from_partner(): return lax.ppermute(value, axis, pairs)  43 us
    ppermute x32, starting transfers between devices, from_partner(): return lax.ppermute(value, axis, pairs)  33.7 us
    dot_general x22, matrix products, inner_product(): lax.dot_general(left, right, (((0,), (0,)), ((), ())), precision=lax.Prec...  21.7 us
    dot_general x22, matrix products, product(): jnp.dot(left, right, precision=lax.Precision.HIGHEST, preferred_element_t...  12.4 us
  transfers between devices with their start and end apart: 33, of which 22 were waited for; matrix products, arithmetic and copies ran while one was open for 12% of the time, Pallas kernels for 0%

commit v1 on v0

v1 whole, which is shorter than its diff:
```python
import jax
import jax.numpy as jnp
from jax import lax
from jax.sharding import PartitionSpec as P

PCOL = 8
TILE = 128
GATHER_LIMIT = 16 * 2**20


def product(left, right):
    return jnp.dot(left, right, precision=lax.Precision.HIGH, preferred_element_type=jnp.float32)


def inner_product(left, right):
    return lax.dot_general(
        left,
        right,
        (((0,), (0,)), ((), ())),
        precision=lax.Precision.HIGH,
        preferred_element_type=jnp.float32,
    )


def swap_bit(value, bit):
    mask = 2**bit
    return lax.ppermute(value, "row", [(i, i ^ mask) for i in range(lax.axis_size("row"))])


def ring_chips(count):
    return list(range(0, count, 2)) + list(range(count - 1, 0, -2))


def ring_pairs(count, shift):
    order = ring_chips(count)
    pairs = []
    for place, chip in enumerate(order):
        target = order[(place + shift) % count]
        pairs += [(2 * chip + core, 2 * target + core) for core in range(2)]
    return pairs


def ring_place(chip, count):
    return jnp.where(chip % 2 == 0, chip // 2, count - 1 - chip // 2)


def ring_chip(place, count):
    return jnp.where(place < count // 2, 2 * place, 2 * (count - 1 - place) + 1)


def masked_links(my_index, anc_links, pattern):
    rows_here = anc_links.shape[0]
    tile_index = (my_index * rows_here + jnp.arange(rows_here, dtype=jnp.int32)) // TILE
    row_keep = jnp.take(pattern, tile_index, axis=1) != 0
    return jnp.where(row_keep[:, :, None], jnp.swapaxes(anc_links, 0, 1), 0.0)


def reduced_links(links, parent_links):
    reduced = [links[0]]
    for node in range(1, links.shape[0]):
        reduced.append(links[node] - product(reduced[-1], parent_links[node - 1]))
    return reduced


def local_chain(parent_links, pivot_inverse):
    inner = [pivot_inverse[0]]
    cross = []
    for node in range(1, pivot_inverse.shape[0]):
        link = parent_links[node - 1]
        cross.append(product(inner[-1], link))
        inner.append(pivot_inverse[node] + inner_product(link, cross[-1]))
    return inner, cross


def gather_rounds(message, my_index, count):
    core = my_index % 2
    place = ring_place(my_index // 2, count)

    def owner(shift, other):
        chip = ring_chip((place + shift + count) % count, count)
        return 2 * chip + jnp.where(other, 1 - core, core)

    ahead, behind = ring_pairs(count, 1), ring_pairs(count, -1)
    arrivals = [(owner(0, False), message), (owner(0, True), swap_bit(message, 0))]
    upward = downward = message
    for step in range(1, (count + 1) // 2):
        upward = lax.ppermute(upward, "row", ahead)
        downward = lax.ppermute(downward, "row", behind)
        arrivals += [(owner(-step, False), upward), (owner(step, False), downward)]
        arrivals += [(owner(-step, True), swap_bit(upward, 0)), (owner(step, True), swap_bit(downward, 0))]
    if count % 2 == 0 and count > 1:
        pairs = [p for p in ahead if p[0] % 2 == 0] + [p for p in behind if p[0] % 2 == 1]
        last = lax.ppermute(jnp.where(core == 0, upward, downward), "row", pairs)
        arrivals += [(owner(count // 2, False), last), (owner(count // 2, True), swap_bit(last, 0))]
    return arrivals


def gather_plan(anc_blocks, anc_links, parent_links, pivot_inverse, pattern):
    my_index = lax.axis_index("row")
    size = lax.axis_size("row")
    rows, nodes, width = anc_links.shape
    order = rows * size
    half = my_index // PCOL
    block = anc_blocks[0].T.reshape(2, rows, order // 2)
    mine = lax.dynamic_index_in_dim(block, half, 0, False)
    theirs = swap_bit(lax.dynamic_index_in_dim(block, 1 - half, 0, False), PCOL.bit_length() - 1)
    low, high = jnp.where(half == 0, mine, theirs), jnp.where(half == 0, theirs, mine)
    links = masked_links(my_index, anc_links, pattern)
    message = jnp.concatenate(reduced_links(links, parent_links) + [low, high], axis=1)
    inner, cross = local_chain(parent_links, pivot_inverse)
    whole = jnp.zeros((order, message.shape[1]), jnp.float32)
    for owner, part in gather_rounds(message, my_index, size // 2):
        whole = lax.dynamic_update_slice(whole, part, (owner * rows, 0))
    links, ancestor = whole[:, : nodes * width], whole[:, nodes * width :]
    image = product(ancestor, links)
    panels = -lax.dynamic_slice_in_dim(image, my_index * rows, rows, 0).reshape(rows, nodes, width)
    column = lambda array, node: array[:, node * width : (node + 1) * width]
    diagonals = [
        inner[node] + inner_product(column(links, node), column(image, node)) for node in range(nodes)
    ]
    parents = [
        inner_product(column(links, node - 1), column(image, node)) - cross[node - 1]
        for node in range(1, nodes)
    ]
    return panels, jnp.stack(parents), jnp.stack(diagonals)


def spread_plan(anc_blocks, anc_links, parent_links, pivot_inverse, pattern):
    my_index = lax.axis_index("row")
    total_bits = lax.axis_size("row").bit_length() - 1
    low_bits = PCOL.bit_length() - 1
    rows, nodes, width = anc_links.shape
    links = jnp.concatenate(reduced_links(masked_links(my_index, anc_links, pattern), parent_links), axis=1)
    segment = links
    for bit in range(low_bits, total_bits):
        partner = swap_bit(segment, bit)
        upper = my_index >> bit & 1
        segment = lax.dynamic_update_slice_in_dim(
            jnp.concatenate([partner, partner], 0), segment, upper * segment.shape[0], 0
        )
    image = product(anc_blocks[0], segment)
    for bit in reversed(range(low_bits)):
        half_rows = image.shape[0] // 2
        upper = my_index >> bit & 1
        retained = lax.dynamic_slice_in_dim(image, upper * half_rows, half_rows, 0)
        outgoing = lax.dynamic_slice_in_dim(image, (1 - upper) * half_rows, half_rows, 0)
        image = retained + swap_bit(outgoing, bit)
    column = lambda array, node: array[:, node * width : (node + 1) * width]
    terms = [inner_product(column(links, node), column(image, node)) for node in range(nodes)]
    terms += [inner_product(column(links, node - 1), column(image, node)) for node in range(1, nodes)]
    totals = lax.psum(jnp.stack(terms), "row")
    inner, cross = local_chain(parent_links, pivot_inverse)
    diagonals = jnp.stack(inner) + totals[:nodes]
    parents = totals[nodes:] - jnp.stack(cross)
    return -image.reshape(rows, nodes, width), parents, diagonals


def on_device(anc_blocks, anc_links, parent_links, pivot_inverse, pattern):
    size = lax.axis_size("row")
    rows, nodes, width = anc_links.shape
    whole_bytes = 4 * size * rows * (nodes * width + size * rows)
    plan = gather_plan if size == 2 * PCOL and whole_bytes <= GATHER_LIMIT else spread_plan
    return plan(anc_blocks, anc_links, parent_links, pivot_inverse, pattern)


def solution(mesh):
    return jax.shard_map(
        on_device,
        mesh=mesh,
        in_specs=(
            P(("pole", "row"), None, None),
            P(("pole", "row"), None, None),
            P("pole", None, None),
            P("pole", None, None),
            P(),
        ),
        out_specs=(P(("pole", "row"), None, None), P("pole", None, None), P("pole", None, None)),
        check_vma=False,
    )
```

time: 254 us -> 166 us (0.65)
  waiting for transfers between devices: 159 us -> 23.2 us
  matrix products: 34.9 us -> 77.6 us
  local copies, waits for them, and re-layouts: 6.31 us -> 43.3 us
  starting transfers between devices: 33.7 us -> 12.7 us
  between operations: 15 us -> 0.97 us
    psum x1 -> x0, waiting for transfers between devices: 116 us -> none  [on_device(): cross_total = lax.psum(inner_product(panels[-1], link_panel), 'row')]
    dot_general x22, matrix products: 21.7 us -> 50.8 us  [inner_product(): lax.dot_general(left, right, (((0,), (0,)), ((), ())), precision=lax.Prec...]
    ppermute x32 -> x16, starting transfers between devices: 33.7 us -> 12.7 us  [the longest x9 5.07 us: swap_bit(): lax.ppermute(value, 'row', [(i, i ^ mask) for i in range(lax.axis_size('r...]
    ppermute x32 -> x16, waiting for transfers between devices: 43 us -> 23.2 us  [the longest x3 23 us: gather_rounds(): upward = lax.ppermute(upward, 'row', ahead)]
    dynamic_update_slice x1 -> x15, local copies, waits for them, and re-layouts: 0.04 us -> 16.9 us  [gather_plan(): whole = lax.dynamic_update_slice(whole, part, (owner * rows, 0))]
    unnamed x36 -> x50, local copies, waits for them, and re-layouts: 1.39 us -> 17.6 us
    dot_general x23 -> x15, matrix products: 13.3 us -> 26.7 us  [product(): jnp.dot(left, right, precision=lax.Precision.HIGH, preferred_element_type...]
    broadcast_in_dim x0 -> x1, local copies, waits for them, and re-layouts: none -> 3.94 us  [gather_plan(): whole = jnp.zeros((order, message.shape[1]), jnp.float32)]
  transfers between devices with their start and end apart: 33 -> 16, of which waited for: 22 -> 4; matrix products, arithmetic and copies ran while one was open for 12% -> 38% of each run, Pallas kernels for 0% -> 0%
where the time goes in v1:
time: 166 us; the launch traced here: 164 us
  matrix products  77.6 us (47%)
  local copies, waits for them, and re-layouts  43.3 us (26%)
  waiting for transfers between devices  23.2 us (14%)
  starting transfers between devices  12.7 us (8%)
  other arithmetic  6.57 us (4%)
    dot_general x22, matrix products, inner_product(): lax.dot_general(left, right, (((0,), (0,)), ((), ())), precision=lax.Prec...  50.8 us
    dot_general x15, matrix products, product(): jnp.dot(left, right, precision=lax.Precision.HIGH, preferred_element_type...  26.7 us
    ppermute x3, waiting for transfers between devices, gather_rounds(): upward = lax.ppermute(upward, 'row', ahead)  23 us
    unnamed x50, local copies, waits for them, and re-layouts  17.6 us
    dynamic_update_slice x15, local copies, waits for them, and re-layouts, gather_plan(): whole = lax.dynamic_update_slice(whole, part, (owner * rows, 0))  16.9 us
    ppermute x9, starting transfers between devices, swap_bit(): lax.ppermute(value, 'row', [(i, i ^ mask) for i in range(lax.axis_size('r...  5.07 us
    ppermute x3, starting transfers between devices, gather_rounds(): upward = lax.ppermute(upward, 'row', ahead)  4.73 us
    broadcast_in_dim x1, local copies, waits for them, and re-layouts, gather_plan(): whole = jnp.zeros((order, message.shape[1]), jnp.float32)  3.94 us
  transfers between devices with their start and end apart: 16, of which 4 were waited for; matrix products, arithmetic and copies ran while one was open for 38% of the time, Pallas kernels for 0%

profile of v1, /device:TPU:0, one launch (start us, length us, event | category | flops | bytes accessed | tf_op | source)
XLA Modules:
  0.0 164.4 jit_solution(16138278124431974538)
XLA Ops:
  2.3 4.0 %collective-permute-start = (f32[48,384]{1,0:T(8,128)}, f32[48,384]{1,0:T(8,128)}, u32[]{:S(2)}, u32[]{:S(2)}) collective-permute-start(f32[48,384]{1,0:T(8,128)} %dynamic-slice_bitcast_fusion), channel_id=1, source_target_pairs={{0,8},{1,9},{2,10},{3,11},{4,12},{5,13},{6,14},{7,15},{8,0},{9,1},... | collective-permute-start | bytes 221192 | tf_op jit(solution)/shard_map/ppermute | solution.py:27
  9.8 2.6 %fusion.126 = (f32[1,256,256]{2,1,0:T(8,128)}, f32[1,256,256]{2,1,0:T(8,128)}, f32[1,256,256]{2,1,0:T(8,128)}, f32[1,256,256]{2,1,0:T(8,128)}, f32[1,256,256]{2,...) fusion(f32[8,256,256]{2,1,0:T(8,128)} %param.8), kind=kLoop, calls=%fused_computation.206 | loop fusion | bytes 4194304 | tf_op jit(solution)/shard_map/slice | solution.py:71
  20.6 1.8 %copy.40 = f32[1,256,256]{1,2,0:T(8,128)} copy(f32[1,256,256]{2,1,0:T(8,128)} %get-tuple-element.9) | data formatting | bytes 524288
  34.8 2.0 %fusion.5 = f32[256,256]{0,1:T(8,128)} fusion(f32[256,256]{1,0:T(8,128)S(1)} %fusion.82, f32[1,256,256]{1,2,0:T(8,128)} %copy.41, f32[7,256,256]{2,1,0:T(8,128)S(1)} %copy-done.1), kind=kOutput, calls=%fused_computation.18 | convolution fusion | flops 100728832 | bytes 1048576 | tf_op jit(solution)/shard_map/dot_general | solution.py:16
  45.8 3.9 %broadcast_in_dim.26 = f32[768,2816]{1,0:T(8,128)} broadcast(f32[]{:T(128)} %constant.148.clone.1), dimensions={} | broadcast | bytes 8650756 | tf_op jit(solution)/shard_map/broadcast_in_dim | solution.py:111
  49.8 1.9 %constant_dynamic-update-slice_fusion.22 = f32[768,2816]{1,0:T(8,128)} fusion(f32[768,2816]{1,0:T(8,128)} %broadcast_in_dim.26, f32[48,2816]{1,0:T(8,128)} %fusion.122, s32[]{:T(128)S(6)} %select_n.262), kind=kLoop, calls=%fused_computation.191 | loop fusion | bytes 1081348 | tf_op jit(solution)/shard_map/dynamic_update_slice | solution.py:113
  51.6 5.7 %collective-permute-done.2 = f32[48,2816]{1,0:T(8,128)S(1)} collective-permute-done((f32[48,2816]{1,0:T(8,128)}, f32[48,2816]{1,0:T(8,128)S(1)}, u32[]{:S(2)}, u32[]{:S(2)}) %collective-permute-start.2) | collective-permute-done | bytes 540704 | tf_op jit(solution)/shard_map/ppermute | solution.py:87
  62.2 9.9 %collective-permute-done.6 = f32[48,2816]{1,0:T(8,128)S(1)} collective-permute-done((f32[48,2816]{1,0:T(8,128)S(1)}, f32[48,2816]{1,0:T(8,128)S(1)}, u32[]{:S(2)}, u32[]{:S(2)}) %collective-permute-start.6) | collective-permute-done | bytes 540704 | tf_op jit(solution)/shard_map/ppermute | solution.py:87
  79.4 7.5 %collective-permute-done.10 = f32[48,2816]{1,0:T(8,128)} collective-permute-done((f32[48,2816]{1,0:T(8,128)S(1)}, f32[48,2816]{1,0:T(8,128)}, u32[]{:S(2)}, u32[]{:S(2)}) %collective-permute-start.10) | collective-permute-done | bytes 540704 | tf_op jit(solution)/shard_map/ppermute | solution.py:87
  86.8 1.9 %constant_dynamic-update-slice_fusion.12 = f32[768,2816]{1,0:T(8,128)} fusion(f32[768,2816]{1,0:T(8,128)} %constant_dynamic-update-slice_fusion.13, f32[48,2816]{1,0:T(8,128)} %collective-permute-done.10, s32[]{:T(128)S(6)} %select_n.282), kind=kLoop, calls=%fused_computation.181 | loop fusion | bytes 1081348 | tf_op jit(solution)/shard_map/dynamic_update_slice | solution.py:113
  89.5 2.1 %broadcast_select_fusion = (f32[48,2816]{1,0:T(8,128)}, f32[768,2816]{1,0:T(8,128)}) fusion(f32[48,2816]{1,0:T(8,128)} %collective-permute-done.10, f32[48,2816]{1,0:T(8,128)S(1)} %collective-permute-done.11, pred[]{:T(512)S(6)} %eq.31, f32[768,2816]{1,0:T(8,128)} %constant_dynamic-update-slice_fusion.12, s32[]{:T(128)S(6)} %select_n.285), kind=kLoop, calls=%fused_computation.103 | loop fusion | flops 135168 | bytes 2162693 | tf_op jit(solution)/shard_map/jit(_where)/select_n | solution.py:93
  94.3 1.8 %copy.36 = f32[1,256,256]{1,2,0:T(8,128)} copy(f32[1,256,256]{2,1,0:T(8,128)} %get-tuple-element.13) | data formatting | bytes 524288
  96.1 1.8 %copy.43 = f32[1,256,256]{1,2,0:T(8,128)} copy(f32[1,256,256]{2,1,0:T(8,128)} %get-tuple-element.6) | data formatting | bytes 524288
  101.3 1.9 %constant_dynamic-update-slice_fusion.10 = f32[768,2816]{1,0:T(8,128)} fusion(f32[768,2816]{1,0:T(8,128)} %get-tuple-element.15, f32[48,2816]{1,0:T(8,128)} %collective-permute-done.12, s32[]{:T(128)S(6)} %select_n.286), kind=kLoop, calls=%fused_computation.179 | loop fusion | bytes 1081348 | tf_op jit(solution)/shard_map/dynamic_update_slice | solution.py:113
  104.0 1.9 %constant_dynamic-update-slice_fusion.8 = f32[768,2816]{1,0:T(8,128)} fusion(f32[768,2816]{1,0:T(8,128)} %constant_dynamic-update-slice_fusion.9, f32[48,2816]{1,0:T(8,128)} %collective-permute-done.14, s32[]{:T(128)S(6)} %select_n.292), kind=kLoop, calls=%fused_computation.177 | loop fusion | bytes 1081348 | tf_op jit(solution)/shard_map/dynamic_update_slice | solution.py:113
  106.9 10.6 %fusion = f32[768,2048]{1,0:T(8,128)S(1)} fusion(f32[768,2816]{1,0:T(8,128)} %constant_dynamic-update-slice_fusion.7), kind=kOutput, calls=%fused_computation.1 | convolution fusion | flops 7247757312 | bytes 14942208 | tf_op jit(solution)/shard_map/dot_general | solution.py:12
  117.5 3.4 %fusion.11 = f32[7,256,256]{2,1,0:T(8,128)} fusion(f32[256,256]{1,0:T(8,128)S(1)} %fusion.71, f32[768,2048]{1,0:T(8,128)S(1)} %fusion, f32[768,2816]{1,0:T(8,128)} %constant_dynamic-update-slice_fusion.7), kind=kOutput, calls=%fused_computation.34 | convolution fusion | flops 302055424 | bytes 2097152 | tf_op jit(solution)/shard_map/dot_general | solution.py:16
  120.9 2.7 %fusion.25 = f32[8,256,256]{1,2,0:T(8,128)} fusion(f32[768,2048]{1,0:T(8,128)S(1)} %fusion, f32[768,2816]{1,0:T(8,128)} %constant_dynamic-update-slice_fusion.7, f32[1,256,256]{1,2,0:T(8,128)S(1)} %copy-done.16), kind=kOutput, calls=%fused_computation.48 | convolution fusion | flops 302055424 | bytes 2097152 | tf_op jit(solution)/shard_map/dot_general | solution.py:16
  123.6 2.7 %fusion.27 = f32[8,256,256]{1,2,0:T(8,128)} fusion(f32[8,256,256]{1,2,0:T(8,128)} %fusion.25, f32[256,256]{0,1:T(8,128)S(1)} %fusion.9, f32[768,2816]{1,0:T(8,128)} %constant_dynamic-update-slice_fusion.7, f32[768,2048]{1,0:T(8,128)S(1)} %fusion), kind=kOutput, calls=%fused_computation.50 | convolution fusion | flops 302055424 | bytes 2097152 | tf_op jit(solution)/shard_map/dot_general | solution.py:16
  126.3 2.7 %fusion.29 = f32[8,256,256]{1,2,0:T(8,128)} fusion(f32[8,256,256]{1,2,0:T(8,128)} %fusion.27, f32[256,256]{0,1:T(8,128)S(1)} %copy-done.3, f32[768,2816]{1,0:T(8,128)} %constant_dynamic-update-slice_fusion.7, f32[768,2048]{1,0:T(8,128)S(1)} %fusion), kind=kOutput, calls=%fused_computation.52 | convolution fusion | flops 302055424 | bytes 2097152 | tf_op jit(solution)/shard_map/dot_general | solution.py:16
  129.0 2.6 %fusion.31 = f32[8,256,256]{1,2,0:T(8,128)} fusion(f32[8,256,256]{1,2,0:T(8,128)} %fusion.29, f32[256,256]{0,1:T(8,128)S(1)} %copy-done.5, f32[768,2816]{1,0:T(8,128)} %constant_dynamic-update-slice_fusion.7, f32[768,2048]{1,0:T(8,128)S(1)} %fusion), kind=kOutput, calls=%fused_computation.54 | convolution fusion | flops 302055424 | bytes 2097152 | tf_op jit(solution)/shard_map/dot_general | solution.py:16
  131.6 2.7 %fusion.33 = f32[8,256,256]{1,2,0:T(8,128)} fusion(f32[8,256,256]{1,2,0:T(8,128)} %fusion.31, f32[256,256]{0,1:T(8,128)S(1)} %copy-done.7, f32[768,2816]{1,0:T(8,128)} %constant_dynamic-update-slice_fusion.7, f32[768,2048]{1,0:T(8,128)S(1)} %fusion), kind=kOutput, calls=%fused_computation.56 | convolution fusion | flops 302055424 | bytes 2097152 | tf_op jit(solution)/shard_map/dot_general | solution.py:16
  134.3 2.7 %fusion.35 = f32[8,256,256]{1,2,0:T(8,128)} fusion(f32[8,256,256]{1,2,0:T(8,128)} %fusion.33, f32[256,256]{0,1:T(8,128)S(1)} %copy-done.8, f32[768,2816]{1,0:T(8,128)} %constant_dynamic-update-slice_fusion.7, f32[768,2048]{1,0:T(8,128)S(1)} %fusion), kind=kOutput, calls=%fused_computation.58 | convolution fusion | flops 302055424 | bytes 2097152 | tf_op jit(solution)/shard_map/dot_general | solution.py:16
  136.9 2.7 %fusion.37 = f32[8,256,256]{1,2,0:T(8,128)} fusion(f32[8,256,256]{1,2,0:T(8,128)} %fusion.35, f32[256,256]{0,1:T(8,128)S(1)} %copy-done.11, f32[768,2816]{1,0:T(8,128)} %constant_dynamic-update-slice_fusion.7, f32[768,2048]{1,0:T(8,128)S(1)} %fusion), kind=kOutput, calls=%fused_computation.60 | convolution fusion | flops 302055424 | bytes 2097152 | tf_op jit(solution)/shard_map/dot_general | solution.py:16
  139.6 2.6 %fusion.39 = f32[8,256,256]{1,2,0:T(8,128)} fusion(f32[8,256,256]{1,2,0:T(8,128)} %fusion.37, f32[256,256]{0,1:T(8,128)S(1)} %fusion.3, f32[768,2816]{1,0:T(8,128)} %constant_dynamic-update-slice_fusion.7, f32[768,2048]{1,0:T(8,128)S(1)} %fusion), kind=kOutput, calls=%fused_computation.62 | convolution fusion | flops 302055424 | bytes 2097152 | tf_op jit(solution)/shard_map/dot_general | solution.py:16
  142.2 2.9 %copy.27 = f32[8,256,256]{2,1,0:T(8,128)} copy(f32[8,256,256]{1,2,0:T(8,128)} %fusion.39) | data formatting | bytes 4194304
  145.2 2.9 %fusion.13 = f32[7,256,256]{2,1,0:T(8,128)} fusion(f32[7,256,256]{2,1,0:T(8,128)} %fusion.11, f32[256,256]{1,0:T(8,128)S(1)} %fusion.94, f32[768,2048]{1,0:T(8,128)} %copy-done, f32[768,2816]{1,0:T(8,128)} %constant_dynamic-update-slice_fusion.7), kind=kOutput, calls=%fused_computation.36 | convolution fusion | flops 302055424 | bytes 2097152 | tf_op jit(solution)/shard_map/dot_general | solution.py:16
  148.1 2.9 %fusion.15 = f32[7,256,256]{2,1,0:T(8,128)} fusion(f32[7,256,256]{2,1,0:T(8,128)} %fusion.13, f32[256,256]{1,0:T(8,128)S(1)} %fusion.90, f32[768,2048]{1,0:T(8,128)} %copy-done, f32[768,2816]{1,0:T(8,128)} %constant_dynamic-update-slice_fusion.7), kind=kOutput, calls=%fused_computation.38 | convolution fusion | flops 302055424 | bytes 2097152 | tf_op jit(solution)/shard_map/dot_general | solution.py:16
  150.9 2.9 %fusion.17 = f32[7,256,256]{2,1,0:T(8,128)} fusion(f32[7,256,256]{2,1,0:T(8,128)} %fusion.15, f32[256,256]{1,0:T(8,128)S(1)} %fusion.86, f32[768,2048]{1,0:T(8,128)} %copy-done, f32[768,2816]{1,0:T(8,128)} %constant_dynamic-update-slice_fusion.7), kind=kOutput, calls=%fused_computation.40 | convolution fusion | flops 302055424 | bytes 2097152 | tf_op jit(solution)/shard_map/dot_general | solution.py:16
  153.8 2.9 %fusion.19 = f32[7,256,256]{2,1,0:T(8,128)} fusion(f32[7,256,256]{2,1,0:T(8,128)} %fusion.17, f32[256,256]{1,0:T(8,128)S(1)} %fusion.82, f32[768,2048]{1,0:T(8,128)} %copy-done, f32[768,2816]{1,0:T(8,128)} %constant_dynamic-update-slice_fusion.7), kind=kOutput, calls=%fused_computation.42 | convolution fusion | flops 302055424 | bytes 2097152 | tf_op jit(solution)/shard_map/dot_general | solution.py:16
  156.7 2.9 %fusion.21 = f32[7,256,256]{2,1,0:T(8,128)} fusion(f32[7,256,256]{2,1,0:T(8,128)} %fusion.19, f32[256,256]{1,0:T(8,128)S(1)} %copy-done.10, f32[768,2048]{1,0:T(8,128)} %copy-done, f32[768,2816]{1,0:T(8,128)} %constant_dynamic-update-slice_fusion.7), kind=kOutput, calls=%fused_computation.44 | convolution fusion | flops 302055424 | bytes 2097152 | tf_op jit(solution)/shard_map/dot_general | solution.py:16
  159.6 2.9 %fusion.23 = f32[7,256,256]{2,1,0:T(8,128)} fusion(f32[7,256,256]{2,1,0:T(8,128)} %fusion.21, f32[256,256]{1,0:T(8,128)S(1)} %copy-done.13, f32[768,2048]{1,0:T(8,128)} %copy-done, f32[768,2816]{1,0:T(8,128)} %constant_dynamic-update-slice_fusion.7), kind=kOutput, calls=%fused_computation.46 | convolution fusion | flops 302055424 | bytes 2097152 | tf_op jit(solution)/shard_map/dot_general | solution.py:16
  (116 shorter events, 57.2 us)
Async XLA Ops:
  0.6 13.1 %copy-start.1 = (f32[7,256,256]{2,1,0:T(8,128)S(1)}, f32[7,256,256]{2,1,0:T(8,128)}, u32[]{:S(2)}) copy-start(f32[7,256,256]{2,1,0:T(8,128)} %param.7) | copy-start | bytes 5505028
  2.3 38.0 %collective-permute-start = (f32[48,384]{1,0:T(8,128)}, f32[48,384]{1,0:T(8,128)}, u32[]{:S(2)}, u32[]{:S(2)}) collective-permute-start(f32[48,384]{1,0:T(8,128)} %dynamic-slice_bitcast_fusion), channel_id=1, source_target_pairs={{0,8},{1,9},{2,10},{3,11},{4,12},{5,13},{6,14},{7,15},{8,0},{9,1},... | collective-permute-start | bytes 221192 | tf_op jit(solution)/shard_map/ppermute | solution.py:27
  9.1 6.3 %copy-start.14 = (f32[8,48,256]{2,1,0:T(8,128)}, f32[8,48,256]{2,1,0:T(8,128)S(1)}, u32[]{:S(2)}) copy-start(f32[8,48,256]{2,1,0:T(8,128)S(1)} %bitcast_select_fusion) | copy-start | bytes 1179652
  17.1 23.2 %copy-start.18 = (f32[1,384,96]{1,2,0:T(8,128)S(1)}, f32[1,384,96]{1,2,0:T(8,128)}, u32[]{:S(2)}) copy-start(f32[1,384,96]{1,2,0:T(8,128)} %param.5) | copy-start | bytes 442372
  20.2 2.2 %copy-start.4 = (f32[256,256]{0,1:T(8,128)}, f32[256,256]{0,1:T(8,128)S(1)}, u32[]{:S(2)}) copy-start(f32[256,256]{0,1:T(8,128)S(1)} %fusion.7) | copy-start | bytes 786436
  42.4 17.2 %collective-permute-start.1 = (f32[48,2816]{1,0:T(8,128)}, f32[48,2816]{1,0:T(8,128)S(1)}, u32[]{:S(2)}, u32[]{:S(2)}) collective-permute-start(f32[48,2816]{1,0:T(8,128)} %fusion.122), channel_id=1, source_target_pairs={{0,1},{1,0},{2,3},{3,2},{4,5},{5,4},{6,7},{7,6},{8,9},{9,8},{10,11... | collective-permute-start | bytes 1622024 | tf_op jit(solution)/shard_map/ppermute | solution.py:27
  42.4 14.9 %collective-permute-start.2 = (f32[48,2816]{1,0:T(8,128)}, f32[48,2816]{1,0:T(8,128)S(1)}, u32[]{:S(2)}, u32[]{:S(2)}) collective-permute-start(f32[48,2816]{1,0:T(8,128)} %fusion.122), channel_id=1, source_target_pairs={{0,4},{1,5},{4,8},{5,9},{8,12},{9,13},{12,14},{13,15},{14,10},{15,... | collective-permute-start | bytes 1622024 | tf_op jit(solution)/shard_map/ppermute | solution.py:87
  44.0 14.9 %collective-permute-start.3 = (f32[48,2816]{1,0:T(8,128)}, f32[48,2816]{1,0:T(8,128)S(1)}, u32[]{:S(2)}, u32[]{:S(2)}) collective-permute-start(f32[48,2816]{1,0:T(8,128)} %fusion.122), channel_id=1, source_target_pairs={{0,2},{1,3},{4,0},{5,1},{8,4},{9,5},{12,8},{13,9},{14,12},{15,13},... | collective-permute-start | bytes 1622024 | tf_op jit(solution)/shard_map/ppermute | solution.py:88
  45.8 47.4 %copy-start.9 = (f32[256,256]{1,0:T(8,128)}, f32[256,256]{1,0:T(8,128)S(1)}, u32[]{:S(2)}) copy-start(f32[256,256]{1,0:T(8,128)S(1)} %fusion.78) | copy-start | bytes 786436
  51.6 41.6 %copy-start.15 = (f32[1,256,256]{1,2,0:T(8,128)S(1)}, f32[1,256,256]{1,2,0:T(8,128)}, u32[]{:S(2)}) copy-start(f32[1,256,256]{1,2,0:T(8,128)} %copy.42) | copy-start | bytes 786436
  57.3 16.5 %collective-permute-start.4 = (f32[48,2816]{1,0:T(8,128)S(1)}, f32[48,2816]{1,0:T(8,128)S(1)}, u32[]{:S(2)}, u32[]{:S(2)}) collective-permute-start(f32[48,2816]{1,0:T(8,128)S(1)} %collective-permute-done.2), channel_id=1, source_target_pairs={{0,1},{1,0},{2,3},{3,2},{4,5},{5,4},{6,7},{7,6},{8,9},{9,8},{10,11... | collective-permute-start | bytes 1622024 | tf_op jit(solution)/shard_map/ppermute | solution.py:27
  57.3 14.7 %collective-permute-start.6 = (f32[48,2816]{1,0:T(8,128)S(1)}, f32[48,2816]{1,0:T(8,128)S(1)}, u32[]{:S(2)}, u32[]{:S(2)}) collective-permute-start(f32[48,2816]{1,0:T(8,128)S(1)} %collective-permute-done.2), channel_id=1, source_target_pairs={{0,4},{1,5},{4,8},{5,9},{8,12},{9,13},{12,14},{13,15},{14,10},{15,... | collective-permute-start | bytes 1622024 | tf_op jit(solution)/shard_map/ppermute | solution.py:87
  58.9 16.2 %collective-permute-start.5 = (f32[48,2816]{1,0:T(8,128)S(1)}, f32[48,2816]{1,0:T(8,128)S(1)}, u32[]{:S(2)}, u32[]{:S(2)}) collective-permute-start(f32[48,2816]{1,0:T(8,128)S(1)} %collective-permute-done.3), channel_id=1, source_target_pairs={{0,1},{1,0},{2,3},{3,2},{4,5},{5,4},{6,7},{7,6},{8,9},{9,8},{10,11... | collective-permute-start | bytes 1622024 | tf_op jit(solution)/shard_map/ppermute | solution.py:27
  59.2 14.5 %collective-permute-start.7 = (f32[48,2816]{1,0:T(8,128)S(1)}, f32[48,2816]{1,0:T(8,128)S(1)}, u32[]{:S(2)}, u32[]{:S(2)}) collective-permute-start(f32[48,2816]{1,0:T(8,128)S(1)} %collective-permute-done.3), channel_id=1, source_target_pairs={{0,2},{1,3},{4,0},{5,1},{8,4},{9,5},{12,8},{13,9},{14,12},{15,13},... | collective-permute-start | bytes 1622024 | tf_op jit(solution)/shard_map/ppermute | solution.py:88
  72.0 5.6 %collective-permute-start.8 = (f32[48,2816]{1,0:T(8,128)S(1)}, f32[48,2816]{1,0:T(8,128)S(1)}, u32[]{:S(2)}, u32[]{:S(2)}) collective-permute-start(f32[48,2816]{1,0:T(8,128)S(1)} %collective-permute-done.6), channel_id=1, source_target_pairs={{0,1},{1,0},{2,3},{3,2},{4,5},{5,4},{6,7},{7,6},{8,9},{9,8},{10,11... | collective-permute-start | bytes 1622024 | tf_op jit(solution)/shard_map/ppermute | solution.py:27
  72.0 14.8 %collective-permute-start.10 = (f32[48,2816]{1,0:T(8,128)S(1)}, f32[48,2816]{1,0:T(8,128)}, u32[]{:S(2)}, u32[]{:S(2)}) collective-permute-start(f32[48,2816]{1,0:T(8,128)S(1)} %collective-permute-done.6), channel_id=1, source_target_pairs={{0,4},{1,5},{4,8},{5,9},{8,12},{9,13},{12,14},{13,15},{14,10},{15,... | collective-permute-start | bytes 1622024 | tf_op jit(solution)/shard_map/ppermute | solution.py:87
  73.6 4.9 %collective-permute-start.9 = (f32[48,2816]{1,0:T(8,128)S(1)}, f32[48,2816]{1,0:T(8,128)S(1)}, u32[]{:S(2)}, u32[]{:S(2)}) collective-permute-start(f32[48,2816]{1,0:T(8,128)S(1)} %collective-permute-done.7), channel_id=1, source_target_pairs={{0,1},{1,0},{2,3},{3,2},{4,5},{5,4},{6,7},{7,6},{8,9},{9,8},{10,11... | collective-permute-start | bytes 1622024 | tf_op jit(solution)/shard_map/ppermute | solution.py:27
  73.9 14.9 %collective-permute-start.11 = (f32[48,2816]{1,0:T(8,128)S(1)}, f32[48,2816]{1,0:T(8,128)S(1)}, u32[]{:S(2)}, u32[]{:S(2)}) collective-permute-start(f32[48,2816]{1,0:T(8,128)S(1)} %collective-permute-done.7), channel_id=1, source_target_pairs={{0,2},{1,3},{4,0},{5,1},{8,4},{9,5},{12,8},{13,9},{14,12},{15,13},... | collective-permute-start | bytes 1622024 | tf_op jit(solution)/shard_map/ppermute | solution.py:88
  91.6 9.7 %collective-permute-start.14 = (f32[48,2816]{1,0:T(8,128)}, f32[48,2816]{1,0:T(8,128)}, u32[]{:S(2)}, u32[]{:S(2)}) collective-permute-start(f32[48,2816]{1,0:T(8,128)} %get-tuple-element.14), channel_id=1, source_target_pairs={{0,4},{4,8},{8,12},{12,14},{14,10},{10,6},{6,2},{2,0},{1,3},{5,1},... | collective-permute-start | bytes 1622024 | tf_op jit(solution)/shard_map/ppermute | solution.py:93
  93.2 8.1 %collective-permute-start.12 = (f32[48,2816]{1,0:T(8,128)}, f32[48,2816]{1,0:T(8,128)}, u32[]{:S(2)}, u32[]{:S(2)}) collective-permute-start(f32[48,2816]{1,0:T(8,128)} %collective-permute-done.10), channel_id=1, source_target_pairs={{0,1},{1,0},{2,3},{3,2},{4,5},{5,4},{6,7},{7,6},{8,9},{9,8},{10,11... | collective-permute-start | bytes 1622024 | tf_op jit(solution)/shard_map/ppermute | solution.py:27
  99.2 1.9 %copy-start.12 = (f32[256,256]{1,0:T(8,128)}, f32[256,256]{1,0:T(8,128)S(1)}, u32[]{:S(2)}) copy-start(f32[256,256]{1,0:T(8,128)S(1)} %fusion.74) | copy-start | bytes 786436
  99.2 3.9 %collective-permute-start.13 = (f32[48,2816]{1,0:T(8,128)}, f32[48,2816]{1,0:T(8,128)S(1)}, u32[]{:S(2)}, u32[]{:S(2)}) collective-permute-start(f32[48,2816]{1,0:T(8,128)} %copy-done.17), channel_id=1, source_target_pairs={{0,1},{1,0},{2,3},{3,2},{4,5},{5,4},{6,7},{7,6},{8,9},{9,8},{10,11... | collective-permute-start | bytes 1622024 | tf_op jit(solution)/shard_map/ppermute | solution.py:27
  101.3 4.7 %collective-permute-start.15 = (f32[48,2816]{1,0:T(8,128)}, f32[48,2816]{1,0:T(8,128)S(1)}, u32[]{:S(2)}, u32[]{:S(2)}) collective-permute-start(f32[48,2816]{1,0:T(8,128)} %collective-permute-done.14), channel_id=1, source_target_pairs={{0,1},{1,0},{2,3},{3,2},{4,5},{5,4},{6,7},{7,6},{8,9},{9,8},{10,11... | collective-permute-start | bytes 1622024 | tf_op jit(solution)/shard_map/ppermute | solution.py:27
  106.9 14.1 %copy-start.16 = (f32[1,256,256]{1,2,0:T(8,128)S(1)}, f32[1,256,256]{1,2,0:T(8,128)}, u32[]{:S(2)}) copy-start(f32[1,256,256]{1,2,0:T(8,128)} %copy.36) | copy-start | bytes 786436
  117.5 22.1 %copy-start = (f32[768,2048]{1,0:T(8,128)}, f32[768,2048]{1,0:T(8,128)S(1)}, u32[]{:S(2)}) copy-start(f32[768,2048]{1,0:T(8,128)S(1)} %fusion) | copy-start | bytes 18874372
  117.5 8.8 %copy-start.3 = (f32[256,256]{0,1:T(8,128)S(1)}, f32[256,256]{0,1:T(8,128)}, u32[]{:S(2)}) copy-start(f32[256,256]{0,1:T(8,128)} %copy-done.2) | copy-start | bytes 786436
  117.5 11.5 %copy-start.5 = (f32[256,256]{0,1:T(8,128)S(1)}, f32[256,256]{0,1:T(8,128)}, u32[]{:S(2)}) copy-start(f32[256,256]{0,1:T(8,128)} %copy-done.4) | copy-start | bytes 786436
  117.5 14.1 %copy-start.7 = (f32[256,256]{0,1:T(8,128)S(1)}, f32[256,256]{0,1:T(8,128)}, u32[]{:S(2)}) copy-start(f32[256,256]{0,1:T(8,128)} %copy-done.6) | copy-start | bytes 786436
  117.5 16.8 %copy-start.8 = (f32[256,256]{0,1:T(8,128)S(1)}, f32[256,256]{0,1:T(8,128)}, u32[]{:S(2)}) copy-start(f32[256,256]{0,1:T(8,128)} %fusion.5) | copy-start | bytes 786436
  120.9 16.0 %copy-start.11 = (f32[256,256]{0,1:T(8,128)S(1)}, f32[256,256]{0,1:T(8,128)}, u32[]{:S(2)}) copy-start(f32[256,256]{0,1:T(8,128)} %fusion.4) | copy-start | bytes 786436
  142.2 14.5 %copy-start.10 = (f32[256,256]{1,0:T(8,128)S(1)}, f32[256,256]{1,0:T(8,128)}, u32[]{:S(2)}) copy-start(f32[256,256]{1,0:T(8,128)} %copy-done.9) | copy-start | bytes 786436
  145.2 14.4 %copy-start.13 = (f32[256,256]{1,0:T(8,128)S(1)}, f32[256,256]{1,0:T(8,128)}, u32[]{:S(2)}) copy-start(f32[256,256]{1,0:T(8,128)} %copy-done.12) | copy-start | bytes 786436
  (3 other events, 2.8 us)

commit v2 on v1

--- a/solution.py
+++ b/solution.py
@@ -1,11 +1,14 @@
 import jax
 import jax.numpy as jnp
 from jax import lax
+from jax.experimental import pallas as pl
+from jax.experimental.pallas import tpu as pltpu
 from jax.sharding import PartitionSpec as P
 
 PCOL = 8
 TILE = 128
 GATHER_LIMIT = 16 * 2**20
+VMEM_LIMIT = 28 * 2**20
 
 
 def product(left, right):
@@ -72,57 +75,313 @@
     return inner, cross
 
 
-def gather_rounds(message, my_index, count):
+def halves(value):
+    high = value.astype(jnp.bfloat16)
+    return high, (value - high.astype(jnp.float32)).astype(jnp.bfloat16)
+
+
+def dot_halves(left, right, dims=((1,), (0,))):
+    def one(a, b):
+        return lax.dot_general(a, b, (dims, ((), ())), preferred_element_type=jnp.float32)
+
+    return one(left[0], right[0]) + (one(left[0], right[1]) + one(left[1], right[0]))
+
+
+def kernel_params(flops, moved, **more):
+    return dict(
+        compiler_params=pltpu.CompilerParams(vmem_limit_bytes=VMEM_LIMIT, **more),
+        cost_estimate=pl.CostEstimate(flops=flops, bytes_accessed=moved, transcendentals=0),
+    )
+
+
+def transposed_block(block):
+    def kernel(block_ref, out_ref):
+        out_ref[...] = block_ref[...].T
+
+    shape = (block.shape[1], block.shape[0])
+    return pl.pallas_call(
+        kernel,
+        out_shape=jax.ShapeDtypeStruct(shape, jnp.float32),
+        name="turn_block",
+        **kernel_params(block.size, 8 * block.size),
+    )(block)
+
+
+def link_chain(anc_links, parent_links, pattern):
+    rows, nodes, width = anc_links.shape
+    tiles = pattern.shape[1]
+
+    def kernel(links_ref, parent_ref, pattern_ref, out_ref):
+        first = lax.axis_index("row") * rows
+        tile = first // TILE
+        next_tile = jnp.minimum(tile + 1, tiles - 1)
+        row = first + lax.broadcasted_iota(jnp.int32, (rows, width), 0)
+        in_first = row < (tile + 1) * TILE
+        reduced = None
+        for node in range(nodes):
+            keep = jnp.where(in_first, pattern_ref[node, tile], pattern_ref[node, next_tile])
+            links = jnp.where(keep != 0, links_ref[:, node, :], 0.0)
+            if node > 0:
+                links = links - dot_halves(halves(reduced), halves(parent_ref[node - 1]))
+            out_ref[:, node * width : (node + 1) * width] = links
+            reduced = links
+
+    return pl.pallas_call(
+        kernel,
+        out_shape=jax.ShapeDtypeStruct((rows, nodes * width), jnp.float32),
+        in_specs=[
+            pl.BlockSpec(memory_space=pltpu.VMEM),
+            pl.BlockSpec(memory_space=pltpu.VMEM),
+            pl.BlockSpec(memory_space=pltpu.SMEM),
+        ],
+        out_specs=pl.BlockSpec(memory_space=pltpu.VMEM),
+        name="link_chain",
+        **kernel_params(12 * rows * nodes * width * width, 4 * parent_links.size),
+    )(anc_links, parent_links, pattern)
+
+
+def inner_chain(parent_links, pivot_inverse):
+    nodes, width, _ = pivot_inverse.shape
+
+    def kernel(parent_ref, pivot_ref, cross_ref, inner_ref, inner):
+        node = pl.program_id(0)
+
+        @pl.when(node == 0)
+        def _():
+            inner[...] = pivot_ref[0]
+
+        @pl.when(node > 0)
+        def _():
+            link = halves(parent_ref[0])
+            cross = dot_halves(halves(inner[...]), link)
+            cross_ref[0] = -cross
+            inner[...] = pivot_ref[0] + dot_halves(link, halves(cross), ((0,), (0,)))
+
+        inner_ref[0] = inner[...]
+
+    below = pl.BlockSpec((1, width, width), lambda node: (jnp.maximum(node - 1, 0), 0, 0))
+    own = pl.BlockSpec((1, width, width), lambda node: (node, 0, 0))
+    return pl.pallas_call(
+        kernel,
+        grid=(nodes,),
+        out_shape=[
+            jax.ShapeDtypeStruct(parent_links.shape, jnp.float32),
+            jax.ShapeDtypeStruct(pivot_inverse.shape, jnp.float32),
+        ],
+        in_specs=[below, own],
+        out_specs=[below, own],
+        scratch_shapes=[pltpu.VMEM((width, width), jnp.float32)],
+        name="inner_chain",
+        **kernel_params(12 * nodes * width**3, 16 * pivot_inverse.size),
+    )(parent_links, pivot_inverse)
+
+
+def assemble(parts):
+    owners = jnp.stack([owner for owner, _ in parts])
+    arrays = [array for _, array in parts]
+    rows, columns = arrays[0].shape[0] // 2, arrays[0].shape[1]
+    count = len(arrays)
+
+    def kernel(owner_ref, *refs):
+        sources, out_ref, sems = refs[:count], refs[count], refs[count + 1]
+        copies = []
+        for place, source in enumerate(sources):
+            owner = owner_ref[place]
+            for piece in range(2):
+                row = (owner % PCOL + PCOL * piece) * rows
+                copies.append(
+                    pltpu.make_async_copy(
+                        source.at[pl.ds(piece * rows, rows), :],
+                        out_ref.at[
+                            pl.ds(pl.multiple_of(row, 8), rows),
+                            pl.ds(pl.multiple_of(owner // PCOL * columns, 128), columns),
+                        ],
+                        sems.at[2 * place + piece],
+                    )
+                )
+        for copy in copies:
+            copy.start()
+        for copy in copies:
+            copy.wait()
+
+    order = 2 * columns
+    return pl.pallas_call(
+        kernel,
+        out_shape=jax.ShapeDtypeStruct((order, order), jnp.float32),
+        in_specs=[pl.BlockSpec(memory_space=pltpu.SMEM)] + [pl.BlockSpec(memory_space=pl.ANY)] * count,
+        out_specs=pl.BlockSpec(memory_space=pl.ANY),
+        scratch_shapes=[pltpu.SemaphoreType.DMA((2 * count,))],
+        name="assemble",
+        **kernel_params(order * order, 8 * order * order),
+    )(owners, *arrays)
+
+
+def border(parts, ancestor, state, parents, diagonals, my_index=None):
+    owners = jnp.stack([owner for owner, _ in parts] + ([my_index] if my_index is not None else []))
+    arrays = [array for _, array in parts]
+    count, last, start = len(arrays), my_index is not None, state is None
+    nodes, width, _ = diagonals.shape
+    rows = arrays[0].shape[0]
+    fresh, order = rows * count, ancestor.shape[0]
+    taken = count + last
+    bf16 = jnp.bfloat16
+
+    def kernel(owner_ref, *refs):
+        refs = list(refs)
+        take = lambda number: [refs.pop(0) for _ in range(number)]
+        new_refs = take(count)
+        (ancestor_ref,) = take(1)
+        state_refs = take(0 if start else 2)
+        parents_ref, diagonals_ref = take(2)
+        parents_out, diagonals_out = take(2)
+        held = take(2)
+        panel_out = take(1)[0] if last else None
+        ancestor_rows, rows_high, rows_low, turned_high, turned_low, total, sems = refs
+        node = pl.program_id(0)
+
+        @pl.when(node == 0)
+        def _():
+            copies = [
+                pltpu.make_async_copy(
+                    ancestor_ref.at[pl.ds(pl.multiple_of(owner_ref[place] * rows, 8), rows), :],
+                    ancestor_rows.at[pl.ds(place * rows, rows), :],
+                    sems.at[place],
+                )
+                for place in range(taken)
+            ]
+            for copy in copies:
+                copy.start()
+            piece = lax.broadcasted_iota(jnp.int32, (1, order), 1) // rows
+            weight = jnp.ones((1, order), jnp.float32)
+            for place in range(count):
+                weight = jnp.where(piece == owner_ref[place], 0.5, weight)
+            for copy in copies:
+                copy.wait()
+            values = ancestor_rows[0:fresh, :] * weight
+            rows_high[0:fresh, :], rows_low[0:fresh, :] = halves(values)
+            if last:
+                rows_high[fresh:, :], rows_low[fresh:, :] = halves(ancestor_rows[fresh:, :])
+            turned_high[1] = jnp.zeros(turned_high.shape[1:], bf16)
+            turned_low[1] = jnp.zeros(turned_low.shape[1:], bf16)
+
+        new = jnp.concatenate([ref[...] for ref in new_refs], axis=0)
+        new_high, new_low = halves(new)
+        for part, values in zip(range(2), (new_high, new_low)):
+            held[part][...] = jnp.zeros((order, width), bf16) if start else state_refs[part][...]
+            for place in range(count):
+                row = pl.multiple_of(owner_ref[place] * rows, 16)
+                held[part][pl.ds(row, rows), :] = values[place * rows : (place + 1) * rows, :]
+        image = dot_halves((rows_high[...], rows_low[...]), (held[0][...], held[1][...]))
+        if last:
+            panel_out[:, pl.ds(node, 1), :] = -image[fresh:, :].reshape(rows, 1, width)
+            image = image[:fresh, :]
+        image_high, image_low = halves(image)
+        slot = lax.rem(node, 2)
+        turned = jnp.concatenate([new, image], axis=0).T
+        turned_high[slot], turned_low[slot] = halves(turned)
+        left = tuple(ref[...].reshape(2 * width, 2 * fresh) for ref in (turned_high, turned_low))
+        right = (
+            jnp.concatenate([image_high, new_high], axis=0),
+            jnp.concatenate([image_low, new_low], axis=0),
+        )
+        total[...] = dot_halves(left, right).reshape(2, width, width)
+        diagonals_out[0] = diagonals_ref[0] + total[slot]
+        parents_out[0] = parents_ref[0] + total[1 - slot]
+
+    column = lambda height: pl.BlockSpec((height, width), lambda node: (0, node))
+    below = pl.BlockSpec((1, width, width), lambda node: (jnp.maximum(node - 1, 0), 0, 0))
+    own = pl.BlockSpec((1, width, width), lambda node: (node, 0, 0))
+    any_place = pl.BlockSpec(memory_space=pl.ANY)
+    in_specs = [pl.BlockSpec(memory_space=pltpu.SMEM)] + [column(rows)] * count + [any_place]
+    operands = [owners, *arrays, ancestor]
+    if not start:
+        in_specs += [column(order)] * 2
+        operands += list(state)
+    aliases = {len(operands): 0, len(operands) + 1: 1}
+    in_specs += [below, own]
+    operands += [parents, diagonals]
+    out_specs = [below, own]
+    out_shape = [
+        jax.ShapeDtypeStruct(parents.shape, jnp.float32),
+        jax.ShapeDtypeStruct(diagonals.shape, jnp.float32),
+    ]
+    scratch = []
+    if last:
+        out_specs.append(pl.BlockSpec((rows, nodes, width), lambda node: (0, 0, 0)))
+        out_shape.append(jax.ShapeDtypeStruct((rows, nodes, width), jnp.float32))
+        scratch += [pltpu.VMEM((order, width), bf16)] * 2
+    else:
+        out_specs += [column(order)] * 2
+        out_shape += [jax.ShapeDtypeStruct((order, nodes * width), bf16)] * 2
+    scratch += [
+        pltpu.VMEM((taken * rows, order), jnp.float32),
+        pltpu.VMEM((taken * rows, order), bf16),
+        pltpu.VMEM((taken * rows, order), bf16),
+        pltpu.VMEM((2, width, 2 * fresh), bf16),
+        pltpu.VMEM((2, width, 2 * fresh), bf16),
+        pltpu.VMEM((2, width, width), jnp.float32),
+        pltpu.SemaphoreType.DMA((taken,)),
+    ]
+
+    def ordered(owner_ref, *refs):
+        refs = list(refs)
+        inputs = len(operands) - 1
+        outputs = refs[inputs : inputs + len(out_shape)]
+        rest = refs[inputs + len(out_shape) :]
+        if last:
+            outputs = outputs[:2] + rest[:2] + outputs[2:]
+            rest = rest[2:]
+        kernel(owner_ref, *refs[:inputs], *outputs, *rest)
+
+    flops = 6 * nodes * (taken * rows * order * width + 4 * fresh * width * width)
+    moved = 16 * diagonals.size + 8 * order * nodes * width
+    parents, diagonals, *others = pl.pallas_call(
+        ordered,
+        grid=(nodes,),
+        out_shape=out_shape,
+        in_specs=in_specs,
+        out_specs=out_specs,
+        scratch_shapes=scratch,
+        input_output_aliases=aliases,
+        name="border_" + str(count),
+        **kernel_params(flops, moved),
+    )(*operands)
+    return parents, diagonals, others
+
+
+def ring(message, my_index, count):
     core = my_index % 2
     place = ring_place(my_index // 2, count)
 
-    def owner(shift, other):
+    def pair(shift, mine):
         chip = ring_chip((place + shift + count) % count, count)
-        return 2 * chip + jnp.where(other, 1 - core, core)
+        return [(2 * chip + core, mine), (2 * chip + 1 - core, swap_bit(mine, 0))]
 
     ahead, behind = ring_pairs(count, 1), ring_pairs(count, -1)
-    arrivals = [(owner(0, False), message), (owner(0, True), swap_bit(message, 0))]
+    yield pair(0, message)
     upward = downward = message
     for step in range(1, (count + 1) // 2):
         upward = lax.ppermute(upward, "row", ahead)
         downward = lax.ppermute(downward, "row", behind)
-        arrivals += [(owner(-step, False), upward), (owner(step, False), downward)]
-        arrivals += [(owner(-step, True), swap_bit(upward, 0)), (owner(step, True), swap_bit(downward, 0))]
-    if count % 2 == 0 and count > 1:
+        yield pair(-step, upward) + pair(step, downward)
+    if count % 2 == 0:
         pairs = [p for p in ahead if p[0] % 2 == 0] + [p for p in behind if p[0] % 2 == 1]
-        last = lax.ppermute(jnp.where(core == 0, upward, downward), "row", pairs)
-        arrivals += [(owner(count // 2, False), last), (owner(count // 2, True), swap_bit(last, 0))]
-    return arrivals
+        yield pair(count // 2, lax.ppermute(jnp.where(core == 0, upward, downward), "row", pairs))
 
 
 def gather_plan(anc_blocks, anc_links, parent_links, pivot_inverse, pattern):
     my_index = lax.axis_index("row")
-    size = lax.axis_size("row")
-    rows, nodes, width = anc_links.shape
-    order = rows * size
-    half = my_index // PCOL
-    block = anc_blocks[0].T.reshape(2, rows, order // 2)
-    mine = lax.dynamic_index_in_dim(block, half, 0, False)
-    theirs = swap_bit(lax.dynamic_index_in_dim(block, 1 - half, 0, False), PCOL.bit_length() - 1)
-    low, high = jnp.where(half == 0, mine, theirs), jnp.where(half == 0, theirs, mine)
-    links = masked_links(my_index, anc_links, pattern)
-    message = jnp.concatenate(reduced_links(links, parent_links) + [low, high], axis=1)
-    inner, cross = local_chain(parent_links, pivot_inverse)
-    whole = jnp.zeros((order, message.shape[1]), jnp.float32)
-    for owner, part in gather_rounds(message, my_index, size // 2):
-        whole = lax.dynamic_update_slice(whole, part, (owner * rows, 0))
-    links, ancestor = whole[:, : nodes * width], whole[:, nodes * width :]
-    image = product(ancestor, links)
-    panels = -lax.dynamic_slice_in_dim(image, my_index * rows, rows, 0).reshape(rows, nodes, width)
-    column = lambda array, node: array[:, node * width : (node + 1) * width]
-    diagonals = [
-        inner[node] + inner_product(column(links, node), column(image, node)) for node in range(nodes)
-    ]
-    parents = [
-        inner_product(column(links, node - 1), column(image, node)) - cross[node - 1]
-        for node in range(1, nodes)
-    ]
-    return panels, jnp.stack(parents), jnp.stack(diagonals)
+    chips = lax.axis_size("row") // 2
+    blocks = list(ring(transposed_block(anc_blocks[0]), my_index, chips))
+    links = list(ring(link_chain(anc_links, parent_links, pattern), my_index, chips))
+    parents, diagonals = inner_chain(parent_links, pivot_inverse)
+    ancestor = assemble(sum(blocks, []))
+    groups = [sum(links[:-2], []), links[-2], links[-1]]
+    state = None
+    for group in groups[:-1]:
+        parents, diagonals, state = border(group, ancestor, state, parents, diagonals)
+    parents, diagonals, panels = border(groups[-1], ancestor, state, parents, diagonals, my_index)
+    return panels[0], parents, diagonals
 
 
 def spread_plan(anc_blocks, anc_links, parent_links, pivot_inverse, pattern):

time: 166 us -> 129 us (0.78)
  matrix products: 77.6 us -> 0 us
  Pallas kernels: 0 us -> 71.5 us
  local copies, waits for them, and re-layouts: 43.3 us -> 6.4 us
  starting transfers between devices: 12.7 us -> 20.9 us
  other arithmetic: 6.57 us -> 0.87 us
  waiting for transfers between devices: 23.2 us -> 28.4 us
    dot_general x37 -> x0, matrix products: 77.6 us -> none  [the longest x22 50.8 us: inner_product(): lax.dot_general(left, right, (((0,), (0,)), ((), ())), precision=lax.Prec...]
    pallas_call x0 -> x7, Pallas kernels: none -> 71.5 us  [the longest x3 61.1 us: border(): pl.pallas_call(ordered, grid=(nodes,), out_shape=out_shape, in_specs=in_s...]
    dynamic_update_slice x15 -> x0, local copies, waits for them, and re-layouts: 16.9 us -> none  [gather_plan(): whole = lax.dynamic_update_slice(whole, part, (owner * rows, 0))]
    unnamed x50 -> x33, local copies, waits for them, and re-layouts: 17.6 us -> 6.22 us
    ppermute x7 -> x14, starting transfers between devices: 7.65 us -> 16.8 us  [the longest x6 12.9 us: ring(): upward = lax.ppermute(upward, 'row', ahead)]
    ppermute x7 -> x14, waiting for transfers between devices: 23.2 us -> 28.3 us  [the longest x6 20.1 us: ring(): upward = lax.ppermute(upward, 'row', ahead)]
    broadcast_in_dim x1 -> x0, local copies, waits for them, and re-layouts: 3.94 us -> none  [gather_plan(): whole = jnp.zeros((order, message.shape[1]), jnp.float32)]
    slice x1 -> x0, local copies, waits for them, and re-layouts: 2.6 us -> none  [local_chain(): inner.append(pivot_inverse[node] + inner_product(link, cross[-1]))]
  transfers between devices with their start and end apart: 16 -> 30, of which waited for: 4 -> 7; matrix products, arithmetic and copies ran while one was open for 38% -> 1% of each run, Pallas kernels for 0% -> 44%
where the time goes in v2:
time: 129 us
  Pallas kernels  71.5 us (55%)
  waiting for transfers between devices  28.4 us (22%)
  starting transfers between devices  20.9 us (16%)
  local copies, waits for them, and re-layouts  6.4 us (5%)
    pallas_call x3, Pallas kernels, border(): pl.pallas_call(ordered, grid=(nodes,), out_shape=out_shape, in_specs=in_s...  61.1 us
    ppermute x6, waiting for transfers between devices, ring(): upward = lax.ppermute(upward, 'row', ahead)  20.1 us
    ppermute x6, starting transfers between devices, ring(): upward = lax.ppermute(upward, 'row', ahead)  12.9 us
    ppermute x2, waiting for transfers between devices, ring(): lax.ppermute(jnp.where(core == 0, upward, downward), 'row', pairs)  6.27 us
    unnamed x33, local copies, waits for them, and re-layouts  6.22 us
    pallas_call x1, Pallas kernels, inner_chain(): pl.pallas_call(kernel, grid=(nodes,), out_shape=[jax.ShapeDtypeStruct(par...  5.93 us
    ppermute x16, starting transfers between devices, swap_bit(): lax.ppermute(value, 'row', [(i, i ^ mask) for i in range(lax.axis_size('r...  4.11 us
    ppermute x2, starting transfers between devices, ring(): lax.ppermute(jnp.where(core == 0, upward, downward), 'row', pairs)  3.21 us
  transfers between devices with their start and end apart: 30, of which 7 were waited for; matrix products, arithmetic and copies ran while one was open for 1% of the time, Pallas kernels for 44%

profile of v2, /device:TPU:0, one launch (start us, length us, event | category | flops | bytes accessed | tf_op | source)
XLA Modules:
  0.0 129.0 jit_solution(254096674405247310)
XLA Ops:
  0.6 1.5 %copy-done = f32[7,256,256]{2,1,0:T(8,128)S(1)} copy-done((f32[7,256,256]{2,1,0:T(8,128)S(1)}, f32[7,256,256]{2,1,0:T(8,128)}, u32[]{:S(2)}) %copy-start) | copy-done | bytes 1835032
  2.1 1.0 copy-done.2
  3.1 0.7 copy-done.11
  3.8 1.9 %link_chain.1.refs_0_ = f32[48,2048]{1,0:T(8,128)S(1)} custom-call(f32[48,8,256]{2,1,0:T(8,128)S(1)} %copy-done.2, f32[7,256,256]{2,1,0:T(8,128)S(1)} %copy-done, s32[8,6]{1,0:T(8,128)S(1)} %copy-done.11), custom_call_target="tpu_custom_call" | custom-call | flops 301989888 | bytes 1835008 | tf_op jit(solution)/shard_map/link_chain/pallas_call | solution.py:129
  5.8 3.1 %collective-permute-start = (f32[48,2048]{1,0:T(8,128)S(1)}, f32[48,2048]{1,0:T(8,128)S(1)}, u32[]{:S(2)}, u32[]{:S(2)}) collective-permute-start(f32[48,2048]{1,0:T(8,128)S(1)} %link_chain.1.refs_0_), channel_id=1, source_target_pairs={{0,4},{1,5},{4,8},{5,9},{8,12},{9,13},{12,14},{13,15},{14,10},{15,... | collective-permute-start | bytes 1179656 | tf_op jit(solution)/shard_map/ppermute | solution.py:364
  9.1 2.1 %collective-permute-start.9 = (f32[96,384]{1,0:T(8,128)S(1)}, f32[96,384]{1,0:T(8,128)}, u32[]{:S(2)}, u32[]{:S(2)}) collective-permute-start(f32[96,384]{1,0:T(8,128)S(1)} %turn_block.1.refs_0_), channel_id=1, source_target_pairs={{0,4},{1,5},{4,8},{5,9},{8,12},{9,13},{12,14},{13,15},{14,10},{15,... | collective-permute-start | bytes 442376 | tf_op jit(solution)/shard_map/ppermute | solution.py:364
  11.2 7.5 %collective-permute-done.refs_2_ = f32[48,2048]{1,0:T(8,128)S(1)} collective-permute-done((f32[48,2048]{1,0:T(8,128)S(1)}, f32[48,2048]{1,0:T(8,128)S(1)}, u32[]{:S(2)}, u32[]{:S(2)}) %collective-permute-start) | collective-permute-done | bytes 393248 | tf_op jit(solution)/shard_map/ppermute | solution.py:364
  18.7 2.1 %collective-permute-start.1 = (f32[48,2048]{1,0:T(8,128)S(1)}, f32[48,2048]{1,0:T(8,128)}, u32[]{:S(2)}, u32[]{:S(2)}) collective-permute-start(f32[48,2048]{1,0:T(8,128)S(1)} %collective-permute-done.refs_2_), channel_id=1, source_target_pairs={{0,4},{1,5},{4,8},{5,9},{8,12},{9,13},{12,14},{13,15},{14,10},{15,... | collective-permute-start | bytes 1179656 | tf_op jit(solution)/shard_map/ppermute | solution.py:364
  21.0 1.0 collective-permute-done.9.refs_2_
  21.9 2.1 %collective-permute-start.13 = (f32[96,384]{1,0:T(8,128)}, f32[96,384]{1,0:T(8,128)S(1)}, u32[]{:S(2)}, u32[]{:S(2)}) collective-permute-start(f32[96,384]{1,0:T(8,128)} %collective-permute-done.9.refs_2_), channel_id=1, source_target_pairs={{0,4},{1,5},{4,8},{5,9},{8,12},{9,13},{12,14},{13,15},{14,10},{15,... | collective-permute-start | bytes 442376 | tf_op jit(solution)/shard_map/ppermute | solution.py:364
  24.1 8.5 %collective-permute-done.13.refs_6_ = f32[96,384]{1,0:T(8,128)S(1)} collective-permute-done((f32[96,384]{1,0:T(8,128)}, f32[96,384]{1,0:T(8,128)S(1)}, u32[]{:S(2)}, u32[]{:S(2)}) %collective-permute-start.13) | collective-permute-done | bytes 147488 | tf_op jit(solution)/shard_map/ppermute | solution.py:364
  32.6 1.8 %collective-permute-start.17 = (f32[96,384]{1,0:T(8,128)S(1)}, f32[96,384]{1,0:T(8,128)S(1)}, u32[]{:S(2)}, u32[]{:S(2)}) collective-permute-start(f32[96,384]{1,0:T(8,128)S(1)} %collective-permute-done.13.refs_6_), channel_id=1, source_target_pairs={{0,4},{1,5},{4,8},{5,9},{8,12},{9,13},{12,14},{13,15},{14,10},{15,... | collective-permute-start | bytes 442376 | tf_op jit(solution)/shard_map/ppermute | solution.py:364
  34.6 3.1 %collective-permute-done.17.refs_10_ = f32[96,384]{1,0:T(8,128)S(1)} collective-permute-done((f32[96,384]{1,0:T(8,128)S(1)}, f32[96,384]{1,0:T(8,128)S(1)}, u32[]{:S(2)}, u32[]{:S(2)}) %collective-permute-start.17) | collective-permute-done | bytes 147488 | tf_op jit(solution)/shard_map/ppermute | solution.py:364
  37.7 1.8 %collective-permute-done.19.refs_12_ = f32[96,384]{1,0:T(8,128)S(1)} collective-permute-done((f32[96,384]{1,0:T(8,128)S(1)}, f32[96,384]{1,0:T(8,128)S(1)}, u32[]{:S(2)}, u32[]{:S(2)}) %collective-permute-start.19) | collective-permute-done | bytes 147488 | tf_op jit(solution)/shard_map/ppermute | solution.py:365
  39.6 1.6 %collective-permute-start.2 = (f32[48,2048]{1,0:T(8,128)}, f32[48,2048]{1,0:T(8,128)S(1)}, u32[]{:S(2)}, u32[]{:S(2)}) collective-permute-start(f32[48,2048]{1,0:T(8,128)} %collective-permute-done.1.refs_6_), channel_id=1, source_target_pairs={{0,4},{1,5},{4,8},{5,9},{8,12},{9,13},{12,14},{13,15},{14,10},{15,... | collective-permute-start | bytes 1179656 | tf_op jit(solution)/shard_map/ppermute | solution.py:364
  41.7 0.7 broadcast_select_fusion.1
  42.4 0.6 copy-done.7
  43.0 0.5 collective-permute-start.16
  43.5 0.7 copy-done.9
  44.2 1.6 %collective-permute-start.21 = (f32[96,384]{1,0:T(8,128)}, f32[96,384]{1,0:T(8,128)}, u32[]{:S(2)}, u32[]{:S(2)}) collective-permute-start(f32[96,384]{1,0:T(8,128)} %broadcast_select_fusion.1), channel_id=1, source_target_pairs={{0,4},{4,8},{8,12},{12,14},{14,10},{10,6},{6,2},{2,0},{1,3},{5,1},... | collective-permute-start | bytes 442376 | tf_op jit(solution)/shard_map/ppermute | solution.py:369
  46.8 6.3 %collective-permute-done.21.refs_14_ = f32[96,384]{1,0:T(8,128)} collective-permute-done((f32[96,384]{1,0:T(8,128)}, f32[96,384]{1,0:T(8,128)}, u32[]{:S(2)}, u32[]{:S(2)}) %collective-permute-start.21) | collective-permute-done | bytes 147488 | tf_op jit(solution)/shard_map/ppermute | solution.py:369
  53.1 1.1 collective-permute-start.22
  54.2 1.6 %copy-done.12 = f32[8,256,256]{2,1,0:T(8,128)S(1)} copy-done((f32[8,256,256]{2,1,0:T(8,128)S(1)}, f32[8,256,256]{2,1,0:T(8,128)}, u32[]{:S(2)}) %copy-start.12) | copy-done | bytes 2097176
  55.8 5.9 %inner_chain.1 = (f32[7,256,256]{2,1,0:T(8,128)}, f32[8,256,256]{2,1,0:T(8,128)}) custom-call(f32[7,256,256]{2,1,0:T(8,128)S(1)} %copy-done.1, f32[8,256,256]{2,1,0:T(8,128)S(1)} %copy-done.12), custom_call_target="tpu_custom_call" | custom-call | flops 1610612736 | bytes 8388608 | tf_op jit(solution)/shard_map/inner_chain/pallas_call | solution.py:164
  61.7 0.5 collective-permute-start.26
  62.3 2.4 %assemble.1.refs_10_.refs_4_.refs_2_ = f32[768,768]{1,0:T(8,128)S(1)} custom-call(s32[16]{0:T(128)S(1)} %stack.97.owner_ref, f32[96,384]{1,0:T(8,128)S(1)} %turn_block.1.refs_0_, f32[96,384]{1,0:T(8,128)} %collective-permute-done.8.refs_1_, f32[96,384]{1,0:T(8,128)} %collective-permute-done.9.refs_2_, f32[96,384]{1,0:T(8,128)S(1)} %copy-done.8, ...), custom_call_target="tpu_custom_call" | custom-call | flops 589824 | bytes 4718592 | tf_op jit(solution)/shard_map/assemble/pallas_call | solution.py:208
  64.7 0.5 collective-permute-start.28
  65.4 1.6 %collective-permute-start.6 = (f32[48,2048]{1,0:T(8,128)S(1)}, f32[48,2048]{1,0:T(8,128)S(1)}, u32[]{:S(2)}, u32[]{:S(2)}) collective-permute-start(f32[48,2048]{1,0:T(8,128)S(1)} %broadcast_select_fusion), channel_id=1, source_target_pairs={{0,4},{4,8},{8,12},{12,14},{14,10},{10,6},{6,2},{2,0},{1,3},{5,1},... | collective-permute-start | bytes 1179656 | tf_op jit(solution)/shard_map/ppermute | solution.py:369
  67.0 0.5 collective-permute-start.24
  67.5 30.1 %border_10.1 = (f32[7,256,256]{2,1,0:T(8,128)}, f32[8,256,256]{2,1,0:T(8,128)}, bf16[768,2048]{1,0:T(8,128)(2,1)S(1)}, bf16[768,2048]{1,0:T(8,128)(2,1)S(1)}) custom-call(s32[10]{0:T(128)S(1)} %stack.99.owner_ref, f32[48,2048]{1,0:T(8,128)S(1)} %link_chain.1.refs_0_, ...), custom_call_target="tpu_custom_call", output_to_operand_aliasing={{0}: (12, {}), {1}: (13, {})} | custom-call | flops 10569646080 | bytes 20971520 | tf_op jit(solution)/shard_map/border_10/pallas_call | solution.py:338
  97.9 17.6 %border_4.1 = (f32[7,256,256]{2,1,0:T(8,128)}, f32[8,256,256]{2,1,0:T(8,128)}, bf16[768,2048]{1,0:T(8,128)(2,1)S(1)}, bf16[768,2048]{1,0:T(8,128)(2,1)S(1)}) custom-call(s32[4]{0:T(128)S(1)} %pad_add_fusion.1.owner_ref, f32[48,2048]{1,0:T(8,128)S(1)} %collective-permute-done.2.refs_0_, ...), custom_call_target="tpu_custom_call", output_to_operand_aliasing={{0}: (8, {}), {1}: (9, {})} | custom-call | flops 4227858432 | bytes 20971520 | tf_op jit(solution)/shard_map/border_4/pallas_call | solution.py:338
  115.5 13.5 %border_2.1 = (f32[7,256,256]{2,1,0:T(8,128)}, f32[8,256,256]{2,1,0:T(8,128)}, f32[48,8,256]{2,1,0:T(8,128)}) custom-call(s32[3]{0:T(128)S(1)} %pad_add_fusion.owner_ref, f32[48,2048]{1,0:T(8,128)S(1)} %collective-permute-done.6.refs_0_, f32[48,2048]{1,0:T(8,128)S(1)} %collective-permute-done.7.refs_1_, ...), custom_call_target="tpu_custom_call", output_to_operand_aliasing={{0}: (6, {}), {1}: (7, {})} | custom-call | flops 2566914048 | bytes 20971520 | tf_op jit(solution)/shard_map/border_2/pallas_call | solution.py:338
  (74 shorter events, 2.5 us)
Async XLA Ops:
  3.8 50.4 %copy-start.1 = (f32[7,256,256]{2,1,0:T(8,128)S(1)}, f32[7,256,256]{2,1,0:T(8,128)}, u32[]{:S(2)}) copy-start(f32[7,256,256]{2,1,0:T(8,128)} %parent_ref.3) | copy-start | bytes 5505028
  5.8 12.9 %collective-permute-start = (f32[48,2048]{1,0:T(8,128)S(1)}, f32[48,2048]{1,0:T(8,128)S(1)}, u32[]{:S(2)}, u32[]{:S(2)}) collective-permute-start(f32[48,2048]{1,0:T(8,128)S(1)} %link_chain.1.refs_0_), channel_id=1, source_target_pairs={{0,4},{1,5},{4,8},{5,9},{8,12},{9,13},{12,14},{13,15},{14,10},{15,... | collective-permute-start | bytes 1179656 | tf_op jit(solution)/shard_map/ppermute | solution.py:364
  8.8 12.1 %collective-permute-start.3 = (f32[48,2048]{1,0:T(8,128)S(1)}, f32[48,2048]{1,0:T(8,128)}, u32[]{:S(2)}, u32[]{:S(2)}) collective-permute-start(f32[48,2048]{1,0:T(8,128)S(1)} %link_chain.1.refs_0_), channel_id=1, source_target_pairs={{0,2},{1,3},{4,0},{5,1},{8,4},{9,5},{12,8},{13,9},{14,12},{15,13},... | collective-permute-start | bytes 1179656 | tf_op jit(solution)/shard_map/ppermute | solution.py:365
  9.1 12.9 %collective-permute-start.9 = (f32[96,384]{1,0:T(8,128)S(1)}, f32[96,384]{1,0:T(8,128)}, u32[]{:S(2)}, u32[]{:S(2)}) collective-permute-start(f32[96,384]{1,0:T(8,128)S(1)} %turn_block.1.refs_0_), channel_id=1, source_target_pairs={{0,4},{1,5},{4,8},{5,9},{8,12},{9,13},{12,14},{13,15},{14,10},{15,... | collective-permute-start | bytes 442376 | tf_op jit(solution)/shard_map/ppermute | solution.py:364
  11.2 12.9 %collective-permute-start.11 = (f32[96,384]{1,0:T(8,128)S(1)}, f32[96,384]{1,0:T(8,128)}, u32[]{:S(2)}, u32[]{:S(2)}) collective-permute-start(f32[96,384]{1,0:T(8,128)S(1)} %turn_block.1.refs_0_), channel_id=1, source_target_pairs={{0,2},{1,3},{4,0},{5,1},{8,4},{9,5},{12,8},{13,9},{14,12},{15,13},... | collective-permute-start | bytes 442376 | tf_op jit(solution)/shard_map/ppermute | solution.py:365
  18.7 20.9 %copy-start.13 = (f32[48,2048]{1,0:T(8,128)}, f32[48,2048]{1,0:T(8,128)S(1)}, u32[]{:S(2)}) copy-start(f32[48,2048]{1,0:T(8,128)S(1)} %collective-permute-done.refs_2_) | copy-start | bytes 1179652
  18.7 20.9 %collective-permute-start.1 = (f32[48,2048]{1,0:T(8,128)S(1)}, f32[48,2048]{1,0:T(8,128)}, u32[]{:S(2)}, u32[]{:S(2)}) collective-permute-start(f32[48,2048]{1,0:T(8,128)S(1)} %collective-permute-done.refs_2_), channel_id=1, source_target_pairs={{0,4},{1,5},{4,8},{5,9},{8,12},{9,13},{12,14},{13,15},{14,10},{15,... | collective-permute-start | bytes 1179656 | tf_op jit(solution)/shard_map/ppermute | solution.py:364
  21.0 20.3 %collective-permute-start.4 = (f32[48,2048]{1,0:T(8,128)}, f32[48,2048]{1,0:T(8,128)}, u32[]{:S(2)}, u32[]{:S(2)}) collective-permute-start(f32[48,2048]{1,0:T(8,128)} %collective-permute-done.3.refs_4_), channel_id=1, source_target_pairs={{0,2},{1,3},{4,0},{5,1},{8,4},{9,5},{12,8},{13,9},{14,12},{15,13},... | collective-permute-start | bytes 1179656 | tf_op jit(solution)/shard_map/ppermute | solution.py:365
  21.9 10.7 %collective-permute-start.13 = (f32[96,384]{1,0:T(8,128)}, f32[96,384]{1,0:T(8,128)S(1)}, u32[]{:S(2)}, u32[]{:S(2)}) collective-permute-start(f32[96,384]{1,0:T(8,128)} %collective-permute-done.9.refs_2_), channel_id=1, source_target_pairs={{0,4},{1,5},{4,8},{5,9},{8,12},{9,13},{12,14},{13,15},{14,10},{15,... | collective-permute-start | bytes 442376 | tf_op jit(solution)/shard_map/ppermute | solution.py:364
  24.1 10.3 %collective-permute-start.15 = (f32[96,384]{1,0:T(8,128)}, f32[96,384]{1,0:T(8,128)S(1)}, u32[]{:S(2)}, u32[]{:S(2)}) collective-permute-start(f32[96,384]{1,0:T(8,128)} %collective-permute-done.11.refs_4_), channel_id=1, source_target_pairs={{0,2},{1,3},{4,0},{5,1},{8,4},{9,5},{12,8},{13,9},{14,12},{15,13},... | collective-permute-start | bytes 442376 | tf_op jit(solution)/shard_map/ppermute | solution.py:365
  32.6 5.1 %collective-permute-start.17 = (f32[96,384]{1,0:T(8,128)S(1)}, f32[96,384]{1,0:T(8,128)S(1)}, u32[]{:S(2)}, u32[]{:S(2)}) collective-permute-start(f32[96,384]{1,0:T(8,128)S(1)} %collective-permute-done.13.refs_6_), channel_id=1, source_target_pairs={{0,4},{1,5},{4,8},{5,9},{8,12},{9,13},{12,14},{13,15},{14,10},{15,... | collective-permute-start | bytes 442376 | tf_op jit(solution)/shard_map/ppermute | solution.py:364
  34.4 5.1 %collective-permute-start.19 = (f32[96,384]{1,0:T(8,128)S(1)}, f32[96,384]{1,0:T(8,128)S(1)}, u32[]{:S(2)}, u32[]{:S(2)}) collective-permute-start(f32[96,384]{1,0:T(8,128)S(1)} %collective-permute-done.15.refs_8_), channel_id=1, source_target_pairs={{0,2},{1,3},{4,0},{5,1},{8,4},{9,5},{12,8},{13,9},{14,12},{15,13},... | collective-permute-start | bytes 442376 | tf_op jit(solution)/shard_map/ppermute | solution.py:365
  34.6 7.7 %collective-permute-start.8 = (f32[96,384]{1,0:T(8,128)S(1)}, f32[96,384]{1,0:T(8,128)}, u32[]{:S(2)}, u32[]{:S(2)}) collective-permute-start(f32[96,384]{1,0:T(8,128)S(1)} %turn_block.1.refs_0_), channel_id=1, source_target_pairs={{0,1},{1,0},{2,3},{3,2},{4,5},{5,4},{6,7},{7,6},{8,9},{9,8},{10,11... | collective-permute-start | bytes 442376 | tf_op jit(solution)/shard_map/ppermute | solution.py:30
  37.7 4.6 %collective-permute-start.10 = (f32[96,384]{1,0:T(8,128)}, f32[96,384]{1,0:T(8,128)S(1)}, u32[]{:S(2)}, u32[]{:S(2)}) collective-permute-start(f32[96,384]{1,0:T(8,128)} %collective-permute-done.9.refs_2_), channel_id=1, source_target_pairs={{0,1},{1,0},{2,3},{3,2},{4,5},{5,4},{6,7},{7,6},{8,9},{9,8},{10,11... | collective-permute-start | bytes 442376 | tf_op jit(solution)/shard_map/ppermute | solution.py:30
  39.6 4.0 %collective-permute-start.12 = (f32[96,384]{1,0:T(8,128)}, f32[96,384]{1,0:T(8,128)S(1)}, u32[]{:S(2)}, u32[]{:S(2)}) collective-permute-start(f32[96,384]{1,0:T(8,128)} %collective-permute-done.11.refs_4_), channel_id=1, source_target_pairs={{0,1},{1,0},{2,3},{3,2},{4,5},{5,4},{6,7},{7,6},{8,9},{9,8},{10,11... | collective-permute-start | bytes 442376 | tf_op jit(solution)/shard_map/ppermute | solution.py:30
  39.6 25.1 %collective-permute-start.2 = (f32[48,2048]{1,0:T(8,128)}, f32[48,2048]{1,0:T(8,128)S(1)}, u32[]{:S(2)}, u32[]{:S(2)}) collective-permute-start(f32[48,2048]{1,0:T(8,128)} %collective-permute-done.1.refs_6_), channel_id=1, source_target_pairs={{0,4},{1,5},{4,8},{5,9},{8,12},{9,13},{12,14},{13,15},{14,10},{15,... | collective-permute-start | bytes 1179656 | tf_op jit(solution)/shard_map/ppermute | solution.py:364
  41.2 24.0 %collective-permute-start.5 = (f32[48,2048]{1,0:T(8,128)}, f32[48,2048]{1,0:T(8,128)S(1)}, u32[]{:S(2)}, u32[]{:S(2)}) collective-permute-start(f32[48,2048]{1,0:T(8,128)} %collective-permute-done.4.refs_8_), channel_id=1, source_target_pairs={{0,2},{1,3},{4,0},{5,1},{8,4},{9,5},{12,8},{13,9},{14,12},{15,13},... | collective-permute-start | bytes 1179656 | tf_op jit(solution)/shard_map/ppermute | solution.py:365
  42.4 3.8 %collective-permute-start.14 = (f32[96,384]{1,0:T(8,128)}, f32[96,384]{1,0:T(8,128)}, u32[]{:S(2)}, u32[]{:S(2)}) collective-permute-start(f32[96,384]{1,0:T(8,128)} %copy-done.3), channel_id=1, source_target_pairs={{0,1},{1,0},{2,3},{3,2},{4,5},{5,4},{6,7},{7,6},{8,9},{9,8},{10,11... | collective-permute-start | bytes 442376 | tf_op jit(solution)/shard_map/ppermute | solution.py:30
  43.0 3.3 %collective-permute-start.16 = (f32[96,384]{1,0:T(8,128)}, f32[96,384]{1,0:T(8,128)}, u32[]{:S(2)}, u32[]{:S(2)}) collective-permute-start(f32[96,384]{1,0:T(8,128)} %copy-done.5), channel_id=1, source_target_pairs={{0,1},{1,0},{2,3},{3,2},{4,5},{5,4},{6,7},{7,6},{8,9},{9,8},{10,11... | collective-permute-start | bytes 442376 | tf_op jit(solution)/shard_map/ppermute | solution.py:30
  44.2 8.9 %collective-permute-start.21 = (f32[96,384]{1,0:T(8,128)}, f32[96,384]{1,0:T(8,128)}, u32[]{:S(2)}, u32[]{:S(2)}) collective-permute-start(f32[96,384]{1,0:T(8,128)} %broadcast_select_fusion.1), channel_id=1, source_target_pairs={{0,4},{4,8},{8,12},{12,14},{14,10},{10,6},{6,2},{2,0},{1,3},{5,1},... | collective-permute-start | bytes 442376 | tf_op jit(solution)/shard_map/ppermute | solution.py:369
  46.2 15.5 %collective-permute-start.18 = (f32[96,384]{1,0:T(8,128)S(1)}, f32[96,384]{1,0:T(8,128)S(1)}, u32[]{:S(2)}, u32[]{:S(2)}) collective-permute-start(f32[96,384]{1,0:T(8,128)S(1)} %collective-permute-done.17.refs_10_), channel_id=1, source_target_pairs={{0,1},{1,0},{2,3},{3,2},{4,5},{5,4},{6,7},{7,6},{8,9},{9,8},{10,11... | collective-permute-start | bytes 442376 | tf_op jit(solution)/shard_map/ppermute | solution.py:30
  46.3 15.4 %collective-permute-start.20 = (f32[96,384]{1,0:T(8,128)S(1)}, f32[96,384]{1,0:T(8,128)S(1)}, u32[]{:S(2)}, u32[]{:S(2)}) collective-permute-start(f32[96,384]{1,0:T(8,128)S(1)} %collective-permute-done.19.refs_12_), channel_id=1, source_target_pairs={{0,1},{1,0},{2,3},{3,2},{4,5},{5,4},{6,7},{7,6},{8,9},{9,8},{10,11... | collective-permute-start | bytes 442376 | tf_op jit(solution)/shard_map/ppermute | solution.py:30
  53.1 9.2 %collective-permute-start.22 = (f32[96,384]{1,0:T(8,128)}, f32[96,384]{1,0:T(8,128)S(1)}, u32[]{:S(2)}, u32[]{:S(2)}) collective-permute-start(f32[96,384]{1,0:T(8,128)} %collective-permute-done.21.refs_14_), channel_id=1, source_target_pairs={{0,1},{1,0},{2,3},{3,2},{4,5},{5,4},{6,7},{7,6},{8,9},{9,8},{10,11... | collective-permute-start | bytes 442376 | tf_op jit(solution)/shard_map/ppermute | solution.py:30
  61.7 3.7 %collective-permute-start.25 = (f32[48,2048]{1,0:T(8,128)S(1)}, f32[48,2048]{1,0:T(8,128)S(1)}, u32[]{:S(2)}, u32[]{:S(2)}) collective-permute-start(f32[48,2048]{1,0:T(8,128)S(1)} %link_chain.1.refs_0_), channel_id=1, source_target_pairs={{0,1},{1,0},{2,3},{3,2},{4,5},{5,4},{6,7},{7,6},{8,9},{9,8},{10,11... | collective-permute-start | bytes 1179656 | tf_op jit(solution)/shard_map/ppermute | solution.py:30
  61.7 5.3 %collective-permute-start.26 = (f32[48,2048]{1,0:T(8,128)S(1)}, f32[48,2048]{1,0:T(8,128)S(1)}, u32[]{:S(2)}, u32[]{:S(2)}) collective-permute-start(f32[48,2048]{1,0:T(8,128)S(1)} %copy-done.14), channel_id=1, source_target_pairs={{0,1},{1,0},{2,3},{3,2},{4,5},{5,4},{6,7},{7,6},{8,9},{9,8},{10,11... | collective-permute-start | bytes 1179656 | tf_op jit(solution)/shard_map/ppermute | solution.py:30
  62.2 4.8 %collective-permute-start.27 = (f32[48,2048]{1,0:T(8,128)}, f32[48,2048]{1,0:T(8,128)S(1)}, u32[]{:S(2)}, u32[]{:S(2)}) collective-permute-start(f32[48,2048]{1,0:T(8,128)} %collective-permute-done.3.refs_4_), channel_id=1, source_target_pairs={{0,1},{1,0},{2,3},{3,2},{4,5},{5,4},{6,7},{7,6},{8,9},{9,8},{10,11... | collective-permute-start | bytes 1179656 | tf_op jit(solution)/shard_map/ppermute | solution.py:30
  64.7 2.8 %collective-permute-start.28 = (f32[48,2048]{1,0:T(8,128)}, f32[48,2048]{1,0:T(8,128)S(1)}, u32[]{:S(2)}, u32[]{:S(2)}) collective-permute-start(f32[48,2048]{1,0:T(8,128)} %collective-permute-done.1.refs_6_), channel_id=1, source_target_pairs={{0,1},{1,0},{2,3},{3,2},{4,5},{5,4},{6,7},{7,6},{8,9},{9,8},{10,11... | collective-permute-start | bytes 1179656 | tf_op jit(solution)/shard_map/ppermute | solution.py:30
  65.3 2.3 %collective-permute-start.29 = (f32[48,2048]{1,0:T(8,128)}, f32[48,2048]{1,0:T(8,128)S(1)}, u32[]{:S(2)}, u32[]{:S(2)}) collective-permute-start(f32[48,2048]{1,0:T(8,128)} %collective-permute-done.4.refs_8_), channel_id=1, source_target_pairs={{0,1},{1,0},{2,3},{3,2},{4,5},{5,4},{6,7},{7,6},{8,9},{9,8},{10,11... | collective-permute-start | bytes 1179656 | tf_op jit(solution)/shard_map/ppermute | solution.py:30
  65.4 32.3 %collective-permute-start.6 = (f32[48,2048]{1,0:T(8,128)S(1)}, f32[48,2048]{1,0:T(8,128)S(1)}, u32[]{:S(2)}, u32[]{:S(2)}) collective-permute-start(f32[48,2048]{1,0:T(8,128)S(1)} %broadcast_select_fusion), channel_id=1, source_target_pairs={{0,4},{4,8},{8,12},{12,14},{14,10},{10,6},{6,2},{2,0},{1,3},{5,1},... | collective-permute-start | bytes 1179656 | tf_op jit(solution)/shard_map/ppermute | solution.py:369
  67.0 30.9 %collective-permute-start.23 = (f32[48,2048]{1,0:T(8,128)S(1)}, f32[48,2048]{1,0:T(8,128)S(1)}, u32[]{:S(2)}, u32[]{:S(2)}) collective-permute-start(f32[48,2048]{1,0:T(8,128)S(1)} %collective-permute-done.2.refs_0_), channel_id=1, source_target_pairs={{0,1},{1,0},{2,3},{3,2},{4,5},{5,4},{6,7},{7,6},{8,9},{9,8},{10,11... | collective-permute-start | bytes 1179656 | tf_op jit(solution)/shard_map/ppermute | solution.py:30
  67.0 30.9 %collective-permute-start.24 = (f32[48,2048]{1,0:T(8,128)S(1)}, f32[48,2048]{1,0:T(8,128)S(1)}, u32[]{:S(2)}, u32[]{:S(2)}) collective-permute-start(f32[48,2048]{1,0:T(8,128)S(1)} %collective-permute-done.5.refs_2_), channel_id=1, source_target_pairs={{0,1},{1,0},{2,3},{3,2},{4,5},{5,4},{6,7},{7,6},{8,9},{9,8},{10,11... | collective-permute-start | bytes 1179656 | tf_op jit(solution)/shard_map/ppermute | solution.py:30
  97.7 17.8 %collective-permute-start.7 = (f32[48,2048]{1,0:T(8,128)S(1)}, f32[48,2048]{1,0:T(8,128)S(1)}, u32[]{:S(2)}, u32[]{:S(2)}) collective-permute-start(f32[48,2048]{1,0:T(8,128)S(1)} %collective-permute-done.6.refs_0_), channel_id=1, source_target_pairs={{0,1},{1,0},{2,3},{3,2},{4,5},{5,4},{6,7},{7,6},{8,9},{9,8},{10,11... | collective-permute-start | bytes 1179656 | tf_op jit(solution)/shard_map/ppermute | solution.py:30
  (14 other events, 93.7 us)

commit v3 on v1

--- a/solution.py
+++ b/solution.py
@@ -1,6 +1,8 @@
 import jax
 import jax.numpy as jnp
 from jax import lax
+from jax.experimental import pallas as pl
+from jax.experimental.pallas import tpu as pltpu
 from jax.sharding import PartitionSpec as P
 
 PCOL = 8
@@ -40,14 +42,6 @@
     return pairs
 
 
-def ring_place(chip, count):
-    return jnp.where(chip % 2 == 0, chip // 2, count - 1 - chip // 2)
-
-
-def ring_chip(place, count):
-    return jnp.where(place < count // 2, 2 * place, 2 * (count - 1 - place) + 1)
-
-
 def masked_links(my_index, anc_links, pattern):
     rows_here = anc_links.shape[0]
     tile_index = (my_index * rows_here + jnp.arange(rows_here, dtype=jnp.int32)) // TILE
@@ -72,57 +66,316 @@
     return inner, cross
 
 
-def gather_rounds(message, my_index, count):
-    core = my_index % 2
-    place = ring_place(my_index // 2, count)
-
-    def owner(shift, other):
-        chip = ring_chip((place + shift + count) % count, count)
-        return 2 * chip + jnp.where(other, 1 - core, core)
-
-    ahead, behind = ring_pairs(count, 1), ring_pairs(count, -1)
-    arrivals = [(owner(0, False), message), (owner(0, True), swap_bit(message, 0))]
-    upward = downward = message
-    for step in range(1, (count + 1) // 2):
-        upward = lax.ppermute(upward, "row", ahead)
-        downward = lax.ppermute(downward, "row", behind)
-        arrivals += [(owner(-step, False), upward), (owner(step, False), downward)]
-        arrivals += [(owner(-step, True), swap_bit(upward, 0)), (owner(step, True), swap_bit(downward, 0))]
-    if count % 2 == 0 and count > 1:
-        pairs = [p for p in ahead if p[0] % 2 == 0] + [p for p in behind if p[0] % 2 == 1]
-        last = lax.ppermute(jnp.where(core == 0, upward, downward), "row", pairs)
-        arrivals += [(owner(count // 2, False), last), (owner(count // 2, True), swap_bit(last, 0))]
-    return arrivals
+def halves(value):
+    high = value.astype(jnp.bfloat16)
+    return high, (value - high.astype(jnp.float32)).astype(jnp.bfloat16)
+
+
+def dot_halves(left, right, dims=((1,), (0,))):
+    def one(a, b):
+        return lax.dot_general(a, b, (dims, ((), ())), preferred_element_type=jnp.float32)
+
+    return one(left[0], right[0]) + (one(left[0], right[1]) + one(left[1], right[0]))
+
+
+def stacked_dot(left, right):
+    height = left[0].shape[0]
+    both = jnp.dot(jnp.concatenate(left, axis=0), right[0], preferred_element_type=jnp.float32)
+    cross = jnp.dot(left[0], right[1], preferred_element_type=jnp.float32)
+    return both[:height] + (both[height:] + cross)
+
+
+def kernel_call(kernel, name, flops, moved, limit=16 * 2**20, **more):
+    return pl.pallas_call(
+        kernel,
+        name=name,
+        compiler_params=pltpu.CompilerParams(vmem_limit_bytes=limit),
+        cost_estimate=pl.CostEstimate(flops=flops, bytes_accessed=moved, transcendentals=0),
+        **more,
+    )
+
+
+def in_vmem(count):
+    return [pl.BlockSpec(memory_space=pltpu.VMEM)] * count
+
+
+def after(value, *others):
+    return lax.optimization_barrier((value, *others))[0]
+
+
+def turned_block(block):
+    def kernel(block_ref, out_ref):
+        out_ref[...] = block_ref[...].T
+
+    shape = (block.shape[1], block.shape[0])
+    return kernel_call(
+        kernel, "turn_block", block.size, 8 * block.size, out_shape=jax.ShapeDtypeStruct(shape, jnp.float32)
+    )(block)
+
+
+def link_chain(anc_links, parent_links, pattern):
+    rows, nodes, width = anc_links.shape
+    tiles = pattern.shape[1]
+
+    def kernel(links_ref, parent_ref, pattern_ref, out_ref):
+        first = lax.axis_index("row") * rows
+        tile = first // TILE
+        next_tile = jnp.minimum(tile + 1, tiles - 1)
+        row = first + lax.broadcasted_iota(jnp.int32, (rows, width), 0)
+        in_first = row < (tile + 1) * TILE
+        reduced = None
+        for node in range(nodes):
+            keep = jnp.where(in_first, pattern_ref[node, tile], pattern_ref[node, next_tile])
+            links = jnp.where(keep != 0, links_ref[:, node, :], 0.0)
+            if node > 0:
+                links = links - dot_halves(halves(reduced), halves(parent_ref[node - 1]))
+            out_ref[:, node * width : (node + 1) * width] = links
+            reduced = links
+
+    return kernel_call(
+        kernel,
+        "link_chain",
+        12 * rows * nodes * width * width,
+        4 * parent_links.size,
+        out_shape=jax.ShapeDtypeStruct((rows, nodes * width), jnp.float32),
+        in_specs=in_vmem(2) + [pl.BlockSpec(memory_space=pltpu.SMEM)],
+        out_specs=in_vmem(1)[0],
+    )(anc_links, parent_links, pattern)
+
+
+def inner_chain(parent_links, pivot_inverse):
+    nodes, width, _ = pivot_inverse.shape
+
+    def kernel(parent_ref, pivot_ref, cross_ref, inner_ref):
+        inner = pivot_ref[0]
+        inner_ref[0] = inner
+        for node in range(1, nodes):
+            link = halves(parent_ref[node - 1])
+            cross = dot_halves(halves(inner), link)
+            cross_ref[node - 1] = -cross
+            inner = pivot_ref[node] + dot_halves(link, halves(cross), ((0,), (0,)))
+            inner_ref[node] = inner
+
+    return kernel_call(
+        kernel,
+        "inner_chain",
+        12 * nodes * width**3,
+        16 * pivot_inverse.size,
+        out_shape=[
+            jax.ShapeDtypeStruct(parent_links.shape, jnp.float32),
+            jax.ShapeDtypeStruct(pivot_inverse.shape, jnp.float32),
+        ],
+        in_specs=in_vmem(2),
+        out_specs=in_vmem(2),
+    )(parent_links, pivot_inverse)
+
+
+def ring_owner(my_index, count, shift, other):
+    core = lax.rem(my_index, 2)
+    chip = my_index // 2
+    place = jnp.where(lax.rem(chip, 2) == 0, chip // 2, count - 1 - chip // 2)
+    place = lax.rem(place + shift + count, count)
+    chip = jnp.where(place < count // 2, 2 * place, 2 * (count - 1 - place) + 1)
+    return 2 * chip + (1 - core if other else core)
+
+
+def opening(blocks, links, parents, diagonals, chips):
+    nodes, width, _ = diagonals.shape
+    rows = links[0][2].shape[0]
+    half_columns = blocks[0][2].shape[1]
+    order, fresh = 2 * half_columns, rows * len(links)
+    bf16 = jnp.bfloat16
+
+    def kernel(*refs):
+        block_refs, refs = refs[: len(blocks)], refs[len(blocks) :]
+        link_refs, refs = refs[: len(links)], refs[len(links) :]
+        parents_ref, diagonals_ref, parents_out, diagonals_out = refs[:4]
+        ancestor, held = refs[4:6], refs[6:8]
+        turned = refs[8:10]
+        me = lax.axis_index("row")
+        for (shift, other, _), ref in zip(blocks, block_refs):
+            owner = ring_owner(me, chips, shift, other)
+            place = pl.multiple_of(owner // PCOL * half_columns, 128)
+            parts = halves(ref[...])
+            for piece in range(2):
+                row = pl.multiple_of((lax.rem(owner, PCOL) + PCOL * piece) * rows, 16)
+                for whole, part in zip(ancestor, parts):
+                    whole[pl.ds(row, rows), pl.ds(place, half_columns)] = part[piece * rows : (piece + 1) * rows]
+        starts = [pl.multiple_of(ring_owner(me, chips, s, o) * rows, 16) for s, o, _ in links]
+        for whole in held:
+            whole[...] = jnp.zeros(whole.shape, bf16)
+        for start, ref in zip(starts, link_refs):
+            for whole, part in zip(held, halves(ref[...])):
+                whole[pl.ds(start, rows), :] = part
+        left = [jnp.concatenate([whole[pl.ds(start, rows), :] for start in starts]) for whole in ancestor]
+        for node in range(nodes):
+            columns = slice(node * width, (node + 1) * width)
+            new = jnp.concatenate([ref[:, columns] for ref in link_refs], axis=0).T
+            for whole, part in zip(turned, halves(new)):
+                whole[columns, :] = part
+        for node in range(nodes):
+            columns = slice(node * width, (node + 1) * width)
+            image = halves(stacked_dot(left, [whole[:, columns] for whole in held]))
+            lower = max(node - 1, 0) * width
+            total = stacked_dot([whole[lower : (node + 1) * width, :] for whole in turned], image)
+            diagonals_out[node] = diagonals_ref[node] + total[-width:]
+            if node > 0:
+                parents_out[node - 1] = parents_ref[node - 1] + total[:width]
+
+    operands = [array for _, _, array in blocks + links] + [parents, diagonals]
+    results = kernel_call(
+        kernel,
+        "opening",
+        6 * nodes * fresh * width * (order + 2 * width),
+        4 * sum(array.size for array in operands),
+        out_shape=[jax.ShapeDtypeStruct(array.shape, jnp.float32) for array in (parents, diagonals)]
+        + [jax.ShapeDtypeStruct((order, order), bf16)] * 2
+        + [jax.ShapeDtypeStruct((order, nodes * width), bf16)] * 2,
+        in_specs=in_vmem(len(operands)),
+        out_specs=in_vmem(6),
+        scratch_shapes=[pltpu.VMEM((nodes * width, fresh), bf16)] * 2,
+    )(*operands)
+    return results[:2], results[2:4], results[4:]
+
+
+def border(links, ancestor, held, parents, diagonals, chips, last):
+    nodes, width, _ = diagonals.shape
+    rows = links[0][2].shape[0]
+    order, fresh = ancestor[0].shape[0], rows * len(links)
+    bf16 = jnp.bfloat16
+
+    def kernel(*refs):
+        link_refs, refs = refs[: len(links)], refs[len(links) :]
+        whole_ancestor, held_before = refs[:2], refs[2:4]
+        parents_ref, diagonals_ref, parents_out, diagonals_out = refs[4:8]
+        copies = []
+
+        def finish(place, source, target):
+            if last:
+                copies.append(pltpu.make_async_copy(source, target, sems.at[place]))
+                copies[-1].start()
+
+        if last:
+            panel_out, refs = refs[8], refs[9:]
+            parents_end, diagonals_end, panel_end = parents_out, diagonals_out, panel_out
+            parents_out, diagonals_out, panel_out, sems = refs[4:8]
+        else:
+            refs = refs[8:]
+            parents_end, diagonals_end = parents_out, diagonals_out
+        held, turned = refs[:2], refs[2:4]
+        me = lax.axis_index("row")
+        owners = [ring_owner(me, chips, shift, other) for shift, other, _ in links]
+        starts = [pl.multiple_of(owner * rows, 16) for owner in owners]
+        for whole, before in zip(held, held_before):
+            whole[...] = before[...]
+        for start, ref in zip(starts, link_refs):
+            for whole, part in zip(held, halves(ref[...])):
+                whole[pl.ds(start, rows), :] = part
+        piece = lax.broadcasted_iota(jnp.int32, (1, order), 1) // rows
+        weight = jnp.ones((1, order), jnp.float32)
+        for owner in owners:
+            weight = jnp.where(piece == owner, 0.5, weight)
+        weight = weight.astype(bf16)
+        left = [
+            jnp.concatenate([whole[pl.ds(start, rows), :] for start in starts], axis=0) * weight
+            for whole in whole_ancestor
+        ]
+        if last:
+            own = pl.multiple_of(me * rows, 16)
+            left = [
+                jnp.concatenate([part, whole[pl.ds(own, rows), :]], axis=0)
+                for part, whole in zip(left, whole_ancestor)
+            ]
+        right = []
+        for node in range(nodes):
+            columns = slice(node * width, (node + 1) * width)
+            image = stacked_dot(left, [whole[:, columns] for whole in held])
+            if last:
+                panel_out[:, node, :] = -image[fresh:]
+            image = image[:fresh]
+            new = jnp.concatenate([ref[:, columns] for ref in link_refs], axis=0)
+            for whole, part in zip(turned, halves(jnp.concatenate([new, image], axis=0).T)):
+                whole[columns, :] = part
+            right.append([jnp.concatenate(pair, axis=0) for pair in zip(halves(image), halves(new))])
+        if last:
+            finish(2 * nodes, panel_out, panel_end)
+        for node in range(nodes):
+            lower = max(node - 1, 0) * width
+            total = stacked_dot([whole[lower : (node + 1) * width, :] for whole in turned], right[node])
+            diagonals_out[node] = diagonals_ref[node] + total[-width:]
+            finish(node, diagonals_out.at[node], diagonals_end.at[node])
+            if node > 0:
+                parents_out[node - 1] = parents_ref[node - 1] + total[:width]
+                finish(nodes + node, parents_out.at[node - 1], parents_end.at[node - 1])
+        for copy in copies:
+            copy.wait()
+
+    operands = [array for _, _, array in links] + [*ancestor, *held, parents, diagonals]
+    count = len(links)
+    shapes = [jax.ShapeDtypeStruct(array.shape, jnp.float32) for array in (parents, diagonals)]
+    scratch = [pltpu.VMEM((nodes * width, 2 * fresh), bf16)] * 2
+    if last:
+        shapes.append(jax.ShapeDtypeStruct((rows, nodes, width), jnp.float32))
+        scratch = [pltpu.VMEM(array.shape, bf16) for array in held] + scratch
+        scratch += [pltpu.VMEM(array.shape, jnp.float32) for array in shapes]
+        scratch.append(pltpu.SemaphoreType.DMA((2 * nodes + 1,)))
+    else:
+        shapes += [jax.ShapeDtypeStruct(array.shape, bf16) for array in held]
+    results = kernel_call(
+        kernel,
+        "border_" + str(count),
+        6 * nodes * fresh * width * (order + 4 * width),
+        4 * sum(array.size for array in operands),
+        out_shape=shapes,
+        in_specs=in_vmem(len(operands)),
+        out_specs=[pl.BlockSpec(memory_space=pl.ANY)] * len(shapes) if last else in_vmem(len(shapes)),
+        scratch_shapes=scratch,
+        limit=24 * 2**20,
+    )(*operands)
+    return results[:2], results[2:]
 
 
 def gather_plan(anc_blocks, anc_links, parent_links, pivot_inverse, pattern):
     my_index = lax.axis_index("row")
-    size = lax.axis_size("row")
-    rows, nodes, width = anc_links.shape
-    order = rows * size
-    half = my_index // PCOL
-    block = anc_blocks[0].T.reshape(2, rows, order // 2)
-    mine = lax.dynamic_index_in_dim(block, half, 0, False)
-    theirs = swap_bit(lax.dynamic_index_in_dim(block, 1 - half, 0, False), PCOL.bit_length() - 1)
-    low, high = jnp.where(half == 0, mine, theirs), jnp.where(half == 0, theirs, mine)
-    links = masked_links(my_index, anc_links, pattern)
-    message = jnp.concatenate(reduced_links(links, parent_links) + [low, high], axis=1)
-    inner, cross = local_chain(parent_links, pivot_inverse)
-    whole = jnp.zeros((order, message.shape[1]), jnp.float32)
-    for owner, part in gather_rounds(message, my_index, size // 2):
-        whole = lax.dynamic_update_slice(whole, part, (owner * rows, 0))
-    links, ancestor = whole[:, : nodes * width], whole[:, nodes * width :]
-    image = product(ancestor, links)
-    panels = -lax.dynamic_slice_in_dim(image, my_index * rows, rows, 0).reshape(rows, nodes, width)
-    column = lambda array, node: array[:, node * width : (node + 1) * width]
-    diagonals = [
-        inner[node] + inner_product(column(links, node), column(image, node)) for node in range(nodes)
-    ]
-    parents = [
-        inner_product(column(links, node - 1), column(image, node)) - cross[node - 1]
-        for node in range(1, nodes)
-    ]
-    return panels, jnp.stack(parents), jnp.stack(diagonals)
+    chips = lax.axis_size("row") // 2
+    ahead, behind = ring_pairs(chips, 1), ring_pairs(chips, -1)
+    across = [p for p in ahead if p[0] % 2 == 0] + [p for p in behind if p[0] % 2 == 1]
+    far = chips // 2
+
+    def move(pair):
+        return [lax.ppermute(value, "row", way) for value, way in zip(pair, (ahead, behind))]
+
+    def turn(pair):
+        return lax.ppermute(jnp.where(my_index % 2 == 0, *pair), "row", across)
+
+    def both(shift, value):
+        return [(shift, False, value), (shift, True, swap_bit(value, 0))]
+
+    def sides(step, pair):
+        return both(-step, pair[0]) + both(step, pair[1])
+
+    blocks = [turned_block(anc_blocks[0])]
+    blocks.append(move(blocks * 2))
+    links = [link_chain(after(anc_links, blocks[0]), parent_links, pattern)]
+    links.append(move(links * 2))
+    totals = inner_chain(after(parent_links, links[0]), pivot_inverse)
+    blocks[1] = list(lax.optimization_barrier((*blocks[1], *totals))[:2])
+    for step in range(2, far):
+        blocks.append(move(blocks[-1]))
+        links.append(move(links[-1]))
+    blocks.append(turn(blocks[-1]))
+    links.append(turn(links[-1]))
+
+    parts = both(0, blocks[0]) + both(far, blocks[-1])
+    for step in range(1, far):
+        parts += sides(step, blocks[step])
+    first = both(0, links[0])
+    for step in range(1, far - 1):
+        first += sides(step, links[step])
+    totals, ancestor, held = opening(parts, first, *totals, chips)
+    totals, held = border(sides(far - 1, links[far - 1]), ancestor, held, *totals, chips, False)
+    totals, panels = border(both(far, links[far]), ancestor, held, *totals, chips, True)
+    return panels[0], *totals
 
 
 def spread_plan(anc_blocks, anc_links, parent_links, pivot_inverse, pattern):

time: 166 us -> 95.9 us (0.58)
  matrix products: 77.6 us -> 0 us
  Pallas kernels: 0 us -> 33.9 us
  local copies, waits for them, and re-layouts: 43.3 us -> 16.1 us
  other arithmetic: 6.57 us -> 0.06 us
  starting transfers between devices: 12.7 us -> 18.5 us
  waiting for transfers between devices: 23.2 us -> 26 us
    dot_general x37 -> x0, matrix products: 77.6 us -> none  [the longest x22 50.8 us: inner_product(): lax.dot_general(left, right, (((0,), (0,)), ((), ())), precision=lax.Prec...]
    pallas_call x0 -> x6, Pallas kernels: none -> 33.9 us  [the longest x1 16.8 us: opening(): kernel_call(kernel, 'opening', 6 * nodes * fresh * width * (order + 2 * w...]
    dynamic_update_slice x15 -> x0, local copies, waits for them, and re-layouts: 16.9 us -> none  [gather_plan(): whole = lax.dynamic_update_slice(whole, part, (owner * rows, 0))]
    ppermute x7 -> x14, starting transfers between devices: 7.65 us -> 14.5 us  [the longest x12 13.2 us: move(): lax.ppermute(value, 'row', way)]
    broadcast_in_dim x1 -> x0, local copies, waits for them, and re-layouts: 3.94 us -> none  [gather_plan(): whole = jnp.zeros((order, message.shape[1]), jnp.float32)]
    select_n x3 -> x2, other arithmetic: 3.28 us -> 0.06 us  [turn(): return lax.ppermute(jnp.where(my_index % 2 == 0, *pair), 'row', across)]
    slice x1 -> x0, local copies, waits for them, and re-layouts: 2.6 us -> none  [local_chain(): inner.append(pivot_inverse[node] + inner_product(link, cross[-1]))]
    ppermute x9 -> x16, waiting for transfers between devices: 0.02 us -> 1.81 us  [swap_bit(): lax.ppermute(value, 'row', [(i, i ^ mask) for i in range(lax.axis_size('r...]
  transfers between devices with their start and end apart: 16 -> 30, of which waited for: 4 -> 8; matrix products, arithmetic and copies ran while one was open for 38% -> 0% of each run, Pallas kernels for 0% -> 28%
where the time goes in v3:
time: 95.9 us; the launch traced here: 95.5 us
  Pallas kernels  33.9 us (35%)
  waiting for transfers between devices  26 us (27%)
  starting transfers between devices  18.5 us (19%)
  local copies, waits for them, and re-layouts  16.1 us (17%)
    ppermute x12, waiting for transfers between devices, move(): lax.ppermute(value, 'row', way)  18.5 us
    pallas_call x1, Pallas kernels, opening(): kernel_call(kernel, 'opening', 6 * nodes * fresh * width * (order + 2 * w...  16.8 us
    unnamed x31, local copies, waits for them, and re-layouts  16.1 us
    ppermute x12, starting transfers between devices, move(): lax.ppermute(value, 'row', way)  13.2 us
    pallas_call x2, Pallas kernels, border(): kernel_call(kernel, 'border_' + str(count), 6 * nodes * fresh * width * (...  10.9 us
    ppermute x2, waiting for transfers between devices, turn(): return lax.ppermute(jnp.where(my_index % 2 == 0, *pair), 'row', across)  5.7 us
    pallas_call x1, Pallas kernels, inner_chain(): kernel_call(kernel, 'inner_chain', 12 * nodes * width ** 3, 16 * pivot_in...  4.18 us
    ppermute x16, starting transfers between devices, swap_bit(): lax.ppermute(value, 'row', [(i, i ^ mask) for i in range(lax.axis_size('r...  4.01 us
  transfers between devices with their start and end apart: 30, of which 8 were waited for; matrix products, arithmetic and copies ran while one was open for 0% of the time, Pallas kernels for 28%

profile of v3, /device:TPU:0, one launch (start us, length us, event | category | flops | bytes accessed | tf_op | source)
XLA Modules:
  0.0 95.5 jit_solution(10731125910934673257)
XLA Ops:
  0.6 1.0 %copy.8 = f32[1,384,96]{2,1,0:T(8,128)S(1)} copy(f32[1,384,96]{1,2,0:T(8,128)} %param.5) | data formatting | bytes 294912 | tf_op args[0]
  1.8 1.5 %copy-done = f32[7,256,256]{2,1,0:T(8,128)S(1)} copy-done((f32[7,256,256]{2,1,0:T(8,128)S(1)}, f32[7,256,256]{2,1,0:T(8,128)}, u32[]{:S(2)}) %copy-start) | copy-done | bytes 1835032
  3.3 1.0 %copy-done.2 = f32[48,8,256]{2,1,0:T(8,128)S(1)} copy-done((f32[48,8,256]{2,1,0:T(8,128)S(1)}, f32[48,8,256]{2,1,0:T(8,128)}, u32[]{:S(2)}) %copy-start.2) | copy-done | bytes 393240
  4.3 0.7 copy-done.3
  5.0 1.9 %link_chain.1.refs_16_ = f32[48,2048]{1,0:T(8,128)S(1)} custom-call(f32[48,8,256]{2,1,0:T(8,128)S(1)} %copy-done.2, f32[7,256,256]{2,1,0:T(8,128)S(1)} %copy-done, s32[8,6]{1,0:T(8,128)S(1)} %copy-done.3), custom_call_target="tpu_custom_call" | custom-call | flops 301989888 | bytes 1835008 | tf_op jit(solution)/shard_map/link_chain/pallas_call | solution.py:135
  6.9 3.1 %collective-permute-start = (f32[48,2048]{1,0:T(8,128)S(1)}, f32[48,2048]{1,0:T(8,128)S(1)}, u32[]{:S(2)}, u32[]{:S(2)}) collective-permute-start(f32[48,2048]{1,0:T(8,128)S(1)} %link_chain.1.refs_16_), channel_id=1, source_target_pairs={{0,4},{1,5},{4,8},{5,9},{8,12},{9,13},{12,14},{13,15},{14,10},{15,... | collective-permute-start | bytes 1179656 | tf_op jit(solution)/shard_map/ppermute | solution.py:346
  10.0 1.9 %collective-permute-start.10 = (f32[96,384]{1,0:T(8,128)S(1)}, f32[96,384]{1,0:T(8,128)S(1)}, u32[]{:S(2)}, u32[]{:S(2)}) collective-permute-start(f32[96,384]{1,0:T(8,128)S(1)} %turn_block.1.refs_0_), channel_id=1, source_target_pairs={{0,2},{1,3},{4,0},{5,1},{8,4},{9,5},{12,8},{13,9},{14,12},{15,13},... | collective-permute-start | bytes 442376 | tf_op jit(solution)/shard_map/ppermute | solution.py:346
  12.1 1.6 %copy-done.4 = f32[8,256,256]{2,1,0:T(8,128)S(1)} copy-done((f32[8,256,256]{2,1,0:T(8,128)S(1)}, f32[8,256,256]{2,1,0:T(8,128)}, u32[]{:S(2)}) %copy-start.4) | copy-done | bytes 2097176
  13.6 4.2 %inner_chain.1 = (f32[7,256,256]{2,1,0:T(8,128)S(1)}, f32[8,256,256]{2,1,0:T(8,128)S(1)}) custom-call(f32[7,256,256]{2,1,0:T(8,128)S(1)} %copy-done.1, f32[8,256,256]{2,1,0:T(8,128)S(1)} %copy-done.4), custom_call_target="tpu_custom_call" | custom-call | flops 1610612736 | bytes 8388608 | tf_op jit(solution)/shard_map/inner_chain/pallas_call | solution.py:159
  17.8 1.3 %copy-done.11 = f32[8,256,256]{2,1,0:T(8,128)} copy-done((f32[8,256,256]{2,1,0:T(8,128)}, f32[8,256,256]{2,1,0:T(8,128)S(1)}, u32[]{:S(2)}) %copy-start.11) | copy-done | bytes 2097176
  19.2 1.2 %copy-done.13 = f32[7,256,256]{2,1,0:T(8,128)} copy-done((f32[7,256,256]{2,1,0:T(8,128)}, f32[7,256,256]{2,1,0:T(8,128)S(1)}, u32[]{:S(2)}) %copy-start.13) | copy-done | bytes 1835032
  20.4 3.3 %collective-permute-done.10.refs_6_ = f32[96,384]{1,0:T(8,128)S(1)} collective-permute-done((f32[96,384]{1,0:T(8,128)S(1)}, f32[96,384]{1,0:T(8,128)S(1)}, u32[]{:S(2)}, u32[]{:S(2)}) %collective-permute-start.10) | collective-permute-done | bytes 147488 | tf_op jit(solution)/shard_map/ppermute | solution.py:346
  23.7 1.6 %collective-permute-start.11 = (f32[96,384]{1,0:T(8,128)S(1)}, f32[96,384]{1,0:T(8,128)}, u32[]{:S(2)}, u32[]{:S(2)}) collective-permute-start(f32[96,384]{1,0:T(8,128)S(1)} %collective-permute-done.9.refs_4_), channel_id=1, source_target_pairs={{0,4},{1,5},{4,8},{5,9},{8,12},{9,13},{12,14},{13,15},{14,10},{15,... | collective-permute-start | bytes 442376 | tf_op jit(solution)/shard_map/ppermute | solution.py:346
  25.3 1.6 %collective-permute-start.1 = (f32[48,2048]{1,0:T(8,128)S(1)}, f32[48,2048]{1,0:T(8,128)S(1)}, u32[]{:S(2)}, u32[]{:S(2)}) collective-permute-start(f32[48,2048]{1,0:T(8,128)S(1)} %collective-permute-done.refs_18_), channel_id=1, source_target_pairs={{0,4},{1,5},{4,8},{5,9},{8,12},{9,13},{12,14},{13,15},{14,10},{15,... | collective-permute-start | bytes 1179656 | tf_op jit(solution)/shard_map/ppermute | solution.py:346
  28.5 2.2 %collective-permute-done.11.refs_8_ = f32[96,384]{1,0:T(8,128)} collective-permute-done((f32[96,384]{1,0:T(8,128)S(1)}, f32[96,384]{1,0:T(8,128)}, u32[]{:S(2)}, u32[]{:S(2)}) %collective-permute-start.11) | collective-permute-done | bytes 147488 | tf_op jit(solution)/shard_map/ppermute | solution.py:346
  30.6 8.6 %collective-permute-done.13.refs_10_ = f32[96,384]{1,0:T(8,128)} collective-permute-done((f32[96,384]{1,0:T(8,128)S(1)}, f32[96,384]{1,0:T(8,128)}, u32[]{:S(2)}, u32[]{:S(2)}) %collective-permute-start.13) | collective-permute-done | bytes 147488 | tf_op jit(solution)/shard_map/ppermute | solution.py:346
  39.9 1.5 %collective-permute-start.12 = (f32[96,384]{1,0:T(8,128)}, f32[96,384]{1,0:T(8,128)S(1)}, u32[]{:S(2)}, u32[]{:S(2)}) collective-permute-start(f32[96,384]{1,0:T(8,128)} %collective-permute-done.11.refs_8_), channel_id=1, source_target_pairs={{0,4},{1,5},{4,8},{5,9},{8,12},{9,13},{12,14},{13,15},{14,10},{15,... | collective-permute-start | bytes 442376 | tf_op jit(solution)/shard_map/ppermute | solution.py:346
  42.6 1.5 %collective-permute-start.2 = (f32[48,2048]{1,0:T(8,128)S(1)}, f32[48,2048]{1,0:T(8,128)S(1)}, u32[]{:S(2)}, u32[]{:S(2)}) collective-permute-start(f32[48,2048]{1,0:T(8,128)S(1)} %collective-permute-done.1.refs_22_), channel_id=1, source_target_pairs={{0,4},{1,5},{4,8},{5,9},{8,12},{9,13},{12,14},{13,15},{14,10},{15,... | collective-permute-start | bytes 1179656 | tf_op jit(solution)/shard_map/ppermute | solution.py:346
  44.6 2.1 %collective-permute-done.12.refs_12_ = f32[96,384]{1,0:T(8,128)S(1)} collective-permute-done((f32[96,384]{1,0:T(8,128)}, f32[96,384]{1,0:T(8,128)S(1)}, u32[]{:S(2)}, u32[]{:S(2)}) %collective-permute-start.12) | collective-permute-done | bytes 147488 | tf_op jit(solution)/shard_map/ppermute | solution.py:346
  46.8 2.2 %collective-permute-done.14.refs_14_ = f32[96,384]{1,0:T(8,128)S(1)} collective-permute-done((f32[96,384]{1,0:T(8,128)}, f32[96,384]{1,0:T(8,128)S(1)}, u32[]{:S(2)}, u32[]{:S(2)}) %collective-permute-start.14) | collective-permute-done | bytes 147488 | tf_op jit(solution)/shard_map/ppermute | solution.py:346
  49.8 0.7 collective-permute-done.20.refs_11_
  50.7 5.7 %collective-permute-done.15.refs_2_ = f32[96,384]{1,0:T(8,128)S(1)} collective-permute-done((f32[96,384]{1,0:T(8,128)S(1)}, f32[96,384]{1,0:T(8,128)S(1)}, u32[]{:S(2)}, u32[]{:S(2)}) %collective-permute-start.15) | collective-permute-done | bytes 147488 | tf_op jit(solution)/shard_map/ppermute | solution.py:349
  56.4 1.7 %collective-permute-start.24 = (f32[48,2048]{1,0:T(8,128)S(1)}, f32[48,2048]{1,0:T(8,128)S(1)}, u32[]{:S(2)}, u32[]{:S(2)}) collective-permute-start(f32[48,2048]{1,0:T(8,128)S(1)} %collective-permute-done.refs_18_), channel_id=1, source_target_pairs={{0,1},{1,0},{2,3},{3,2},{4,5},{5,4},{6,7},{7,6},{8,9},{9,8},{10,11... | collective-permute-start | bytes 1179656 | tf_op jit(solution)/shard_map/ppermute | solution.py:29
  59.2 1.0 %collective-permute-done.16.refs_3_ = f32[96,384]{1,0:T(8,128)S(1)} collective-permute-done((f32[96,384]{1,0:T(8,128)S(1)}, f32[96,384]{1,0:T(8,128)S(1)}, u32[]{:S(2)}, u32[]{:S(2)}) %collective-permute-start.16) | collective-permute-done | bytes 147488 | tf_op jit(solution)/shard_map/ppermute | solution.py:29
  61.3 0.9 copy-done.6
  62.3 0.9 copy-done.8
  63.2 0.9 copy-done.10
  64.1 1.6 %copy-done.12 = f32[8,256,256]{2,1,0:T(8,128)S(1)} copy-done((f32[8,256,256]{2,1,0:T(8,128)S(1)}, f32[8,256,256]{2,1,0:T(8,128)}, u32[]{:S(2)}) %copy-start.12) | copy-done | bytes 2097176
  65.7 1.5 %copy-done.14 = f32[7,256,256]{2,1,0:T(8,128)S(1)} copy-done((f32[7,256,256]{2,1,0:T(8,128)S(1)}, f32[7,256,256]{2,1,0:T(8,128)}, u32[]{:S(2)}) %copy-start.14) | copy-done | bytes 1835032
  67.2 16.8 %opening.1 = (f32[7,256,256]{2,1,0:T(8,128)S(1)}, f32[8,256,256]{2,1,0:T(8,128)S(1)}, bf16[768,768]{1,0:T(8,128)(2,1)S(1)}, bf16[768,768]{1,0:T(8,128)(2,1)S(1)}...) custom-call(f32[96,384]{1,0:T(8,128)S(1)} %turn_block.1.refs_0_, f32[96,384]{1,0:T(8,128)S(1)} %copy-done.6, ...), custom_call_target="tpu_custom_call" | custom-call | flops 7549747200 | bytes 10223616 | tf_op jit(solution)/shard_map/opening/pallas_call | solution.py:226
  84.4 6.0 %border_4.1 = (f32[7,256,256]{2,1,0:T(8,128)S(1)}, f32[8,256,256]{2,1,0:T(8,128)S(1)}, bf16[768,2048]{1,0:T(8,128)(2,1)S(1)}, bf16[768,2048]{1,0:T(8,128)(2,1)S(1)}) custom-call(f32[48,2048]{1,0:T(8,128)S(1)} %collective-permute-done.2.refs_0_, f32[48,2048]{1,0:T(8,128)S(1)} %collective-permute-done.28.refs_1_, ...), custom_call_target="tpu_custom_call" | custom-call | flops 4227858432 | bytes 22806528 | tf_op jit(solution)/shard_map/border_4/pallas_call | solution.py:324
  90.4 4.9 %border_2.1 = (f32[7,256,256]{2,1,0:T(8,128)}, f32[8,256,256]{2,1,0:T(8,128)}, f32[48,8,256]{2,1,0:T(8,128)}) custom-call(f32[48,2048]{1,0:T(8,128)S(1)} %collective-permute-done.6.refs_0_, f32[48,2048]{1,0:T(8,128)S(1)} %collective-permute-done.7.refs_1_, bf16[768,768]{1,0:T(8,128)(2,1)S(1)} %get-tuple-element.28.refs_4_.refs_2_, ...), custom_call_target="tpu_custom_call" | custom-call | flops 2113929216 | bytes 22020096 | tf_op jit(solution)/shard_map/border_2/pallas_call | solution.py:324
  (67 shorter events, 7.9 us)
Async XLA Ops:
  5.0 7.1 %copy-start.1 = (f32[7,256,256]{2,1,0:T(8,128)S(1)}, f32[7,256,256]{2,1,0:T(8,128)}, u32[]{:S(2)}) copy-start(f32[7,256,256]{2,1,0:T(8,128)} %parent_ref.2) | copy-start | bytes 5505028
  6.9 18.4 %collective-permute-start = (f32[48,2048]{1,0:T(8,128)S(1)}, f32[48,2048]{1,0:T(8,128)S(1)}, u32[]{:S(2)}, u32[]{:S(2)}) collective-permute-start(f32[48,2048]{1,0:T(8,128)S(1)} %link_chain.1.refs_16_), channel_id=1, source_target_pairs={{0,4},{1,5},{4,8},{5,9},{8,12},{9,13},{12,14},{13,15},{14,10},{15,... | collective-permute-start | bytes 1179656 | tf_op jit(solution)/shard_map/ppermute | solution.py:346
  10.0 16.9 %collective-permute-start.3 = (f32[48,2048]{1,0:T(8,128)S(1)}, f32[48,2048]{1,0:T(8,128)S(1)}, u32[]{:S(2)}, u32[]{:S(2)}) collective-permute-start(f32[48,2048]{1,0:T(8,128)S(1)} %link_chain.1.refs_16_), channel_id=1, source_target_pairs={{0,2},{1,3},{4,0},{5,1},{8,4},{9,5},{12,8},{13,9},{14,12},{15,13},... | collective-permute-start | bytes 1179656 | tf_op jit(solution)/shard_map/ppermute | solution.py:346
  10.0 13.7 %collective-permute-start.10 = (f32[96,384]{1,0:T(8,128)S(1)}, f32[96,384]{1,0:T(8,128)S(1)}, u32[]{:S(2)}, u32[]{:S(2)}) collective-permute-start(f32[96,384]{1,0:T(8,128)S(1)} %turn_block.1.refs_0_), channel_id=1, source_target_pairs={{0,2},{1,3},{4,0},{5,1},{8,4},{9,5},{12,8},{13,9},{14,12},{15,13},... | collective-permute-start | bytes 442376 | tf_op jit(solution)/shard_map/ppermute | solution.py:346
  11.9 11.8 %collective-permute-start.9 = (f32[96,384]{1,0:T(8,128)S(1)}, f32[96,384]{1,0:T(8,128)S(1)}, u32[]{:S(2)}, u32[]{:S(2)}) collective-permute-start(f32[96,384]{1,0:T(8,128)S(1)} %turn_block.1.refs_0_), channel_id=1, source_target_pairs={{0,4},{1,5},{4,8},{5,9},{8,12},{9,13},{12,14},{13,15},{14,10},{15,... | collective-permute-start | bytes 442376 | tf_op jit(solution)/shard_map/ppermute | solution.py:346
  12.0 15.7 %collective-permute-start.8 = (f32[96,384]{1,0:T(8,128)S(1)}, f32[96,384]{1,0:T(8,128)S(1)}, u32[]{:S(2)}, u32[]{:S(2)}) collective-permute-start(f32[96,384]{1,0:T(8,128)S(1)} %turn_block.1.refs_0_), channel_id=1, source_target_pairs={{0,1},{1,0},{2,3},{3,2},{4,5},{5,4},{6,7},{7,6},{8,9},{9,8},{10,11... | collective-permute-start | bytes 442376 | tf_op jit(solution)/shard_map/ppermute | solution.py:29
  12.1 1.6 %copy-start.4 = (f32[8,256,256]{2,1,0:T(8,128)S(1)}, f32[8,256,256]{2,1,0:T(8,128)}, u32[]{:S(2)}) copy-start(f32[8,256,256]{2,1,0:T(8,128)} %pivot_ref.1) | copy-start | bytes 6291460
  23.7 6.9 %collective-permute-start.11 = (f32[96,384]{1,0:T(8,128)S(1)}, f32[96,384]{1,0:T(8,128)}, u32[]{:S(2)}, u32[]{:S(2)}) collective-permute-start(f32[96,384]{1,0:T(8,128)S(1)} %collective-permute-done.9.refs_4_), channel_id=1, source_target_pairs={{0,4},{1,5},{4,8},{5,9},{8,12},{9,13},{12,14},{13,15},{14,10},{15,... | collective-permute-start | bytes 442376 | tf_op jit(solution)/shard_map/ppermute | solution.py:346
  25.3 17.3 %collective-permute-start.1 = (f32[48,2048]{1,0:T(8,128)S(1)}, f32[48,2048]{1,0:T(8,128)S(1)}, u32[]{:S(2)}, u32[]{:S(2)}) collective-permute-start(f32[48,2048]{1,0:T(8,128)S(1)} %collective-permute-done.refs_18_), channel_id=1, source_target_pairs={{0,4},{1,5},{4,8},{5,9},{8,12},{9,13},{12,14},{13,15},{14,10},{15,... | collective-permute-start | bytes 1179656 | tf_op jit(solution)/shard_map/ppermute | solution.py:346
  26.9 17.2 %collective-permute-start.4 = (f32[48,2048]{1,0:T(8,128)S(1)}, f32[48,2048]{1,0:T(8,128)S(1)}, u32[]{:S(2)}, u32[]{:S(2)}) collective-permute-start(f32[48,2048]{1,0:T(8,128)S(1)} %collective-permute-done.3.refs_20_), channel_id=1, source_target_pairs={{0,2},{1,3},{4,0},{5,1},{8,4},{9,5},{12,8},{13,9},{14,12},{15,13},... | collective-permute-start | bytes 1179656 | tf_op jit(solution)/shard_map/ppermute | solution.py:346
  27.3 11.9 %collective-permute-start.13 = (f32[96,384]{1,0:T(8,128)S(1)}, f32[96,384]{1,0:T(8,128)}, u32[]{:S(2)}, u32[]{:S(2)}) collective-permute-start(f32[96,384]{1,0:T(8,128)S(1)} %collective-permute-done.10.refs_6_), channel_id=1, source_target_pairs={{0,2},{1,3},{4,0},{5,1},{8,4},{9,5},{12,8},{13,9},{14,12},{15,13},... | collective-permute-start | bytes 442376 | tf_op jit(solution)/shard_map/ppermute | solution.py:346
  28.4 10.8 %collective-permute-start.17 = (f32[96,384]{1,0:T(8,128)S(1)}, f32[96,384]{1,0:T(8,128)S(1)}, u32[]{:S(2)}, u32[]{:S(2)}) collective-permute-start(f32[96,384]{1,0:T(8,128)S(1)} %collective-permute-done.9.refs_4_), channel_id=1, source_target_pairs={{0,1},{1,0},{2,3},{3,2},{4,5},{5,4},{6,7},{7,6},{8,9},{9,8},{10,11... | collective-permute-start | bytes 442376 | tf_op jit(solution)/shard_map/ppermute | solution.py:29
  30.6 10.8 %collective-permute-start.18 = (f32[96,384]{1,0:T(8,128)S(1)}, f32[96,384]{1,0:T(8,128)S(1)}, u32[]{:S(2)}, u32[]{:S(2)}) collective-permute-start(f32[96,384]{1,0:T(8,128)S(1)} %collective-permute-done.10.refs_6_), channel_id=1, source_target_pairs={{0,1},{1,0},{2,3},{3,2},{4,5},{5,4},{6,7},{7,6},{8,9},{9,8},{10,11... | collective-permute-start | bytes 442376 | tf_op jit(solution)/shard_map/ppermute | solution.py:29
  39.3 9.7 %collective-permute-start.23 = (f32[48,2048]{1,0:T(8,128)S(1)}, f32[48,2048]{1,0:T(8,128)}, u32[]{:S(2)}, u32[]{:S(2)}) collective-permute-start(f32[48,2048]{1,0:T(8,128)S(1)} %link_chain.1.refs_16_), channel_id=1, source_target_pairs={{0,1},{1,0},{2,3},{3,2},{4,5},{5,4},{6,7},{7,6},{8,9},{9,8},{10,11... | collective-permute-start | bytes 1179656 | tf_op jit(solution)/shard_map/ppermute | solution.py:29
  39.9 6.9 %collective-permute-start.12 = (f32[96,384]{1,0:T(8,128)}, f32[96,384]{1,0:T(8,128)S(1)}, u32[]{:S(2)}, u32[]{:S(2)}) collective-permute-start(f32[96,384]{1,0:T(8,128)} %collective-permute-done.11.refs_8_), channel_id=1, source_target_pairs={{0,4},{1,5},{4,8},{5,9},{8,12},{9,13},{12,14},{13,15},{14,10},{15,... | collective-permute-start | bytes 442376 | tf_op jit(solution)/shard_map/ppermute | solution.py:346
  42.1 6.9 %collective-permute-start.14 = (f32[96,384]{1,0:T(8,128)}, f32[96,384]{1,0:T(8,128)S(1)}, u32[]{:S(2)}, u32[]{:S(2)}) collective-permute-start(f32[96,384]{1,0:T(8,128)} %collective-permute-done.13.refs_10_), channel_id=1, source_target_pairs={{0,2},{1,3},{4,0},{5,1},{8,4},{9,5},{12,8},{13,9},{14,12},{15,13},... | collective-permute-start | bytes 442376 | tf_op jit(solution)/shard_map/ppermute | solution.py:346
  42.6 16.0 %collective-permute-start.2 = (f32[48,2048]{1,0:T(8,128)S(1)}, f32[48,2048]{1,0:T(8,128)S(1)}, u32[]{:S(2)}, u32[]{:S(2)}) collective-permute-start(f32[48,2048]{1,0:T(8,128)S(1)} %collective-permute-done.1.refs_22_), channel_id=1, source_target_pairs={{0,4},{1,5},{4,8},{5,9},{8,12},{9,13},{12,14},{13,15},{14,10},{15,... | collective-permute-start | bytes 1179656 | tf_op jit(solution)/shard_map/ppermute | solution.py:346
  44.1 14.6 %collective-permute-start.5 = (f32[48,2048]{1,0:T(8,128)S(1)}, f32[48,2048]{1,0:T(8,128)S(1)}, u32[]{:S(2)}, u32[]{:S(2)}) collective-permute-start(f32[48,2048]{1,0:T(8,128)S(1)} %collective-permute-done.4.refs_24_), channel_id=1, source_target_pairs={{0,2},{1,3},{4,0},{5,1},{8,4},{9,5},{12,8},{13,9},{14,12},{15,13},... | collective-permute-start | bytes 1179656 | tf_op jit(solution)/shard_map/ppermute | solution.py:346
  46.8 2.9 %collective-permute-start.19 = (f32[96,384]{1,0:T(8,128)}, f32[96,384]{1,0:T(8,128)S(1)}, u32[]{:S(2)}, u32[]{:S(2)}) collective-permute-start(f32[96,384]{1,0:T(8,128)} %collective-permute-done.11.refs_8_), channel_id=1, source_target_pairs={{0,1},{1,0},{2,3},{3,2},{4,5},{5,4},{6,7},{7,6},{8,9},{9,8},{10,11... | collective-permute-start | bytes 442376 | tf_op jit(solution)/shard_map/ppermute | solution.py:29
  49.0 1.6 %collective-permute-start.20 = (f32[96,384]{1,0:T(8,128)}, f32[96,384]{1,0:T(8,128)S(1)}, u32[]{:S(2)}, u32[]{:S(2)}) collective-permute-start(f32[96,384]{1,0:T(8,128)} %collective-permute-done.13.refs_10_), channel_id=1, source_target_pairs={{0,1},{1,0},{2,3},{3,2},{4,5},{5,4},{6,7},{7,6},{8,9},{9,8},{10,11... | collective-permute-start | bytes 442376 | tf_op jit(solution)/shard_map/ppermute | solution.py:29
  49.0 7.4 %collective-permute-start.15 = (f32[96,384]{1,0:T(8,128)S(1)}, f32[96,384]{1,0:T(8,128)S(1)}, u32[]{:S(2)}, u32[]{:S(2)}) collective-permute-start(f32[96,384]{1,0:T(8,128)S(1)} %broadcast_select_fusion.1), channel_id=1, source_target_pairs={{0,4},{4,8},{8,12},{12,14},{14,10},{10,6},{6,2},{2,0},{1,3},{5,1},... | collective-permute-start | bytes 442376 | tf_op jit(solution)/shard_map/ppermute | solution.py:349
  49.6 8.4 %collective-permute-start.21 = (f32[96,384]{1,0:T(8,128)S(1)}, f32[96,384]{1,0:T(8,128)S(1)}, u32[]{:S(2)}, u32[]{:S(2)}) collective-permute-start(f32[96,384]{1,0:T(8,128)S(1)} %collective-permute-done.12.refs_12_), channel_id=1, source_target_pairs={{0,1},{1,0},{2,3},{3,2},{4,5},{5,4},{6,7},{7,6},{8,9},{9,8},{10,11... | collective-permute-start | bytes 442376 | tf_op jit(solution)/shard_map/ppermute | solution.py:29
  50.5 7.6 %collective-permute-start.22 = (f32[96,384]{1,0:T(8,128)S(1)}, f32[96,384]{1,0:T(8,128)S(1)}, u32[]{:S(2)}, u32[]{:S(2)}) collective-permute-start(f32[96,384]{1,0:T(8,128)S(1)} %collective-permute-done.14.refs_14_), channel_id=1, source_target_pairs={{0,1},{1,0},{2,3},{3,2},{4,5},{5,4},{6,7},{7,6},{8,9},{9,8},{10,11... | collective-permute-start | bytes 442376 | tf_op jit(solution)/shard_map/ppermute | solution.py:29
  56.4 4.4 %collective-permute-start.24 = (f32[48,2048]{1,0:T(8,128)S(1)}, f32[48,2048]{1,0:T(8,128)S(1)}, u32[]{:S(2)}, u32[]{:S(2)}) collective-permute-start(f32[48,2048]{1,0:T(8,128)S(1)} %collective-permute-done.refs_18_), channel_id=1, source_target_pairs={{0,1},{1,0},{2,3},{3,2},{4,5},{5,4},{6,7},{7,6},{8,9},{9,8},{10,11... | collective-permute-start | bytes 1179656 | tf_op jit(solution)/shard_map/ppermute | solution.py:29
  58.1 2.8 %collective-permute-start.25 = (f32[48,2048]{1,0:T(8,128)S(1)}, f32[48,2048]{1,0:T(8,128)S(1)}, u32[]{:S(2)}, u32[]{:S(2)}) collective-permute-start(f32[48,2048]{1,0:T(8,128)S(1)} %collective-permute-done.3.refs_20_), channel_id=1, source_target_pairs={{0,1},{1,0},{2,3},{3,2},{4,5},{5,4},{6,7},{7,6},{8,9},{9,8},{10,11... | collective-permute-start | bytes 1179656 | tf_op jit(solution)/shard_map/ppermute | solution.py:29
  58.1 2.1 %collective-permute-start.16 = (f32[96,384]{1,0:T(8,128)S(1)}, f32[96,384]{1,0:T(8,128)S(1)}, u32[]{:S(2)}, u32[]{:S(2)}) collective-permute-start(f32[96,384]{1,0:T(8,128)S(1)} %collective-permute-done.15.refs_2_), channel_id=1, source_target_pairs={{0,1},{1,0},{2,3},{3,2},{4,5},{5,4},{6,7},{7,6},{8,9},{9,8},{10,11... | collective-permute-start | bytes 442376 | tf_op jit(solution)/shard_map/ppermute | solution.py:29
  58.6 2.7 %collective-permute-start.26 = (f32[48,2048]{1,0:T(8,128)S(1)}, f32[48,2048]{1,0:T(8,128)S(1)}, u32[]{:S(2)}, u32[]{:S(2)}) collective-permute-start(f32[48,2048]{1,0:T(8,128)S(1)} %collective-permute-done.1.refs_22_), channel_id=1, source_target_pairs={{0,1},{1,0},{2,3},{3,2},{4,5},{5,4},{6,7},{7,6},{8,9},{9,8},{10,11... | collective-permute-start | bytes 1179656 | tf_op jit(solution)/shard_map/ppermute | solution.py:29
  58.7 2.7 %collective-permute-start.27 = (f32[48,2048]{1,0:T(8,128)S(1)}, f32[48,2048]{1,0:T(8,128)S(1)}, u32[]{:S(2)}, u32[]{:S(2)}) collective-permute-start(f32[48,2048]{1,0:T(8,128)S(1)} %collective-permute-done.4.refs_24_), channel_id=1, source_target_pairs={{0,1},{1,0},{2,3},{3,2},{4,5},{5,4},{6,7},{7,6},{8,9},{9,8},{10,11... | collective-permute-start | bytes 1179656 | tf_op jit(solution)/shard_map/ppermute | solution.py:29
  60.2 23.7 %collective-permute-start.6 = (f32[48,2048]{1,0:T(8,128)S(1)}, f32[48,2048]{1,0:T(8,128)S(1)}, u32[]{:S(2)}, u32[]{:S(2)}) collective-permute-start(f32[48,2048]{1,0:T(8,128)S(1)} %broadcast_select_fusion), channel_id=1, source_target_pairs={{0,4},{4,8},{8,12},{12,14},{14,10},{10,6},{6,2},{2,0},{1,3},{5,1},... | collective-permute-start | bytes 1179656 | tf_op jit(solution)/shard_map/ppermute | solution.py:349
  60.8 23.6 %collective-permute-start.28 = (f32[48,2048]{1,0:T(8,128)S(1)}, f32[48,2048]{1,0:T(8,128)S(1)}, u32[]{:S(2)}, u32[]{:S(2)}) collective-permute-start(f32[48,2048]{1,0:T(8,128)S(1)} %collective-permute-done.2.refs_0_), channel_id=1, source_target_pairs={{0,1},{1,0},{2,3},{3,2},{4,5},{5,4},{6,7},{7,6},{8,9},{9,8},{10,11... | collective-permute-start | bytes 1179656 | tf_op jit(solution)/shard_map/ppermute | solution.py:29
  60.9 23.5 %collective-permute-start.29 = (f32[48,2048]{1,0:T(8,128)S(1)}, f32[48,2048]{1,0:T(8,128)S(1)}, u32[]{:S(2)}, u32[]{:S(2)}) collective-permute-start(f32[48,2048]{1,0:T(8,128)S(1)} %collective-permute-done.5.refs_2_), channel_id=1, source_target_pairs={{0,1},{1,0},{2,3},{3,2},{4,5},{5,4},{6,7},{7,6},{8,9},{9,8},{10,11... | collective-permute-start | bytes 1179656 | tf_op jit(solution)/shard_map/ppermute | solution.py:29
  84.0 6.4 %collective-permute-start.7 = (f32[48,2048]{1,0:T(8,128)S(1)}, f32[48,2048]{1,0:T(8,128)S(1)}, u32[]{:S(2)}, u32[]{:S(2)}) collective-permute-start(f32[48,2048]{1,0:T(8,128)S(1)} %collective-permute-done.6.refs_0_), channel_id=1, source_target_pairs={{0,1},{1,0},{2,3},{3,2},{4,5},{5,4},{6,7},{7,6},{8,9},{9,8},{10,11... | collective-permute-start | bytes 1179656 | tf_op jit(solution)/shard_map/ppermute | solution.py:29
  (13 other events, 13.5 us)

commit v4 on v3

v4 whole, which is shorter than its diff:
```python
import jax
import jax.numpy as jnp
from jax import lax
from jax.experimental import pallas as pl
from jax.experimental.pallas import tpu as pltpu
from jax.sharding import PartitionSpec as P

PCOL = 8
TILE = 128
LEAD = 2
GATHER_LIMIT = 16 * 2**20


def product(left, right):
    return jnp.dot(left, right, precision=lax.Precision.HIGH, preferred_element_type=jnp.float32)


def inner_product(left, right):
    return lax.dot_general(
        left,
        right,
        (((0,), (0,)), ((), ())),
        precision=lax.Precision.HIGH,
        preferred_element_type=jnp.float32,
    )


def swap_bit(value, bit):
    mask = 2**bit
    return lax.ppermute(value, "row", [(i, i ^ mask) for i in range(lax.axis_size("row"))])


def ring_chips(count):
    return list(range(0, count, 2)) + list(range(count - 1, 0, -2))


def ring_pairs(count, shift):
    order = ring_chips(count)
    pairs = []
    for place, chip in enumerate(order):
        target = order[(place + shift) % count]
        pairs += [(2 * chip + core, 2 * target + core) for core in range(2)]
    return pairs


def masked_links(my_index, anc_links, pattern):
    rows_here = anc_links.shape[0]
    tile_index = (my_index * rows_here + jnp.arange(rows_here, dtype=jnp.int32)) // TILE
    row_keep = jnp.take(pattern, tile_index, axis=1) != 0
    return jnp.where(row_keep[:, :, None], jnp.swapaxes(anc_links, 0, 1), 0.0)


def reduced_links(links, parent_links):
    reduced = [links[0]]
    for node in range(1, links.shape[0]):
        reduced.append(links[node] - product(reduced[-1], parent_links[node - 1]))
    return reduced


def local_chain(parent_links, pivot_inverse):
    inner = [pivot_inverse[0]]
    cross = []
    for node in range(1, pivot_inverse.shape[0]):
        link = parent_links[node - 1]
        cross.append(product(inner[-1], link))
        inner.append(pivot_inverse[node] + inner_product(link, cross[-1]))
    return inner, cross


def halves(value):
    high = value.astype(jnp.bfloat16)
    return high, (value - high.astype(jnp.float32)).astype(jnp.bfloat16)


def dot_halves(left, right, dims=((1,), (0,))):
    def one(a, b):
        return lax.dot_general(a, b, (dims, ((), ())), preferred_element_type=jnp.float32)

    return one(left[0], right[0]) + (one(left[0], right[1]) + one(left[1], right[0]))


def stacked_dot(left, right):
    height = left[0].shape[0]
    both = jnp.dot(jnp.concatenate(left, axis=0), right[0], preferred_element_type=jnp.float32)
    cross = jnp.dot(left[0], right[1], preferred_element_type=jnp.float32)
    return both[:height] + (both[height:] + cross)


def kernel_call(kernel, name, flops, moved, limit=16 * 2**20, **more):
    return pl.pallas_call(
        kernel,
        name=name,
        compiler_params=pltpu.CompilerParams(vmem_limit_bytes=limit),
        cost_estimate=pl.CostEstimate(flops=flops, bytes_accessed=moved, transcendentals=0),
        **more,
    )


def in_vmem(count):
    return [pl.BlockSpec(memory_space=pltpu.VMEM)] * count


def after(value, *others):
    return lax.optimization_barrier((value, *others))[0]


def at_home(count):
    return [pl.BlockSpec(memory_space=pltpu.HBM)] * count


def turned_rows(block):
    columns, both = block.shape
    rows = both // 2

    def kernel(block_ref, mine_ref, theirs_ref, here, sem):
        fetch = pltpu.make_async_copy(block_ref, here, sem)
        fetch.start()
        fetch.wait()
        turned = here[...].T
        low = lax.axis_index("row") < PCOL
        mine_ref[...] = jnp.where(low, turned[:rows], turned[rows:])
        theirs_ref[...] = jnp.where(low, turned[rows:], turned[:rows])

    return kernel_call(
        kernel,
        "turned_rows",
        block.size,
        8 * block.size,
        limit=63 * 2**20,
        out_shape=[jax.ShapeDtypeStruct((rows, columns), jnp.float32)] * 2,
        in_specs=at_home(1),
        out_specs=in_vmem(2),
        scratch_shapes=[pltpu.VMEM(block.shape, jnp.float32), pltpu.SemaphoreType.DMA],
    )(block)


def link_chain(anc_links, parent_links, pattern):
    rows, nodes, width = anc_links.shape
    tiles = pattern.shape[1]

    def kernel(links_home, parent_home, pattern_ref, first_ref, rest_ref, links_ref, parent_ref, sems):
        fetches = [pltpu.make_async_copy(links_home, links_ref, sems.at[0])]
        for node in range(1, nodes):
            fetches.append(
                pltpu.make_async_copy(parent_home.at[node - 1], parent_ref.at[node - 1], sems.at[node])
            )
        for fetch in fetches:
            fetch.start()
        first = lax.axis_index("row") * rows
        tile = first // TILE
        next_tile = jnp.minimum(tile + 1, tiles - 1)
        row = first + lax.broadcasted_iota(jnp.int32, (rows, width), 0)
        in_first = row < (tile + 1) * TILE
        reduced = None
        for node in range(nodes):
            fetches[node].wait()
            keep = jnp.where(in_first, pattern_ref[node, tile], pattern_ref[node, next_tile])
            links = jnp.where(keep != 0, links_ref[:, node, :], 0.0)
            if node > 0:
                links = links - dot_halves(halves(reduced), halves(parent_ref[node - 1]))
            target, place = (first_ref, node) if node < LEAD else (rest_ref, node - LEAD)
            target[:, place * width : (place + 1) * width] = links
            reduced = links

    return kernel_call(
        kernel,
        "link_chain",
        12 * rows * nodes * width * width,
        4 * parent_links.size,
        limit=63 * 2**20,
        out_shape=[
            jax.ShapeDtypeStruct((rows, LEAD * width), jnp.float32),
            jax.ShapeDtypeStruct((rows, (nodes - LEAD) * width), jnp.float32),
        ],
        in_specs=at_home(2) + [pl.BlockSpec(memory_space=pltpu.SMEM)],
        out_specs=in_vmem(2),
        scratch_shapes=[
            pltpu.VMEM(anc_links.shape, jnp.float32),
            pltpu.VMEM(parent_links.shape, jnp.float32),
            pltpu.SemaphoreType.DMA((nodes,)),
        ],
    )(anc_links, parent_links, pattern)


def lead_message(mine, theirs, first):
    rows, columns = mine.shape

    def kernel(mine_ref, theirs_ref, first_ref, out_ref):
        low = lax.axis_index("row") < PCOL
        out_ref[:, :columns] = jnp.where(low, mine_ref[...], theirs_ref[...])
        out_ref[:, columns : 2 * columns] = jnp.where(low, theirs_ref[...], mine_ref[...])
        out_ref[:, 2 * columns :] = first_ref[...]

    return kernel_call(
        kernel,
        "lead_message",
        mine.size,
        8 * (mine.size + theirs.size + first.size),
        out_shape=jax.ShapeDtypeStruct((rows, 2 * columns + first.shape[1]), jnp.float32),
        in_specs=in_vmem(3),
        out_specs=in_vmem(1)[0],
    )(mine, theirs, first)


def inner_chain(parent_links, pivot_inverse):
    nodes, width, _ = pivot_inverse.shape

    def kernel(parent_home, pivot_home, cross_ref, inner_ref, parent_ref, pivot_ref, sems):
        fetches = [pltpu.make_async_copy(pivot_home.at[0], pivot_ref.at[0], sems.at[0, 0])]
        for node in range(1, nodes):
            for place, home, here, piece in (
                (1, parent_home, parent_ref, node - 1),
                (0, pivot_home, pivot_ref, node),
            ):
                fetches.append(pltpu.make_async_copy(home.at[piece], here.at[piece], sems.at[place, node]))
        for fetch in fetches:
            fetch.start()
        fetches[0].wait()
        inner = pivot_ref[0]
        inner_ref[0] = inner
        for node in range(1, nodes):
            fetches[2 * node - 1].wait()
            link = halves(parent_ref[node - 1])
            cross = dot_halves(halves(inner), link)
            cross_ref[node - 1] = -cross
            fetches[2 * node].wait()
            inner = pivot_ref[node] + dot_halves(link, halves(cross), ((0,), (0,)))
            inner_ref[node] = inner

    shapes = [jax.ShapeDtypeStruct(array.shape, jnp.float32) for array in (parent_links, pivot_inverse)]
    return kernel_call(
        kernel,
        "inner_chain",
        12 * nodes * width**3,
        16 * pivot_inverse.size,
        out_shape=shapes,
        in_specs=at_home(2),
        out_specs=in_vmem(2),
        scratch_shapes=[pltpu.VMEM(shape.shape, jnp.float32) for shape in shapes]
        + [pltpu.SemaphoreType.DMA((2, nodes))],
    )(parent_links, pivot_inverse)


def ring_owner(my_index, count, shift, other):
    core = lax.rem(my_index, 2)
    chip = my_index // 2
    place = jnp.where(lax.rem(chip, 2) == 0, chip // 2, count - 1 - chip // 2)
    place = lax.rem(place + shift + count, count)
    chip = jnp.where(place < count // 2, 2 * place, 2 * (count - 1 - place) + 1)
    return 2 * chip + (1 - core if other else core)


def border(arrivals, held, parents, diagonals, chips, last=False):
    nodes, width, _ = diagonals.shape
    rows = arrivals[0][2].shape[0]
    order = arrivals[0][2].shape[1] - LEAD * width
    count = len(arrivals)
    fresh = rows * count
    bf16 = jnp.bfloat16

    def kernel(*refs):
        refs = list(refs)
        take = lambda number: [refs.pop(0) for _ in range(number)]
        lead_refs, rest_refs = take(count), take(count)
        own_ref = take(1)[0] if last else None
        held_before = take(2) if held else None
        parents_ref, diagonals_ref, parents_out, diagonals_out = take(4)
        copies = []

        def finish(place, source, target):
            if last:
                copies.append(pltpu.make_async_copy(source, target, sems.at[place]))
                copies[-1].start()

        parents_end, diagonals_end = parents_out, diagonals_out
        if last:
            (panel_end,) = take(1)
        held_now = take(2)
        turned = take(2)
        if last:
            parents_out, diagonals_out, panel_out, sems = take(4)
        me = lax.axis_index("row")
        owners = [ring_owner(me, chips, shift, other) for shift, other, _, _ in arrivals]

        for part, whole in enumerate(held_now):
            whole[...] = held_before[part][...] if held else jnp.zeros(whole.shape, bf16)
        for owner, lead, rest in zip(owners, lead_refs, rest_refs):
            start = pl.multiple_of(owner * rows, 16)
            for whole, part in zip(held_now, halves(lead[:, order:])):
                whole[pl.ds(start, rows), : LEAD * width] = part
            for whole, part in zip(held_now, halves(rest[...])):
                whole[pl.ds(start, rows), LEAD * width :] = part
        piece = lax.broadcasted_iota(jnp.int32, (1, order), 1) // rows
        weight = jnp.ones((1, order), jnp.float32)
        for owner in owners:
            weight = jnp.where(piece == owner, 0.5, weight)
        left = [ref[:, :order] * weight for ref in lead_refs]
        if last:
            left.append(own_ref[:, :order])
        left = halves(jnp.concatenate(left, axis=0))
        right = []
        for node in range(nodes):
            columns = slice(node * width, (node + 1) * width)
            image = stacked_dot(left, [whole[:, columns] for whole in held_now])
            if last:
                panel_out[:, node, :] = -image[fresh:]
            image = image[:fresh]
            if node < LEAD:
                new = [ref[:, order + node * width : order + (node + 1) * width] for ref in lead_refs]
            else:
                new = [ref[:, (node - LEAD) * width : (node - LEAD + 1) * width] for ref in rest_refs]
            new = jnp.concatenate(new, axis=0)
            for whole, part in zip(turned, halves(jnp.concatenate([new, image], axis=0).T)):
                whole[columns, :] = part
            right.append([jnp.concatenate(pair, axis=0) for pair in zip(halves(image), halves(new))])
        if last:
            finish(2 * nodes, panel_out, panel_end)
        for node in range(nodes):
            lower = max(node - 1, 0) * width
            total = stacked_dot([whole[lower : (node + 1) * width, :] for whole in turned], right[node])
            diagonals_out[node] = diagonals_ref[node] + total[-width:]
            finish(node, diagonals_out.at[node], diagonals_end.at[node])
            if node > 0:
                parents_out[node - 1] = parents_ref[node - 1] + total[:width]
                finish(nodes + node, parents_out.at[node - 1], parents_end.at[node - 1])
        for copy in copies:
            copy.wait()

    operands = [lead for _, _, lead, _ in arrivals] + [rest for _, _, _, rest in arrivals]
    operands += [last] if last is not False else []
    operands += [*(held or []), parents, diagonals]
    last = last is not False
    state = [(order, nodes * width)] * 2
    shapes = [jax.ShapeDtypeStruct(array.shape, jnp.float32) for array in (parents, diagonals)]
    scratch = [pltpu.VMEM((nodes * width, 2 * fresh), bf16)] * 2
    if last:
        shapes.append(jax.ShapeDtypeStruct((rows, nodes, width), jnp.float32))
        scratch = [pltpu.VMEM(shape, bf16) for shape in state] + scratch
        scratch += [pltpu.VMEM(array.shape, jnp.float32) for array in shapes]
        scratch.append(pltpu.SemaphoreType.DMA((2 * nodes + 1,)))
    else:
        shapes += [jax.ShapeDtypeStruct(shape, bf16) for shape in state]
    results = kernel_call(
        kernel,
        "border" + ("_end" if last else "" if held else "_start"),
        6 * nodes * fresh * width * (order + 4 * width),
        4 * sum(array.size for array in operands),
        out_shape=shapes,
        in_specs=in_vmem(len(operands)),
        out_specs=at_home(len(shapes)) if last else in_vmem(len(shapes)),
        scratch_shapes=scratch,
        limit=24 * 2**20 if last else 16 * 2**20,
    )(*operands)
    return results[:2], results[2:]


def gather_plan(anc_blocks, anc_links, parent_links, pivot_inverse, pattern):
    my_index = lax.axis_index("row")
    chips = lax.axis_size("row") // 2
    far = chips // 2
    ahead, behind = ring_pairs(chips, 1), ring_pairs(chips, -1)
    across = [p for p in ahead if p[0] % 2 == 0] + [p for p in behind if p[0] % 2 == 1]

    def move(pair):
        return [lax.ppermute(value, "row", way) for value, way in zip(pair, (ahead, behind))]

    def turn(pair):
        return lax.ppermute(jnp.where(my_index % 2 == 0, *pair), "row", across)

    def both(shift, lead, rest):
        return [(shift, False, lead, rest), (shift, True, swap_bit(lead, 0), swap_bit(rest, 0))]

    mine, theirs = turned_rows(anc_blocks[0])
    theirs = swap_bit(theirs, PCOL.bit_length() - 1)
    first, rest = link_chain(after(anc_links, mine), parent_links, pattern)
    lead = lead_message(mine, theirs, first)
    totals = inner_chain(after(parent_links, lead), pivot_inverse)
    leads, rests = [lead] * 2, [rest] * 2
    arrivals, held = both(0, lead, rest), None
    for step in range(1, far):
        leads, totals = lax.optimization_barrier((move(leads), totals))
        totals, held = border(arrivals, held, *totals, chips)
        rests, totals = lax.optimization_barrier((move(rests), totals))
        arrivals = both(-step, leads[0], rests[0]) + both(step, leads[1], rests[1])
    totals, held = border(arrivals, held, *totals, chips)
    totals, panels = border(both(far, turn(leads), turn(rests)), held, *totals, chips, last=lead)
    return panels[0], *totals


def spread_plan(anc_blocks, anc_links, parent_links, pivot_inverse, pattern):
    my_index = lax.axis_index("row")
    total_bits = lax.axis_size("row").bit_length() - 1
    low_bits = PCOL.bit_length() - 1
    rows, nodes, width = anc_links.shape
    links = jnp.concatenate(reduced_links(masked_links(my_index, anc_links, pattern), parent_links), axis=1)
    segment = links
    for bit in range(low_bits, total_bits):
        partner = swap_bit(segment, bit)
        upper = my_index >> bit & 1
        segment = lax.dynamic_update_slice_in_dim(
            jnp.concatenate([partner, partner], 0), segment, upper * segment.shape[0], 0
        )
    image = product(anc_blocks[0], segment)
    for bit in reversed(range(low_bits)):
        half_rows = image.shape[0] // 2
        upper = my_index >> bit & 1
        retained = lax.dynamic_slice_in_dim(image, upper * half_rows, half_rows, 0)
        outgoing = lax.dynamic_slice_in_dim(image, (1 - upper) * half_rows, half_rows, 0)
        image = retained + swap_bit(outgoing, bit)
    column = lambda array, node: array[:, node * width : (node + 1) * width]
    terms = [inner_product(column(links, node), column(image, node)) for node in range(nodes)]
    terms += [inner_product(column(links, node - 1), column(image, node)) for node in range(1, nodes)]
    totals = lax.psum(jnp.stack(terms), "row")
    inner, cross = local_chain(parent_links, pivot_inverse)
    diagonals = jnp.stack(inner) + totals[:nodes]
    parents = totals[nodes:] - jnp.stack(cross)
    return -image.reshape(rows, nodes, width), parents, diagonals


def on_device(anc_blocks, anc_links, parent_links, pivot_inverse, pattern):
    size = lax.axis_size("row")
    rows, nodes, width = anc_links.shape
    whole_bytes = 4 * size * rows * (nodes * width + size * rows)
    plan = gather_plan if size == 2 * PCOL and whole_bytes <= GATHER_LIMIT else spread_plan
    return plan(anc_blocks, anc_links, parent_links, pivot_inverse, pattern)


def solution(mesh):
    return jax.shard_map(
        on_device,
        mesh=mesh,
        in_specs=(
            P(("pole", "row"), None, None),
            P(("pole", "row"), None, None),
            P("pole", None, None),
            P("pole", None, None),
            P(),
        ),
        out_specs=(P(("pole", "row"), None, None), P("pole", None, None), P("pole", None, None)),
        check_vma=False,
    )
```

time: 95.9 us -> 105 us (1.095)
  starting transfers between devices: 18.5 us -> 23.7 us
  Pallas kernels: 33.9 us -> 37.1 us
  local copies, waits for them, and re-layouts: 16.1 us -> 18.4 us
  waiting for transfers between devices: 26 us -> 24.6 us
    ppermute x16 -> x17, starting transfers between devices: 4.01 us -> 7.97 us  [swap_bit(): lax.ppermute(value, 'row', [(i, i ^ mask) for i in range(lax.axis_size('r...]
    unnamed x31 -> x27, local copies, waits for them, and re-layouts: 16.1 us -> 18.4 us
    pallas_call x1, Pallas kernels: 1.93 us -> 4.16 us  [link_chain(): kernel_call(kernel, 'link_chain', 12 * rows * nodes * width * width, 4 *...]
    ppermute x16 -> x17, waiting for transfers between devices: 1.81 us -> 0.04 us  [swap_bit(): lax.ppermute(value, 'row', [(i, i ^ mask) for i in range(lax.axis_size('r...]
    pallas_call x1, Pallas kernels: 4.18 us -> 5.53 us  [inner_chain(): kernel_call(kernel, 'inner_chain', 12 * nodes * width ** 3, 16 * pivot_in...]
    pallas_call x4 -> x7, Pallas kernels: 27.8 us -> 27.4 us  [the longest x5 25.6 us: border(): kernel_call(kernel, 'border' + ('_end' if last else '' if held else '_sta...]
  transfers between devices with their start and end apart: 30 -> 31, of which waited for: 8 -> 5; matrix products, arithmetic and copies ran while one was open for 0% -> 0% of each run, Pallas kernels for 28% -> 29%
where the time goes in v4:
time: 105 us
  Pallas kernels  37.1 us (35%)
  waiting for transfers between devices  24.6 us (23%)
  starting transfers between devices  23.7 us (23%)
  local copies, waits for them, and re-layouts  18.4 us (18%)
  between operations  1.05 us (1%)
    pallas_call x5, Pallas kernels, border(): kernel_call(kernel, 'border' + ('_end' if last else '' if held else '_sta...  25.6 us
    unnamed x27, local copies, waits for them, and re-layouts  18.4 us
    ppermute x12, waiting for transfers between devices, move(): lax.ppermute(value, 'row', way)  18 us
    ppermute x12, starting transfers between devices, move(): lax.ppermute(value, 'row', way)  13.5 us
    ppermute x17, starting transfers between devices, swap_bit(): lax.ppermute(value, 'row', [(i, i ^ mask) for i in range(lax.axis_size('r...  7.97 us
    ppermute x2, waiting for transfers between devices, turn(): return lax.ppermute(jnp.where(my_index % 2 == 0, *pair), 'row', across)  6.57 us
    pallas_call x1, Pallas kernels, inner_chain(): kernel_call(kernel, 'inner_chain', 12 * nodes * width ** 3, 16 * pivot_in...  5.53 us
    pallas_call x1, Pallas kernels, link_chain(): kernel_call(kernel, 'link_chain', 12 * rows * nodes * width * width, 4 *...  4.16 us
  transfers between devices with their start and end apart: 31, of which 5 were waited for; matrix products, arithmetic and copies ran while one was open for 0% of the time, Pallas kernels for 29%

profile of v4, /device:TPU:0, one launch (start us, length us, event | category | flops | bytes accessed | tf_op | source)
XLA Modules:
  0.0 104.9 jit_solution(12618830286540222418)
XLA Ops:
  0.6 1.7 %copy.8 = f32[1,384,96]{2,1,0:T(8,128)} copy(f32[1,384,96]{1,2,0:T(8,128)} %param.5) | data formatting | bytes 294912 | tf_op args[0]
  2.3 1.7 %turned_rows.1 = (f32[48,384]{1,0:T(8,128)}, f32[48,384]{1,0:T(8,128)}) custom-call(f32[384,96]{1,0:T(8,128)} %bitcast.1), custom_call_target="tpu_custom_call" | custom-call | flops 36864 | bytes 294912 | tf_op jit(solution)/shard_map/turned_rows/pallas_call | solution.py:124
  4.1 4.1 %collective-permute-start = (f32[48,384]{1,0:T(8,128)}, f32[48,384]{1,0:T(8,128)S(1)}, u32[]{:S(2)}, u32[]{:S(2)}) collective-permute-start(f32[48,384]{1,0:T(8,128)} %get-tuple-element.55), channel_id=1, source_target_pairs={{0,8},{1,9},{2,10},{3,11},{4,12},{5,13},{6,14},{7,15},{8,0},{9,1},... | collective-permute-start | bytes 221192 | tf_op jit(solution)/shard_map/ppermute | solution.py:30
  8.2 4.2 %link_chain.1 = (f32[48,512]{1,0:T(8,128)}, f32[48,1536]{1,0:T(8,128)}) custom-call(f32[48,8,256]{2,1,0:T(8,128)} %links_home, f32[7,256,256]{2,1,0:T(8,128)} %parent_home.2, s32[8,6]{1,0:T(8,128)} %pattern_ref.1), custom_call_target="tpu_custom_call" | custom-call | flops 301989888 | bytes 1835008 | tf_op jit(solution)/shard_map/link_chain/pallas_call | solution.py:165
  13.3 1.6 %collective-permute-start.1 = (f32[48,1280]{1,0:T(8,128)S(1)}, f32[48,1280]{1,0:T(8,128)S(1)}, u32[]{:S(2)}, u32[]{:S(2)}) collective-permute-start(f32[48,1280]{1,0:T(8,128)S(1)} %lead_message.1.refs_0_.refs_4_), channel_id=1, source_target_pairs={{0,4},{1,5},{4,8},{5,9},{8,12},{9,13},{12,14},{13,15},{14,10},{15,... | collective-permute-start | bytes 737288 | tf_op jit(solution)/shard_map/ppermute | solution.py:365
  15.6 1.6 %collective-permute-start.5 = (f32[48,1536]{1,0:T(8,128)}, f32[48,1536]{1,0:T(8,128)S(1)}, u32[]{:S(2)}, u32[]{:S(2)}) collective-permute-start(f32[48,1536]{1,0:T(8,128)} %get-tuple-element.63.refs_2_), channel_id=1, source_target_pairs={{0,4},{1,5},{4,8},{5,9},{8,12},{9,13},{12,14},{13,15},{14,10},{15,... | collective-permute-start | bytes 884744 | tf_op jit(solution)/shard_map/ppermute | solution.py:365
  17.2 5.0 %collective-permute-done.1.refs_0_ = f32[48,1280]{1,0:T(8,128)S(1)} collective-permute-done((f32[48,1280]{1,0:T(8,128)S(1)}, f32[48,1280]{1,0:T(8,128)S(1)}, u32[]{:S(2)}, u32[]{:S(2)}) %collective-permute-start.1) | collective-permute-done | bytes 245792 | tf_op jit(solution)/shard_map/ppermute | solution.py:365
  22.2 1.6 %collective-permute-start.6 = (f32[48,1536]{1,0:T(8,128)}, f32[48,1536]{1,0:T(8,128)S(1)}, u32[]{:S(2)}, u32[]{:S(2)}) collective-permute-start(f32[48,1536]{1,0:T(8,128)} %get-tuple-element.63.refs_2_), channel_id=1, source_target_pairs={{0,2},{1,3},{4,0},{5,1},{8,4},{9,5},{12,8},{13,9},{14,12},{15,13},... | collective-permute-start | bytes 884744 | tf_op jit(solution)/shard_map/ppermute | solution.py:365
  23.9 1.5 %copy-done = f32[7,256,256]{2,1,0:T(8,128)S(1)} copy-done((f32[7,256,256]{2,1,0:T(8,128)S(1)}, f32[7,256,256]{2,1,0:T(8,128)}, u32[]{:S(2)}) %copy-start) | copy-done | bytes 1835032
  25.4 1.6 %copy-done.3 = f32[8,256,256]{2,1,0:T(8,128)S(1)} copy-done((f32[8,256,256]{2,1,0:T(8,128)S(1)}, f32[8,256,256]{2,1,0:T(8,128)}, u32[]{:S(2)}) %copy-start.3) | copy-done | bytes 2097176
  27.0 5.5 %inner_chain.1 = (f32[7,256,256]{2,1,0:T(8,128)S(1)}, f32[8,256,256]{2,1,0:T(8,128)S(1)}) custom-call(f32[7,256,256]{2,1,0:T(8,128)S(1)} %copy-done, f32[8,256,256]{2,1,0:T(8,128)S(1)} %copy-done.3), custom_call_target="tpu_custom_call" | custom-call | flops 1610612736 | bytes 8388608 | tf_op jit(solution)/shard_map/inner_chain/pallas_call | solution.py:231
  33.0 3.4 %border_start.1 = (f32[7,256,256]{2,1,0:T(8,128)S(1)}, f32[8,256,256]{2,1,0:T(8,128)S(1)}, bf16[768,2048]{1,0:T(8,128)(2,1)S(1)}, bf16[768,2048]{1,0:T(8,128)(2,1)S(1)}) custom-call(f32[48,1280]{1,0:T(8,128)S(1)} %lead_message.1.refs_0_.refs_4_, f32[48,1280]{1,0:T(8,128)S(1)} %collective-permute-done.7.refs_1_, f32[48,1536]{1,0:T(8,128)S(1)} %copy-done.4, ...), custom_call_target="tpu_custom_call" | custom-call | flops 2113929216 | bytes 5013504 | tf_op jit(solution)/shard_map/border_start/pallas_call | solution.py:343
  37.0 1.6 %collective-permute-start.4 = (f32[48,1280]{1,0:T(8,128)S(1)}, f32[48,1280]{1,0:T(8,128)S(1)}, u32[]{:S(2)}, u32[]{:S(2)}) collective-permute-start(f32[48,1280]{1,0:T(8,128)S(1)} %collective-permute-done.2.refs_2_), channel_id=1, source_target_pairs={{0,2},{1,3},{4,0},{5,1},{8,4},{9,5},{12,8},{13,9},{14,12},{15,13},... | collective-permute-start | bytes 737288 | tf_op jit(solution)/shard_map/ppermute | solution.py:365
  39.1 5.8 %collective-permute-done.4.refs_2_ = f32[48,1280]{1,0:T(8,128)S(1)} collective-permute-done((f32[48,1280]{1,0:T(8,128)S(1)}, f32[48,1280]{1,0:T(8,128)S(1)}, u32[]{:S(2)}, u32[]{:S(2)}) %collective-permute-start.4) | collective-permute-done | bytes 245792 | tf_op jit(solution)/shard_map/ppermute | solution.py:365
  44.9 1.6 %collective-permute-start.11 = (f32[48,1536]{1,0:T(8,128)S(1)}, f32[48,1536]{1,0:T(8,128)S(1)}, u32[]{:S(2)}, u32[]{:S(2)}) collective-permute-start(f32[48,1536]{1,0:T(8,128)S(1)} %collective-permute-done.5.refs_4_), channel_id=1, source_target_pairs={{0,4},{1,5},{4,8},{5,9},{8,12},{9,13},{12,14},{13,15},{14,10},{15,... | collective-permute-start | bytes 884744 | tf_op jit(solution)/shard_map/ppermute | solution.py:365
  47.0 1.6 %collective-permute-start.10 = (f32[48,1280]{1,0:T(8,128)S(1)}, f32[48,1280]{1,0:T(8,128)S(1)}, u32[]{:S(2)}, u32[]{:S(2)}) collective-permute-start(f32[48,1280]{1,0:T(8,128)S(1)} %collective-permute-done.4.refs_2_), channel_id=1, source_target_pairs={{0,2},{1,3},{4,0},{5,1},{8,4},{9,5},{12,8},{13,9},{14,12},{15,13},... | collective-permute-start | bytes 737288 | tf_op jit(solution)/shard_map/ppermute | solution.py:365
  48.6 5.8 %border.3 = (f32[7,256,256]{2,1,0:T(8,128)S(1)}, f32[8,256,256]{2,1,0:T(8,128)S(1)}, bf16[768,2048]{1,0:T(8,128)(2,1)S(1)}, bf16[768,2048]{1,0:T(8,128)(2,1)S(1)}) custom-call(f32[48,1280]{1,0:T(8,128)S(1)} %collective-permute-done.1.refs_0_, f32[48,1280]{1,0:T(8,128)S(1)} %collective-permute-done.13.refs_1_, f32[48,1280]{1,0:T(8,128)S(1)} %collective-permute-done.2.refs_2_, ...), custom_call_target="tpu_custom_call" | custom-call | flops 4227858432 | bytes 18677760 | tf_op jit(solution)/shard_map/border/pallas_call | solution.py:343
  54.4 1.6 %copy-done.5 = bf16[768,2048]{1,0:T(8,128)(2,1)} copy-done((bf16[768,2048]{1,0:T(8,128)(2,1)}, bf16[768,2048]{1,0:T(8,128)(2,1)S(1)}, u32[]{:S(2)}) %copy-start.5) | copy-done | bytes 3145752
  56.0 1.7 %copy-done.7 = bf16[768,2048]{1,0:T(8,128)(2,1)} copy-done((bf16[768,2048]{1,0:T(8,128)(2,1)}, bf16[768,2048]{1,0:T(8,128)(2,1)S(1)}, u32[]{:S(2)}) %copy-start.7) | copy-done | bytes 3145752
  57.7 1.3 %copy-done.9 = f32[8,256,256]{2,1,0:T(8,128)} copy-done((f32[8,256,256]{2,1,0:T(8,128)}, f32[8,256,256]{2,1,0:T(8,128)S(1)}, u32[]{:S(2)}) %copy-start.9) | copy-done | bytes 2097176
  59.0 1.2 %copy-done.11 = f32[7,256,256]{2,1,0:T(8,128)} copy-done((f32[7,256,256]{2,1,0:T(8,128)}, f32[7,256,256]{2,1,0:T(8,128)S(1)}, u32[]{:S(2)}) %copy-start.11) | copy-done | bytes 1835032
  61.6 7.0 %collective-permute-done.9.refs_0_ = f32[48,1280]{1,0:T(8,128)S(1)} collective-permute-done((f32[48,1280]{1,0:T(8,128)S(1)}, f32[48,1280]{1,0:T(8,128)S(1)}, u32[]{:S(2)}, u32[]{:S(2)}) %collective-permute-start.9) | collective-permute-done | bytes 245792 | tf_op jit(solution)/shard_map/ppermute | solution.py:365
  69.1 1.6 %collective-permute-start.20 = (f32[48,1536]{1,0:T(8,128)S(1)}, f32[48,1536]{1,0:T(8,128)S(1)}, u32[]{:S(2)}, u32[]{:S(2)}) collective-permute-start(f32[48,1536]{1,0:T(8,128)S(1)} %collective-permute-done.12.refs_6_), channel_id=1, source_target_pairs={{0,2},{1,3},{4,0},{5,1},{8,4},{9,5},{12,8},{13,9},{14,12},{15,13},... | collective-permute-start | bytes 884744 | tf_op jit(solution)/shard_map/ppermute | solution.py:365
  70.7 1.9 %copy-done.6 = bf16[768,2048]{1,0:T(8,128)(2,1)S(1)} copy-done((bf16[768,2048]{1,0:T(8,128)(2,1)S(1)}, bf16[768,2048]{1,0:T(8,128)(2,1)}, u32[]{:S(2)}) %copy-start.6) | copy-done | bytes 3145752
  72.6 1.9 %copy-done.8 = bf16[768,2048]{1,0:T(8,128)(2,1)S(1)} copy-done((bf16[768,2048]{1,0:T(8,128)(2,1)S(1)}, bf16[768,2048]{1,0:T(8,128)(2,1)}, u32[]{:S(2)}) %copy-start.8) | copy-done | bytes 3145752
  74.5 1.6 %copy-done.10 = f32[8,256,256]{2,1,0:T(8,128)S(1)} copy-done((f32[8,256,256]{2,1,0:T(8,128)S(1)}, f32[8,256,256]{2,1,0:T(8,128)}, u32[]{:S(2)}) %copy-start.10) | copy-done | bytes 2097176
  76.1 1.5 %copy-done.12 = f32[7,256,256]{2,1,0:T(8,128)S(1)} copy-done((f32[7,256,256]{2,1,0:T(8,128)S(1)}, f32[7,256,256]{2,1,0:T(8,128)}, u32[]{:S(2)}) %copy-start.12) | copy-done | bytes 1835032
  77.6 5.8 %border.4 = (f32[7,256,256]{2,1,0:T(8,128)S(1)}, f32[8,256,256]{2,1,0:T(8,128)S(1)}, bf16[768,2048]{1,0:T(8,128)(2,1)S(1)}, bf16[768,2048]{1,0:T(8,128)(2,1)S(1)}) custom-call(f32[48,1280]{1,0:T(8,128)S(1)} %collective-permute-done.3.refs_0_, f32[48,1280]{1,0:T(8,128)S(1)} %collective-permute-done.21.refs_1_, f32[48,1280]{1,0:T(8,128)S(1)} %collective-permute-done.4.refs_2_, ...), custom_call_target="tpu_custom_call" | custom-call | flops 4227858432 | bytes 18677760 | tf_op jit(solution)/shard_map/border/pallas_call | solution.py:343
  84.5 1.9 %collective-permute-start.17 = (f32[48,1280]{1,0:T(8,128)S(1)}, f32[48,1280]{1,0:T(8,128)S(1)}, u32[]{:S(2)}, u32[]{:S(2)}) collective-permute-start(f32[48,1280]{1,0:T(8,128)S(1)} %broadcast_select_fusion.1), channel_id=1, source_target_pairs={{0,4},{4,8},{8,12},{12,14},{14,10},{10,6},{6,2},{2,0},{1,3},{5,1},... | collective-permute-start | bytes 737288 | tf_op jit(solution)/shard_map/ppermute | solution.py:368
  86.9 6.6 %collective-permute-done.17.refs_0_ = f32[48,1280]{1,0:T(8,128)S(1)} collective-permute-done((f32[48,1280]{1,0:T(8,128)S(1)}, f32[48,1280]{1,0:T(8,128)S(1)}, u32[]{:S(2)}, u32[]{:S(2)}) %collective-permute-start.17) | collective-permute-done | bytes 245792 | tf_op jit(solution)/shard_map/ppermute | solution.py:368
  94.0 5.8 %border.5 = (f32[7,256,256]{2,1,0:T(8,128)S(1)}, f32[8,256,256]{2,1,0:T(8,128)S(1)}, bf16[768,2048]{1,0:T(8,128)(2,1)S(1)}, bf16[768,2048]{1,0:T(8,128)(2,1)S(1)}) custom-call(f32[48,1280]{1,0:T(8,128)S(1)} %collective-permute-done.9.refs_0_, f32[48,1280]{1,0:T(8,128)S(1)} %collective-permute-done.27.refs_1_, ...), custom_call_target="tpu_custom_call" | custom-call | flops 4227858432 | bytes 18677760 | tf_op jit(solution)/shard_map/border/pallas_call | solution.py:343
  99.8 4.9 %border_end.1 = (f32[7,256,256]{2,1,0:T(8,128)}, f32[8,256,256]{2,1,0:T(8,128)}, f32[48,8,256]{2,1,0:T(8,128)}) custom-call(f32[48,1280]{1,0:T(8,128)S(1)} %collective-permute-done.17.refs_0_, f32[48,1280]{1,0:T(8,128)S(1)} %collective-permute-done.18.refs_1_, f32[48,1536]{1,0:T(8,128)S(1)} %collective-permute-done.25.refs_2_, ...), custom_call_target="tpu_custom_call" | custom-call | flops 2113929216 | bytes 17842176 | tf_op jit(solution)/shard_map/border_end/pallas_call | solution.py:343
  (68 shorter events, 7.6 us)
Async XLA Ops:
  4.1 8.3 %collective-permute-start = (f32[48,384]{1,0:T(8,128)}, f32[48,384]{1,0:T(8,128)S(1)}, u32[]{:S(2)}, u32[]{:S(2)}) collective-permute-start(f32[48,384]{1,0:T(8,128)} %get-tuple-element.55), channel_id=1, source_target_pairs={{0,8},{1,9},{2,10},{3,11},{4,12},{5,13},{6,14},{7,15},{8,0},{9,1},... | collective-permute-start | bytes 221192 | tf_op jit(solution)/shard_map/ppermute | solution.py:30
  13.3 19.7 %copy-start.4 = (f32[48,1536]{1,0:T(8,128)S(1)}, f32[48,1536]{1,0:T(8,128)}, u32[]{:S(2)}) copy-start(f32[48,1536]{1,0:T(8,128)} %get-tuple-element.63.refs_2_) | copy-start | bytes 884740
  13.3 8.9 %collective-permute-start.1 = (f32[48,1280]{1,0:T(8,128)S(1)}, f32[48,1280]{1,0:T(8,128)S(1)}, u32[]{:S(2)}, u32[]{:S(2)}) collective-permute-start(f32[48,1280]{1,0:T(8,128)S(1)} %lead_message.1.refs_0_.refs_4_), channel_id=1, source_target_pairs={{0,4},{1,5},{4,8},{5,9},{8,12},{9,13},{12,14},{13,15},{14,10},{15,... | collective-permute-start | bytes 737288 | tf_op jit(solution)/shard_map/ppermute | solution.py:365
  14.9 18.0 %collective-permute-start.8 = (f32[48,1536]{1,0:T(8,128)}, f32[48,1536]{1,0:T(8,128)S(1)}, u32[]{:S(2)}, u32[]{:S(2)}) collective-permute-start(f32[48,1536]{1,0:T(8,128)} %get-tuple-element.63.refs_2_), channel_id=1, source_target_pairs={{0,1},{1,0},{2,3},{3,2},{4,5},{5,4},{6,7},{7,6},{8,9},{9,8},{10,11... | collective-permute-start | bytes 884744 | tf_op jit(solution)/shard_map/ppermute | solution.py:30
  14.9 17.6 %collective-permute-start.2 = (f32[48,1280]{1,0:T(8,128)S(1)}, f32[48,1280]{1,0:T(8,128)S(1)}, u32[]{:S(2)}, u32[]{:S(2)}) collective-permute-start(f32[48,1280]{1,0:T(8,128)S(1)} %lead_message.1.refs_0_.refs_4_), channel_id=1, source_target_pairs={{0,2},{1,3},{4,0},{5,1},{8,4},{9,5},{12,8},{13,9},{14,12},{15,13},... | collective-permute-start | bytes 737288 | tf_op jit(solution)/shard_map/ppermute | solution.py:365
  15.4 17.6 %collective-permute-start.7 = (f32[48,1280]{1,0:T(8,128)S(1)}, f32[48,1280]{1,0:T(8,128)S(1)}, u32[]{:S(2)}, u32[]{:S(2)}) collective-permute-start(f32[48,1280]{1,0:T(8,128)S(1)} %lead_message.1.refs_0_.refs_4_), channel_id=1, source_target_pairs={{0,1},{1,0},{2,3},{3,2},{4,5},{5,4},{6,7},{7,6},{8,9},{9,8},{10,11... | collective-permute-start | bytes 737288 | tf_op jit(solution)/shard_map/ppermute | solution.py:30
  15.6 20.8 %collective-permute-start.5 = (f32[48,1536]{1,0:T(8,128)}, f32[48,1536]{1,0:T(8,128)S(1)}, u32[]{:S(2)}, u32[]{:S(2)}) collective-permute-start(f32[48,1536]{1,0:T(8,128)} %get-tuple-element.63.refs_2_), channel_id=1, source_target_pairs={{0,4},{1,5},{4,8},{5,9},{8,12},{9,13},{12,14},{13,15},{14,10},{15,... | collective-permute-start | bytes 884744 | tf_op jit(solution)/shard_map/ppermute | solution.py:365
  22.2 14.2 %collective-permute-start.6 = (f32[48,1536]{1,0:T(8,128)}, f32[48,1536]{1,0:T(8,128)S(1)}, u32[]{:S(2)}, u32[]{:S(2)}) collective-permute-start(f32[48,1536]{1,0:T(8,128)} %get-tuple-element.63.refs_2_), channel_id=1, source_target_pairs={{0,2},{1,3},{4,0},{5,1},{8,4},{9,5},{12,8},{13,9},{14,12},{15,13},... | collective-permute-start | bytes 884744 | tf_op jit(solution)/shard_map/ppermute | solution.py:365
  32.5 6.2 %collective-permute-start.3 = (f32[48,1280]{1,0:T(8,128)S(1)}, f32[48,1280]{1,0:T(8,128)S(1)}, u32[]{:S(2)}, u32[]{:S(2)}) collective-permute-start(f32[48,1280]{1,0:T(8,128)S(1)} %collective-permute-done.1.refs_0_), channel_id=1, source_target_pairs={{0,4},{1,5},{4,8},{5,9},{8,12},{9,13},{12,14},{13,15},{14,10},{15,... | collective-permute-start | bytes 737288 | tf_op jit(solution)/shard_map/ppermute | solution.py:365
  36.4 12.2 %collective-permute-start.15 = (f32[48,1536]{1,0:T(8,128)S(1)}, f32[48,1536]{1,0:T(8,128)S(1)}, u32[]{:S(2)}, u32[]{:S(2)}) collective-permute-start(f32[48,1536]{1,0:T(8,128)S(1)} %collective-permute-done.5.refs_4_), channel_id=1, source_target_pairs={{0,1},{1,0},{2,3},{3,2},{4,5},{5,4},{6,7},{7,6},{8,9},{9,8},{10,11... | collective-permute-start | bytes 884744 | tf_op jit(solution)/shard_map/ppermute | solution.py:30
  36.5 12.1 %collective-permute-start.16 = (f32[48,1536]{1,0:T(8,128)S(1)}, f32[48,1536]{1,0:T(8,128)S(1)}, u32[]{:S(2)}, u32[]{:S(2)}) collective-permute-start(f32[48,1536]{1,0:T(8,128)S(1)} %collective-permute-done.6.refs_6_), channel_id=1, source_target_pairs={{0,1},{1,0},{2,3},{3,2},{4,5},{5,4},{6,7},{7,6},{8,9},{9,8},{10,11... | collective-permute-start | bytes 884744 | tf_op jit(solution)/shard_map/ppermute | solution.py:30
  37.0 7.9 %collective-permute-start.4 = (f32[48,1280]{1,0:T(8,128)S(1)}, f32[48,1280]{1,0:T(8,128)S(1)}, u32[]{:S(2)}, u32[]{:S(2)}) collective-permute-start(f32[48,1280]{1,0:T(8,128)S(1)} %collective-permute-done.2.refs_2_), channel_id=1, source_target_pairs={{0,2},{1,3},{4,0},{5,1},{8,4},{9,5},{12,8},{13,9},{14,12},{15,13},... | collective-permute-start | bytes 737288 | tf_op jit(solution)/shard_map/ppermute | solution.py:365
  38.6 7.9 %collective-permute-start.13 = (f32[48,1280]{1,0:T(8,128)S(1)}, f32[48,1280]{1,0:T(8,128)S(1)}, u32[]{:S(2)}, u32[]{:S(2)}) collective-permute-start(f32[48,1280]{1,0:T(8,128)S(1)} %collective-permute-done.1.refs_0_), channel_id=1, source_target_pairs={{0,1},{1,0},{2,3},{3,2},{4,5},{5,4},{6,7},{7,6},{8,9},{9,8},{10,11... | collective-permute-start | bytes 737288 | tf_op jit(solution)/shard_map/ppermute | solution.py:30
  38.8 8.2 %collective-permute-start.14 = (f32[48,1280]{1,0:T(8,128)S(1)}, f32[48,1280]{1,0:T(8,128)S(1)}, u32[]{:S(2)}, u32[]{:S(2)}) collective-permute-start(f32[48,1280]{1,0:T(8,128)S(1)} %collective-permute-done.2.refs_2_), channel_id=1, source_target_pairs={{0,1},{1,0},{2,3},{3,2},{4,5},{5,4},{6,7},{7,6},{8,9},{9,8},{10,11... | collective-permute-start | bytes 737288 | tf_op jit(solution)/shard_map/ppermute | solution.py:30
  44.9 15.3 %collective-permute-start.11 = (f32[48,1536]{1,0:T(8,128)S(1)}, f32[48,1536]{1,0:T(8,128)S(1)}, u32[]{:S(2)}, u32[]{:S(2)}) collective-permute-start(f32[48,1536]{1,0:T(8,128)S(1)} %collective-permute-done.5.refs_4_), channel_id=1, source_target_pairs={{0,4},{1,5},{4,8},{5,9},{8,12},{9,13},{12,14},{13,15},{14,10},{15,... | collective-permute-start | bytes 884744 | tf_op jit(solution)/shard_map/ppermute | solution.py:365
  46.5 13.7 %collective-permute-start.12 = (f32[48,1536]{1,0:T(8,128)S(1)}, f32[48,1536]{1,0:T(8,128)S(1)}, u32[]{:S(2)}, u32[]{:S(2)}) collective-permute-start(f32[48,1536]{1,0:T(8,128)S(1)} %collective-permute-done.6.refs_6_), channel_id=1, source_target_pairs={{0,2},{1,3},{4,0},{5,1},{8,4},{9,5},{12,8},{13,9},{14,12},{15,13},... | collective-permute-start | bytes 884744 | tf_op jit(solution)/shard_map/ppermute | solution.py:365
  47.0 14.2 %collective-permute-start.10 = (f32[48,1280]{1,0:T(8,128)S(1)}, f32[48,1280]{1,0:T(8,128)S(1)}, u32[]{:S(2)}, u32[]{:S(2)}) collective-permute-start(f32[48,1280]{1,0:T(8,128)S(1)} %collective-permute-done.4.refs_2_), channel_id=1, source_target_pairs={{0,2},{1,3},{4,0},{5,1},{8,4},{9,5},{12,8},{13,9},{14,12},{15,13},... | collective-permute-start | bytes 737288 | tf_op jit(solution)/shard_map/ppermute | solution.py:365
  60.2 10.5 %collective-permute-start.23 = (f32[48,1536]{1,0:T(8,128)S(1)}, f32[48,1536]{1,0:T(8,128)S(1)}, u32[]{:S(2)}, u32[]{:S(2)}) collective-permute-start(f32[48,1536]{1,0:T(8,128)S(1)} %collective-permute-done.11.refs_4_), channel_id=1, source_target_pairs={{0,1},{1,0},{2,3},{3,2},{4,5},{5,4},{6,7},{7,6},{8,9},{9,8},{10,11... | collective-permute-start | bytes 884744 | tf_op jit(solution)/shard_map/ppermute | solution.py:30
  60.2 10.5 %collective-permute-start.24 = (f32[48,1536]{1,0:T(8,128)S(1)}, f32[48,1536]{1,0:T(8,128)S(1)}, u32[]{:S(2)}, u32[]{:S(2)}) collective-permute-start(f32[48,1536]{1,0:T(8,128)S(1)} %collective-permute-done.12.refs_6_), channel_id=1, source_target_pairs={{0,1},{1,0},{2,3},{3,2},{4,5},{5,4},{6,7},{7,6},{8,9},{9,8},{10,11... | collective-permute-start | bytes 884744 | tf_op jit(solution)/shard_map/ppermute | solution.py:30
  60.7 7.9 %collective-permute-start.9 = (f32[48,1280]{1,0:T(8,128)S(1)}, f32[48,1280]{1,0:T(8,128)S(1)}, u32[]{:S(2)}, u32[]{:S(2)}) collective-permute-start(f32[48,1280]{1,0:T(8,128)S(1)} %collective-permute-done.3.refs_0_), channel_id=1, source_target_pairs={{0,4},{1,5},{4,8},{5,9},{8,12},{9,13},{12,14},{13,15},{14,10},{15,... | collective-permute-start | bytes 737288 | tf_op jit(solution)/shard_map/ppermute | solution.py:365
  61.1 7.9 %collective-permute-start.21 = (f32[48,1280]{1,0:T(8,128)S(1)}, f32[48,1280]{1,0:T(8,128)S(1)}, u32[]{:S(2)}, u32[]{:S(2)}) collective-permute-start(f32[48,1280]{1,0:T(8,128)S(1)} %collective-permute-done.3.refs_0_), channel_id=1, source_target_pairs={{0,1},{1,0},{2,3},{3,2},{4,5},{5,4},{6,7},{7,6},{8,9},{9,8},{10,11... | collective-permute-start | bytes 737288 | tf_op jit(solution)/shard_map/ppermute | solution.py:30
  61.1 9.6 %collective-permute-start.22 = (f32[48,1280]{1,0:T(8,128)S(1)}, f32[48,1280]{1,0:T(8,128)S(1)}, u32[]{:S(2)}, u32[]{:S(2)}) collective-permute-start(f32[48,1280]{1,0:T(8,128)S(1)} %collective-permute-done.4.refs_2_), channel_id=1, source_target_pairs={{0,1},{1,0},{2,3},{3,2},{4,5},{5,4},{6,7},{7,6},{8,9},{9,8},{10,11... | collective-permute-start | bytes 737288 | tf_op jit(solution)/shard_map/ppermute | solution.py:30
  68.7 14.7 %collective-permute-start.19 = (f32[48,1536]{1,0:T(8,128)S(1)}, f32[48,1536]{1,0:T(8,128)S(1)}, u32[]{:S(2)}, u32[]{:S(2)}) collective-permute-start(f32[48,1536]{1,0:T(8,128)S(1)} %collective-permute-done.11.refs_4_), channel_id=1, source_target_pairs={{0,4},{1,5},{4,8},{5,9},{8,12},{9,13},{12,14},{13,15},{14,10},{15,... | collective-permute-start | bytes 884744 | tf_op jit(solution)/shard_map/ppermute | solution.py:365
  69.1 14.3 %collective-permute-start.20 = (f32[48,1536]{1,0:T(8,128)S(1)}, f32[48,1536]{1,0:T(8,128)S(1)}, u32[]{:S(2)}, u32[]{:S(2)}) collective-permute-start(f32[48,1536]{1,0:T(8,128)S(1)} %collective-permute-done.12.refs_6_), channel_id=1, source_target_pairs={{0,2},{1,3},{4,0},{5,1},{8,4},{9,5},{12,8},{13,9},{14,12},{15,13},... | collective-permute-start | bytes 884744 | tf_op jit(solution)/shard_map/ppermute | solution.py:365
  70.7 15.7 %collective-permute-start.27 = (f32[48,1280]{1,0:T(8,128)S(1)}, f32[48,1280]{1,0:T(8,128)S(1)}, u32[]{:S(2)}, u32[]{:S(2)}) collective-permute-start(f32[48,1280]{1,0:T(8,128)S(1)} %collective-permute-done.9.refs_0_), channel_id=1, source_target_pairs={{0,1},{1,0},{2,3},{3,2},{4,5},{5,4},{6,7},{7,6},{8,9},{9,8},{10,11... | collective-permute-start | bytes 737288 | tf_op jit(solution)/shard_map/ppermute | solution.py:30
  83.4 10.6 %collective-permute-start.29 = (f32[48,1536]{1,0:T(8,128)S(1)}, f32[48,1536]{1,0:T(8,128)S(1)}, u32[]{:S(2)}, u32[]{:S(2)}) collective-permute-start(f32[48,1536]{1,0:T(8,128)S(1)} %collective-permute-done.19.refs_4_), channel_id=1, source_target_pairs={{0,1},{1,0},{2,3},{3,2},{4,5},{5,4},{6,7},{7,6},{8,9},{9,8},{10,11... | collective-permute-start | bytes 884744 | tf_op jit(solution)/shard_map/ppermute | solution.py:30
  84.0 10.0 %collective-permute-start.30 = (f32[48,1536]{1,0:T(8,128)S(1)}, f32[48,1536]{1,0:T(8,128)S(1)}, u32[]{:S(2)}, u32[]{:S(2)}) collective-permute-start(f32[48,1536]{1,0:T(8,128)S(1)} %collective-permute-done.20.refs_6_), channel_id=1, source_target_pairs={{0,1},{1,0},{2,3},{3,2},{4,5},{5,4},{6,7},{7,6},{8,9},{9,8},{10,11... | collective-permute-start | bytes 884744 | tf_op jit(solution)/shard_map/ppermute | solution.py:30
  84.1 9.4 %collective-permute-start.25 = (f32[48,1536]{1,0:T(8,128)S(1)}, f32[48,1536]{1,0:T(8,128)S(1)}, u32[]{:S(2)}, u32[]{:S(2)}) collective-permute-start(f32[48,1536]{1,0:T(8,128)S(1)} %broadcast_select_fusion), channel_id=1, source_target_pairs={{0,4},{4,8},{8,12},{12,14},{14,10},{10,6},{6,2},{2,0},{1,3},{5,1},... | collective-permute-start | bytes 884744 | tf_op jit(solution)/shard_map/ppermute | solution.py:368
  84.5 9.0 %collective-permute-start.17 = (f32[48,1280]{1,0:T(8,128)S(1)}, f32[48,1280]{1,0:T(8,128)S(1)}, u32[]{:S(2)}, u32[]{:S(2)}) collective-permute-start(f32[48,1280]{1,0:T(8,128)S(1)} %broadcast_select_fusion.1), channel_id=1, source_target_pairs={{0,4},{4,8},{8,12},{12,14},{14,10},{10,6},{6,2},{2,0},{1,3},{5,1},... | collective-permute-start | bytes 737288 | tf_op jit(solution)/shard_map/ppermute | solution.py:368
  86.4 7.6 %collective-permute-start.28 = (f32[48,1280]{1,0:T(8,128)S(1)}, f32[48,1280]{1,0:T(8,128)S(1)}, u32[]{:S(2)}, u32[]{:S(2)}) collective-permute-start(f32[48,1280]{1,0:T(8,128)S(1)} %collective-permute-done.10.refs_2_), channel_id=1, source_target_pairs={{0,1},{1,0},{2,3},{3,2},{4,5},{5,4},{6,7},{7,6},{8,9},{9,8},{10,11... | collective-permute-start | bytes 737288 | tf_op jit(solution)/shard_map/ppermute | solution.py:30
  93.5 6.3 %collective-permute-start.18 = (f32[48,1280]{1,0:T(8,128)S(1)}, f32[48,1280]{1,0:T(8,128)S(1)}, u32[]{:S(2)}, u32[]{:S(2)}) collective-permute-start(f32[48,1280]{1,0:T(8,128)S(1)} %collective-permute-done.17.refs_0_), channel_id=1, source_target_pairs={{0,1},{1,0},{2,3},{3,2},{4,5},{5,4},{6,7},{7,6},{8,9},{9,8},{10,11... | collective-permute-start | bytes 737288 | tf_op jit(solution)/shard_map/ppermute | solution.py:30
  93.5 6.3 %collective-permute-start.26 = (f32[48,1536]{1,0:T(8,128)S(1)}, f32[48,1536]{1,0:T(8,128)S(1)}, u32[]{:S(2)}, u32[]{:S(2)}) collective-permute-start(f32[48,1536]{1,0:T(8,128)S(1)} %collective-permute-done.25.refs_2_), channel_id=1, source_target_pairs={{0,1},{1,0},{2,3},{3,2},{4,5},{5,4},{6,7},{7,6},{8,9},{9,8},{10,11... | collective-permute-start | bytes 884744 | tf_op jit(solution)/shard_map/ppermute | solution.py:30
  (12 other events, 25.0 us)

commit v5 on v4

--- a/solution.py
+++ b/solution.py
@@ -9,6 +9,7 @@
 TILE = 128
 LEAD = 2
 GATHER_LIMIT = 16 * 2**20
+LINK_LIMIT = 65_600_000
 
 
 def product(left, right):
@@ -86,12 +87,12 @@
     return both[:height] + (both[height:] + cross)
 
 
-def kernel_call(kernel, name, flops, moved, limit=16 * 2**20, **more):
+def kernel_call(kernel, name, limit=16 * 2**20, **more):
     return pl.pallas_call(
         kernel,
         name=name,
         compiler_params=pltpu.CompilerParams(vmem_limit_bytes=limit),
-        cost_estimate=pl.CostEstimate(flops=flops, bytes_accessed=moved, transcendentals=0),
+        cost_estimate=pl.CostEstimate(flops=0, bytes_accessed=0, transcendentals=0),
         **more,
     )
 
@@ -108,30 +109,32 @@
     return [pl.BlockSpec(memory_space=pltpu.HBM)] * count
 
 
-def turned_rows(block):
-    columns, both = block.shape
-    rows = both // 2
-
-    def kernel(block_ref, mine_ref, theirs_ref, here, sem):
-        fetch = pltpu.make_async_copy(block_ref, here, sem)
-        fetch.start()
-        fetch.wait()
-        turned = here[...].T
-        low = lax.axis_index("row") < PCOL
-        mine_ref[...] = jnp.where(low, turned[:rows], turned[rows:])
-        theirs_ref[...] = jnp.where(low, turned[rows:], turned[:rows])
+def partner_rows(turned):
+    rows, columns = turned.shape[0] // 2, turned.shape[1]
+
+    def kernel(turned_ref, out_ref):
+        out_ref[...] = jnp.where(lax.axis_index("row") < PCOL, turned_ref[rows:], turned_ref[:rows])
 
     return kernel_call(
         kernel,
-        "turned_rows",
-        block.size,
-        8 * block.size,
-        limit=63 * 2**20,
-        out_shape=[jax.ShapeDtypeStruct((rows, columns), jnp.float32)] * 2,
-        in_specs=at_home(1),
-        out_specs=in_vmem(2),
-        scratch_shapes=[pltpu.VMEM(block.shape, jnp.float32), pltpu.SemaphoreType.DMA],
-    )(block)
+        "partner_rows",
+        out_shape=jax.ShapeDtypeStruct((rows, columns), jnp.float32),
+        in_specs=in_vmem(1),
+        out_specs=in_vmem(1)[0],
+    )(turned)
+
+
+def pick(pair):
+    def kernel(first_ref, second_ref, out_ref):
+        out_ref[...] = jnp.where(lax.rem(lax.axis_index("row"), 2) == 0, first_ref[...], second_ref[...])
+
+    return kernel_call(
+        kernel,
+        "pick",
+        out_shape=jax.ShapeDtypeStruct(pair[0].shape, jnp.float32),
+        in_specs=in_vmem(2),
+        out_specs=in_vmem(1)[0],
+    )(*pair)
 
 
 def link_chain(anc_links, parent_links, pattern):
@@ -165,9 +168,7 @@
     return kernel_call(
         kernel,
         "link_chain",
-        12 * rows * nodes * width * width,
-        4 * parent_links.size,
-        limit=63 * 2**20,
+        limit=LINK_LIMIT,
         out_shape=[
             jax.ShapeDtypeStruct((rows, LEAD * width), jnp.float32),
             jax.ShapeDtypeStruct((rows, (nodes - LEAD) * width), jnp.float32),
@@ -182,62 +183,43 @@
     )(anc_links, parent_links, pattern)
 
 
-def lead_message(mine, theirs, first):
-    rows, columns = mine.shape
-
-    def kernel(mine_ref, theirs_ref, first_ref, out_ref):
+def lead_message(turned, theirs, first):
+    rows, columns = theirs.shape
+
+    def kernel(turned_ref, theirs_ref, first_ref, out_ref):
         low = lax.axis_index("row") < PCOL
-        out_ref[:, :columns] = jnp.where(low, mine_ref[...], theirs_ref[...])
-        out_ref[:, columns : 2 * columns] = jnp.where(low, theirs_ref[...], mine_ref[...])
+        out_ref[:, :columns] = jnp.where(low, turned_ref[:rows], theirs_ref[...])
+        out_ref[:, columns : 2 * columns] = jnp.where(low, theirs_ref[...], turned_ref[rows:])
         out_ref[:, 2 * columns :] = first_ref[...]
 
     return kernel_call(
         kernel,
         "lead_message",
-        mine.size,
-        8 * (mine.size + theirs.size + first.size),
         out_shape=jax.ShapeDtypeStruct((rows, 2 * columns + first.shape[1]), jnp.float32),
         in_specs=in_vmem(3),
         out_specs=in_vmem(1)[0],
-    )(mine, theirs, first)
+    )(turned, theirs, first)
 
 
 def inner_chain(parent_links, pivot_inverse):
     nodes, width, _ = pivot_inverse.shape
 
-    def kernel(parent_home, pivot_home, cross_ref, inner_ref, parent_ref, pivot_ref, sems):
-        fetches = [pltpu.make_async_copy(pivot_home.at[0], pivot_ref.at[0], sems.at[0, 0])]
-        for node in range(1, nodes):
-            for place, home, here, piece in (
-                (1, parent_home, parent_ref, node - 1),
-                (0, pivot_home, pivot_ref, node),
-            ):
-                fetches.append(pltpu.make_async_copy(home.at[piece], here.at[piece], sems.at[place, node]))
-        for fetch in fetches:
-            fetch.start()
-        fetches[0].wait()
+    def kernel(parent_ref, pivot_ref, cross_ref, inner_ref):
         inner = pivot_ref[0]
         inner_ref[0] = inner
         for node in range(1, nodes):
-            fetches[2 * node - 1].wait()
             link = halves(parent_ref[node - 1])
             cross = dot_halves(halves(inner), link)
             cross_ref[node - 1] = -cross
-            fetches[2 * node].wait()
             inner = pivot_ref[node] + dot_halves(link, halves(cross), ((0,), (0,)))
             inner_ref[node] = inner
 
-    shapes = [jax.ShapeDtypeStruct(array.shape, jnp.float32) for array in (parent_links, pivot_inverse)]
     return kernel_call(
         kernel,
         "inner_chain",
-        12 * nodes * width**3,
-        16 * pivot_inverse.size,
-        out_shape=shapes,
-        in_specs=at_home(2),
+        out_shape=[jax.ShapeDtypeStruct(array.shape, jnp.float32) for array in (parent_links, pivot_inverse)],
+        in_specs=in_vmem(2),
         out_specs=in_vmem(2),
-        scratch_shapes=[pltpu.VMEM(shape.shape, jnp.float32) for shape in shapes]
-        + [pltpu.SemaphoreType.DMA((2, nodes))],
     )(parent_links, pivot_inverse)
 
 
@@ -343,8 +325,6 @@
     results = kernel_call(
         kernel,
         "border" + ("_end" if last else "" if held else "_start"),
-        6 * nodes * fresh * width * (order + 4 * width),
-        4 * sum(array.size for array in operands),
         out_shape=shapes,
         in_specs=in_vmem(len(operands)),
         out_specs=at_home(len(shapes)) if last else in_vmem(len(shapes)),
@@ -355,7 +335,6 @@
 
 
 def gather_plan(anc_blocks, anc_links, parent_links, pivot_inverse, pattern):
-    my_index = lax.axis_index("row")
     chips = lax.axis_size("row") // 2
     far = chips // 2
     ahead, behind = ring_pairs(chips, 1), ring_pairs(chips, -1)
@@ -364,26 +343,28 @@
     def move(pair):
         return [lax.ppermute(value, "row", way) for value, way in zip(pair, (ahead, behind))]
 
-    def turn(pair):
-        return lax.ppermute(jnp.where(my_index % 2 == 0, *pair), "row", across)
-
     def both(shift, lead, rest):
         return [(shift, False, lead, rest), (shift, True, swap_bit(lead, 0), swap_bit(rest, 0))]
 
-    mine, theirs = turned_rows(anc_blocks[0])
-    theirs = swap_bit(theirs, PCOL.bit_length() - 1)
-    first, rest = link_chain(after(anc_links, mine), parent_links, pattern)
-    lead = lead_message(mine, theirs, first)
+    turned = anc_blocks[0].T
+    theirs = partner_rows(turned)
+    first, rest = link_chain(after(anc_links, theirs), parent_links, pattern)
+    lead = lead_message(turned, swap_bit(theirs, PCOL.bit_length() - 1), first)
     totals = inner_chain(after(parent_links, lead), pivot_inverse)
     leads, rests = [lead] * 2, [rest] * 2
     arrivals, held = both(0, lead, rest), None
     for step in range(1, far):
-        leads, totals = lax.optimization_barrier((move(leads), totals))
+        leads = move(leads)
+        last_lead = pick(leads) if step == far - 1 else lead
+        leads, last_lead, totals = lax.optimization_barrier((leads, last_lead, totals))
         totals, held = border(arrivals, held, *totals, chips)
         rests, totals = lax.optimization_barrier((move(rests), totals))
         arrivals = both(-step, leads[0], rests[0]) + both(step, leads[1], rests[1])
+    last_rest, totals = lax.optimization_barrier((pick(rests), totals))
     totals, held = border(arrivals, held, *totals, chips)
-    totals, panels = border(both(far, turn(leads), turn(rests)), held, *totals, chips, last=lead)
+    last = [lax.ppermute(value, "row", across) for value in (last_lead, last_rest)]
+    last, totals = lax.optimization_barrier((last, totals))
+    totals, panels = border(both(far, *last), held, *totals, chips, last=lead)
     return panels[0], *totals
 
 

time: 105 us -> 80.5 us (0.77)
  local copies, waits for them, and re-layouts: 18.4 us -> 4.89 us
  waiting for transfers between devices: 24.6 us -> 18.2 us
  Pallas kernels: 37.1 us -> 34.1 us
  starting transfers between devices: 23.7 us -> 22.1 us
    unnamed x27 -> x12, local copies, waits for them, and re-layouts: 18.4 us -> 4.89 us
    ppermute x2, waiting for transfers between devices: 6.57 us -> 0.33 us  [gather_plan(): lax.ppermute(value, 'row', across)]
    pallas_call x4 -> x6, Pallas kernels: 11.4 us -> 8.44 us  [the longest x1 4.18 us: inner_chain(): kernel_call(kernel, 'inner_chain', out_shape=[jax.ShapeDtypeStruct(array....]
    ppermute x12, waiting for transfers between devices: 18 us -> 16.4 us  [move(): lax.ppermute(value, 'row', way)]
    ppermute x17, starting transfers between devices: 7.97 us -> 6.51 us  [swap_bit(): lax.ppermute(value, 'row', [(i, i ^ mask) for i in range(lax.axis_size('r...]
    ppermute x17, waiting for transfers between devices: 0.04 us -> 1.48 us  [swap_bit(): lax.ppermute(value, 'row', [(i, i ^ mask) for i in range(lax.axis_size('r...]
    ppermute x12, starting transfers between devices: 13.5 us -> 12.3 us  [move(): lax.ppermute(value, 'row', way)]
  transfers between devices with their start and end apart: 31 -> 31, of which waited for: 5 -> 8; matrix products, arithmetic and copies ran while one was open for 0% -> 0% of each run, Pallas kernels for 29% -> 36%
where the time goes in v5:
time: 80.5 us; the launch traced here: 80.2 us
  Pallas kernels  34.1 us (42%)
  starting transfers between devices  22.1 us (27%)
  waiting for transfers between devices  18.2 us (23%)
  local copies, waits for them, and re-layouts  4.89 us (6%)
  between operations  1 us (1%)
    pallas_call x5, Pallas kernels, border(): kernel_call(kernel, 'border' + ('_end' if last else '' if held else '_sta...  25.6 us
    ppermute x12, waiting for transfers between devices, move(): lax.ppermute(value, 'row', way)  16.4 us
    ppermute x12, starting transfers between devices, move(): lax.ppermute(value, 'row', way)  12.3 us
    ppermute x17, starting transfers between devices, swap_bit(): lax.ppermute(value, 'row', [(i, i ^ mask) for i in range(lax.axis_size('r...  6.51 us
    unnamed x12, local copies, waits for them, and re-layouts  4.89 us
    pallas_call x1, Pallas kernels, inner_chain(): kernel_call(kernel, 'inner_chain', out_shape=[jax.ShapeDtypeStruct(array....  4.18 us
    pallas_call x1, Pallas kernels, link_chain(): kernel_call(kernel, 'link_chain', limit=LINK_LIMIT, out_shape=[jax.ShapeD...  4.16 us
    ppermute x2, starting transfers between devices, gather_plan(): lax.ppermute(value, 'row', across)  3.29 us
  transfers between devices with their start and end apart: 31, of which 8 were waited for; matrix products, arithmetic and copies ran while one was open for 0% of the time, Pallas kernels for 36%

profile of v5, /device:TPU:0, one launch (start us, length us, event | category | flops | bytes accessed | tf_op | source)
XLA Modules:
  0.0 80.2 jit_solution(16664957706217777989)
XLA Ops:
  0.6 0.9 %copy-done.2 = f32[1,384,96]{1,2,0:T(8,128)S(1)} copy-done((f32[1,384,96]{1,2,0:T(8,128)S(1)}, f32[1,384,96]{1,2,0:T(8,128)}, u32[]{:S(2)}) %copy-start.2) | copy-done | bytes 147480
  1.6 4.1 %collective-permute-start = (f32[48,384]{1,0:T(8,128)S(1)}, f32[48,384]{1,0:T(8,128)S(1)}, u32[]{:S(2)}, u32[]{:S(2)}) collective-permute-start(f32[48,384]{1,0:T(8,128)S(1)} %partner_rows.1), channel_id=1, source_target_pairs={{0,8},{1,9},{2,10},{3,11},{4,12},{5,13},{6,14},{7,15},{8,0},{9,1},... | collective-permute-start | bytes 221192 | tf_op jit(solution)/shard_map/ppermute | solution.py:31
  5.7 4.2 %link_chain.1 = (f32[48,512]{1,0:T(8,128)}, f32[48,1536]{1,0:T(8,128)}) custom-call(f32[48,8,256]{2,1,0:T(8,128)} %links_home, f32[7,256,256]{2,1,0:T(8,128)} %parent_ref, s32[8,6]{1,0:T(8,128)} %pattern_ref.1), custom_call_target="tpu_custom_call" | custom-call | tf_op jit(solution)/shard_map/link_chain/pallas_call | solution.py:168
  9.9 0.9 %copy-done.5 = f32[48,512]{1,0:T(8,128)S(1)} copy-done((f32[48,512]{1,0:T(8,128)S(1)}, f32[48,512]{1,0:T(8,128)}, u32[]{:S(2)}) %copy-start.5) | copy-done | bytes 98328
  10.8 1.6 %collective-permute-start.1 = (f32[48,1280]{1,0:T(8,128)S(1)}, f32[48,1280]{1,0:T(8,128)S(1)}, u32[]{:S(2)}, u32[]{:S(2)}) collective-permute-start(f32[48,1280]{1,0:T(8,128)S(1)} %lead_message.1.refs_0_.refs_4_), channel_id=1, source_target_pairs={{0,4},{1,5},{4,8},{5,9},{8,12},{9,13},{12,14},{13,15},{14,10},{15,... | collective-permute-start | bytes 737288 | tf_op jit(solution)/shard_map/ppermute | solution.py:344
  12.9 1.6 %collective-permute-start.5 = (f32[48,1536]{1,0:T(8,128)}, f32[48,1536]{1,0:T(8,128)S(1)}, u32[]{:S(2)}, u32[]{:S(2)}) collective-permute-start(f32[48,1536]{1,0:T(8,128)} %get-tuple-element.67.refs_2_), channel_id=1, source_target_pairs={{0,4},{1,5},{4,8},{5,9},{8,12},{9,13},{12,14},{13,15},{14,10},{15,... | collective-permute-start | bytes 884744 | tf_op jit(solution)/shard_map/ppermute | solution.py:344
  14.9 4.8 %collective-permute-done.1.refs_0_ = f32[48,1280]{1,0:T(8,128)S(1)} collective-permute-done((f32[48,1280]{1,0:T(8,128)S(1)}, f32[48,1280]{1,0:T(8,128)S(1)}, u32[]{:S(2)}, u32[]{:S(2)}) %collective-permute-start.1) | collective-permute-done | bytes 245792 | tf_op jit(solution)/shard_map/ppermute | solution.py:344
  19.7 1.5 %copy-done = f32[7,256,256]{2,1,0:T(8,128)S(1)} copy-done((f32[7,256,256]{2,1,0:T(8,128)S(1)}, f32[7,256,256]{2,1,0:T(8,128)}, u32[]{:S(2)}) %copy-start) | copy-done | bytes 1835032
  21.2 1.6 %copy-done.1 = f32[8,256,256]{2,1,0:T(8,128)S(1)} copy-done((f32[8,256,256]{2,1,0:T(8,128)S(1)}, f32[8,256,256]{2,1,0:T(8,128)}, u32[]{:S(2)}) %copy-start.1) | copy-done | bytes 2097176
  22.8 4.2 %inner_chain.1 = (f32[7,256,256]{2,1,0:T(8,128)S(1)}, f32[8,256,256]{2,1,0:T(8,128)S(1)}) custom-call(f32[7,256,256]{2,1,0:T(8,128)S(1)} %copy-done, f32[8,256,256]{2,1,0:T(8,128)S(1)} %copy-done.1), custom_call_target="tpu_custom_call" | custom-call | tf_op jit(solution)/shard_map/inner_chain/pallas_call | solution.py:217
  27.0 1.6 %collective-permute-start.3 = (f32[48,1280]{1,0:T(8,128)S(1)}, f32[48,1280]{1,0:T(8,128)S(1)}, u32[]{:S(2)}, u32[]{:S(2)}) collective-permute-start(f32[48,1280]{1,0:T(8,128)S(1)} %collective-permute-done.1.refs_0_), channel_id=1, source_target_pairs={{0,4},{1,5},{4,8},{5,9},{8,12},{9,13},{12,14},{13,15},{14,10},{15,... | collective-permute-start | bytes 737288 | tf_op jit(solution)/shard_map/ppermute | solution.py:344
  29.1 3.4 %border_start.1 = (f32[7,256,256]{2,1,0:T(8,128)S(1)}, f32[8,256,256]{2,1,0:T(8,128)S(1)}, bf16[768,2048]{1,0:T(8,128)(2,1)S(1)}, bf16[768,2048]{1,0:T(8,128)(2,1)S(1)}) custom-call(f32[48,1280]{1,0:T(8,128)S(1)} %lead_message.1.refs_0_.refs_4_, f32[48,1280]{1,0:T(8,128)S(1)} %collective-permute-done.7.refs_1_, f32[48,1536]{1,0:T(8,128)S(1)} %copy-done.4, ...), custom_call_target="tpu_custom_call" | custom-call | tf_op jit(solution)/shard_map/border_start/pallas_call | solution.py:325
  32.5 0.6 collective-permute-start.15
  33.2 2.2 %collective-permute-done.3.refs_0_ = f32[48,1280]{1,0:T(8,128)S(1)} collective-permute-done((f32[48,1280]{1,0:T(8,128)S(1)}, f32[48,1280]{1,0:T(8,128)S(1)}, u32[]{:S(2)}, u32[]{:S(2)}) %collective-permute-start.3) | collective-permute-done | bytes 245792 | tf_op jit(solution)/shard_map/ppermute | solution.py:344
  35.4 1.3 %collective-permute-done.4.refs_2_ = f32[48,1280]{1,0:T(8,128)S(1)} collective-permute-done((f32[48,1280]{1,0:T(8,128)S(1)}, f32[48,1280]{1,0:T(8,128)S(1)}, u32[]{:S(2)}, u32[]{:S(2)}) %collective-permute-start.4) | collective-permute-done | bytes 245792 | tf_op jit(solution)/shard_map/ppermute | solution.py:344
  36.7 1.0 %collective-permute-start.11 = (f32[48,1536]{1,0:T(8,128)S(1)}, f32[48,1536]{1,0:T(8,128)S(1)}, u32[]{:S(2)}, u32[]{:S(2)}) collective-permute-start(f32[48,1536]{1,0:T(8,128)S(1)} %collective-permute-done.5.refs_4_), channel_id=1, source_target_pairs={{0,4},{1,5},{4,8},{5,9},{8,12},{9,13},{12,14},{13,15},{14,10},{15,... | collective-permute-start | bytes 884744 | tf_op jit(solution)/shard_map/ppermute | solution.py:344
  37.7 1.0 %collective-permute-start.12 = (f32[48,1536]{1,0:T(8,128)S(1)}, f32[48,1536]{1,0:T(8,128)S(1)}, u32[]{:S(2)}, u32[]{:S(2)}) collective-permute-start(f32[48,1536]{1,0:T(8,128)S(1)} %collective-permute-done.6.refs_6_), channel_id=1, source_target_pairs={{0,2},{1,3},{4,0},{5,1},{8,4},{9,5},{12,8},{13,9},{14,12},{15,13},... | collective-permute-start | bytes 884744 | tf_op jit(solution)/shard_map/ppermute | solution.py:344
  39.2 1.6 %collective-permute-start.9 = (f32[48,1280]{1,0:T(8,128)S(1)}, f32[48,1280]{1,0:T(8,128)S(1)}, u32[]{:S(2)}, u32[]{:S(2)}) collective-permute-start(f32[48,1280]{1,0:T(8,128)S(1)} %collective-permute-done.3.refs_0_), channel_id=1, source_target_pairs={{0,4},{1,5},{4,8},{5,9},{8,12},{9,13},{12,14},{13,15},{14,10},{15,... | collective-permute-start | bytes 737288 | tf_op jit(solution)/shard_map/ppermute | solution.py:344
  40.8 5.9 %collective-permute-done.11.refs_4_ = f32[48,1536]{1,0:T(8,128)S(1)} collective-permute-done((f32[48,1536]{1,0:T(8,128)S(1)}, f32[48,1536]{1,0:T(8,128)S(1)}, u32[]{:S(2)}, u32[]{:S(2)}) %collective-permute-start.11) | collective-permute-done | bytes 294944 | tf_op jit(solution)/shard_map/ppermute | solution.py:344
  46.7 5.8 %border.3 = (f32[7,256,256]{2,1,0:T(8,128)S(1)}, f32[8,256,256]{2,1,0:T(8,128)S(1)}, bf16[768,2048]{1,0:T(8,128)(2,1)S(1)}, bf16[768,2048]{1,0:T(8,128)(2,1)S(1)}) custom-call(f32[48,1280]{1,0:T(8,128)S(1)} %collective-permute-done.1.refs_0_, f32[48,1280]{1,0:T(8,128)S(1)} %collective-permute-done.13.refs_1_, f32[48,1280]{1,0:T(8,128)S(1)} %collective-permute-done.2.refs_2_, ...), custom_call_target="tpu_custom_call" | custom-call | tf_op jit(solution)/shard_map/border/pallas_call | solution.py:325
  52.4 0.6 collective-permute-start.22
  53.1 0.9 %collective-permute-start.18 = (f32[48,1536]{1,0:T(8,128)S(1)}, f32[48,1536]{1,0:T(8,128)S(1)}, u32[]{:S(2)}, u32[]{:S(2)}) collective-permute-start(f32[48,1536]{1,0:T(8,128)S(1)} %collective-permute-done.11.refs_4_), channel_id=1, source_target_pairs={{0,4},{1,5},{4,8},{5,9},{8,12},{9,13},{12,14},{13,15},{14,10},{15,... | collective-permute-start | bytes 884744 | tf_op jit(solution)/shard_map/ppermute | solution.py:344
  54.1 1.1 %collective-permute-start.19 = (f32[48,1536]{1,0:T(8,128)S(1)}, f32[48,1536]{1,0:T(8,128)S(1)}, u32[]{:S(2)}, u32[]{:S(2)}) collective-permute-start(f32[48,1536]{1,0:T(8,128)S(1)} %collective-permute-done.12.refs_6_), channel_id=1, source_target_pairs={{0,2},{1,3},{4,0},{5,1},{8,4},{9,5},{12,8},{13,9},{14,12},{15,13},... | collective-permute-start | bytes 884744 | tf_op jit(solution)/shard_map/ppermute | solution.py:344
  55.3 5.8 %border.4 = (f32[7,256,256]{2,1,0:T(8,128)S(1)}, f32[8,256,256]{2,1,0:T(8,128)S(1)}, bf16[768,2048]{1,0:T(8,128)(2,1)S(1)}, bf16[768,2048]{1,0:T(8,128)(2,1)S(1)}) custom-call(f32[48,1280]{1,0:T(8,128)S(1)} %collective-permute-done.3.refs_0_, f32[48,1280]{1,0:T(8,128)S(1)} %collective-permute-done.20.refs_1_, f32[48,1280]{1,0:T(8,128)S(1)} %collective-permute-done.4.refs_2_, ...), custom_call_target="tpu_custom_call" | custom-call | tf_op jit(solution)/shard_map/border/pallas_call | solution.py:325
  61.0 1.4 %collective-permute-done.18.first_ref.refs_4_ = f32[48,1536]{1,0:T(8,128)S(1)} collective-permute-done((f32[48,1536]{1,0:T(8,128)S(1)}, f32[48,1536]{1,0:T(8,128)S(1)}, u32[]{:S(2)}, u32[]{:S(2)}) %collective-permute-start.18) | collective-permute-done | bytes 294944 | tf_op jit(solution)/shard_map/ppermute | solution.py:344
  62.5 0.7 collective-permute-done.19.second_ref.refs_6_
  63.7 1.8 %collective-permute-start.24 = (f32[48,1536]{1,0:T(8,128)S(1)}, f32[48,1536]{1,0:T(8,128)S(1)}, u32[]{:S(2)}, u32[]{:S(2)}) collective-permute-start(f32[48,1536]{1,0:T(8,128)S(1)} %pick.3), channel_id=1, source_target_pairs={{0,4},{4,8},{8,12},{12,14},{14,10},{10,6},{6,2},{2,0},{1,3},{5,1},... | collective-permute-start | bytes 884744 | tf_op jit(solution)/shard_map/ppermute | solution.py:365
  65.5 1.5 %collective-permute-start.17 = (f32[48,1280]{1,0:T(8,128)S(1)}, f32[48,1280]{1,0:T(8,128)S(1)}, u32[]{:S(2)}, u32[]{:S(2)}) collective-permute-start(f32[48,1280]{1,0:T(8,128)S(1)} %pick.2), channel_id=1, source_target_pairs={{0,4},{4,8},{8,12},{12,14},{14,10},{10,6},{6,2},{2,0},{1,3},{5,1},... | collective-permute-start | bytes 737288 | tf_op jit(solution)/shard_map/ppermute | solution.py:365
  67.0 5.8 %border.5 = (f32[7,256,256]{2,1,0:T(8,128)S(1)}, f32[8,256,256]{2,1,0:T(8,128)S(1)}, bf16[768,2048]{1,0:T(8,128)(2,1)S(1)}, bf16[768,2048]{1,0:T(8,128)(2,1)S(1)}) custom-call(f32[48,1280]{1,0:T(8,128)S(1)} %collective-permute-done.9.first_ref.refs_0_, f32[48,1280]{1,0:T(8,128)S(1)} %collective-permute-done.25.refs_1_, ...), custom_call_target="tpu_custom_call" | custom-call | tf_op jit(solution)/shard_map/border/pallas_call | solution.py:325
  73.1 0.5 collective-permute-start.29
  73.6 1.4 %collective-permute-done.29.refs_1_ = f32[48,1280]{1,0:T(8,128)S(1)} collective-permute-done((f32[48,1280]{1,0:T(8,128)S(1)}, f32[48,1280]{1,0:T(8,128)S(1)}, u32[]{:S(2)}, u32[]{:S(2)}) %collective-permute-start.29) | collective-permute-done | bytes 245792 | tf_op jit(solution)/shard_map/ppermute | solution.py:31
  75.1 4.9 %border_end.1 = (f32[7,256,256]{2,1,0:T(8,128)}, f32[8,256,256]{2,1,0:T(8,128)}, f32[48,8,256]{2,1,0:T(8,128)}) custom-call(f32[48,1280]{1,0:T(8,128)S(1)} %collective-permute-done.17.refs_0_, f32[48,1280]{1,0:T(8,128)S(1)} %collective-permute-done.29.refs_1_, f32[48,1536]{1,0:T(8,128)S(1)} %collective-permute-done.24.refs_2_, ...), custom_call_target="tpu_custom_call" | custom-call | tf_op jit(solution)/shard_map/border_end/pallas_call | solution.py:325
  (53 shorter events, 3.1 us)
Async XLA Ops:
  1.6 8.3 %collective-permute-start = (f32[48,384]{1,0:T(8,128)S(1)}, f32[48,384]{1,0:T(8,128)S(1)}, u32[]{:S(2)}, u32[]{:S(2)}) collective-permute-start(f32[48,384]{1,0:T(8,128)S(1)} %partner_rows.1), channel_id=1, source_target_pairs={{0,8},{1,9},{2,10},{3,11},{4,12},{5,13},{6,14},{7,15},{8,0},{9,1},... | collective-permute-start | bytes 221192 | tf_op jit(solution)/shard_map/ppermute | solution.py:31
  10.7 18.3 %copy-start.4 = (f32[48,1536]{1,0:T(8,128)S(1)}, f32[48,1536]{1,0:T(8,128)}, u32[]{:S(2)}) copy-start(f32[48,1536]{1,0:T(8,128)} %get-tuple-element.67.refs_2_) | copy-start | bytes 884740
  10.8 8.9 %collective-permute-start.1 = (f32[48,1280]{1,0:T(8,128)S(1)}, f32[48,1280]{1,0:T(8,128)S(1)}, u32[]{:S(2)}, u32[]{:S(2)}) collective-permute-start(f32[48,1280]{1,0:T(8,128)S(1)} %lead_message.1.refs_0_.refs_4_), channel_id=1, source_target_pairs={{0,4},{1,5},{4,8},{5,9},{8,12},{9,13},{12,14},{13,15},{14,10},{15,... | collective-permute-start | bytes 737288 | tf_op jit(solution)/shard_map/ppermute | solution.py:344
  12.4 14.6 %collective-permute-start.2 = (f32[48,1280]{1,0:T(8,128)S(1)}, f32[48,1280]{1,0:T(8,128)S(1)}, u32[]{:S(2)}, u32[]{:S(2)}) collective-permute-start(f32[48,1280]{1,0:T(8,128)S(1)} %lead_message.1.refs_0_.refs_4_), channel_id=1, source_target_pairs={{0,2},{1,3},{4,0},{5,1},{8,4},{9,5},{12,8},{13,9},{14,12},{15,13},... | collective-permute-start | bytes 737288 | tf_op jit(solution)/shard_map/ppermute | solution.py:344
  12.9 15.8 %collective-permute-start.8 = (f32[48,1536]{1,0:T(8,128)}, f32[48,1536]{1,0:T(8,128)S(1)}, u32[]{:S(2)}, u32[]{:S(2)}) collective-permute-start(f32[48,1536]{1,0:T(8,128)} %get-tuple-element.67.refs_2_), channel_id=1, source_target_pairs={{0,1},{1,0},{2,3},{3,2},{4,5},{5,4},{6,7},{7,6},{8,9},{9,8},{10,11... | collective-permute-start | bytes 884744 | tf_op jit(solution)/shard_map/ppermute | solution.py:31
  12.9 19.7 %collective-permute-start.5 = (f32[48,1536]{1,0:T(8,128)}, f32[48,1536]{1,0:T(8,128)S(1)}, u32[]{:S(2)}, u32[]{:S(2)}) collective-permute-start(f32[48,1536]{1,0:T(8,128)} %get-tuple-element.67.refs_2_), channel_id=1, source_target_pairs={{0,4},{1,5},{4,8},{5,9},{8,12},{9,13},{12,14},{13,15},{14,10},{15,... | collective-permute-start | bytes 884744 | tf_op jit(solution)/shard_map/ppermute | solution.py:344
  14.4 18.1 %collective-permute-start.6 = (f32[48,1536]{1,0:T(8,128)}, f32[48,1536]{1,0:T(8,128)S(1)}, u32[]{:S(2)}, u32[]{:S(2)}) collective-permute-start(f32[48,1536]{1,0:T(8,128)} %get-tuple-element.67.refs_2_), channel_id=1, source_target_pairs={{0,2},{1,3},{4,0},{5,1},{8,4},{9,5},{12,8},{13,9},{14,12},{15,13},... | collective-permute-start | bytes 884744 | tf_op jit(solution)/shard_map/ppermute | solution.py:344
  19.7 9.4 %collective-permute-start.7 = (f32[48,1280]{1,0:T(8,128)S(1)}, f32[48,1280]{1,0:T(8,128)S(1)}, u32[]{:S(2)}, u32[]{:S(2)}) collective-permute-start(f32[48,1280]{1,0:T(8,128)S(1)} %lead_message.1.refs_0_.refs_4_), channel_id=1, source_target_pairs={{0,1},{1,0},{2,3},{3,2},{4,5},{5,4},{6,7},{7,6},{8,9},{9,8},{10,11... | collective-permute-start | bytes 737288 | tf_op jit(solution)/shard_map/ppermute | solution.py:31
  27.0 8.4 %collective-permute-start.3 = (f32[48,1280]{1,0:T(8,128)S(1)}, f32[48,1280]{1,0:T(8,128)S(1)}, u32[]{:S(2)}, u32[]{:S(2)}) collective-permute-start(f32[48,1280]{1,0:T(8,128)S(1)} %collective-permute-done.1.refs_0_), channel_id=1, source_target_pairs={{0,4},{1,5},{4,8},{5,9},{8,12},{9,13},{12,14},{13,15},{14,10},{15,... | collective-permute-start | bytes 737288 | tf_op jit(solution)/shard_map/ppermute | solution.py:344
  28.6 8.1 %collective-permute-start.4 = (f32[48,1280]{1,0:T(8,128)S(1)}, f32[48,1280]{1,0:T(8,128)S(1)}, u32[]{:S(2)}, u32[]{:S(2)}) collective-permute-start(f32[48,1280]{1,0:T(8,128)S(1)} %collective-permute-done.2.refs_2_), channel_id=1, source_target_pairs={{0,2},{1,3},{4,0},{5,1},{8,4},{9,5},{12,8},{13,9},{14,12},{15,13},... | collective-permute-start | bytes 737288 | tf_op jit(solution)/shard_map/ppermute | solution.py:344
  29.1 8.6 %collective-permute-start.13 = (f32[48,1280]{1,0:T(8,128)S(1)}, f32[48,1280]{1,0:T(8,128)S(1)}, u32[]{:S(2)}, u32[]{:S(2)}) collective-permute-start(f32[48,1280]{1,0:T(8,128)S(1)} %collective-permute-done.1.refs_0_), channel_id=1, source_target_pairs={{0,1},{1,0},{2,3},{3,2},{4,5},{5,4},{6,7},{7,6},{8,9},{9,8},{10,11... | collective-permute-start | bytes 737288 | tf_op jit(solution)/shard_map/ppermute | solution.py:31
  32.5 6.7 %collective-permute-start.15 = (f32[48,1536]{1,0:T(8,128)S(1)}, f32[48,1536]{1,0:T(8,128)S(1)}, u32[]{:S(2)}, u32[]{:S(2)}) collective-permute-start(f32[48,1536]{1,0:T(8,128)S(1)} %collective-permute-done.5.refs_4_), channel_id=1, source_target_pairs={{0,1},{1,0},{2,3},{3,2},{4,5},{5,4},{6,7},{7,6},{8,9},{9,8},{10,11... | collective-permute-start | bytes 884744 | tf_op jit(solution)/shard_map/ppermute | solution.py:31
  33.1 7.7 %collective-permute-start.16 = (f32[48,1536]{1,0:T(8,128)S(1)}, f32[48,1536]{1,0:T(8,128)S(1)}, u32[]{:S(2)}, u32[]{:S(2)}) collective-permute-start(f32[48,1536]{1,0:T(8,128)S(1)} %collective-permute-done.6.refs_6_), channel_id=1, source_target_pairs={{0,1},{1,0},{2,3},{3,2},{4,5},{5,4},{6,7},{7,6},{8,9},{9,8},{10,11... | collective-permute-start | bytes 884744 | tf_op jit(solution)/shard_map/ppermute | solution.py:31
  35.4 3.3 %collective-permute-start.14 = (f32[48,1280]{1,0:T(8,128)S(1)}, f32[48,1280]{1,0:T(8,128)S(1)}, u32[]{:S(2)}, u32[]{:S(2)}) collective-permute-start(f32[48,1280]{1,0:T(8,128)S(1)} %collective-permute-done.2.refs_2_), channel_id=1, source_target_pairs={{0,1},{1,0},{2,3},{3,2},{4,5},{5,4},{6,7},{7,6},{8,9},{9,8},{10,11... | collective-permute-start | bytes 737288 | tf_op jit(solution)/shard_map/ppermute | solution.py:31
  36.7 9.9 %collective-permute-start.11 = (f32[48,1536]{1,0:T(8,128)S(1)}, f32[48,1536]{1,0:T(8,128)S(1)}, u32[]{:S(2)}, u32[]{:S(2)}) collective-permute-start(f32[48,1536]{1,0:T(8,128)S(1)} %collective-permute-done.5.refs_4_), channel_id=1, source_target_pairs={{0,4},{1,5},{4,8},{5,9},{8,12},{9,13},{12,14},{13,15},{14,10},{15,... | collective-permute-start | bytes 884744 | tf_op jit(solution)/shard_map/ppermute | solution.py:344
  37.7 14.7 %collective-permute-start.12 = (f32[48,1536]{1,0:T(8,128)S(1)}, f32[48,1536]{1,0:T(8,128)S(1)}, u32[]{:S(2)}, u32[]{:S(2)}) collective-permute-start(f32[48,1536]{1,0:T(8,128)S(1)} %collective-permute-done.6.refs_6_), channel_id=1, source_target_pairs={{0,2},{1,3},{4,0},{5,1},{8,4},{9,5},{12,8},{13,9},{14,12},{15,13},... | collective-permute-start | bytes 884744 | tf_op jit(solution)/shard_map/ppermute | solution.py:344
  38.8 14.3 %collective-permute-start.10 = (f32[48,1280]{1,0:T(8,128)S(1)}, f32[48,1280]{1,0:T(8,128)S(1)}, u32[]{:S(2)}, u32[]{:S(2)}) collective-permute-start(f32[48,1280]{1,0:T(8,128)S(1)} %collective-permute-done.4.refs_2_), channel_id=1, source_target_pairs={{0,2},{1,3},{4,0},{5,1},{8,4},{9,5},{12,8},{13,9},{14,12},{15,13},... | collective-permute-start | bytes 737288 | tf_op jit(solution)/shard_map/ppermute | solution.py:344
  39.2 13.9 %collective-permute-start.9 = (f32[48,1280]{1,0:T(8,128)S(1)}, f32[48,1280]{1,0:T(8,128)S(1)}, u32[]{:S(2)}, u32[]{:S(2)}) collective-permute-start(f32[48,1280]{1,0:T(8,128)S(1)} %collective-permute-done.3.refs_0_), channel_id=1, source_target_pairs={{0,4},{1,5},{4,8},{5,9},{8,12},{9,13},{12,14},{13,15},{14,10},{15,... | collective-permute-start | bytes 737288 | tf_op jit(solution)/shard_map/ppermute | solution.py:344
  40.8 13.3 %collective-permute-start.20 = (f32[48,1280]{1,0:T(8,128)S(1)}, f32[48,1280]{1,0:T(8,128)S(1)}, u32[]{:S(2)}, u32[]{:S(2)}) collective-permute-start(f32[48,1280]{1,0:T(8,128)S(1)} %collective-permute-done.3.refs_0_), channel_id=1, source_target_pairs={{0,1},{1,0},{2,3},{3,2},{4,5},{5,4},{6,7},{7,6},{8,9},{9,8},{10,11... | collective-permute-start | bytes 737288 | tf_op jit(solution)/shard_map/ppermute | solution.py:31
  46.7 8.5 %collective-permute-start.21 = (f32[48,1280]{1,0:T(8,128)S(1)}, f32[48,1280]{1,0:T(8,128)S(1)}, u32[]{:S(2)}, u32[]{:S(2)}) collective-permute-start(f32[48,1280]{1,0:T(8,128)S(1)} %collective-permute-done.4.refs_2_), channel_id=1, source_target_pairs={{0,1},{1,0},{2,3},{3,2},{4,5},{5,4},{6,7},{7,6},{8,9},{9,8},{10,11... | collective-permute-start | bytes 737288 | tf_op jit(solution)/shard_map/ppermute | solution.py:31
  52.4 2.8 %collective-permute-start.22 = (f32[48,1536]{1,0:T(8,128)S(1)}, f32[48,1536]{1,0:T(8,128)S(1)}, u32[]{:S(2)}, u32[]{:S(2)}) collective-permute-start(f32[48,1536]{1,0:T(8,128)S(1)} %collective-permute-done.11.refs_4_), channel_id=1, source_target_pairs={{0,1},{1,0},{2,3},{3,2},{4,5},{5,4},{6,7},{7,6},{8,9},{9,8},{10,11... | collective-permute-start | bytes 884744 | tf_op jit(solution)/shard_map/ppermute | solution.py:31
  53.0 2.3 %collective-permute-start.23 = (f32[48,1536]{1,0:T(8,128)S(1)}, f32[48,1536]{1,0:T(8,128)S(1)}, u32[]{:S(2)}, u32[]{:S(2)}) collective-permute-start(f32[48,1536]{1,0:T(8,128)S(1)} %collective-permute-done.12.refs_6_), channel_id=1, source_target_pairs={{0,1},{1,0},{2,3},{3,2},{4,5},{5,4},{6,7},{7,6},{8,9},{9,8},{10,11... | collective-permute-start | bytes 884744 | tf_op jit(solution)/shard_map/ppermute | solution.py:31
  53.1 9.4 %collective-permute-start.18 = (f32[48,1536]{1,0:T(8,128)S(1)}, f32[48,1536]{1,0:T(8,128)S(1)}, u32[]{:S(2)}, u32[]{:S(2)}) collective-permute-start(f32[48,1536]{1,0:T(8,128)S(1)} %collective-permute-done.11.refs_4_), channel_id=1, source_target_pairs={{0,4},{1,5},{4,8},{5,9},{8,12},{9,13},{12,14},{13,15},{14,10},{15,... | collective-permute-start | bytes 884744 | tf_op jit(solution)/shard_map/ppermute | solution.py:344
  54.1 9.1 %collective-permute-start.19 = (f32[48,1536]{1,0:T(8,128)S(1)}, f32[48,1536]{1,0:T(8,128)S(1)}, u32[]{:S(2)}, u32[]{:S(2)}) collective-permute-start(f32[48,1536]{1,0:T(8,128)S(1)} %collective-permute-done.12.refs_6_), channel_id=1, source_target_pairs={{0,2},{1,3},{4,0},{5,1},{8,4},{9,5},{12,8},{13,9},{14,12},{15,13},... | collective-permute-start | bytes 884744 | tf_op jit(solution)/shard_map/ppermute | solution.py:344
  55.2 10.3 %collective-permute-start.25 = (f32[48,1280]{1,0:T(8,128)S(1)}, f32[48,1280]{1,0:T(8,128)S(1)}, u32[]{:S(2)}, u32[]{:S(2)}) collective-permute-start(f32[48,1280]{1,0:T(8,128)S(1)} %collective-permute-done.9.first_ref.refs_0_), channel_id=1, source_target_pairs={{0,1},{1,0},{2,3},{3,2},{4,5},{5,4},{6,7},{7,6},{8,9},{9,8},{10,11... | collective-permute-start | bytes 737288 | tf_op jit(solution)/shard_map/ppermute | solution.py:31
  63.2 3.9 %collective-permute-start.27 = (f32[48,1536]{1,0:T(8,128)S(1)}, f32[48,1536]{1,0:T(8,128)S(1)}, u32[]{:S(2)}, u32[]{:S(2)}) collective-permute-start(f32[48,1536]{1,0:T(8,128)S(1)} %collective-permute-done.18.first_ref.refs_4_), channel_id=1, source_target_pairs={{0,1},{1,0},{2,3},{3,2},{4,5},{5,4},{6,7},{7,6},{8,9},{9,8},{10,11... | collective-permute-start | bytes 884744 | tf_op jit(solution)/shard_map/ppermute | solution.py:31
  63.2 3.9 %collective-permute-start.28 = (f32[48,1536]{1,0:T(8,128)S(1)}, f32[48,1536]{1,0:T(8,128)S(1)}, u32[]{:S(2)}, u32[]{:S(2)}) collective-permute-start(f32[48,1536]{1,0:T(8,128)S(1)} %collective-permute-done.19.second_ref.refs_6_), channel_id=1, source_target_pairs={{0,1},{1,0},{2,3},{3,2},{4,5},{5,4},{6,7},{7,6},{8,9},{9,8},{10,11... | collective-permute-start | bytes 884744 | tf_op jit(solution)/shard_map/ppermute | solution.py:31
  63.7 9.4 %collective-permute-start.24 = (f32[48,1536]{1,0:T(8,128)S(1)}, f32[48,1536]{1,0:T(8,128)S(1)}, u32[]{:S(2)}, u32[]{:S(2)}) collective-permute-start(f32[48,1536]{1,0:T(8,128)S(1)} %pick.3), channel_id=1, source_target_pairs={{0,4},{4,8},{8,12},{12,14},{14,10},{10,6},{6,2},{2,0},{1,3},{5,1},... | collective-permute-start | bytes 884744 | tf_op jit(solution)/shard_map/ppermute | solution.py:365
  65.5 1.5 %collective-permute-start.26 = (f32[48,1280]{1,0:T(8,128)S(1)}, f32[48,1280]{1,0:T(8,128)S(1)}, u32[]{:S(2)}, u32[]{:S(2)}) collective-permute-start(f32[48,1280]{1,0:T(8,128)S(1)} %collective-permute-done.10.second_ref.refs_2_), channel_id=1, source_target_pairs={{0,1},{1,0},{2,3},{3,2},{4,5},{5,4},{6,7},{7,6},{8,9},{9,8},{10,11... | collective-permute-start | bytes 737288 | tf_op jit(solution)/shard_map/ppermute | solution.py:31
  65.5 7.6 %collective-permute-start.17 = (f32[48,1280]{1,0:T(8,128)S(1)}, f32[48,1280]{1,0:T(8,128)S(1)}, u32[]{:S(2)}, u32[]{:S(2)}) collective-permute-start(f32[48,1280]{1,0:T(8,128)S(1)} %pick.2), channel_id=1, source_target_pairs={{0,4},{4,8},{8,12},{12,14},{14,10},{10,6},{6,2},{2,0},{1,3},{5,1},... | collective-permute-start | bytes 737288 | tf_op jit(solution)/shard_map/ppermute | solution.py:365
  73.1 1.9 %collective-permute-start.30 = (f32[48,1536]{1,0:T(8,128)S(1)}, f32[48,1536]{1,0:T(8,128)S(1)}, u32[]{:S(2)}, u32[]{:S(2)}) collective-permute-start(f32[48,1536]{1,0:T(8,128)S(1)} %collective-permute-done.24.refs_2_), channel_id=1, source_target_pairs={{0,1},{1,0},{2,3},{3,2},{4,5},{5,4},{6,7},{7,6},{8,9},{9,8},{10,11... | collective-permute-start | bytes 884744 | tf_op jit(solution)/shard_map/ppermute | solution.py:31
  73.1 1.9 %collective-permute-start.29 = (f32[48,1280]{1,0:T(8,128)S(1)}, f32[48,1280]{1,0:T(8,128)S(1)}, u32[]{:S(2)}, u32[]{:S(2)}) collective-permute-start(f32[48,1280]{1,0:T(8,128)S(1)} %collective-permute-done.17.refs_0_), channel_id=1, source_target_pairs={{0,1},{1,0},{2,3},{3,2},{4,5},{5,4},{6,7},{7,6},{8,9},{9,8},{10,11... | collective-permute-start | bytes 737288 | tf_op jit(solution)/shard_map/ppermute | solution.py:31
  (5 other events, 13.2 us)

commit v6 on v5

--- a/solution.py
+++ b/solution.py
@@ -7,7 +7,7 @@
 
 PCOL = 8
 TILE = 128
-LEAD = 2
+BORDER_FLOPS = 0
 GATHER_LIMIT = 16 * 2**20
 LINK_LIMIT = 65_600_000
 
@@ -87,12 +87,12 @@
     return both[:height] + (both[height:] + cross)
 
 
-def kernel_call(kernel, name, limit=16 * 2**20, **more):
+def kernel_call(kernel, name, limit=16 * 2**20, flops=0, **more):
     return pl.pallas_call(
         kernel,
         name=name,
         compiler_params=pltpu.CompilerParams(vmem_limit_bytes=limit),
-        cost_estimate=pl.CostEstimate(flops=0, bytes_accessed=0, transcendentals=0),
+        cost_estimate=pl.CostEstimate(flops=flops, bytes_accessed=0, transcendentals=0),
         **more,
     )
 
@@ -141,7 +141,7 @@
     rows, nodes, width = anc_links.shape
     tiles = pattern.shape[1]
 
-    def kernel(links_home, parent_home, pattern_ref, first_ref, rest_ref, links_ref, parent_ref, sems):
+    def kernel(links_home, parent_home, pattern_ref, out_ref, links_ref, parent_ref, sems):
         fetches = [pltpu.make_async_copy(links_home, links_ref, sems.at[0])]
         for node in range(1, nodes):
             fetches.append(
@@ -161,20 +161,16 @@
             links = jnp.where(keep != 0, links_ref[:, node, :], 0.0)
             if node > 0:
                 links = links - dot_halves(halves(reduced), halves(parent_ref[node - 1]))
-            target, place = (first_ref, node) if node < LEAD else (rest_ref, node - LEAD)
-            target[:, place * width : (place + 1) * width] = links
+            out_ref[:, node * width : (node + 1) * width] = links
             reduced = links
 
     return kernel_call(
         kernel,
         "link_chain",
         limit=LINK_LIMIT,
-        out_shape=[
-            jax.ShapeDtypeStruct((rows, LEAD * width), jnp.float32),
-            jax.ShapeDtypeStruct((rows, (nodes - LEAD) * width), jnp.float32),
-        ],
+        out_shape=jax.ShapeDtypeStruct((rows, nodes * width), jnp.float32),
         in_specs=at_home(2) + [pl.BlockSpec(memory_space=pltpu.SMEM)],
-        out_specs=in_vmem(2),
+        out_specs=in_vmem(1)[0],
         scratch_shapes=[
             pltpu.VMEM(anc_links.shape, jnp.float32),
             pltpu.VMEM(parent_links.shape, jnp.float32),
@@ -183,22 +179,22 @@
     )(anc_links, parent_links, pattern)
 
 
-def lead_message(turned, theirs, first):
+def whole_message(turned, theirs, links):
     rows, columns = theirs.shape
 
-    def kernel(turned_ref, theirs_ref, first_ref, out_ref):
+    def kernel(turned_ref, theirs_ref, links_ref, out_ref):
         low = lax.axis_index("row") < PCOL
         out_ref[:, :columns] = jnp.where(low, turned_ref[:rows], theirs_ref[...])
         out_ref[:, columns : 2 * columns] = jnp.where(low, theirs_ref[...], turned_ref[rows:])
-        out_ref[:, 2 * columns :] = first_ref[...]
+        out_ref[:, 2 * columns :] = links_ref[...]
 
     return kernel_call(
         kernel,
-        "lead_message",
-        out_shape=jax.ShapeDtypeStruct((rows, 2 * columns + first.shape[1]), jnp.float32),
+        "whole_message",
+        out_shape=jax.ShapeDtypeStruct((rows, 2 * columns + links.shape[1]), jnp.float32),
         in_specs=in_vmem(3),
         out_specs=in_vmem(1)[0],
-    )(turned, theirs, first)
+    )(turned, theirs, links)
 
 
 def inner_chain(parent_links, pivot_inverse):
@@ -235,7 +231,7 @@
 def border(arrivals, held, parents, diagonals, chips, last=False):
     nodes, width, _ = diagonals.shape
     rows = arrivals[0][2].shape[0]
-    order = arrivals[0][2].shape[1] - LEAD * width
+    order = arrivals[0][2].shape[1] - nodes * width
     count = len(arrivals)
     fresh = rows * count
     bf16 = jnp.bfloat16
@@ -243,7 +239,7 @@
     def kernel(*refs):
         refs = list(refs)
         take = lambda number: [refs.pop(0) for _ in range(number)]
-        lead_refs, rest_refs = take(count), take(count)
+        part_refs = take(count)
         own_ref = take(1)[0] if last else None
         held_before = take(2) if held else None
         parents_ref, diagonals_ref, parents_out, diagonals_out = take(4)
@@ -262,21 +258,19 @@
         if last:
             parents_out, diagonals_out, panel_out, sems = take(4)
         me = lax.axis_index("row")
-        owners = [ring_owner(me, chips, shift, other) for shift, other, _, _ in arrivals]
+        owners = [ring_owner(me, chips, shift, other) for shift, other, _ in arrivals]
 
         for part, whole in enumerate(held_now):
             whole[...] = held_before[part][...] if held else jnp.zeros(whole.shape, bf16)
-        for owner, lead, rest in zip(owners, lead_refs, rest_refs):
+        for owner, ref in zip(owners, part_refs):
             start = pl.multiple_of(owner * rows, 16)
-            for whole, part in zip(held_now, halves(lead[:, order:])):
-                whole[pl.ds(start, rows), : LEAD * width] = part
-            for whole, part in zip(held_now, halves(rest[...])):
-                whole[pl.ds(start, rows), LEAD * width :] = part
+            for whole, part in zip(held_now, halves(ref[:, order:])):
+                whole[pl.ds(start, rows), :] = part
         piece = lax.broadcasted_iota(jnp.int32, (1, order), 1) // rows
         weight = jnp.ones((1, order), jnp.float32)
         for owner in owners:
             weight = jnp.where(piece == owner, 0.5, weight)
-        left = [ref[:, :order] * weight for ref in lead_refs]
+        left = [ref[:, :order] * weight for ref in part_refs]
         if last:
             left.append(own_ref[:, :order])
         left = halves(jnp.concatenate(left, axis=0))
@@ -287,11 +281,8 @@
             if last:
                 panel_out[:, node, :] = -image[fresh:]
             image = image[:fresh]
-            if node < LEAD:
-                new = [ref[:, order + node * width : order + (node + 1) * width] for ref in lead_refs]
-            else:
-                new = [ref[:, (node - LEAD) * width : (node - LEAD + 1) * width] for ref in rest_refs]
-            new = jnp.concatenate(new, axis=0)
+            there = slice(order + node * width, order + (node + 1) * width)
+            new = jnp.concatenate([ref[:, there] for ref in part_refs], axis=0)
             for whole, part in zip(turned, halves(jnp.concatenate([new, image], axis=0).T)):
                 whole[columns, :] = part
             right.append([jnp.concatenate(pair, axis=0) for pair in zip(halves(image), halves(new))])
@@ -308,7 +299,7 @@
         for copy in copies:
             copy.wait()
 
-    operands = [lead for _, _, lead, _ in arrivals] + [rest for _, _, _, rest in arrivals]
+    operands = [part for _, _, part in arrivals]
     operands += [last] if last is not False else []
     operands += [*(held or []), parents, diagonals]
     last = last is not False
@@ -330,6 +321,7 @@
         out_specs=at_home(len(shapes)) if last else in_vmem(len(shapes)),
         scratch_shapes=scratch,
         limit=24 * 2**20 if last else 16 * 2**20,
+        flops=BORDER_FLOPS,
     )(*operands)
     return results[:2], results[2:]
 
@@ -343,28 +335,24 @@
     def move(pair):
         return [lax.ppermute(value, "row", way) for value, way in zip(pair, (ahead, behind))]
 
-    def both(shift, lead, rest):
-        return [(shift, False, lead, rest), (shift, True, swap_bit(lead, 0), swap_bit(rest, 0))]
+    def both(shift, value):
+        return [(shift, False, value), (shift, True, swap_bit(value, 0))]
 
     turned = anc_blocks[0].T
     theirs = partner_rows(turned)
-    first, rest = link_chain(after(anc_links, theirs), parent_links, pattern)
-    lead = lead_message(turned, swap_bit(theirs, PCOL.bit_length() - 1), first)
-    totals = inner_chain(after(parent_links, lead), pivot_inverse)
-    leads, rests = [lead] * 2, [rest] * 2
-    arrivals, held = both(0, lead, rest), None
+    links = link_chain(after(anc_links, theirs), parent_links, pattern)
+    own = whole_message(turned, swap_bit(theirs, PCOL.bit_length() - 1), links)
+    totals, held = inner_chain(after(parent_links, own), pivot_inverse), None
+    arrivals, pair = both(0, own), [own] * 2
     for step in range(1, far):
-        leads = move(leads)
-        last_lead = pick(leads) if step == far - 1 else lead
-        leads, last_lead, totals = lax.optimization_barrier((leads, last_lead, totals))
+        pair = move(pair)
         totals, held = border(arrivals, held, *totals, chips)
-        rests, totals = lax.optimization_barrier((move(rests), totals))
-        arrivals = both(-step, leads[0], rests[0]) + both(step, leads[1], rests[1])
-    last_rest, totals = lax.optimization_barrier((pick(rests), totals))
+        pair, totals = lax.optimization_barrier((pair, totals))
+        arrivals = both(-step, pair[0]) + both(step, pair[1])
+    last, totals = lax.optimization_barrier((pick(pair), totals))
     totals, held = border(arrivals, held, *totals, chips)
-    last = [lax.ppermute(value, "row", across) for value in (last_lead, last_rest)]
-    last, totals = lax.optimization_barrier((last, totals))
-    totals, panels = border(both(far, *last), held, *totals, chips, last=lead)
+    last, totals = lax.optimization_barrier((lax.ppermute(last, "row", across), totals))
+    totals, panels = border(both(far, last), held, *totals, chips, last=own)
     return panels[0], *totals
 
 

time: 80.5 us -> 75.2 us (0.934)
  starting transfers between devices: 22.1 us -> 12.9 us
  waiting for transfers between devices: 18.2 us -> 21.9 us
    ppermute x12 -> x6, starting transfers between devices: 12.3 us -> 6.13 us  [move(): lax.ppermute(value, 'row', way)]
    ppermute x2 -> x1, starting transfers between devices: 3.29 us -> 0.98 us  [gather_plan(): lax.ppermute(last, 'row', across)]
    ppermute x17 -> x9, waiting for transfers between devices: 1.48 us -> 3.36 us  [swap_bit(): lax.ppermute(value, 'row', [(i, i ^ mask) for i in range(lax.axis_size('r...]
    ppermute x2 -> x1, waiting for transfers between devices: 0.33 us -> 1.49 us  [gather_plan(): lax.ppermute(last, 'row', across)]
    ppermute x17 -> x9, starting transfers between devices: 6.51 us -> 5.77 us  [swap_bit(): lax.ppermute(value, 'row', [(i, i ^ mask) for i in range(lax.axis_size('r...]
    ppermute x12 -> x6, waiting for transfers between devices: 16.4 us -> 17 us  [move(): lax.ppermute(value, 'row', way)]
    unnamed x12 -> x10, local copies, waits for them, and re-layouts: 4.89 us -> 4.99 us
  transfers between devices with their start and end apart: 31 -> 16, of which waited for: 8 -> 12; matrix products, arithmetic and copies ran while one was open for 0% -> 0% of each run, Pallas kernels for 36% -> 39%
where the time goes in v6:
time: 75.2 us; the launch traced here: 74.9 us
  Pallas kernels  34.2 us (45%)
  waiting for transfers between devices  21.9 us (29%)
  starting transfers between devices  12.9 us (17%)
  local copies, waits for them, and re-layouts  4.99 us (7%)
  between operations  0.94 us (1%)
    pallas_call x5, Pallas kernels, border(): kernel_call(kernel, 'border' + ('_end' if last else '' if held else '_sta...  25.8 us
    ppermute x6, waiting for transfers between devices, move(): lax.ppermute(value, 'row', way)  17 us
    ppermute x6, starting transfers between devices, move(): lax.ppermute(value, 'row', way)  6.13 us
    ppermute x9, starting transfers between devices, swap_bit(): lax.ppermute(value, 'row', [(i, i ^ mask) for i in range(lax.axis_size('r...  5.77 us
    unnamed x10, local copies, waits for them, and re-layouts  4.99 us
    pallas_call x1, Pallas kernels, link_chain(): kernel_call(kernel, 'link_chain', limit=LINK_LIMIT, out_shape=jax.ShapeDt...  4.19 us
    pallas_call x1, Pallas kernels, inner_chain(): kernel_call(kernel, 'inner_chain', out_shape=[jax.ShapeDtypeStruct(array....  4.18 us
    ppermute x9, waiting for transfers between devices, swap_bit(): lax.ppermute(value, 'row', [(i, i ^ mask) for i in range(lax.axis_size('r...  3.36 us
  transfers between devices with their start and end apart: 16, of which 12 were waited for; matrix products, arithmetic and copies ran while one was open for 0% of the time, Pallas kernels for 39%

profile of v6, /device:TPU:0, one launch (start us, length us, event | category | flops | bytes accessed | tf_op | source)
XLA Modules:
  0.0 74.9 jit_solution(17885050867294559055)
XLA Ops:
  0.6 0.9 %copy-done.3 = f32[1,384,96]{1,2,0:T(8,128)S(1)} copy-done((f32[1,384,96]{1,2,0:T(8,128)S(1)}, f32[1,384,96]{1,2,0:T(8,128)}, u32[]{:S(2)}) %copy-start.3) | copy-done | bytes 147480
  1.6 4.1 %collective-permute-start = (f32[48,384]{1,0:T(8,128)S(1)}, f32[48,384]{1,0:T(8,128)S(1)}, u32[]{:S(2)}, u32[]{:S(2)}) collective-permute-start(f32[48,384]{1,0:T(8,128)S(1)} %partner_rows.1), channel_id=1, source_target_pairs={{0,8},{1,9},{2,10},{3,11},{4,12},{5,13},{6,14},{7,15},{8,0},{9,1},... | collective-permute-start | bytes 221192 | tf_op jit(solution)/shard_map/ppermute | solution.py:31
  5.7 4.2 %link_chain.1.links_ref = f32[48,2048]{1,0:T(8,128)} custom-call(f32[48,8,256]{2,1,0:T(8,128)} %links_home, f32[7,256,256]{2,1,0:T(8,128)} %parent_ref, s32[8,6]{1,0:T(8,128)} %pattern_ref.1), custom_call_target="tpu_custom_call" | custom-call | tf_op jit(solution)/shard_map/link_chain/pallas_call | solution.py:167
  9.9 1.0 %copy-done.2 = f32[48,2048]{1,0:T(8,128)S(1)} copy-done((f32[48,2048]{1,0:T(8,128)S(1)}, f32[48,2048]{1,0:T(8,128)}, u32[]{:S(2)}) %copy-start.2) | copy-done | bytes 393240
  11.0 1.5 %collective-permute-start.2 = (f32[48,2816]{1,0:T(8,128)S(1)}, f32[48,2816]{1,0:T(8,128)S(1)}, u32[]{:S(2)}, u32[]{:S(2)}) collective-permute-start(f32[48,2816]{1,0:T(8,128)S(1)} %whole_message.1.refs_0_.refs_2_), channel_id=1, source_target_pairs={{0,2},{1,3},{4,0},{5,1},{8,4},{9,5},{12,8},{13,9},{14,12},{15,13},... | collective-permute-start | bytes 1622024 | tf_op jit(solution)/shard_map/ppermute | solution.py:336
  12.5 0.5 collective-permute-start.1
  13.1 1.5 %copy-done = f32[7,256,256]{2,1,0:T(8,128)S(1)} copy-done((f32[7,256,256]{2,1,0:T(8,128)S(1)}, f32[7,256,256]{2,1,0:T(8,128)}, u32[]{:S(2)}) %copy-start) | copy-done | bytes 1835032
  14.6 1.6 %copy-done.1 = f32[8,256,256]{2,1,0:T(8,128)S(1)} copy-done((f32[8,256,256]{2,1,0:T(8,128)S(1)}, f32[8,256,256]{2,1,0:T(8,128)}, u32[]{:S(2)}) %copy-start.1) | copy-done | bytes 2097176
  16.2 4.2 %inner_chain.1 = (f32[7,256,256]{2,1,0:T(8,128)S(1)}, f32[8,256,256]{2,1,0:T(8,128)S(1)}) custom-call(f32[7,256,256]{2,1,0:T(8,128)S(1)} %copy-done, f32[8,256,256]{2,1,0:T(8,128)S(1)} %copy-done.1), custom_call_target="tpu_custom_call" | custom-call | tf_op jit(solution)/shard_map/inner_chain/pallas_call | solution.py:213
  20.4 3.4 %border_start.1 = (f32[7,256,256]{2,1,0:T(8,128)S(1)}, f32[8,256,256]{2,1,0:T(8,128)S(1)}, bf16[768,2048]{1,0:T(8,128)(2,1)S(1)}, bf16[768,2048]{1,0:T(8,128)(2,1)S(1)}) custom-call(f32[48,2816]{1,0:T(8,128)S(1)} %whole_message.1.refs_0_.refs_2_, f32[48,2816]{1,0:T(8,128)S(1)} %collective-permute-done.3.refs_1_, ...), custom_call_target="tpu_custom_call" | custom-call | tf_op jit(solution)/shard_map/border_start/pallas_call | solution.py:316
  23.8 1.9 %collective-permute-done.2.refs_2_ = f32[48,2816]{1,0:T(8,128)S(1)} collective-permute-done((f32[48,2816]{1,0:T(8,128)S(1)}, f32[48,2816]{1,0:T(8,128)S(1)}, u32[]{:S(2)}, u32[]{:S(2)}) %collective-permute-start.2) | collective-permute-done | bytes 540704 | tf_op jit(solution)/shard_map/ppermute | solution.py:336
  25.7 1.2 %collective-permute-done.1.refs_0_ = f32[48,2816]{1,0:T(8,128)S(1)} collective-permute-done((f32[48,2816]{1,0:T(8,128)S(1)}, f32[48,2816]{1,0:T(8,128)S(1)}, u32[]{:S(2)}, u32[]{:S(2)}) %collective-permute-start.1) | collective-permute-done | bytes 540704 | tf_op jit(solution)/shard_map/ppermute | solution.py:336
  26.9 0.5 collective-permute-start.7
  27.4 0.5 collective-permute-start.4
  27.9 1.5 %collective-permute-start.5 = (f32[48,2816]{1,0:T(8,128)S(1)}, f32[48,2816]{1,0:T(8,128)S(1)}, u32[]{:S(2)}, u32[]{:S(2)}) collective-permute-start(f32[48,2816]{1,0:T(8,128)S(1)} %collective-permute-done.2.refs_2_), channel_id=1, source_target_pairs={{0,2},{1,3},{4,0},{5,1},{8,4},{9,5},{12,8},{13,9},{14,12},{15,13},... | collective-permute-start | bytes 1622024 | tf_op jit(solution)/shard_map/ppermute | solution.py:336
  29.6 5.8 %border.3 = (f32[7,256,256]{2,1,0:T(8,128)S(1)}, f32[8,256,256]{2,1,0:T(8,128)S(1)}, bf16[768,2048]{1,0:T(8,128)(2,1)S(1)}, bf16[768,2048]{1,0:T(8,128)(2,1)S(1)}) custom-call(f32[48,2816]{1,0:T(8,128)S(1)} %collective-permute-done.1.refs_0_, f32[48,2816]{1,0:T(8,128)S(1)} %collective-permute-done.6.refs_1_, f32[48,2816]{1,0:T(8,128)S(1)} %collective-permute-done.2.refs_2_, ...), custom_call_target="tpu_custom_call" | custom-call | tf_op jit(solution)/shard_map/border/pallas_call | solution.py:316
  35.4 6.2 %collective-permute-done.4.refs_0_ = f32[48,2816]{1,0:T(8,128)S(1)} collective-permute-done((f32[48,2816]{1,0:T(8,128)S(1)}, f32[48,2816]{1,0:T(8,128)S(1)}, u32[]{:S(2)}, u32[]{:S(2)}) %collective-permute-start.4) | collective-permute-done | bytes 540704 | tf_op jit(solution)/shard_map/ppermute | solution.py:336
  41.6 0.3 collective-permute-done.5.refs_2_
  41.8 0.5 collective-permute-start.11
  42.4 1.6 %collective-permute-start.8 = (f32[48,2816]{1,0:T(8,128)S(1)}, f32[48,2816]{1,0:T(8,128)S(1)}, u32[]{:S(2)}, u32[]{:S(2)}) collective-permute-start(f32[48,2816]{1,0:T(8,128)S(1)} %collective-permute-done.4.refs_0_), channel_id=1, source_target_pairs={{0,4},{1,5},{4,8},{5,9},{8,12},{9,13},{12,14},{13,15},{14,10},{15,... | collective-permute-start | bytes 1622024 | tf_op jit(solution)/shard_map/ppermute | solution.py:336
  43.9 0.4 collective-permute-start.9
  44.6 5.8 %border.4 = (f32[7,256,256]{2,1,0:T(8,128)S(1)}, f32[8,256,256]{2,1,0:T(8,128)S(1)}, bf16[768,2048]{1,0:T(8,128)(2,1)S(1)}, bf16[768,2048]{1,0:T(8,128)(2,1)S(1)}) custom-call(f32[48,2816]{1,0:T(8,128)S(1)} %collective-permute-done.4.refs_0_, f32[48,2816]{1,0:T(8,128)S(1)} %collective-permute-done.10.refs_1_, f32[48,2816]{1,0:T(8,128)S(1)} %collective-permute-done.5.refs_2_, ...), custom_call_target="tpu_custom_call" | custom-call | tf_op jit(solution)/shard_map/border/pallas_call | solution.py:316
  50.3 6.2 %collective-permute-done.8.first_ref.refs_0_ = f32[48,2816]{1,0:T(8,128)S(1)} collective-permute-done((f32[48,2816]{1,0:T(8,128)S(1)}, f32[48,2816]{1,0:T(8,128)S(1)}, u32[]{:S(2)}, u32[]{:S(2)}) %collective-permute-start.8) | collective-permute-done | bytes 540704 | tf_op jit(solution)/shard_map/ppermute | solution.py:336
  56.5 1.3 %collective-permute-done.9.second_ref.refs_2_ = f32[48,2816]{1,0:T(8,128)S(1)} collective-permute-done((f32[48,2816]{1,0:T(8,128)S(1)}, f32[48,2816]{1,0:T(8,128)S(1)}, u32[]{:S(2)}, u32[]{:S(2)}) %collective-permute-start.9) | collective-permute-done | bytes 540704 | tf_op jit(solution)/shard_map/ppermute | solution.py:336
  57.9 0.6 collective-permute-start.14
  58.5 1.0 %collective-permute-start.12 = (f32[48,2816]{1,0:T(8,128)S(1)}, f32[48,2816]{1,0:T(8,128)S(1)}, u32[]{:S(2)}, u32[]{:S(2)}) collective-permute-start(f32[48,2816]{1,0:T(8,128)S(1)} %pick.1), channel_id=1, source_target_pairs={{0,4},{4,8},{8,12},{12,14},{14,10},{10,6},{6,2},{2,0},{1,3},{5,1},... | collective-permute-start | bytes 1622024 | tf_op jit(solution)/shard_map/ppermute | solution.py:354
  59.5 0.3 collective-permute-done.13.refs_1_
  59.8 0.8 %collective-permute-done.14.refs_3_ = f32[48,2816]{1,0:T(8,128)S(1)} collective-permute-done((f32[48,2816]{1,0:T(8,128)S(1)}, f32[48,2816]{1,0:T(8,128)S(1)}, u32[]{:S(2)}, u32[]{:S(2)}) %collective-permute-start.14) | collective-permute-done | bytes 540704 | tf_op jit(solution)/shard_map/ppermute | solution.py:31
  60.5 5.8 %border.5 = (f32[7,256,256]{2,1,0:T(8,128)S(1)}, f32[8,256,256]{2,1,0:T(8,128)S(1)}, bf16[768,2048]{1,0:T(8,128)(2,1)S(1)}, bf16[768,2048]{1,0:T(8,128)(2,1)S(1)}) custom-call(f32[48,2816]{1,0:T(8,128)S(1)} %collective-permute-done.8.first_ref.refs_0_, f32[48,2816]{1,0:T(8,128)S(1)} %collective-permute-done.13.refs_1_, ...), custom_call_target="tpu_custom_call" | custom-call | tf_op jit(solution)/shard_map/border/pallas_call | solution.py:316
  66.3 1.5 %collective-permute-done.12.refs_0_ = f32[48,2816]{1,0:T(8,128)S(1)} collective-permute-done((f32[48,2816]{1,0:T(8,128)S(1)}, f32[48,2816]{1,0:T(8,128)S(1)}, u32[]{:S(2)}, u32[]{:S(2)}) %collective-permute-start.12) | collective-permute-done | bytes 540704 | tf_op jit(solution)/shard_map/ppermute | solution.py:354
  67.8 1.9 %collective-permute-done.15.refs_1_ = f32[48,2816]{1,0:T(8,128)S(1)} collective-permute-done((f32[48,2816]{1,0:T(8,128)S(1)}, f32[48,2816]{1,0:T(8,128)S(1)}, u32[]{:S(2)}, u32[]{:S(2)}) %collective-permute-start.15) | collective-permute-done | bytes 540704 | tf_op jit(solution)/shard_map/ppermute | solution.py:31
  69.8 4.9 %border_end.1 = (f32[7,256,256]{2,1,0:T(8,128)}, f32[8,256,256]{2,1,0:T(8,128)}, f32[48,8,256]{2,1,0:T(8,128)}) custom-call(f32[48,2816]{1,0:T(8,128)S(1)} %collective-permute-done.12.refs_0_, f32[48,2816]{1,0:T(8,128)S(1)} %collective-permute-done.15.refs_1_, f32[48,2816]{1,0:T(8,128)S(1)} %whole_message.1.refs_0_.refs_2_, ...), custom_call_target="tpu_custom_call" | custom-call | tf_op jit(solution)/shard_map/border_end/pallas_call | solution.py:316
  (20 shorter events, 0.6 us)
Async XLA Ops:
  0.6 0.9 %copy-start.3 = (f32[1,384,96]{1,2,0:T(8,128)S(1)}, f32[1,384,96]{1,2,0:T(8,128)}, u32[]{:S(2)}) copy-start(f32[1,384,96]{1,2,0:T(8,128)} %param.5) | copy-start | bytes 442372
  1.5 8.3 %copy-start.4 = (f32[1,384,96]{1,2,0:T(8,128)S(1)}, f32[1,384,96]{1,2,0:T(8,128)}, u32[]{:S(2)}) copy-start(f32[1,384,96]{1,2,0:T(8,128)} %param.5) | copy-start | bytes 442372
  1.6 8.3 %collective-permute-start = (f32[48,384]{1,0:T(8,128)S(1)}, f32[48,384]{1,0:T(8,128)S(1)}, u32[]{:S(2)}, u32[]{:S(2)}) collective-permute-start(f32[48,384]{1,0:T(8,128)S(1)} %partner_rows.1), channel_id=1, source_target_pairs={{0,8},{1,9},{2,10},{3,11},{4,12},{5,13},{6,14},{7,15},{8,0},{9,1},... | collective-permute-start | bytes 221192 | tf_op jit(solution)/shard_map/ppermute | solution.py:31
  9.9 1.0 %copy-start.2 = (f32[48,2048]{1,0:T(8,128)S(1)}, f32[48,2048]{1,0:T(8,128)}, u32[]{:S(2)}) copy-start(f32[48,2048]{1,0:T(8,128)} %link_chain.1.links_ref) | copy-start | bytes 1179652
  10.9 9.4 %collective-permute-start.3 = (f32[48,2816]{1,0:T(8,128)S(1)}, f32[48,2816]{1,0:T(8,128)S(1)}, u32[]{:S(2)}, u32[]{:S(2)}) collective-permute-start(f32[48,2816]{1,0:T(8,128)S(1)} %whole_message.1.refs_0_.refs_2_), channel_id=1, source_target_pairs={{0,1},{1,0},{2,3},{3,2},{4,5},{5,4},{6,7},{7,6},{8,9},{9,8},{10,11... | collective-permute-start | bytes 1622024 | tf_op jit(solution)/shard_map/ppermute | solution.py:31
  11.0 14.7 %collective-permute-start.2 = (f32[48,2816]{1,0:T(8,128)S(1)}, f32[48,2816]{1,0:T(8,128)S(1)}, u32[]{:S(2)}, u32[]{:S(2)}) collective-permute-start(f32[48,2816]{1,0:T(8,128)S(1)} %whole_message.1.refs_0_.refs_2_), channel_id=1, source_target_pairs={{0,2},{1,3},{4,0},{5,1},{8,4},{9,5},{12,8},{13,9},{14,12},{15,13},... | collective-permute-start | bytes 1622024 | tf_op jit(solution)/shard_map/ppermute | solution.py:336
  12.5 14.3 %collective-permute-start.1 = (f32[48,2816]{1,0:T(8,128)S(1)}, f32[48,2816]{1,0:T(8,128)S(1)}, u32[]{:S(2)}, u32[]{:S(2)}) collective-permute-start(f32[48,2816]{1,0:T(8,128)S(1)} %whole_message.1.refs_0_.refs_2_), channel_id=1, source_target_pairs={{0,4},{1,5},{4,8},{5,9},{8,12},{9,13},{12,14},{13,15},{14,10},{15,... | collective-permute-start | bytes 1622024 | tf_op jit(solution)/shard_map/ppermute | solution.py:336
  13.1 1.5 %copy-start = (f32[7,256,256]{2,1,0:T(8,128)S(1)}, f32[7,256,256]{2,1,0:T(8,128)}, u32[]{:S(2)}) copy-start(f32[7,256,256]{2,1,0:T(8,128)} %parent_ref) | copy-start | bytes 5505028
  14.6 1.6 %copy-start.1 = (f32[8,256,256]{2,1,0:T(8,128)S(1)}, f32[8,256,256]{2,1,0:T(8,128)}, u32[]{:S(2)}) copy-start(f32[8,256,256]{2,1,0:T(8,128)} %pivot_ref.1) | copy-start | bytes 6291460
  26.9 2.5 %collective-permute-start.6 = (f32[48,2816]{1,0:T(8,128)S(1)}, f32[48,2816]{1,0:T(8,128)S(1)}, u32[]{:S(2)}, u32[]{:S(2)}) collective-permute-start(f32[48,2816]{1,0:T(8,128)S(1)} %collective-permute-done.1.refs_0_), channel_id=1, source_target_pairs={{0,1},{1,0},{2,3},{3,2},{4,5},{5,4},{6,7},{7,6},{8,9},{9,8},{10,11... | collective-permute-start | bytes 1622024 | tf_op jit(solution)/shard_map/ppermute | solution.py:31
  26.9 2.7 %collective-permute-start.7 = (f32[48,2816]{1,0:T(8,128)S(1)}, f32[48,2816]{1,0:T(8,128)S(1)}, u32[]{:S(2)}, u32[]{:S(2)}) collective-permute-start(f32[48,2816]{1,0:T(8,128)S(1)} %collective-permute-done.2.refs_2_), channel_id=1, source_target_pairs={{0,1},{1,0},{2,3},{3,2},{4,5},{5,4},{6,7},{7,6},{8,9},{9,8},{10,11... | collective-permute-start | bytes 1622024 | tf_op jit(solution)/shard_map/ppermute | solution.py:31
  27.4 14.2 %collective-permute-start.4 = (f32[48,2816]{1,0:T(8,128)S(1)}, f32[48,2816]{1,0:T(8,128)S(1)}, u32[]{:S(2)}, u32[]{:S(2)}) collective-permute-start(f32[48,2816]{1,0:T(8,128)S(1)} %collective-permute-done.1.refs_0_), channel_id=1, source_target_pairs={{0,4},{1,5},{4,8},{5,9},{8,12},{9,13},{12,14},{13,15},{14,10},{15,... | collective-permute-start | bytes 1622024 | tf_op jit(solution)/shard_map/ppermute | solution.py:336
  27.9 13.9 %collective-permute-start.5 = (f32[48,2816]{1,0:T(8,128)S(1)}, f32[48,2816]{1,0:T(8,128)S(1)}, u32[]{:S(2)}, u32[]{:S(2)}) collective-permute-start(f32[48,2816]{1,0:T(8,128)S(1)} %collective-permute-done.2.refs_2_), channel_id=1, source_target_pairs={{0,2},{1,3},{4,0},{5,1},{8,4},{9,5},{12,8},{13,9},{14,12},{15,13},... | collective-permute-start | bytes 1622024 | tf_op jit(solution)/shard_map/ppermute | solution.py:336
  41.8 2.5 %collective-permute-start.10 = (f32[48,2816]{1,0:T(8,128)S(1)}, f32[48,2816]{1,0:T(8,128)S(1)}, u32[]{:S(2)}, u32[]{:S(2)}) collective-permute-start(f32[48,2816]{1,0:T(8,128)S(1)} %collective-permute-done.4.refs_0_), channel_id=1, source_target_pairs={{0,1},{1,0},{2,3},{3,2},{4,5},{5,4},{6,7},{7,6},{8,9},{9,8},{10,11... | collective-permute-start | bytes 1622024 | tf_op jit(solution)/shard_map/ppermute | solution.py:31
  41.8 2.7 %collective-permute-start.11 = (f32[48,2816]{1,0:T(8,128)S(1)}, f32[48,2816]{1,0:T(8,128)S(1)}, u32[]{:S(2)}, u32[]{:S(2)}) collective-permute-start(f32[48,2816]{1,0:T(8,128)S(1)} %collective-permute-done.5.refs_2_), channel_id=1, source_target_pairs={{0,1},{1,0},{2,3},{3,2},{4,5},{5,4},{6,7},{7,6},{8,9},{9,8},{10,11... | collective-permute-start | bytes 1622024 | tf_op jit(solution)/shard_map/ppermute | solution.py:31
  42.4 14.2 %collective-permute-start.8 = (f32[48,2816]{1,0:T(8,128)S(1)}, f32[48,2816]{1,0:T(8,128)S(1)}, u32[]{:S(2)}, u32[]{:S(2)}) collective-permute-start(f32[48,2816]{1,0:T(8,128)S(1)} %collective-permute-done.4.refs_0_), channel_id=1, source_target_pairs={{0,4},{1,5},{4,8},{5,9},{8,12},{9,13},{12,14},{13,15},{14,10},{15,... | collective-permute-start | bytes 1622024 | tf_op jit(solution)/shard_map/ppermute | solution.py:336
  43.9 13.9 %collective-permute-start.9 = (f32[48,2816]{1,0:T(8,128)S(1)}, f32[48,2816]{1,0:T(8,128)S(1)}, u32[]{:S(2)}, u32[]{:S(2)}) collective-permute-start(f32[48,2816]{1,0:T(8,128)S(1)} %collective-permute-done.5.refs_2_), channel_id=1, source_target_pairs={{0,2},{1,3},{4,0},{5,1},{8,4},{9,5},{12,8},{13,9},{14,12},{15,13},... | collective-permute-start | bytes 1622024 | tf_op jit(solution)/shard_map/ppermute | solution.py:336
  57.8 1.9 %collective-permute-start.13 = (f32[48,2816]{1,0:T(8,128)S(1)}, f32[48,2816]{1,0:T(8,128)S(1)}, u32[]{:S(2)}, u32[]{:S(2)}) collective-permute-start(f32[48,2816]{1,0:T(8,128)S(1)} %collective-permute-done.8.first_ref.refs_0_), channel_id=1, source_target_pairs={{0,1},{1,0},{2,3},{3,2},{4,5},{5,4},{6,7},{7,6},{8,9},{9,8},{10,11... | collective-permute-start | bytes 1622024 | tf_op jit(solution)/shard_map/ppermute | solution.py:31
  57.9 2.6 %collective-permute-start.14 = (f32[48,2816]{1,0:T(8,128)S(1)}, f32[48,2816]{1,0:T(8,128)S(1)}, u32[]{:S(2)}, u32[]{:S(2)}) collective-permute-start(f32[48,2816]{1,0:T(8,128)S(1)} %collective-permute-done.9.second_ref.refs_2_), channel_id=1, source_target_pairs={{0,1},{1,0},{2,3},{3,2},{4,5},{5,4},{6,7},{7,6},{8,9},{9,8},{10,11... | collective-permute-start | bytes 1622024 | tf_op jit(solution)/shard_map/ppermute | solution.py:31
  58.5 9.4 %collective-permute-start.12 = (f32[48,2816]{1,0:T(8,128)S(1)}, f32[48,2816]{1,0:T(8,128)S(1)}, u32[]{:S(2)}, u32[]{:S(2)}) collective-permute-start(f32[48,2816]{1,0:T(8,128)S(1)} %pick.1), channel_id=1, source_target_pairs={{0,4},{4,8},{8,12},{12,14},{14,10},{10,6},{6,2},{2,0},{1,3},{5,1},... | collective-permute-start | bytes 1622024 | tf_op jit(solution)/shard_map/ppermute | solution.py:354
  67.8 1.9 %collective-permute-start.15 = (f32[48,2816]{1,0:T(8,128)S(1)}, f32[48,2816]{1,0:T(8,128)S(1)}, u32[]{:S(2)}, u32[]{:S(2)}) collective-permute-start(f32[48,2816]{1,0:T(8,128)S(1)} %collective-permute-done.12.refs_0_), channel_id=1, source_target_pairs={{0,1},{1,0},{2,3},{3,2},{4,5},{5,4},{6,7},{7,6},{8,9},{9,8},{10,11... | collective-permute-start | bytes 1622024 | tf_op jit(solution)/shard_map/ppermute | solution.py:31

commit v7 on v6

--- a/solution.py
+++ b/solution.py
@@ -275,7 +275,8 @@
             left.append(own_ref[:, :order])
         left = halves(jnp.concatenate(left, axis=0))
         right = []
-        for node in range(nodes):
+
+        def multiply(node):
             columns = slice(node * width, (node + 1) * width)
             image = stacked_dot(left, [whole[:, columns] for whole in held_now])
             if last:
@@ -286,9 +287,8 @@
             for whole, part in zip(turned, halves(jnp.concatenate([new, image], axis=0).T)):
                 whole[columns, :] = part
             right.append([jnp.concatenate(pair, axis=0) for pair in zip(halves(image), halves(new))])
-        if last:
-            finish(2 * nodes, panel_out, panel_end)
-        for node in range(nodes):
+
+        def add(node):
             lower = max(node - 1, 0) * width
             total = stacked_dot([whole[lower : (node + 1) * width, :] for whole in turned], right[node])
             diagonals_out[node] = diagonals_ref[node] + total[-width:]
@@ -296,6 +296,14 @@
             if node > 0:
                 parents_out[node - 1] = parents_ref[node - 1] + total[:width]
                 finish(nodes + node, parents_out.at[node - 1], parents_end.at[node - 1])
+
+        for node in range(nodes):
+            multiply(node)
+            if node > 0:
+                add(node - 1)
+        if last:
+            finish(2 * nodes, panel_out, panel_end)
+        add(nodes - 1)
         for copy in copies:
             copy.wait()
 
@@ -347,7 +355,7 @@
     for step in range(1, far):
         pair = move(pair)
         totals, held = border(arrivals, held, *totals, chips)
-        pair, totals = lax.optimization_barrier((pair, totals))
+        pair = [after(value, *totals) for value in pair]
         arrivals = both(-step, pair[0]) + both(step, pair[1])
     last, totals = lax.optimization_barrier((pick(pair), totals))
     totals, held = border(arrivals, held, *totals, chips)

time: 75.2 us -> 76 us (1.011)
    ppermute x6, waiting for transfers between devices: 17 us -> 18.6 us  [move(): lax.ppermute(value, 'row', way)]
    ppermute x9, starting transfers between devices: 5.77 us -> 4.7 us  [swap_bit(): lax.ppermute(value, 'row', [(i, i ^ mask) for i in range(lax.axis_size('r...]
    ppermute x9, waiting for transfers between devices: 3.36 us -> 2.32 us  [swap_bit(): lax.ppermute(value, 'row', [(i, i ^ mask) for i in range(lax.axis_size('r...]
    ppermute x1, starting transfers between devices: 0.98 us -> 1.76 us  [gather_plan(): lax.ppermute(last, 'row', across)]
  transfers between devices with their start and end apart: 16 -> 16, of which waited for: 12 -> 9; matrix products, arithmetic and copies ran while one was open for 0% -> 0% of each run, Pallas kernels for 39% -> 39%
where the time goes in v7:
time: 76 us; the launch traced here: 75.7 us
  Pallas kernels  34.8 us (46%)
  waiting for transfers between devices  22.5 us (30%)
  starting transfers between devices  12.6 us (17%)
  local copies, waits for them, and re-layouts  4.99 us (7%)
  between operations  0.93 us (1%)
    pallas_call x5, Pallas kernels, border(): kernel_call(kernel, 'border' + ('_end' if last else '' if held else '_sta...  26.3 us
    ppermute x6, waiting for transfers between devices, move(): lax.ppermute(value, 'row', way)  18.6 us
    ppermute x6, starting transfers between devices, move(): lax.ppermute(value, 'row', way)  6.13 us
    unnamed x10, local copies, waits for them, and re-layouts  4.99 us
    ppermute x9, starting transfers between devices, swap_bit(): lax.ppermute(value, 'row', [(i, i ^ mask) for i in range(lax.axis_size('r...  4.7 us
    pallas_call x1, Pallas kernels, link_chain(): kernel_call(kernel, 'link_chain', limit=LINK_LIMIT, out_shape=jax.ShapeDt...  4.19 us
    pallas_call x1, Pallas kernels, inner_chain(): kernel_call(kernel, 'inner_chain', out_shape=[jax.ShapeDtypeStruct(array....  4.18 us
    ppermute x9, waiting for transfers between devices, swap_bit(): lax.ppermute(value, 'row', [(i, i ^ mask) for i in range(lax.axis_size('r...  2.32 us
  transfers between devices with their start and end apart: 16, of which 9 were waited for; matrix products, arithmetic and copies ran while one was open for 0% of the time, Pallas kernels for 39%

profile of v7, /device:TPU:0, one launch (start us, length us, event | category | flops | bytes accessed | tf_op | source)
XLA Modules:
  0.0 75.7 jit_solution(6013459953906936724)
XLA Ops:
  0.6 0.9 %copy-done.3 = f32[1,384,96]{1,2,0:T(8,128)S(1)} copy-done((f32[1,384,96]{1,2,0:T(8,128)S(1)}, f32[1,384,96]{1,2,0:T(8,128)}, u32[]{:S(2)}) %copy-start.3) | copy-done | bytes 147480
  1.6 4.1 %collective-permute-start = (f32[48,384]{1,0:T(8,128)S(1)}, f32[48,384]{1,0:T(8,128)S(1)}, u32[]{:S(2)}, u32[]{:S(2)}) collective-permute-start(f32[48,384]{1,0:T(8,128)S(1)} %partner_rows.1), channel_id=1, source_target_pairs={{0,8},{1,9},{2,10},{3,11},{4,12},{5,13},{6,14},{7,15},{8,0},{9,1},... | collective-permute-start | bytes 221192 | tf_op jit(solution)/shard_map/ppermute | solution.py:31
  5.7 4.2 %link_chain.1.links_ref = f32[48,2048]{1,0:T(8,128)} custom-call(f32[48,8,256]{2,1,0:T(8,128)} %links_home, f32[7,256,256]{2,1,0:T(8,128)} %parent_ref, s32[8,6]{1,0:T(8,128)} %pattern_ref.1), custom_call_target="tpu_custom_call" | custom-call | tf_op jit(solution)/shard_map/link_chain/pallas_call | solution.py:167
  9.9 0.0 copy-start.2
  9.9 1.0 %copy-done.2 = f32[48,2048]{1,0:T(8,128)S(1)} copy-done((f32[48,2048]{1,0:T(8,128)S(1)}, f32[48,2048]{1,0:T(8,128)}, u32[]{:S(2)}) %copy-start.2) | copy-done | bytes 393240
  10.9 0.1 collective-permute-start.2
  11.0 1.6 %collective-permute-start.1 = (f32[48,2816]{1,0:T(8,128)S(1)}, f32[48,2816]{1,0:T(8,128)S(1)}, u32[]{:S(2)}, u32[]{:S(2)}) collective-permute-start(f32[48,2816]{1,0:T(8,128)S(1)} %whole_message.1.refs_0_.refs_2_), channel_id=1, source_target_pairs={{0,4},{1,5},{4,8},{5,9},{8,12},{9,13},{12,14},{13,15},{14,10},{15,... | collective-permute-start | bytes 1622024 | tf_op jit(solution)/shard_map/ppermute | solution.py:344
  12.6 0.4 collective-permute-start.5
  13.1 1.5 %copy-done = f32[7,256,256]{2,1,0:T(8,128)S(1)} copy-done((f32[7,256,256]{2,1,0:T(8,128)S(1)}, f32[7,256,256]{2,1,0:T(8,128)}, u32[]{:S(2)}) %copy-start) | copy-done | bytes 1835032
  14.6 1.6 %copy-done.1 = f32[8,256,256]{2,1,0:T(8,128)S(1)} copy-done((f32[8,256,256]{2,1,0:T(8,128)S(1)}, f32[8,256,256]{2,1,0:T(8,128)}, u32[]{:S(2)}) %copy-start.1) | copy-done | bytes 2097176
  16.2 4.2 %inner_chain.1 = (f32[7,256,256]{2,1,0:T(8,128)S(1)}, f32[8,256,256]{2,1,0:T(8,128)S(1)}) custom-call(f32[7,256,256]{2,1,0:T(8,128)S(1)} %copy-done, f32[8,256,256]{2,1,0:T(8,128)S(1)} %copy-done.1), custom_call_target="tpu_custom_call" | custom-call | tf_op jit(solution)/shard_map/inner_chain/pallas_call | solution.py:213
  20.4 3.7 %border_start.1 = (f32[7,256,256]{2,1,0:T(8,128)S(1)}, f32[8,256,256]{2,1,0:T(8,128)S(1)}, bf16[768,2048]{1,0:T(8,128)(2,1)S(1)}, bf16[768,2048]{1,0:T(8,128)(2,1)S(1)}) custom-call(f32[48,2816]{1,0:T(8,128)S(1)} %whole_message.1.refs_0_.refs_2_, f32[48,2816]{1,0:T(8,128)S(1)} %collective-permute-done.2.refs_1_, ...), custom_call_target="tpu_custom_call" | custom-call | tf_op jit(solution)/shard_map/border_start/pallas_call | solution.py:324
  24.0 1.6 %collective-permute-done.1.refs_0_ = f32[48,2816]{1,0:T(8,128)S(1)} collective-permute-done((f32[48,2816]{1,0:T(8,128)S(1)}, f32[48,2816]{1,0:T(8,128)S(1)}, u32[]{:S(2)}, u32[]{:S(2)}) %collective-permute-start.1) | collective-permute-done | bytes 540704 | tf_op jit(solution)/shard_map/ppermute | solution.py:344
  25.7 1.3 %collective-permute-done.5.refs_2_ = f32[48,2816]{1,0:T(8,128)S(1)} collective-permute-done((f32[48,2816]{1,0:T(8,128)S(1)}, f32[48,2816]{1,0:T(8,128)S(1)}, u32[]{:S(2)}, u32[]{:S(2)}) %collective-permute-start.5) | collective-permute-done | bytes 540704 | tf_op jit(solution)/shard_map/ppermute | solution.py:344
  27.0 1.0 %collective-permute-start.3 = (f32[48,2816]{1,0:T(8,128)S(1)}, f32[48,2816]{1,0:T(8,128)S(1)}, u32[]{:S(2)}, u32[]{:S(2)}) collective-permute-start(f32[48,2816]{1,0:T(8,128)S(1)} %collective-permute-done.1.refs_0_), channel_id=1, source_target_pairs={{0,4},{1,5},{4,8},{5,9},{8,12},{9,13},{12,14},{13,15},{14,10},{15,... | collective-permute-start | bytes 1622024 | tf_op jit(solution)/shard_map/ppermute | solution.py:344
  28.0 1.0 %collective-permute-start.9 = (f32[48,2816]{1,0:T(8,128)S(1)}, f32[48,2816]{1,0:T(8,128)S(1)}, u32[]{:S(2)}, u32[]{:S(2)}) collective-permute-start(f32[48,2816]{1,0:T(8,128)S(1)} %collective-permute-done.5.refs_2_), channel_id=1, source_target_pairs={{0,2},{1,3},{4,0},{5,1},{8,4},{9,5},{12,8},{13,9},{14,12},{15,13},... | collective-permute-start | bytes 1622024 | tf_op jit(solution)/shard_map/ppermute | solution.py:344
  29.0 5.9 %border.3 = (f32[7,256,256]{2,1,0:T(8,128)S(1)}, f32[8,256,256]{2,1,0:T(8,128)S(1)}, bf16[768,2048]{1,0:T(8,128)(2,1)S(1)}, bf16[768,2048]{1,0:T(8,128)(2,1)S(1)}) custom-call(f32[48,2816]{1,0:T(8,128)S(1)} %collective-permute-done.1.refs_0_, f32[48,2816]{1,0:T(8,128)S(1)} %collective-permute-done.4.refs_1_, f32[48,2816]{1,0:T(8,128)S(1)} %collective-permute-done.5.refs_2_, ...), custom_call_target="tpu_custom_call" | custom-call | tf_op jit(solution)/shard_map/border/pallas_call | solution.py:324
  34.9 6.7 %collective-permute-done.3.refs_0_ = f32[48,2816]{1,0:T(8,128)S(1)} collective-permute-done((f32[48,2816]{1,0:T(8,128)S(1)}, f32[48,2816]{1,0:T(8,128)S(1)}, u32[]{:S(2)}, u32[]{:S(2)}) %collective-permute-start.3) | collective-permute-done | bytes 540704 | tf_op jit(solution)/shard_map/ppermute | solution.py:344
  41.7 0.7 collective-permute-done.9.refs_2_
  42.4 1.7 %collective-permute-start.7 = (f32[48,2816]{1,0:T(8,128)S(1)}, f32[48,2816]{1,0:T(8,128)S(1)}, u32[]{:S(2)}, u32[]{:S(2)}) collective-permute-start(f32[48,2816]{1,0:T(8,128)S(1)} %collective-permute-done.3.refs_0_), channel_id=1, source_target_pairs={{0,4},{1,5},{4,8},{5,9},{8,12},{9,13},{12,14},{13,15},{14,10},{15,... | collective-permute-start | bytes 1622024 | tf_op jit(solution)/shard_map/ppermute | solution.py:344
  44.1 0.3 collective-permute-start.11
  44.4 5.9 %border.4 = (f32[7,256,256]{2,1,0:T(8,128)S(1)}, f32[8,256,256]{2,1,0:T(8,128)S(1)}, bf16[768,2048]{1,0:T(8,128)(2,1)S(1)}, bf16[768,2048]{1,0:T(8,128)(2,1)S(1)}) custom-call(f32[48,2816]{1,0:T(8,128)S(1)} %collective-permute-done.3.refs_0_, f32[48,2816]{1,0:T(8,128)S(1)} %collective-permute-done.8.refs_1_, f32[48,2816]{1,0:T(8,128)S(1)} %collective-permute-done.9.refs_2_, ...), custom_call_target="tpu_custom_call" | custom-call | tf_op jit(solution)/shard_map/border/pallas_call | solution.py:324
  50.3 6.7 %collective-permute-done.7.first_ref.refs_0_ = f32[48,2816]{1,0:T(8,128)S(1)} collective-permute-done((f32[48,2816]{1,0:T(8,128)S(1)}, f32[48,2816]{1,0:T(8,128)S(1)}, u32[]{:S(2)}, u32[]{:S(2)}) %collective-permute-start.7) | collective-permute-done | bytes 540704 | tf_op jit(solution)/shard_map/ppermute | solution.py:344
  57.1 1.5 %collective-permute-done.11.second_ref.refs_2_ = f32[48,2816]{1,0:T(8,128)S(1)} collective-permute-done((f32[48,2816]{1,0:T(8,128)S(1)}, f32[48,2816]{1,0:T(8,128)S(1)}, u32[]{:S(2)}, u32[]{:S(2)}) %collective-permute-start.11) | collective-permute-done | bytes 540704 | tf_op jit(solution)/shard_map/ppermute | solution.py:344
  58.5 0.5 collective-permute-start.14
  59.0 0.1 pick.1
  59.1 1.8 %collective-permute-start.12 = (f32[48,2816]{1,0:T(8,128)S(1)}, f32[48,2816]{1,0:T(8,128)S(1)}, u32[]{:S(2)}, u32[]{:S(2)}) collective-permute-start(f32[48,2816]{1,0:T(8,128)S(1)} %pick.1), channel_id=1, source_target_pairs={{0,4},{4,8},{8,12},{12,14},{14,10},{10,6},{6,2},{2,0},{1,3},{5,1},... | collective-permute-start | bytes 1622024 | tf_op jit(solution)/shard_map/ppermute | solution.py:362
  60.9 0.4 collective-permute-done.14.refs_3_
  61.2 5.9 %border.5 = (f32[7,256,256]{2,1,0:T(8,128)S(1)}, f32[8,256,256]{2,1,0:T(8,128)S(1)}, bf16[768,2048]{1,0:T(8,128)(2,1)S(1)}, bf16[768,2048]{1,0:T(8,128)(2,1)S(1)}) custom-call(f32[48,2816]{1,0:T(8,128)S(1)} %collective-permute-done.7.first_ref.refs_0_, f32[48,2816]{1,0:T(8,128)S(1)} %collective-permute-done.13.refs_1_, ...), custom_call_target="tpu_custom_call" | custom-call | tf_op jit(solution)/shard_map/border/pallas_call | solution.py:324
  67.2 1.6 %collective-permute-done.12.refs_0_ = f32[48,2816]{1,0:T(8,128)S(1)} collective-permute-done((f32[48,2816]{1,0:T(8,128)S(1)}, f32[48,2816]{1,0:T(8,128)S(1)}, u32[]{:S(2)}, u32[]{:S(2)}) %collective-permute-start.12) | collective-permute-done | bytes 540704 | tf_op jit(solution)/shard_map/ppermute | solution.py:362
  68.7 1.9 %collective-permute-done.15.refs_1_ = f32[48,2816]{1,0:T(8,128)S(1)} collective-permute-done((f32[48,2816]{1,0:T(8,128)S(1)}, f32[48,2816]{1,0:T(8,128)S(1)}, u32[]{:S(2)}, u32[]{:S(2)}) %collective-permute-start.15) | collective-permute-done | bytes 540704 | tf_op jit(solution)/shard_map/ppermute | solution.py:31
  70.7 4.9 %border_end.1 = (f32[7,256,256]{2,1,0:T(8,128)}, f32[8,256,256]{2,1,0:T(8,128)}, f32[48,8,256]{2,1,0:T(8,128)}) custom-call(f32[48,2816]{1,0:T(8,128)S(1)} %collective-permute-done.12.refs_0_, f32[48,2816]{1,0:T(8,128)S(1)} %collective-permute-done.15.refs_1_, f32[48,2816]{1,0:T(8,128)S(1)} %whole_message.1.refs_0_.refs_2_, ...), custom_call_target="tpu_custom_call" | custom-call | tf_op jit(solution)/shard_map/border_end/pallas_call | solution.py:324
  (20 shorter events, 0.1 us)
Async XLA Ops:
  0.6 0.9 %copy-start.3 = (f32[1,384,96]{1,2,0:T(8,128)S(1)}, f32[1,384,96]{1,2,0:T(8,128)}, u32[]{:S(2)}) copy-start(f32[1,384,96]{1,2,0:T(8,128)} %param.5) | copy-start | bytes 442372
  1.5 8.3 %copy-start.4 = (f32[1,384,96]{1,2,0:T(8,128)S(1)}, f32[1,384,96]{1,2,0:T(8,128)}, u32[]{:S(2)}) copy-start(f32[1,384,96]{1,2,0:T(8,128)} %param.5) | copy-start | bytes 442372
  1.6 8.3 %collective-permute-start = (f32[48,384]{1,0:T(8,128)S(1)}, f32[48,384]{1,0:T(8,128)S(1)}, u32[]{:S(2)}, u32[]{:S(2)}) collective-permute-start(f32[48,384]{1,0:T(8,128)S(1)} %partner_rows.1), channel_id=1, source_target_pairs={{0,8},{1,9},{2,10},{3,11},{4,12},{5,13},{6,14},{7,15},{8,0},{9,1},... | collective-permute-start | bytes 221192 | tf_op jit(solution)/shard_map/ppermute | solution.py:31
  9.9 1.0 %copy-start.2 = (f32[48,2048]{1,0:T(8,128)S(1)}, f32[48,2048]{1,0:T(8,128)}, u32[]{:S(2)}) copy-start(f32[48,2048]{1,0:T(8,128)} %link_chain.1.links_ref) | copy-start | bytes 1179652
  10.9 9.4 %collective-permute-start.2 = (f32[48,2816]{1,0:T(8,128)S(1)}, f32[48,2816]{1,0:T(8,128)S(1)}, u32[]{:S(2)}, u32[]{:S(2)}) collective-permute-start(f32[48,2816]{1,0:T(8,128)S(1)} %whole_message.1.refs_0_.refs_2_), channel_id=1, source_target_pairs={{0,1},{1,0},{2,3},{3,2},{4,5},{5,4},{6,7},{7,6},{8,9},{9,8},{10,11... | collective-permute-start | bytes 1622024 | tf_op jit(solution)/shard_map/ppermute | solution.py:31
  11.0 14.7 %collective-permute-start.1 = (f32[48,2816]{1,0:T(8,128)S(1)}, f32[48,2816]{1,0:T(8,128)S(1)}, u32[]{:S(2)}, u32[]{:S(2)}) collective-permute-start(f32[48,2816]{1,0:T(8,128)S(1)} %whole_message.1.refs_0_.refs_2_), channel_id=1, source_target_pairs={{0,4},{1,5},{4,8},{5,9},{8,12},{9,13},{12,14},{13,15},{14,10},{15,... | collective-permute-start | bytes 1622024 | tf_op jit(solution)/shard_map/ppermute | solution.py:344
  12.6 14.3 %collective-permute-start.5 = (f32[48,2816]{1,0:T(8,128)S(1)}, f32[48,2816]{1,0:T(8,128)S(1)}, u32[]{:S(2)}, u32[]{:S(2)}) collective-permute-start(f32[48,2816]{1,0:T(8,128)S(1)} %whole_message.1.refs_0_.refs_2_), channel_id=1, source_target_pairs={{0,2},{1,3},{4,0},{5,1},{8,4},{9,5},{12,8},{13,9},{14,12},{15,13},... | collective-permute-start | bytes 1622024 | tf_op jit(solution)/shard_map/ppermute | solution.py:344
  13.1 1.5 %copy-start = (f32[7,256,256]{2,1,0:T(8,128)S(1)}, f32[7,256,256]{2,1,0:T(8,128)}, u32[]{:S(2)}) copy-start(f32[7,256,256]{2,1,0:T(8,128)} %parent_ref) | copy-start | bytes 5505028
  14.6 1.6 %copy-start.1 = (f32[8,256,256]{2,1,0:T(8,128)S(1)}, f32[8,256,256]{2,1,0:T(8,128)}, u32[]{:S(2)}) copy-start(f32[8,256,256]{2,1,0:T(8,128)} %pivot_ref.1) | copy-start | bytes 6291460
  25.7 3.3 %collective-permute-start.4 = (f32[48,2816]{1,0:T(8,128)S(1)}, f32[48,2816]{1,0:T(8,128)S(1)}, u32[]{:S(2)}, u32[]{:S(2)}) collective-permute-start(f32[48,2816]{1,0:T(8,128)S(1)} %collective-permute-done.1.refs_0_), channel_id=1, source_target_pairs={{0,1},{1,0},{2,3},{3,2},{4,5},{5,4},{6,7},{7,6},{8,9},{9,8},{10,11... | collective-permute-start | bytes 1622024 | tf_op jit(solution)/shard_map/ppermute | solution.py:31
  27.0 2.0 %collective-permute-start.6 = (f32[48,2816]{1,0:T(8,128)S(1)}, f32[48,2816]{1,0:T(8,128)S(1)}, u32[]{:S(2)}, u32[]{:S(2)}) collective-permute-start(f32[48,2816]{1,0:T(8,128)S(1)} %collective-permute-done.5.refs_2_), channel_id=1, source_target_pairs={{0,1},{1,0},{2,3},{3,2},{4,5},{5,4},{6,7},{7,6},{8,9},{9,8},{10,11... | collective-permute-start | bytes 1622024 | tf_op jit(solution)/shard_map/ppermute | solution.py:31
  27.0 14.7 %collective-permute-start.3 = (f32[48,2816]{1,0:T(8,128)S(1)}, f32[48,2816]{1,0:T(8,128)S(1)}, u32[]{:S(2)}, u32[]{:S(2)}) collective-permute-start(f32[48,2816]{1,0:T(8,128)S(1)} %collective-permute-done.1.refs_0_), channel_id=1, source_target_pairs={{0,4},{1,5},{4,8},{5,9},{8,12},{9,13},{12,14},{13,15},{14,10},{15,... | collective-permute-start | bytes 1622024 | tf_op jit(solution)/shard_map/ppermute | solution.py:344
  28.0 14.4 %collective-permute-start.9 = (f32[48,2816]{1,0:T(8,128)S(1)}, f32[48,2816]{1,0:T(8,128)S(1)}, u32[]{:S(2)}, u32[]{:S(2)}) collective-permute-start(f32[48,2816]{1,0:T(8,128)S(1)} %collective-permute-done.5.refs_2_), channel_id=1, source_target_pairs={{0,2},{1,3},{4,0},{5,1},{8,4},{9,5},{12,8},{13,9},{14,12},{15,13},... | collective-permute-start | bytes 1622024 | tf_op jit(solution)/shard_map/ppermute | solution.py:344
  41.7 2.7 %collective-permute-start.8 = (f32[48,2816]{1,0:T(8,128)S(1)}, f32[48,2816]{1,0:T(8,128)S(1)}, u32[]{:S(2)}, u32[]{:S(2)}) collective-permute-start(f32[48,2816]{1,0:T(8,128)S(1)} %collective-permute-done.3.refs_0_), channel_id=1, source_target_pairs={{0,1},{1,0},{2,3},{3,2},{4,5},{5,4},{6,7},{7,6},{8,9},{9,8},{10,11... | collective-permute-start | bytes 1622024 | tf_op jit(solution)/shard_map/ppermute | solution.py:31
  42.4 2.0 %collective-permute-start.10 = (f32[48,2816]{1,0:T(8,128)S(1)}, f32[48,2816]{1,0:T(8,128)S(1)}, u32[]{:S(2)}, u32[]{:S(2)}) collective-permute-start(f32[48,2816]{1,0:T(8,128)S(1)} %collective-permute-done.9.refs_2_), channel_id=1, source_target_pairs={{0,1},{1,0},{2,3},{3,2},{4,5},{5,4},{6,7},{7,6},{8,9},{9,8},{10,11... | collective-permute-start | bytes 1622024 | tf_op jit(solution)/shard_map/ppermute | solution.py:31
  42.4 14.7 %collective-permute-start.7 = (f32[48,2816]{1,0:T(8,128)S(1)}, f32[48,2816]{1,0:T(8,128)S(1)}, u32[]{:S(2)}, u32[]{:S(2)}) collective-permute-start(f32[48,2816]{1,0:T(8,128)S(1)} %collective-permute-done.3.refs_0_), channel_id=1, source_target_pairs={{0,4},{1,5},{4,8},{5,9},{8,12},{9,13},{12,14},{13,15},{14,10},{15,... | collective-permute-start | bytes 1622024 | tf_op jit(solution)/shard_map/ppermute | solution.py:344
  44.1 14.4 %collective-permute-start.11 = (f32[48,2816]{1,0:T(8,128)S(1)}, f32[48,2816]{1,0:T(8,128)S(1)}, u32[]{:S(2)}, u32[]{:S(2)}) collective-permute-start(f32[48,2816]{1,0:T(8,128)S(1)} %collective-permute-done.9.refs_2_), channel_id=1, source_target_pairs={{0,2},{1,3},{4,0},{5,1},{8,4},{9,5},{12,8},{13,9},{14,12},{15,13},... | collective-permute-start | bytes 1622024 | tf_op jit(solution)/shard_map/ppermute | solution.py:344
  58.5 2.3 %collective-permute-start.13 = (f32[48,2816]{1,0:T(8,128)S(1)}, f32[48,2816]{1,0:T(8,128)S(1)}, u32[]{:S(2)}, u32[]{:S(2)}) collective-permute-start(f32[48,2816]{1,0:T(8,128)S(1)} %collective-permute-done.7.first_ref.refs_0_), channel_id=1, source_target_pairs={{0,1},{1,0},{2,3},{3,2},{4,5},{5,4},{6,7},{7,6},{8,9},{9,8},{10,11... | collective-permute-start | bytes 1622024 | tf_op jit(solution)/shard_map/ppermute | solution.py:31
  58.5 2.7 %collective-permute-start.14 = (f32[48,2816]{1,0:T(8,128)S(1)}, f32[48,2816]{1,0:T(8,128)S(1)}, u32[]{:S(2)}, u32[]{:S(2)}) collective-permute-start(f32[48,2816]{1,0:T(8,128)S(1)} %collective-permute-done.11.second_ref.refs_2_), channel_id=1, source_target_pairs={{0,1},{1,0},{2,3},{3,2},{4,5},{5,4},{6,7},{7,6},{8,9},{9,8},{10,11... | collective-permute-start | bytes 1622024 | tf_op jit(solution)/shard_map/ppermute | solution.py:31
  59.1 9.6 %collective-permute-start.12 = (f32[48,2816]{1,0:T(8,128)S(1)}, f32[48,2816]{1,0:T(8,128)S(1)}, u32[]{:S(2)}, u32[]{:S(2)}) collective-permute-start(f32[48,2816]{1,0:T(8,128)S(1)} %pick.1), channel_id=1, source_target_pairs={{0,4},{4,8},{8,12},{12,14},{14,10},{10,6},{6,2},{2,0},{1,3},{5,1},... | collective-permute-start | bytes 1622024 | tf_op jit(solution)/shard_map/ppermute | solution.py:362
  68.7 1.9 %collective-permute-start.15 = (f32[48,2816]{1,0:T(8,128)S(1)}, f32[48,2816]{1,0:T(8,128)S(1)}, u32[]{:S(2)}, u32[]{:S(2)}) collective-permute-start(f32[48,2816]{1,0:T(8,128)S(1)} %collective-permute-done.12.refs_0_), channel_id=1, source_target_pairs={{0,1},{1,0},{2,3},{3,2},{4,5},{5,4},{6,7},{7,6},{8,9},{9,8},{10,11... | collective-permute-start | bytes 1622024 | tf_op jit(solution)/shard_map/ppermute | solution.py:31

commit v8 on v6

--- a/solution.py
+++ b/solution.py
@@ -7,7 +7,6 @@
 
 PCOL = 8
 TILE = 128
-BORDER_FLOPS = 0
 GATHER_LIMIT = 16 * 2**20
 LINK_LIMIT = 65_600_000
 
@@ -179,21 +178,33 @@
     )(anc_links, parent_links, pattern)
 
 
+def window_of(count, rows):
+    columns = (count // 2 + 1) * rows
+    return columns, -(-columns // 128) * 128
+
+
 def whole_message(turned, theirs, links):
-    rows, columns = theirs.shape
-
-    def kernel(turned_ref, theirs_ref, links_ref, out_ref):
-        low = lax.axis_index("row") < PCOL
-        out_ref[:, :columns] = jnp.where(low, turned_ref[:rows], theirs_ref[...])
-        out_ref[:, columns : 2 * columns] = jnp.where(low, theirs_ref[...], turned_ref[rows:])
-        out_ref[:, 2 * columns :] = links_ref[...]
-
+    rows, half = theirs.shape
+    columns, lanes = window_of(2 * half // rows, rows)
+
+    def kernel(turned_ref, theirs_ref, links_ref, own_ref, out_ref):
+        me = lax.axis_index("row")
+        low = me < PCOL
+        own_ref[:, :half] = jnp.where(low, turned_ref[:rows], theirs_ref[...])
+        own_ref[:, half:] = jnp.where(low, theirs_ref[...], turned_ref[rows:])
+        lane = lax.broadcasted_iota(jnp.int32, (1, lanes), 1)
+        weight = jnp.where((lane < rows) | (lane >= columns - rows), 0.5, 1.0)
+        weight = jnp.where(lane < columns, weight, 0.0)
+        out_ref[:, :lanes] = pltpu.roll(own_ref[...], lax.rem(2 * half - me * rows, 2 * half), 1)[:, :lanes] * weight
+        out_ref[:, lanes:] = links_ref[...]
+
+    shapes = [(rows, 2 * half), (rows, lanes + links.shape[1])]
     return kernel_call(
         kernel,
         "whole_message",
-        out_shape=jax.ShapeDtypeStruct((rows, 2 * columns + links.shape[1]), jnp.float32),
+        out_shape=[jax.ShapeDtypeStruct(shape, jnp.float32) for shape in shapes],
         in_specs=in_vmem(3),
-        out_specs=in_vmem(1)[0],
+        out_specs=in_vmem(2),
     )(turned, theirs, links)
 
 
@@ -228,10 +239,12 @@
     return 2 * chip + (1 - core if other else core)
 
 
-def border(arrivals, held, parents, diagonals, chips, last=False):
+def border(arrivals, state, parents, diagonals, chips, own=None):
+    last, begin = own is not None, state is None
     nodes, width, _ = diagonals.shape
-    rows = arrivals[0][2].shape[0]
-    order = arrivals[0][2].shape[1] - nodes * width
+    rows, total_lanes = arrivals[0][2].shape
+    lanes = total_lanes - nodes * width
+    order = 2 * chips * rows
     count = len(arrivals)
     fresh = rows * count
     bf16 = jnp.bfloat16
@@ -239,9 +252,9 @@
     def kernel(*refs):
         refs = list(refs)
         take = lambda number: [refs.pop(0) for _ in range(number)]
-        part_refs = take(count)
-        own_ref = take(1)[0] if last else None
-        held_before = take(2) if held else None
+        part_refs, own_ref = take(count), take(last)
+        kept_before = take(0 if begin else 1)
+        held_before = take(0 if begin else 2)
         parents_ref, diagonals_ref, parents_out, diagonals_out = take(4)
         copies = []
 
@@ -251,29 +264,39 @@
                 copies[-1].start()
 
         parents_end, diagonals_end = parents_out, diagonals_out
-        if last:
-            (panel_end,) = take(1)
+        panel_end = take(last)
+        kept_now = take(not last)
         held_now = take(2)
         turned = take(2)
         if last:
             parents_out, diagonals_out, panel_out, sems = take(4)
         me = lax.axis_index("row")
         owners = [ring_owner(me, chips, shift, other) for shift, other, _ in arrivals]
+        starts = [pl.multiple_of(owner * rows, 16) for owner in owners]
 
         for part, whole in enumerate(held_now):
-            whole[...] = held_before[part][...] if held else jnp.zeros(whole.shape, bf16)
-        for owner, ref in zip(owners, part_refs):
-            start = pl.multiple_of(owner * rows, 16)
-            for whole, part in zip(held_now, halves(ref[:, order:])):
+            whole[...] = jnp.zeros(whole.shape, bf16) if begin else held_before[part][...]
+        for start, ref in zip(starts, part_refs):
+            for whole, part in zip(held_now, halves(ref[:, lanes:])):
                 whole[pl.ds(start, rows), :] = part
-        piece = lax.broadcasted_iota(jnp.int32, (1, order), 1) // rows
-        weight = jnp.ones((1, order), jnp.float32)
-        for owner in owners:
-            weight = jnp.where(piece == owner, 0.5, weight)
-        left = [ref[:, :order] * weight for ref in part_refs]
-        if last:
-            left.append(own_ref[:, :order])
-        left = halves(jnp.concatenate(left, axis=0))
+        rest = jnp.zeros((rows, order - lanes), jnp.float32)
+        sent = [pltpu.roll(jnp.concatenate([ref[:, :lanes], rest], axis=1), start, 1) for start, ref in zip(starts, part_refs)]
+        left = list(sent)
+        if not begin:
+            core = lax.rem(me, 2)
+            for pair in range(0, count, 2):
+                start = lax.div(owners[pair], 2) * (2 * rows)
+                base = pl.multiple_of(lax.div(start, 128) * 128, 128)
+                window = pltpu.roll(kept_before[0][:, pl.ds(base, 256)], lax.rem(256 + base - start, 256), 1)
+                back = window[:, :128].T
+                first, second = back[:rows], back[rows : 2 * rows]
+                left[pair] += jnp.where(core == 0, first, second)
+                left[pair + 1] += jnp.where(core == 0, second, first)
+        if not last:
+            kept_now[0][...] = jnp.zeros(kept_now[0].shape, jnp.float32) if begin else kept_before[0][...]
+            for start, part in zip(starts, sent):
+                kept_now[0][pl.ds(start, rows), :order] = part
+        left = halves(jnp.concatenate(left + [ref[...] for ref in own_ref], axis=0))
         right = []
         for node in range(nodes):
             columns = slice(node * width, (node + 1) * width)
@@ -281,13 +304,13 @@
             if last:
                 panel_out[:, node, :] = -image[fresh:]
             image = image[:fresh]
-            there = slice(order + node * width, order + (node + 1) * width)
+            there = slice(lanes + node * width, lanes + (node + 1) * width)
             new = jnp.concatenate([ref[:, there] for ref in part_refs], axis=0)
             for whole, part in zip(turned, halves(jnp.concatenate([new, image], axis=0).T)):
                 whole[columns, :] = part
             right.append([jnp.concatenate(pair, axis=0) for pair in zip(halves(image), halves(new))])
         if last:
-            finish(2 * nodes, panel_out, panel_end)
+            finish(2 * nodes, panel_out, panel_end[0])
         for node in range(nodes):
             lower = max(node - 1, 0) * width
             total = stacked_dot([whole[lower : (node + 1) * width, :] for whole in turned], right[node])
@@ -299,29 +322,26 @@
         for copy in copies:
             copy.wait()
 
-    operands = [part for _, _, part in arrivals]
-    operands += [last] if last is not False else []
-    operands += [*(held or []), parents, diagonals]
-    last = last is not False
-    state = [(order, nodes * width)] * 2
+    operands = [part for _, _, part in arrivals] + ([own] if last else []) + list(state or [])
+    operands += [parents, diagonals]
     shapes = [jax.ShapeDtypeStruct(array.shape, jnp.float32) for array in (parents, diagonals)]
+    held = [jax.ShapeDtypeStruct((order, nodes * width), bf16)] * 2
     scratch = [pltpu.VMEM((nodes * width, 2 * fresh), bf16)] * 2
     if last:
         shapes.append(jax.ShapeDtypeStruct((rows, nodes, width), jnp.float32))
-        scratch = [pltpu.VMEM(shape, bf16) for shape in state] + scratch
+        scratch = [pltpu.VMEM(shape.shape, bf16) for shape in held] + scratch
         scratch += [pltpu.VMEM(array.shape, jnp.float32) for array in shapes]
         scratch.append(pltpu.SemaphoreType.DMA((2 * nodes + 1,)))
     else:
-        shapes += [jax.ShapeDtypeStruct(shape, bf16) for shape in state]
+        shapes += [jax.ShapeDtypeStruct((order, order + 128), jnp.float32)] + held
     results = kernel_call(
         kernel,
-        "border" + ("_end" if last else "" if held else "_start"),
+        "border" + ("_end" if last else "_begin" if begin else ""),
         out_shape=shapes,
         in_specs=in_vmem(len(operands)),
         out_specs=at_home(len(shapes)) if last else in_vmem(len(shapes)),
         scratch_shapes=scratch,
         limit=24 * 2**20 if last else 16 * 2**20,
-        flops=BORDER_FLOPS,
     )(*operands)
     return results[:2], results[2:]
 
@@ -341,18 +361,18 @@
     turned = anc_blocks[0].T
     theirs = partner_rows(turned)
     links = link_chain(after(anc_links, theirs), parent_links, pattern)
-    own = whole_message(turned, swap_bit(theirs, PCOL.bit_length() - 1), links)
-    totals, held = inner_chain(after(parent_links, own), pivot_inverse), None
+    rows, own = whole_message(turned, swap_bit(theirs, PCOL.bit_length() - 1), links)
+    totals, state = inner_chain(after(parent_links, own), pivot_inverse), None
     arrivals, pair = both(0, own), [own] * 2
     for step in range(1, far):
         pair = move(pair)
-        totals, held = border(arrivals, held, *totals, chips)
-        pair, totals = lax.optimization_barrier((pair, totals))
+        totals, state = border(arrivals, state, *totals, chips)
+        pair = [after(value, *totals) for value in pair]
         arrivals = both(-step, pair[0]) + both(step, pair[1])
     last, totals = lax.optimization_barrier((pick(pair), totals))
-    totals, held = border(arrivals, held, *totals, chips)
+    totals, state = border(arrivals, state, *totals, chips)
     last, totals = lax.optimization_barrier((lax.ppermute(last, "row", across), totals))
-    totals, panels = border(both(far, last), held, *totals, chips, last=own)
+    totals, panels = border(both(far, last), state, *totals, chips, rows)
     return panels[0], *totals
 
 

time: 75.2 us -> 72.7 us (0.967)
  waiting for transfers between devices: 21.9 us -> 16.4 us
  Pallas kernels: 34.2 us -> 37.6 us
    pallas_call x6, Pallas kernels: 25.8 us -> 29.1 us  [the longest x5 29 us: border(): kernel_call(kernel, 'border' + ('_end' if last else '_begin' if begin els...]
    ppermute x6, waiting for transfers between devices: 17 us -> 13.9 us  [move(): lax.ppermute(value, 'row', way)]
    ppermute x9, waiting for transfers between devices: 3.36 us -> 2.11 us  [swap_bit(): lax.ppermute(value, 'row', [(i, i ^ mask) for i in range(lax.axis_size('r...]
    ppermute x9, starting transfers between devices: 5.77 us -> 4.7 us  [swap_bit(): lax.ppermute(value, 'row', [(i, i ^ mask) for i in range(lax.axis_size('r...]
    ppermute x1, waiting for transfers between devices: 1.49 us -> 0.42 us  [gather_plan(): lax.ppermute(last, 'row', across)]
    ppermute x1, starting transfers between devices: 0.98 us -> 1.76 us  [gather_plan(): lax.ppermute(last, 'row', across)]
  transfers between devices with their start and end apart: 16 -> 16, of which waited for: 12 -> 9; matrix products, arithmetic and copies ran while one was open for 0% -> 0% of each run, Pallas kernels for 39% -> 44%
where the time goes in v8:
time: 72.7 us; the launch traced here: 72.5 us
  Pallas kernels  37.6 us (52%)
  waiting for transfers between devices  16.4 us (23%)
  starting transfers between devices  12.6 us (17%)
  local copies, waits for them, and re-layouts  4.99 us (7%)
  between operations  0.94 us (1%)
    pallas_call x5, Pallas kernels, border(): kernel_call(kernel, 'border' + ('_end' if last else '_begin' if begin els...  29 us
    ppermute x6, waiting for transfers between devices, move(): lax.ppermute(value, 'row', way)  13.9 us
    ppermute x6, starting transfers between devices, move(): lax.ppermute(value, 'row', way)  6.13 us
    unnamed x10, local copies, waits for them, and re-layouts  4.99 us
    ppermute x9, starting transfers between devices, swap_bit(): lax.ppermute(value, 'row', [(i, i ^ mask) for i in range(lax.axis_size('r...  4.7 us
    pallas_call x1, Pallas kernels, link_chain(): kernel_call(kernel, 'link_chain', limit=LINK_LIMIT, out_shape=jax.ShapeDt...  4.19 us
    pallas_call x1, Pallas kernels, inner_chain(): kernel_call(kernel, 'inner_chain', out_shape=[jax.ShapeDtypeStruct(array....  4.18 us
    ppermute x9, waiting for transfers between devices, swap_bit(): lax.ppermute(value, 'row', [(i, i ^ mask) for i in range(lax.axis_size('r...  2.11 us
  transfers between devices with their start and end apart: 16, of which 9 were waited for; matrix products, arithmetic and copies ran while one was open for 0% of the time, Pallas kernels for 44%

profile of v8, /device:TPU:0, one launch (start us, length us, event | category | flops | bytes accessed | tf_op | source)
XLA Modules:
  0.0 72.5 jit_solution(16170810795783389572)
XLA Ops:
  0.6 0.9 %copy-done.3 = f32[1,384,96]{1,2,0:T(8,128)S(1)} copy-done((f32[1,384,96]{1,2,0:T(8,128)S(1)}, f32[1,384,96]{1,2,0:T(8,128)}, u32[]{:S(2)}) %copy-start.3) | copy-done | bytes 147480
  1.6 4.1 %collective-permute-start = (f32[48,384]{1,0:T(8,128)S(1)}, f32[48,384]{1,0:T(8,128)S(1)}, u32[]{:S(2)}, u32[]{:S(2)}) collective-permute-start(f32[48,384]{1,0:T(8,128)S(1)} %partner_rows.1), channel_id=1, source_target_pairs={{0,8},{1,9},{2,10},{3,11},{4,12},{5,13},{6,14},{7,15},{8,0},{9,1},... | collective-permute-start | bytes 221192 | tf_op jit(solution)/shard_map/ppermute | solution.py:30
  5.7 4.2 %link_chain.1.links_ref = f32[48,2048]{1,0:T(8,128)} custom-call(f32[48,8,256]{2,1,0:T(8,128)} %links_home, f32[7,256,256]{2,1,0:T(8,128)} %parent_ref, s32[8,6]{1,0:T(8,128)} %pattern_ref.1), custom_call_target="tpu_custom_call" | custom-call | tf_op jit(solution)/shard_map/link_chain/pallas_call | solution.py:166
  9.9 1.0 %copy-done.2 = f32[48,2048]{1,0:T(8,128)S(1)} copy-done((f32[48,2048]{1,0:T(8,128)S(1)}, f32[48,2048]{1,0:T(8,128)}, u32[]{:S(2)}) %copy-start.2) | copy-done | bytes 393240
  10.9 0.1 whole_message.1
  11.0 0.1 collective-permute-start.2
  11.1 1.6 %collective-permute-start.1 = (f32[48,2560]{1,0:T(8,128)S(1)}, f32[48,2560]{1,0:T(8,128)S(1)}, u32[]{:S(2)}, u32[]{:S(2)}) collective-permute-start(f32[48,2560]{1,0:T(8,128)S(1)} %get-tuple-element.45.refs_0_), channel_id=1, source_target_pairs={{0,4},{1,5},{4,8},{5,9},{8,12},{9,13},{12,14},{13,15},{14,10},{15,... | collective-permute-start | bytes 1474568 | tf_op jit(solution)/shard_map/ppermute | solution.py:356
  12.7 0.4 collective-permute-start.5
  13.2 1.5 %copy-done = f32[7,256,256]{2,1,0:T(8,128)S(1)} copy-done((f32[7,256,256]{2,1,0:T(8,128)S(1)}, f32[7,256,256]{2,1,0:T(8,128)}, u32[]{:S(2)}) %copy-start) | copy-done | bytes 1835032
  14.7 1.6 %copy-done.1 = f32[8,256,256]{2,1,0:T(8,128)S(1)} copy-done((f32[8,256,256]{2,1,0:T(8,128)S(1)}, f32[8,256,256]{2,1,0:T(8,128)}, u32[]{:S(2)}) %copy-start.1) | copy-done | bytes 2097176
  16.3 4.2 %inner_chain.1 = (f32[7,256,256]{2,1,0:T(8,128)S(1)}, f32[8,256,256]{2,1,0:T(8,128)S(1)}) custom-call(f32[7,256,256]{2,1,0:T(8,128)S(1)} %copy-done, f32[8,256,256]{2,1,0:T(8,128)S(1)} %copy-done.1), custom_call_target="tpu_custom_call" | custom-call | tf_op jit(solution)/shard_map/inner_chain/pallas_call | solution.py:224
  20.5 3.7 %border_begin.1 = (f32[7,256,256]{2,1,0:T(8,128)S(1)}, f32[8,256,256]{2,1,0:T(8,128)S(1)}, f32[768,896]{1,0:T(8,128)S(1)}, bf16[768,2048]{1,0:T(8,128)(2,1)S(1)}, bf16[768,2048]{1,0:T(8,128)(2,1)S(1)}) custom-call(f32[48,2560]{1,0:T(8,128)S(1)} %get-tuple-element.45.refs_0_, f32[48,2560]{1,0:T(8,128)S(1)} %collective-permute-done.2.refs_1_, ...), custom_call_target="tpu_custom_call" | custom-call | tf_op jit(solution)/shard_map/border_begin/pallas_call | solution.py:337
  24.1 0.6 collective-permute-done.1.refs_0_
  24.7 1.3 %collective-permute-done.5.refs_2_ = f32[48,2560]{1,0:T(8,128)S(1)} collective-permute-done((f32[48,2560]{1,0:T(8,128)S(1)}, f32[48,2560]{1,0:T(8,128)S(1)}, u32[]{:S(2)}, u32[]{:S(2)}) %collective-permute-start.5) | collective-permute-done | bytes 491552 | tf_op jit(solution)/shard_map/ppermute | solution.py:356
  26.0 1.0 %collective-permute-start.3 = (f32[48,2560]{1,0:T(8,128)S(1)}, f32[48,2560]{1,0:T(8,128)S(1)}, u32[]{:S(2)}, u32[]{:S(2)}) collective-permute-start(f32[48,2560]{1,0:T(8,128)S(1)} %collective-permute-done.1.refs_0_), channel_id=1, source_target_pairs={{0,4},{1,5},{4,8},{5,9},{8,12},{9,13},{12,14},{13,15},{14,10},{15,... | collective-permute-start | bytes 1474568 | tf_op jit(solution)/shard_map/ppermute | solution.py:356
  27.0 1.0 %collective-permute-start.9 = (f32[48,2560]{1,0:T(8,128)S(1)}, f32[48,2560]{1,0:T(8,128)S(1)}, u32[]{:S(2)}, u32[]{:S(2)}) collective-permute-start(f32[48,2560]{1,0:T(8,128)S(1)} %collective-permute-done.5.refs_2_), channel_id=1, source_target_pairs={{0,2},{1,3},{4,0},{5,1},{8,4},{9,5},{12,8},{13,9},{14,12},{15,13},... | collective-permute-start | bytes 1474568 | tf_op jit(solution)/shard_map/ppermute | solution.py:356
  28.1 6.7 %border.3 = (f32[7,256,256]{2,1,0:T(8,128)S(1)}, f32[8,256,256]{2,1,0:T(8,128)S(1)}, f32[768,896]{1,0:T(8,128)S(1)}, bf16[768,2048]{1,0:T(8,128)(2,1)S(1)}, bf16[768,2048]{1,0:T(8,128)(2,1)S(1)}) custom-call(f32[48,2560]{1,0:T(8,128)S(1)} %collective-permute-done.1.refs_0_, f32[48,2560]{1,0:T(8,128)S(1)} %collective-permute-done.4.refs_1_, ...), custom_call_target="tpu_custom_call" | custom-call | tf_op jit(solution)/shard_map/border/pallas_call | solution.py:337
  34.8 4.9 %collective-permute-done.3.refs_0_ = f32[48,2560]{1,0:T(8,128)S(1)} collective-permute-done((f32[48,2560]{1,0:T(8,128)S(1)}, f32[48,2560]{1,0:T(8,128)S(1)}, u32[]{:S(2)}, u32[]{:S(2)}) %collective-permute-start.3) | collective-permute-done | bytes 491552 | tf_op jit(solution)/shard_map/ppermute | solution.py:356
  39.7 0.7 collective-permute-done.9.refs_2_
  40.4 1.7 %collective-permute-start.7 = (f32[48,2560]{1,0:T(8,128)S(1)}, f32[48,2560]{1,0:T(8,128)S(1)}, u32[]{:S(2)}, u32[]{:S(2)}) collective-permute-start(f32[48,2560]{1,0:T(8,128)S(1)} %collective-permute-done.3.refs_0_), channel_id=1, source_target_pairs={{0,4},{1,5},{4,8},{5,9},{8,12},{9,13},{12,14},{13,15},{14,10},{15,... | collective-permute-start | bytes 1474568 | tf_op jit(solution)/shard_map/ppermute | solution.py:356
  42.1 0.3 collective-permute-start.11
  42.4 6.7 %border.4 = (f32[7,256,256]{2,1,0:T(8,128)S(1)}, f32[8,256,256]{2,1,0:T(8,128)S(1)}, f32[768,896]{1,0:T(8,128)S(1)}, bf16[768,2048]{1,0:T(8,128)(2,1)S(1)}, bf16[768,2048]{1,0:T(8,128)(2,1)S(1)}) custom-call(f32[48,2560]{1,0:T(8,128)S(1)} %collective-permute-done.3.refs_0_, f32[48,2560]{1,0:T(8,128)S(1)} %collective-permute-done.8.refs_1_, ...), custom_call_target="tpu_custom_call" | custom-call | tf_op jit(solution)/shard_map/border/pallas_call | solution.py:337
  49.1 4.9 %collective-permute-done.7.first_ref.refs_0_ = f32[48,2560]{1,0:T(8,128)S(1)} collective-permute-done((f32[48,2560]{1,0:T(8,128)S(1)}, f32[48,2560]{1,0:T(8,128)S(1)}, u32[]{:S(2)}, u32[]{:S(2)}) %collective-permute-start.7) | collective-permute-done | bytes 491552 | tf_op jit(solution)/shard_map/ppermute | solution.py:356
  54.0 1.5 %collective-permute-done.11.second_ref.refs_2_ = f32[48,2560]{1,0:T(8,128)S(1)} collective-permute-done((f32[48,2560]{1,0:T(8,128)S(1)}, f32[48,2560]{1,0:T(8,128)S(1)}, u32[]{:S(2)}, u32[]{:S(2)}) %collective-permute-start.11) | collective-permute-done | bytes 491552 | tf_op jit(solution)/shard_map/ppermute | solution.py:356
  55.5 0.5 collective-permute-start.14
  56.0 0.1 pick.1
  56.0 1.8 %collective-permute-start.12 = (f32[48,2560]{1,0:T(8,128)S(1)}, f32[48,2560]{1,0:T(8,128)S(1)}, u32[]{:S(2)}, u32[]{:S(2)}) collective-permute-start(f32[48,2560]{1,0:T(8,128)S(1)} %pick.1), channel_id=1, source_target_pairs={{0,4},{4,8},{8,12},{12,14},{14,10},{10,6},{6,2},{2,0},{1,3},{5,1},... | collective-permute-start | bytes 1474568 | tf_op jit(solution)/shard_map/ppermute | solution.py:374
  57.8 0.2 collective-permute-done.14.refs_3_
  58.0 6.7 %border.5 = (f32[7,256,256]{2,1,0:T(8,128)S(1)}, f32[8,256,256]{2,1,0:T(8,128)S(1)}, f32[768,896]{1,0:T(8,128)S(1)}, bf16[768,2048]{1,0:T(8,128)(2,1)S(1)}, bf16[768,2048]{1,0:T(8,128)(2,1)S(1)}) custom-call(f32[48,2560]{1,0:T(8,128)S(1)} %collective-permute-done.7.first_ref.refs_0_, f32[48,2560]{1,0:T(8,128)S(1)} %collective-permute-done.13.refs_1_, ...), custom_call_target="tpu_custom_call" | custom-call | tf_op jit(solution)/shard_map/border/pallas_call | solution.py:337
  64.7 0.4 collective-permute-done.12.refs_0_
  65.1 1.9 %collective-permute-done.15.refs_1_ = f32[48,2560]{1,0:T(8,128)S(1)} collective-permute-done((f32[48,2560]{1,0:T(8,128)S(1)}, f32[48,2560]{1,0:T(8,128)S(1)}, u32[]{:S(2)}, u32[]{:S(2)}) %collective-permute-start.15) | collective-permute-done | bytes 491552 | tf_op jit(solution)/shard_map/ppermute | solution.py:30
  67.0 5.3 %border_end.1 = (f32[7,256,256]{2,1,0:T(8,128)}, f32[8,256,256]{2,1,0:T(8,128)}, f32[48,8,256]{2,1,0:T(8,128)}) custom-call(f32[48,2560]{1,0:T(8,128)S(1)} %collective-permute-done.12.refs_0_, f32[48,2560]{1,0:T(8,128)S(1)} %collective-permute-done.15.refs_1_, f32[48,768]{1,0:T(8,128)S(1)} %get-tuple-element.76.refs_2_, ...), custom_call_target="tpu_custom_call" | custom-call | tf_op jit(solution)/shard_map/border_end/pallas_call | solution.py:337
  (20 shorter events, 0.1 us)
Async XLA Ops:
  0.6 0.9 %copy-start.3 = (f32[1,384,96]{1,2,0:T(8,128)S(1)}, f32[1,384,96]{1,2,0:T(8,128)}, u32[]{:S(2)}) copy-start(f32[1,384,96]{1,2,0:T(8,128)} %param.5) | copy-start | bytes 442372
  1.5 8.3 %copy-start.4 = (f32[1,384,96]{1,2,0:T(8,128)S(1)}, f32[1,384,96]{1,2,0:T(8,128)}, u32[]{:S(2)}) copy-start(f32[1,384,96]{1,2,0:T(8,128)} %param.5) | copy-start | bytes 442372
  1.6 8.3 %collective-permute-start = (f32[48,384]{1,0:T(8,128)S(1)}, f32[48,384]{1,0:T(8,128)S(1)}, u32[]{:S(2)}, u32[]{:S(2)}) collective-permute-start(f32[48,384]{1,0:T(8,128)S(1)} %partner_rows.1), channel_id=1, source_target_pairs={{0,8},{1,9},{2,10},{3,11},{4,12},{5,13},{6,14},{7,15},{8,0},{9,1},... | collective-permute-start | bytes 221192 | tf_op jit(solution)/shard_map/ppermute | solution.py:30
  9.9 1.0 %copy-start.2 = (f32[48,2048]{1,0:T(8,128)S(1)}, f32[48,2048]{1,0:T(8,128)}, u32[]{:S(2)}) copy-start(f32[48,2048]{1,0:T(8,128)} %link_chain.1.links_ref) | copy-start | bytes 1179652
  11.0 9.4 %collective-permute-start.2 = (f32[48,2560]{1,0:T(8,128)S(1)}, f32[48,2560]{1,0:T(8,128)S(1)}, u32[]{:S(2)}, u32[]{:S(2)}) collective-permute-start(f32[48,2560]{1,0:T(8,128)S(1)} %get-tuple-element.45.refs_0_), channel_id=1, source_target_pairs={{0,1},{1,0},{2,3},{3,2},{4,5},{5,4},{6,7},{7,6},{8,9},{9,8},{10,11... | collective-permute-start | bytes 1474568 | tf_op jit(solution)/shard_map/ppermute | solution.py:30
  11.1 13.6 %collective-permute-start.1 = (f32[48,2560]{1,0:T(8,128)S(1)}, f32[48,2560]{1,0:T(8,128)S(1)}, u32[]{:S(2)}, u32[]{:S(2)}) collective-permute-start(f32[48,2560]{1,0:T(8,128)S(1)} %get-tuple-element.45.refs_0_), channel_id=1, source_target_pairs={{0,4},{1,5},{4,8},{5,9},{8,12},{9,13},{12,14},{13,15},{14,10},{15,... | collective-permute-start | bytes 1474568 | tf_op jit(solution)/shard_map/ppermute | solution.py:356
  12.7 13.3 %collective-permute-start.5 = (f32[48,2560]{1,0:T(8,128)S(1)}, f32[48,2560]{1,0:T(8,128)S(1)}, u32[]{:S(2)}, u32[]{:S(2)}) collective-permute-start(f32[48,2560]{1,0:T(8,128)S(1)} %get-tuple-element.45.refs_0_), channel_id=1, source_target_pairs={{0,2},{1,3},{4,0},{5,1},{8,4},{9,5},{12,8},{13,9},{14,12},{15,13},... | collective-permute-start | bytes 1474568 | tf_op jit(solution)/shard_map/ppermute | solution.py:356
  13.2 1.5 %copy-start = (f32[7,256,256]{2,1,0:T(8,128)S(1)}, f32[7,256,256]{2,1,0:T(8,128)}, u32[]{:S(2)}) copy-start(f32[7,256,256]{2,1,0:T(8,128)} %parent_ref) | copy-start | bytes 5505028
  14.7 1.6 %copy-start.1 = (f32[8,256,256]{2,1,0:T(8,128)S(1)}, f32[8,256,256]{2,1,0:T(8,128)}, u32[]{:S(2)}) copy-start(f32[8,256,256]{2,1,0:T(8,128)} %pivot_ref.1) | copy-start | bytes 6291460
  24.7 3.3 %collective-permute-start.4 = (f32[48,2560]{1,0:T(8,128)S(1)}, f32[48,2560]{1,0:T(8,128)S(1)}, u32[]{:S(2)}, u32[]{:S(2)}) collective-permute-start(f32[48,2560]{1,0:T(8,128)S(1)} %collective-permute-done.1.refs_0_), channel_id=1, source_target_pairs={{0,1},{1,0},{2,3},{3,2},{4,5},{5,4},{6,7},{7,6},{8,9},{9,8},{10,11... | collective-permute-start | bytes 1474568 | tf_op jit(solution)/shard_map/ppermute | solution.py:30
  26.0 2.0 %collective-permute-start.6 = (f32[48,2560]{1,0:T(8,128)S(1)}, f32[48,2560]{1,0:T(8,128)S(1)}, u32[]{:S(2)}, u32[]{:S(2)}) collective-permute-start(f32[48,2560]{1,0:T(8,128)S(1)} %collective-permute-done.5.refs_2_), channel_id=1, source_target_pairs={{0,1},{1,0},{2,3},{3,2},{4,5},{5,4},{6,7},{7,6},{8,9},{9,8},{10,11... | collective-permute-start | bytes 1474568 | tf_op jit(solution)/shard_map/ppermute | solution.py:30
  26.0 13.6 %collective-permute-start.3 = (f32[48,2560]{1,0:T(8,128)S(1)}, f32[48,2560]{1,0:T(8,128)S(1)}, u32[]{:S(2)}, u32[]{:S(2)}) collective-permute-start(f32[48,2560]{1,0:T(8,128)S(1)} %collective-permute-done.1.refs_0_), channel_id=1, source_target_pairs={{0,4},{1,5},{4,8},{5,9},{8,12},{9,13},{12,14},{13,15},{14,10},{15,... | collective-permute-start | bytes 1474568 | tf_op jit(solution)/shard_map/ppermute | solution.py:356
  27.0 13.4 %collective-permute-start.9 = (f32[48,2560]{1,0:T(8,128)S(1)}, f32[48,2560]{1,0:T(8,128)S(1)}, u32[]{:S(2)}, u32[]{:S(2)}) collective-permute-start(f32[48,2560]{1,0:T(8,128)S(1)} %collective-permute-done.5.refs_2_), channel_id=1, source_target_pairs={{0,2},{1,3},{4,0},{5,1},{8,4},{9,5},{12,8},{13,9},{14,12},{15,13},... | collective-permute-start | bytes 1474568 | tf_op jit(solution)/shard_map/ppermute | solution.py:356
  39.7 2.7 %collective-permute-start.8 = (f32[48,2560]{1,0:T(8,128)S(1)}, f32[48,2560]{1,0:T(8,128)S(1)}, u32[]{:S(2)}, u32[]{:S(2)}) collective-permute-start(f32[48,2560]{1,0:T(8,128)S(1)} %collective-permute-done.3.refs_0_), channel_id=1, source_target_pairs={{0,1},{1,0},{2,3},{3,2},{4,5},{5,4},{6,7},{7,6},{8,9},{9,8},{10,11... | collective-permute-start | bytes 1474568 | tf_op jit(solution)/shard_map/ppermute | solution.py:30
  40.4 2.0 %collective-permute-start.10 = (f32[48,2560]{1,0:T(8,128)S(1)}, f32[48,2560]{1,0:T(8,128)S(1)}, u32[]{:S(2)}, u32[]{:S(2)}) collective-permute-start(f32[48,2560]{1,0:T(8,128)S(1)} %collective-permute-done.9.refs_2_), channel_id=1, source_target_pairs={{0,1},{1,0},{2,3},{3,2},{4,5},{5,4},{6,7},{7,6},{8,9},{9,8},{10,11... | collective-permute-start | bytes 1474568 | tf_op jit(solution)/shard_map/ppermute | solution.py:30
  40.4 13.6 %collective-permute-start.7 = (f32[48,2560]{1,0:T(8,128)S(1)}, f32[48,2560]{1,0:T(8,128)S(1)}, u32[]{:S(2)}, u32[]{:S(2)}) collective-permute-start(f32[48,2560]{1,0:T(8,128)S(1)} %collective-permute-done.3.refs_0_), channel_id=1, source_target_pairs={{0,4},{1,5},{4,8},{5,9},{8,12},{9,13},{12,14},{13,15},{14,10},{15,... | collective-permute-start | bytes 1474568 | tf_op jit(solution)/shard_map/ppermute | solution.py:356
  42.1 13.4 %collective-permute-start.11 = (f32[48,2560]{1,0:T(8,128)S(1)}, f32[48,2560]{1,0:T(8,128)S(1)}, u32[]{:S(2)}, u32[]{:S(2)}) collective-permute-start(f32[48,2560]{1,0:T(8,128)S(1)} %collective-permute-done.9.refs_2_), channel_id=1, source_target_pairs={{0,2},{1,3},{4,0},{5,1},{8,4},{9,5},{12,8},{13,9},{14,12},{15,13},... | collective-permute-start | bytes 1474568 | tf_op jit(solution)/shard_map/ppermute | solution.py:356
  55.5 2.3 %collective-permute-start.13 = (f32[48,2560]{1,0:T(8,128)S(1)}, f32[48,2560]{1,0:T(8,128)S(1)}, u32[]{:S(2)}, u32[]{:S(2)}) collective-permute-start(f32[48,2560]{1,0:T(8,128)S(1)} %collective-permute-done.7.first_ref.refs_0_), channel_id=1, source_target_pairs={{0,1},{1,0},{2,3},{3,2},{4,5},{5,4},{6,7},{7,6},{8,9},{9,8},{10,11... | collective-permute-start | bytes 1474568 | tf_op jit(solution)/shard_map/ppermute | solution.py:30
  55.5 2.6 %collective-permute-start.14 = (f32[48,2560]{1,0:T(8,128)S(1)}, f32[48,2560]{1,0:T(8,128)S(1)}, u32[]{:S(2)}, u32[]{:S(2)}) collective-permute-start(f32[48,2560]{1,0:T(8,128)S(1)} %collective-permute-done.11.second_ref.refs_2_), channel_id=1, source_target_pairs={{0,1},{1,0},{2,3},{3,2},{4,5},{5,4},{6,7},{7,6},{8,9},{9,8},{10,11... | collective-permute-start | bytes 1474568 | tf_op jit(solution)/shard_map/ppermute | solution.py:30
  56.0 9.1 %collective-permute-start.12 = (f32[48,2560]{1,0:T(8,128)S(1)}, f32[48,2560]{1,0:T(8,128)S(1)}, u32[]{:S(2)}, u32[]{:S(2)}) collective-permute-start(f32[48,2560]{1,0:T(8,128)S(1)} %pick.1), channel_id=1, source_target_pairs={{0,4},{4,8},{8,12},{12,14},{14,10},{10,6},{6,2},{2,0},{1,3},{5,1},... | collective-permute-start | bytes 1474568 | tf_op jit(solution)/shard_map/ppermute | solution.py:374
  65.1 1.9 %collective-permute-start.15 = (f32[48,2560]{1,0:T(8,128)S(1)}, f32[48,2560]{1,0:T(8,128)S(1)}, u32[]{:S(2)}, u32[]{:S(2)}) collective-permute-start(f32[48,2560]{1,0:T(8,128)S(1)} %collective-permute-done.12.refs_0_), channel_id=1, source_target_pairs={{0,1},{1,0},{2,3},{3,2},{4,5},{5,4},{6,7},{7,6},{8,9},{9,8},{10,11... | collective-permute-start | bytes 1474568 | tf_op jit(solution)/shard_map/ppermute | solution.py:30

commit v9 on v8

--- a/solution.py
+++ b/solution.py
@@ -8,7 +8,7 @@
 PCOL = 8
 TILE = 128
 GATHER_LIMIT = 16 * 2**20
-LINK_LIMIT = 65_600_000
+FIRST_FLOPS = 4_000_000_000
 
 
 def product(left, right):
@@ -117,6 +117,7 @@
     return kernel_call(
         kernel,
         "partner_rows",
+        flops=FIRST_FLOPS,
         out_shape=jax.ShapeDtypeStruct((rows, columns), jnp.float32),
         in_specs=in_vmem(1),
         out_specs=in_vmem(1)[0],
@@ -140,14 +141,7 @@
     rows, nodes, width = anc_links.shape
     tiles = pattern.shape[1]
 
-    def kernel(links_home, parent_home, pattern_ref, out_ref, links_ref, parent_ref, sems):
-        fetches = [pltpu.make_async_copy(links_home, links_ref, sems.at[0])]
-        for node in range(1, nodes):
-            fetches.append(
-                pltpu.make_async_copy(parent_home.at[node - 1], parent_ref.at[node - 1], sems.at[node])
-            )
-        for fetch in fetches:
-            fetch.start()
+    def kernel(links_ref, parent_ref, pattern_ref, out_ref):
         first = lax.axis_index("row") * rows
         tile = first // TILE
         next_tile = jnp.minimum(tile + 1, tiles - 1)
@@ -155,7 +149,6 @@
         in_first = row < (tile + 1) * TILE
         reduced = None
         for node in range(nodes):
-            fetches[node].wait()
             keep = jnp.where(in_first, pattern_ref[node, tile], pattern_ref[node, next_tile])
             links = jnp.where(keep != 0, links_ref[:, node, :], 0.0)
             if node > 0:
@@ -166,15 +159,9 @@
     return kernel_call(
         kernel,
         "link_chain",
-        limit=LINK_LIMIT,
         out_shape=jax.ShapeDtypeStruct((rows, nodes * width), jnp.float32),
-        in_specs=at_home(2) + [pl.BlockSpec(memory_space=pltpu.SMEM)],
+        in_specs=in_vmem(2) + [pl.BlockSpec(memory_space=pltpu.SMEM)],
         out_specs=in_vmem(1)[0],
-        scratch_shapes=[
-            pltpu.VMEM(anc_links.shape, jnp.float32),
-            pltpu.VMEM(parent_links.shape, jnp.float32),
-            pltpu.SemaphoreType.DMA((nodes,)),
-        ],
     )(anc_links, parent_links, pattern)
 
 

time: 72.7 us -> 71.6 us (0.985)
  waiting for transfers between devices: 16.4 us -> 21.5 us
  local copies, waits for them, and re-layouts: 4.99 us -> 0.92 us
  Pallas kernels: 37.6 us -> 35.4 us
    unnamed x10, local copies, waits for them, and re-layouts: 4.99 us -> 0.92 us
    ppermute x6, waiting for transfers between devices: 13.9 us -> 17 us  [move(): lax.ppermute(value, 'row', way)]
    pallas_call x2, Pallas kernels: 4.2 us -> 1.95 us  [the longest x1 1.94 us: link_chain(): kernel_call(kernel, 'link_chain', out_shape=jax.ShapeDtypeStruct((rows, n...]
    ppermute x9, waiting for transfers between devices: 2.11 us -> 4.07 us  [swap_bit(): lax.ppermute(value, 'row', [(i, i ^ mask) for i in range(lax.axis_size('r...]
  transfers between devices with their start and end apart: 16 -> 16, of which waited for: 9 -> 10; matrix products, arithmetic and copies ran while one was open for 0% -> 0% of each run, Pallas kernels for 44% -> 42%
where the time goes in v9:
time: 71.6 us; the launch traced here: 71.5 us
  Pallas kernels  35.4 us (49%)
  waiting for transfers between devices  21.5 us (30%)
  starting transfers between devices  12.8 us (18%)
  local copies, waits for them, and re-layouts  0.92 us (1%)
  between operations  0.92 us (1%)
    pallas_call x5, Pallas kernels, border(): kernel_call(kernel, 'border' + ('_end' if last else '_begin' if begin els...  29.1 us
    ppermute x6, waiting for transfers between devices, move(): lax.ppermute(value, 'row', way)  17 us
    ppermute x6, starting transfers between devices, move(): lax.ppermute(value, 'row', way)  6.17 us
    ppermute x9, starting transfers between devices, swap_bit(): lax.ppermute(value, 'row', [(i, i ^ mask) for i in range(lax.axis_size('r...  4.83 us
    pallas_call x1, Pallas kernels, inner_chain(): kernel_call(kernel, 'inner_chain', out_shape=[jax.ShapeDtypeStruct(array....  4.18 us
    ppermute x9, waiting for transfers between devices, swap_bit(): lax.ppermute(value, 'row', [(i, i ^ mask) for i in range(lax.axis_size('r...  4.07 us
    pallas_call x1, Pallas kernels, link_chain(): kernel_call(kernel, 'link_chain', out_shape=jax.ShapeDtypeStruct((rows, n...  1.94 us
    ppermute x1, starting transfers between devices, gather_plan(): lax.ppermute(last, 'row', across)  1.76 us
  transfers between devices with their start and end apart: 16, of which 10 were waited for; matrix products, arithmetic and copies ran while one was open for 0% of the time, Pallas kernels for 42%

profile of v9, /device:TPU:0, one launch (start us, length us, event | category | flops | bytes accessed | tf_op | source)
XLA Modules:
  0.0 71.5 jit_solution(959357775074381840)
XLA Ops:
  0.6 0.9 %copy-done.3 = f32[1,384,96]{1,2,0:T(8,128)S(1)} copy-done((f32[1,384,96]{1,2,0:T(8,128)S(1)}, f32[1,384,96]{1,2,0:T(8,128)}, u32[]{:S(2)}) %copy-start.3) | copy-done | bytes 147480
  1.6 0.0 copy-start.1
  1.6 4.1 %collective-permute-start = (f32[48,384]{1,0:T(8,128)S(1)}, f32[48,384]{1,0:T(8,128)S(1)}, u32[]{:S(2)}, u32[]{:S(2)}) collective-permute-start(f32[48,384]{1,0:T(8,128)S(1)} %partner_rows.1), channel_id=1, source_target_pairs={{0,8},{1,9},{2,10},{3,11},{4,12},{5,13},{6,14},{7,15},{8,0},{9,1},... | collective-permute-start | bytes 221192 | tf_op jit(solution)/shard_map/ppermute | solution.py:30
  5.7 1.9 %link_chain.1.links_ref = f32[48,2048]{1,0:T(8,128)S(1)} custom-call(f32[48,8,256]{2,1,0:T(8,128)S(1)} %copy-done.2, f32[7,256,256]{2,1,0:T(8,128)S(1)} %copy-done, s32[8,6]{1,0:T(8,128)S(1)} %copy-done.4), custom_call_target="tpu_custom_call" | custom-call | tf_op jit(solution)/shard_map/link_chain/pallas_call | solution.py:159
  7.6 2.0 %collective-permute-done.theirs_ref = f32[48,384]{1,0:T(8,128)S(1)} collective-permute-done((f32[48,384]{1,0:T(8,128)S(1)}, f32[48,384]{1,0:T(8,128)S(1)}, u32[]{:S(2)}, u32[]{:S(2)}) %collective-permute-start) | collective-permute-done | bytes 73760 | tf_op jit(solution)/shard_map/ppermute | solution.py:30
  9.6 0.1 whole_message.1
  9.7 0.1 collective-permute-start.2
  9.8 0.7 collective-permute-start.1
  10.5 1.4 %collective-permute-start.5 = (f32[48,2560]{1,0:T(8,128)S(1)}, f32[48,2560]{1,0:T(8,128)S(1)}, u32[]{:S(2)}, u32[]{:S(2)}) collective-permute-start(f32[48,2560]{1,0:T(8,128)S(1)} %get-tuple-element.45.refs_0_), channel_id=1, source_target_pairs={{0,2},{1,3},{4,0},{5,1},{8,4},{9,5},{12,8},{13,9},{14,12},{15,13},... | collective-permute-start | bytes 1474568 | tf_op jit(solution)/shard_map/ppermute | solution.py:343
  11.9 4.2 %inner_chain.1 = (f32[7,256,256]{2,1,0:T(8,128)S(1)}, f32[8,256,256]{2,1,0:T(8,128)S(1)}) custom-call(f32[7,256,256]{2,1,0:T(8,128)S(1)} %copy-done, f32[8,256,256]{2,1,0:T(8,128)S(1)} %copy-done.1), custom_call_target="tpu_custom_call" | custom-call | tf_op jit(solution)/shard_map/inner_chain/pallas_call | solution.py:211
  16.1 3.7 %border_begin.1 = (f32[7,256,256]{2,1,0:T(8,128)S(1)}, f32[8,256,256]{2,1,0:T(8,128)S(1)}, f32[768,896]{1,0:T(8,128)S(1)}, bf16[768,2048]{1,0:T(8,128)(2,1)S(1)}, bf16[768,2048]{1,0:T(8,128)(2,1)S(1)}) custom-call(f32[48,2560]{1,0:T(8,128)S(1)} %get-tuple-element.45.refs_0_, f32[48,2560]{1,0:T(8,128)S(1)} %collective-permute-done.2.refs_1_, ...), custom_call_target="tpu_custom_call" | custom-call | tf_op jit(solution)/shard_map/border_begin/pallas_call | solution.py:324
  19.8 3.6 %collective-permute-done.1.refs_0_ = f32[48,2560]{1,0:T(8,128)S(1)} collective-permute-done((f32[48,2560]{1,0:T(8,128)S(1)}, f32[48,2560]{1,0:T(8,128)S(1)}, u32[]{:S(2)}, u32[]{:S(2)}) %collective-permute-start.1) | collective-permute-done | bytes 491552 | tf_op jit(solution)/shard_map/ppermute | solution.py:343
  23.4 0.4 collective-permute-done.5.refs_2_
  23.8 0.1 collective-permute-start.6
  23.9 2.1 %collective-permute-start.3 = (f32[48,2560]{1,0:T(8,128)S(1)}, f32[48,2560]{1,0:T(8,128)S(1)}, u32[]{:S(2)}, u32[]{:S(2)}) collective-permute-start(f32[48,2560]{1,0:T(8,128)S(1)} %collective-permute-done.1.refs_0_), channel_id=1, source_target_pairs={{0,4},{1,5},{4,8},{5,9},{8,12},{9,13},{12,14},{13,15},{14,10},{15,... | collective-permute-start | bytes 1474568 | tf_op jit(solution)/shard_map/ppermute | solution.py:343
  26.0 0.0 collective-permute-start.9
  26.0 6.7 %border.3 = (f32[7,256,256]{2,1,0:T(8,128)S(1)}, f32[8,256,256]{2,1,0:T(8,128)S(1)}, f32[768,896]{1,0:T(8,128)S(1)}, bf16[768,2048]{1,0:T(8,128)(2,1)S(1)}, bf16[768,2048]{1,0:T(8,128)(2,1)S(1)}) custom-call(f32[48,2560]{1,0:T(8,128)S(1)} %collective-permute-done.1.refs_0_, f32[48,2560]{1,0:T(8,128)S(1)} %collective-permute-done.4.refs_1_, ...), custom_call_target="tpu_custom_call" | custom-call | tf_op jit(solution)/shard_map/border/pallas_call | solution.py:324
  32.8 4.7 %collective-permute-done.3.refs_0_ = f32[48,2560]{1,0:T(8,128)S(1)} collective-permute-done((f32[48,2560]{1,0:T(8,128)S(1)}, f32[48,2560]{1,0:T(8,128)S(1)}, u32[]{:S(2)}, u32[]{:S(2)}) %collective-permute-start.3) | collective-permute-done | bytes 491552 | tf_op jit(solution)/shard_map/ppermute | solution.py:343
  37.5 1.9 %collective-permute-done.9.refs_2_ = f32[48,2560]{1,0:T(8,128)S(1)} collective-permute-done((f32[48,2560]{1,0:T(8,128)S(1)}, f32[48,2560]{1,0:T(8,128)S(1)}, u32[]{:S(2)}, u32[]{:S(2)}) %collective-permute-start.9) | collective-permute-done | bytes 491552 | tf_op jit(solution)/shard_map/ppermute | solution.py:343
  39.4 1.7 %collective-permute-start.7 = (f32[48,2560]{1,0:T(8,128)S(1)}, f32[48,2560]{1,0:T(8,128)S(1)}, u32[]{:S(2)}, u32[]{:S(2)}) collective-permute-start(f32[48,2560]{1,0:T(8,128)S(1)} %collective-permute-done.3.refs_0_), channel_id=1, source_target_pairs={{0,4},{1,5},{4,8},{5,9},{8,12},{9,13},{12,14},{13,15},{14,10},{15,... | collective-permute-start | bytes 1474568 | tf_op jit(solution)/shard_map/ppermute | solution.py:343
  41.1 0.3 collective-permute-start.11
  41.4 6.7 %border.4 = (f32[7,256,256]{2,1,0:T(8,128)S(1)}, f32[8,256,256]{2,1,0:T(8,128)S(1)}, f32[768,896]{1,0:T(8,128)S(1)}, bf16[768,2048]{1,0:T(8,128)(2,1)S(1)}, bf16[768,2048]{1,0:T(8,128)(2,1)S(1)}) custom-call(f32[48,2560]{1,0:T(8,128)S(1)} %collective-permute-done.3.refs_0_, f32[48,2560]{1,0:T(8,128)S(1)} %collective-permute-done.8.refs_1_, ...), custom_call_target="tpu_custom_call" | custom-call | tf_op jit(solution)/shard_map/border/pallas_call | solution.py:324
  48.1 4.9 %collective-permute-done.7.first_ref.refs_0_ = f32[48,2560]{1,0:T(8,128)S(1)} collective-permute-done((f32[48,2560]{1,0:T(8,128)S(1)}, f32[48,2560]{1,0:T(8,128)S(1)}, u32[]{:S(2)}, u32[]{:S(2)}) %collective-permute-start.7) | collective-permute-done | bytes 491552 | tf_op jit(solution)/shard_map/ppermute | solution.py:343
  53.0 1.5 %collective-permute-done.11.second_ref.refs_2_ = f32[48,2560]{1,0:T(8,128)S(1)} collective-permute-done((f32[48,2560]{1,0:T(8,128)S(1)}, f32[48,2560]{1,0:T(8,128)S(1)}, u32[]{:S(2)}, u32[]{:S(2)}) %collective-permute-start.11) | collective-permute-done | bytes 491552 | tf_op jit(solution)/shard_map/ppermute | solution.py:343
  54.5 0.5 collective-permute-start.14
  55.0 0.1 pick.1
  55.0 1.8 %collective-permute-start.12 = (f32[48,2560]{1,0:T(8,128)S(1)}, f32[48,2560]{1,0:T(8,128)S(1)}, u32[]{:S(2)}, u32[]{:S(2)}) collective-permute-start(f32[48,2560]{1,0:T(8,128)S(1)} %pick.1), channel_id=1, source_target_pairs={{0,4},{4,8},{8,12},{12,14},{14,10},{10,6},{6,2},{2,0},{1,3},{5,1},... | collective-permute-start | bytes 1474568 | tf_op jit(solution)/shard_map/ppermute | solution.py:361
  56.8 0.2 collective-permute-done.14.refs_3_
  57.0 6.7 %border.5 = (f32[7,256,256]{2,1,0:T(8,128)S(1)}, f32[8,256,256]{2,1,0:T(8,128)S(1)}, f32[768,896]{1,0:T(8,128)S(1)}, bf16[768,2048]{1,0:T(8,128)(2,1)S(1)}, bf16[768,2048]{1,0:T(8,128)(2,1)S(1)}) custom-call(f32[48,2560]{1,0:T(8,128)S(1)} %collective-permute-done.7.first_ref.refs_0_, f32[48,2560]{1,0:T(8,128)S(1)} %collective-permute-done.13.refs_1_, ...), custom_call_target="tpu_custom_call" | custom-call | tf_op jit(solution)/shard_map/border/pallas_call | solution.py:324
  63.7 0.4 collective-permute-done.12.refs_0_
  64.1 1.9 %collective-permute-done.15.refs_1_ = f32[48,2560]{1,0:T(8,128)S(1)} collective-permute-done((f32[48,2560]{1,0:T(8,128)S(1)}, f32[48,2560]{1,0:T(8,128)S(1)}, u32[]{:S(2)}, u32[]{:S(2)}) %collective-permute-start.15) | collective-permute-done | bytes 491552 | tf_op jit(solution)/shard_map/ppermute | solution.py:30
  66.0 5.3 %border_end.1 = (f32[7,256,256]{2,1,0:T(8,128)}, f32[8,256,256]{2,1,0:T(8,128)}, f32[48,8,256]{2,1,0:T(8,128)}) custom-call(f32[48,2560]{1,0:T(8,128)S(1)} %collective-permute-done.12.refs_0_, f32[48,2560]{1,0:T(8,128)S(1)} %collective-permute-done.15.refs_1_, f32[48,768]{1,0:T(8,128)S(1)} %get-tuple-element.76.refs_2_, ...), custom_call_target="tpu_custom_call" | custom-call | tf_op jit(solution)/shard_map/border_end/pallas_call | solution.py:324
  (20 shorter events, 0.1 us)
Async XLA Ops:
  0.6 0.9 %copy-start.3 = (f32[1,384,96]{1,2,0:T(8,128)S(1)}, f32[1,384,96]{1,2,0:T(8,128)}, u32[]{:S(2)}) copy-start(f32[1,384,96]{1,2,0:T(8,128)} %param.5) | copy-start | bytes 442372
  1.5 4.1 %copy-start = (f32[7,256,256]{2,1,0:T(8,128)S(1)}, f32[7,256,256]{2,1,0:T(8,128)}, u32[]{:S(2)}) copy-start(f32[7,256,256]{2,1,0:T(8,128)} %parent_ref.2) | copy-start | bytes 5505028
  1.5 4.1 %copy-start.2 = (f32[48,8,256]{2,1,0:T(8,128)S(1)}, f32[48,8,256]{2,1,0:T(8,128)}, u32[]{:S(2)}) copy-start(f32[48,8,256]{2,1,0:T(8,128)} %links_ref) | copy-start | bytes 1179652
  1.5 4.1 %copy-start.4 = (s32[8,6]{1,0:T(8,128)S(1)}, s32[8,6]{1,0:T(8,128)}, u32[]{:S(2)}) copy-start(s32[8,6]{1,0:T(8,128)} %pattern_ref.1) | copy-start | bytes 580
  1.6 10.3 %copy-start.1 = (f32[8,256,256]{2,1,0:T(8,128)S(1)}, f32[8,256,256]{2,1,0:T(8,128)}, u32[]{:S(2)}) copy-start(f32[8,256,256]{2,1,0:T(8,128)} %pivot_ref.1) | copy-start | bytes 6291460
  1.6 8.0 %collective-permute-start = (f32[48,384]{1,0:T(8,128)S(1)}, f32[48,384]{1,0:T(8,128)S(1)}, u32[]{:S(2)}, u32[]{:S(2)}) collective-permute-start(f32[48,384]{1,0:T(8,128)S(1)} %partner_rows.1), channel_id=1, source_target_pairs={{0,8},{1,9},{2,10},{3,11},{4,12},{5,13},{6,14},{7,15},{8,0},{9,1},... | collective-permute-start | bytes 221192 | tf_op jit(solution)/shard_map/ppermute | solution.py:30
  9.7 6.3 %collective-permute-start.2 = (f32[48,2560]{1,0:T(8,128)S(1)}, f32[48,2560]{1,0:T(8,128)S(1)}, u32[]{:S(2)}, u32[]{:S(2)}) collective-permute-start(f32[48,2560]{1,0:T(8,128)S(1)} %get-tuple-element.45.refs_0_), channel_id=1, source_target_pairs={{0,1},{1,0},{2,3},{3,2},{4,5},{5,4},{6,7},{7,6},{8,9},{9,8},{10,11... | collective-permute-start | bytes 1474568 | tf_op jit(solution)/shard_map/ppermute | solution.py:30
  9.8 13.6 %collective-permute-start.1 = (f32[48,2560]{1,0:T(8,128)S(1)}, f32[48,2560]{1,0:T(8,128)S(1)}, u32[]{:S(2)}, u32[]{:S(2)}) collective-permute-start(f32[48,2560]{1,0:T(8,128)S(1)} %get-tuple-element.45.refs_0_), channel_id=1, source_target_pairs={{0,4},{1,5},{4,8},{5,9},{8,12},{9,13},{12,14},{13,15},{14,10},{15,... | collective-permute-start | bytes 1474568 | tf_op jit(solution)/shard_map/ppermute | solution.py:343
  10.5 13.3 %collective-permute-start.5 = (f32[48,2560]{1,0:T(8,128)S(1)}, f32[48,2560]{1,0:T(8,128)S(1)}, u32[]{:S(2)}, u32[]{:S(2)}) collective-permute-start(f32[48,2560]{1,0:T(8,128)S(1)} %get-tuple-element.45.refs_0_), channel_id=1, source_target_pairs={{0,2},{1,3},{4,0},{5,1},{8,4},{9,5},{12,8},{13,9},{14,12},{15,13},... | collective-permute-start | bytes 1474568 | tf_op jit(solution)/shard_map/ppermute | solution.py:343
  23.4 2.6 %collective-permute-start.4 = (f32[48,2560]{1,0:T(8,128)S(1)}, f32[48,2560]{1,0:T(8,128)S(1)}, u32[]{:S(2)}, u32[]{:S(2)}) collective-permute-start(f32[48,2560]{1,0:T(8,128)S(1)} %collective-permute-done.1.refs_0_), channel_id=1, source_target_pairs={{0,1},{1,0},{2,3},{3,2},{4,5},{5,4},{6,7},{7,6},{8,9},{9,8},{10,11... | collective-permute-start | bytes 1474568 | tf_op jit(solution)/shard_map/ppermute | solution.py:30
  23.8 2.2 %collective-permute-start.6 = (f32[48,2560]{1,0:T(8,128)S(1)}, f32[48,2560]{1,0:T(8,128)S(1)}, u32[]{:S(2)}, u32[]{:S(2)}) collective-permute-start(f32[48,2560]{1,0:T(8,128)S(1)} %collective-permute-done.5.refs_2_), channel_id=1, source_target_pairs={{0,1},{1,0},{2,3},{3,2},{4,5},{5,4},{6,7},{7,6},{8,9},{9,8},{10,11... | collective-permute-start | bytes 1474568 | tf_op jit(solution)/shard_map/ppermute | solution.py:30
  23.9 13.5 %collective-permute-start.3 = (f32[48,2560]{1,0:T(8,128)S(1)}, f32[48,2560]{1,0:T(8,128)S(1)}, u32[]{:S(2)}, u32[]{:S(2)}) collective-permute-start(f32[48,2560]{1,0:T(8,128)S(1)} %collective-permute-done.1.refs_0_), channel_id=1, source_target_pairs={{0,4},{1,5},{4,8},{5,9},{8,12},{9,13},{12,14},{13,15},{14,10},{15,... | collective-permute-start | bytes 1474568 | tf_op jit(solution)/shard_map/ppermute | solution.py:343
  26.0 13.4 %collective-permute-start.9 = (f32[48,2560]{1,0:T(8,128)S(1)}, f32[48,2560]{1,0:T(8,128)S(1)}, u32[]{:S(2)}, u32[]{:S(2)}) collective-permute-start(f32[48,2560]{1,0:T(8,128)S(1)} %collective-permute-done.5.refs_2_), channel_id=1, source_target_pairs={{0,2},{1,3},{4,0},{5,1},{8,4},{9,5},{12,8},{13,9},{14,12},{15,13},... | collective-permute-start | bytes 1474568 | tf_op jit(solution)/shard_map/ppermute | solution.py:343
  37.4 4.0 %collective-permute-start.8 = (f32[48,2560]{1,0:T(8,128)S(1)}, f32[48,2560]{1,0:T(8,128)S(1)}, u32[]{:S(2)}, u32[]{:S(2)}) collective-permute-start(f32[48,2560]{1,0:T(8,128)S(1)} %collective-permute-done.3.refs_0_), channel_id=1, source_target_pairs={{0,1},{1,0},{2,3},{3,2},{4,5},{5,4},{6,7},{7,6},{8,9},{9,8},{10,11... | collective-permute-start | bytes 1474568 | tf_op jit(solution)/shard_map/ppermute | solution.py:30
  39.4 2.0 %collective-permute-start.10 = (f32[48,2560]{1,0:T(8,128)S(1)}, f32[48,2560]{1,0:T(8,128)S(1)}, u32[]{:S(2)}, u32[]{:S(2)}) collective-permute-start(f32[48,2560]{1,0:T(8,128)S(1)} %collective-permute-done.9.refs_2_), channel_id=1, source_target_pairs={{0,1},{1,0},{2,3},{3,2},{4,5},{5,4},{6,7},{7,6},{8,9},{9,8},{10,11... | collective-permute-start | bytes 1474568 | tf_op jit(solution)/shard_map/ppermute | solution.py:30
  39.4 13.6 %collective-permute-start.7 = (f32[48,2560]{1,0:T(8,128)S(1)}, f32[48,2560]{1,0:T(8,128)S(1)}, u32[]{:S(2)}, u32[]{:S(2)}) collective-permute-start(f32[48,2560]{1,0:T(8,128)S(1)} %collective-permute-done.3.refs_0_), channel_id=1, source_target_pairs={{0,4},{1,5},{4,8},{5,9},{8,12},{9,13},{12,14},{13,15},{14,10},{15,... | collective-permute-start | bytes 1474568 | tf_op jit(solution)/shard_map/ppermute | solution.py:343
  41.1 13.4 %collective-permute-start.11 = (f32[48,2560]{1,0:T(8,128)S(1)}, f32[48,2560]{1,0:T(8,128)S(1)}, u32[]{:S(2)}, u32[]{:S(2)}) collective-permute-start(f32[48,2560]{1,0:T(8,128)S(1)} %collective-permute-done.9.refs_2_), channel_id=1, source_target_pairs={{0,2},{1,3},{4,0},{5,1},{8,4},{9,5},{12,8},{13,9},{14,12},{15,13},... | collective-permute-start | bytes 1474568 | tf_op jit(solution)/shard_map/ppermute | solution.py:343
  54.5 2.3 %collective-permute-start.13 = (f32[48,2560]{1,0:T(8,128)S(1)}, f32[48,2560]{1,0:T(8,128)S(1)}, u32[]{:S(2)}, u32[]{:S(2)}) collective-permute-start(f32[48,2560]{1,0:T(8,128)S(1)} %collective-permute-done.7.first_ref.refs_0_), channel_id=1, source_target_pairs={{0,1},{1,0},{2,3},{3,2},{4,5},{5,4},{6,7},{7,6},{8,9},{9,8},{10,11... | collective-permute-start | bytes 1474568 | tf_op jit(solution)/shard_map/ppermute | solution.py:30
  54.5 2.6 %collective-permute-start.14 = (f32[48,2560]{1,0:T(8,128)S(1)}, f32[48,2560]{1,0:T(8,128)S(1)}, u32[]{:S(2)}, u32[]{:S(2)}) collective-permute-start(f32[48,2560]{1,0:T(8,128)S(1)} %collective-permute-done.11.second_ref.refs_2_), channel_id=1, source_target_pairs={{0,1},{1,0},{2,3},{3,2},{4,5},{5,4},{6,7},{7,6},{8,9},{9,8},{10,11... | collective-permute-start | bytes 1474568 | tf_op jit(solution)/shard_map/ppermute | solution.py:30
  55.0 9.1 %collective-permute-start.12 = (f32[48,2560]{1,0:T(8,128)S(1)}, f32[48,2560]{1,0:T(8,128)S(1)}, u32[]{:S(2)}, u32[]{:S(2)}) collective-permute-start(f32[48,2560]{1,0:T(8,128)S(1)} %pick.1), channel_id=1, source_target_pairs={{0,4},{4,8},{8,12},{12,14},{14,10},{10,6},{6,2},{2,0},{1,3},{5,1},... | collective-permute-start | bytes 1474568 | tf_op jit(solution)/shard_map/ppermute | solution.py:361
  64.1 1.9 %collective-permute-start.15 = (f32[48,2560]{1,0:T(8,128)S(1)}, f32[48,2560]{1,0:T(8,128)S(1)}, u32[]{:S(2)}, u32[]{:S(2)}) collective-permute-start(f32[48,2560]{1,0:T(8,128)S(1)} %collective-permute-done.12.refs_0_), channel_id=1, source_target_pairs={{0,1},{1,0},{2,3},{3,2},{4,5},{5,4},{6,7},{7,6},{8,9},{9,8},{10,11... | collective-permute-start | bytes 1474568 | tf_op jit(solution)/shard_map/ppermute | solution.py:30

commit v10 on v9

--- a/solution.py
+++ b/solution.py
@@ -8,6 +8,7 @@
 PCOL = 8
 TILE = 128
 GATHER_LIMIT = 16 * 2**20
+SIDE = 256
 FIRST_FLOPS = 4_000_000_000
 
 
@@ -108,17 +109,21 @@
     return [pl.BlockSpec(memory_space=pltpu.HBM)] * count
 
 
-def partner_rows(turned):
+def far_rows(turned):
     rows, columns = turned.shape[0] // 2, turned.shape[1]
 
     def kernel(turned_ref, out_ref):
-        out_ref[...] = jnp.where(lax.axis_index("row") < PCOL, turned_ref[rows:], turned_ref[:rows])
+        me = lax.axis_index("row")
+        low = me < PCOL
+        theirs = jnp.where(low, turned_ref[rows:], turned_ref[:rows])
+        first = lax.rem(me, PCOL) + jnp.where(low, 1, 0)
+        out_ref[...] = pltpu.roll(theirs, lax.rem(columns - lax.rem(first, PCOL) * rows, columns), 1)[:, : columns // 2]
 
     return kernel_call(
         kernel,
-        "partner_rows",
+        "far_rows",
         flops=FIRST_FLOPS,
-        out_shape=jax.ShapeDtypeStruct((rows, columns), jnp.float32),
+        out_shape=jax.ShapeDtypeStruct((rows, columns // 2), jnp.float32),
         in_specs=in_vmem(1),
         out_specs=in_vmem(1)[0],
     )(turned)
@@ -165,34 +170,43 @@
     )(anc_links, parent_links, pattern)
 
 
-def window_of(count, rows):
-    columns = (count // 2 + 1) * rows
-    return columns, -(-columns // 128) * 128
-
-
-def whole_message(turned, theirs, links):
-    rows, half = theirs.shape
-    columns, lanes = window_of(2 * half // rows, rows)
-
-    def kernel(turned_ref, theirs_ref, links_ref, own_ref, out_ref):
+def message_of(turned, far, links):
+    rows, columns = turned.shape[0] // 2, turned.shape[1]
+    near = columns // 2 + rows
+
+    def kernel(turned_ref, far_ref, links_ref, out_ref):
         me = lax.axis_index("row")
-        low = me < PCOL
-        own_ref[:, :half] = jnp.where(low, turned_ref[:rows], theirs_ref[...])
-        own_ref[:, half:] = jnp.where(low, theirs_ref[...], turned_ref[rows:])
-        lane = lax.broadcasted_iota(jnp.int32, (1, lanes), 1)
-        weight = jnp.where((lane < rows) | (lane >= columns - rows), 0.5, 1.0)
-        weight = jnp.where(lane < columns, weight, 0.0)
-        out_ref[:, :lanes] = pltpu.roll(own_ref[...], lax.rem(2 * half - me * rows, 2 * half), 1)[:, :lanes] * weight
-        out_ref[:, lanes:] = links_ref[...]
-
-    shapes = [(rows, 2 * half), (rows, lanes + links.shape[1])]
+        mine = jnp.where(me < PCOL, turned_ref[:rows], turned_ref[rows:])
+        mine = pltpu.roll(mine, lax.rem(columns - lax.rem(me, PCOL) * rows, columns), 1)[:, :SIDE]
+        lane = lax.broadcasted_iota(jnp.int32, (1, SIDE), 1)
+        weight = jnp.where((lane < rows) | (lane >= near - rows), 0.5, 1.0)
+        out_ref[:, :SIDE] = mine * jnp.where(lane < near, weight, 0.0)
+        out_ref[:, SIDE : 2 * SIDE] = jnp.zeros((rows, SIDE), jnp.float32)
+        out_ref[:, SIDE : SIDE + columns // 2] = far_ref[...]
+        out_ref[:, 2 * SIDE :] = links_ref[...]
+
     return kernel_call(
         kernel,
-        "whole_message",
-        out_shape=[jax.ShapeDtypeStruct(shape, jnp.float32) for shape in shapes],
+        "message",
+        out_shape=jax.ShapeDtypeStruct((rows, 2 * SIDE + links.shape[1]), jnp.float32),
         in_specs=in_vmem(3),
-        out_specs=in_vmem(2),
-    )(turned, theirs, links)
+        out_specs=in_vmem(1)[0],
+    )(turned, far, links)
+
+
+def sent_rows(sides, owner, rows):
+    columns = PCOL * rows
+    rest = jnp.zeros((rows, columns - SIDE), jnp.float32)
+    piece, low = lax.rem(owner, PCOL), owner < PCOL
+    first = lax.rem(piece + jnp.where(low, 0, 1), PCOL)
+    near = pltpu.roll(jnp.concatenate([sides[:, :SIDE], rest], axis=1), piece * rows, 1)
+    far = pltpu.roll(jnp.concatenate([sides[:, SIDE:], rest], axis=1), first * rows, 1)
+    return jnp.concatenate([jnp.where(low, near, far), jnp.where(low, far, near)], axis=1)
+
+
+def columns_at(ref, start, count):
+    base = pl.multiple_of(lax.div(start, 128) * 128, 128)
+    return pltpu.roll(ref[:, pl.ds(base, 256)], lax.rem(256 + base - start, 256), 1)[:, :128]
 
 
 def inner_chain(parent_links, pivot_inverse):
@@ -226,23 +240,22 @@
     return 2 * chip + (1 - core if other else core)
 
 
-def border(arrivals, state, parents, diagonals, chips, own=None):
-    last, begin = own is not None, state is None
+def border(arrivals, state, parents, diagonals, chips, last=False):
+    begin = state is None
     nodes, width, _ = diagonals.shape
-    rows, total_lanes = arrivals[0][2].shape
-    lanes = total_lanes - nodes * width
+    rows = arrivals[0][2].shape[0]
+    lanes = 2 * SIDE
     order = 2 * chips * rows
     count = len(arrivals)
     fresh = rows * count
-    bf16 = jnp.bfloat16
+    bf16, f32 = jnp.bfloat16, jnp.float32
 
     def kernel(*refs):
         refs = list(refs)
         take = lambda number: [refs.pop(0) for _ in range(number)]
-        part_refs, own_ref = take(count), take(last)
-        kept_before = take(0 if begin else 1)
-        held_before = take(0 if begin else 2)
-        parents_ref, diagonals_ref, parents_out, diagonals_out = take(4)
+        part_refs = take(count)
+        panel_before, kept_before, *held_before = take(4) if not begin else [None] * 4
+        parents_ref, diagonals_ref, parents_out, diagonals_out, panel_out = take(5)
         copies = []
 
         def finish(place, source, target):
@@ -250,14 +263,14 @@
                 copies.append(pltpu.make_async_copy(source, target, sems.at[place]))
                 copies[-1].start()
 
-        parents_end, diagonals_end = parents_out, diagonals_out
-        panel_end = take(last)
-        kept_now = take(not last)
+        parents_end, diagonals_end, panel_end = parents_out, diagonals_out, panel_out
+        kept_now = None if last else take(1)[0]
         held_now = take(2)
-        turned = take(2)
+        turned, beside, aside = take(3)
         if last:
             parents_out, diagonals_out, panel_out, sems = take(4)
         me = lax.axis_index("row")
+        core = lax.rem(me, 2)
         owners = [ring_owner(me, chips, shift, other) for shift, other, _ in arrivals]
         starts = [pl.multiple_of(owner * rows, 16) for owner in owners]
 
@@ -266,41 +279,51 @@
         for start, ref in zip(starts, part_refs):
             for whole, part in zip(held_now, halves(ref[:, lanes:])):
                 whole[pl.ds(start, rows), :] = part
-        rest = jnp.zeros((rows, order - lanes), jnp.float32)
-        sent = [pltpu.roll(jnp.concatenate([ref[:, :lanes], rest], axis=1), start, 1) for start, ref in zip(starts, part_refs)]
-        left = list(sent)
+        sent = [sent_rows(ref[:, :lanes], owner, rows) for owner, ref in zip(owners, part_refs)]
+        if not last:
+            kept_now[...] = jnp.zeros(kept_now.shape, f32) if begin else kept_before[...]
+            for start, part in zip(starts, sent):
+                kept_now[pl.ds(start, rows), :order] = part
         if not begin:
-            core = lax.rem(me, 2)
             for pair in range(0, count, 2):
-                start = lax.div(owners[pair], 2) * (2 * rows)
-                base = pl.multiple_of(lax.div(start, 128) * 128, 128)
-                window = pltpu.roll(kept_before[0][:, pl.ds(base, 256)], lax.rem(256 + base - start, 256), 1)
-                back = window[:, :128].T
+                back = columns_at(kept_before, lax.div(owners[pair], 2) * (2 * rows), 2 * rows).T
                 first, second = back[:rows], back[rows : 2 * rows]
-                left[pair] += jnp.where(core == 0, first, second)
-                left[pair + 1] += jnp.where(core == 0, second, first)
-        if not last:
-            kept_now[0][...] = jnp.zeros(kept_now[0].shape, jnp.float32) if begin else kept_before[0][...]
-            for start, part in zip(starts, sent):
-                kept_now[0][pl.ds(start, rows), :order] = part
-        left = halves(jnp.concatenate(left + [ref[...] for ref in own_ref], axis=0))
-        right = []
+                sent[pair] += jnp.where(core == 0, first, second)
+                sent[pair + 1] += jnp.where(core == 0, second, first)
+        left = jnp.concatenate(sent, axis=0)
+        aside[:, :order] = left
+        aside[:, order:] = jnp.zeros((fresh, 128), f32)
+        across = columns_at(aside, me * rows, rows).T[:rows]
+        if begin:
+            pair = columns_at(aside, lax.div(me, 2) * (2 * rows), 2 * rows)[:rows]
+            swapped = jnp.concatenate([pair[:, rows : 2 * rows], pair[:, :rows]], axis=1)
+            across += jnp.where(core == 0, pair[:, : 2 * rows], swapped)
+        left, across = halves(left), halves(across)
         for node in range(nodes):
             columns = slice(node * width, (node + 1) * width)
             image = stacked_dot(left, [whole[:, columns] for whole in held_now])
-            if last:
-                panel_out[:, node, :] = -image[fresh:]
-            image = image[:fresh]
             there = slice(lanes + node * width, lanes + (node + 1) * width)
             new = jnp.concatenate([ref[:, there] for ref in part_refs], axis=0)
-            for whole, part in zip(turned, halves(jnp.concatenate([new, image], axis=0).T)):
-                whole[columns, :] = part
-            right.append([jnp.concatenate(pair, axis=0) for pair in zip(halves(image), halves(new))])
+            new_high, new_low = halves(new)
+            image_high, image_low = halves(image)
+            own = stacked_dot(across, [new_high, new_low])
+            if not begin:
+                own += panel_before[:, columns]
+            if last:
+                panel_out[:, node, :] = -own
+            else:
+                panel_out[:, columns] = own
+            high, low = halves(jnp.concatenate([new, image], axis=0).T)
+            for place, part in enumerate((high, low, high)):
+                turned[columns, 2 * fresh * place : 2 * fresh * (place + 1)] = part
+            for place, part in enumerate((image_high, new_high, image_high, new_high, image_low, new_low)):
+                beside[fresh * place : fresh * (place + 1), columns] = part
         if last:
-            finish(2 * nodes, panel_out, panel_end[0])
+            finish(2 * nodes, panel_out, panel_end)
         for node in range(nodes):
             lower = max(node - 1, 0) * width
-            total = stacked_dot([whole[lower : (node + 1) * width, :] for whole in turned], right[node])
+            columns = slice(node * width, (node + 1) * width)
+            total = jnp.dot(turned[lower : columns.stop, :], beside[:, columns], preferred_element_type=f32)
             diagonals_out[node] = diagonals_ref[node] + total[-width:]
             finish(node, diagonals_out.at[node], diagonals_end.at[node])
             if node > 0:
@@ -309,18 +332,19 @@
         for copy in copies:
             copy.wait()
 
-    operands = [part for _, _, part in arrivals] + ([own] if last else []) + list(state or [])
-    operands += [parents, diagonals]
-    shapes = [jax.ShapeDtypeStruct(array.shape, jnp.float32) for array in (parents, diagonals)]
-    held = [jax.ShapeDtypeStruct((order, nodes * width), bf16)] * 2
-    scratch = [pltpu.VMEM((nodes * width, 2 * fresh), bf16)] * 2
+    operands = [part for _, _, part in arrivals] + list(state or []) + [parents, diagonals]
+    shape_of = jax.ShapeDtypeStruct
+    shapes = [shape_of(parents.shape, f32), shape_of(diagonals.shape, f32)]
+    held = [shape_of((order, nodes * width), bf16)] * 2
+    scratch = [((nodes * width, 6 * fresh), bf16), ((6 * fresh, nodes * width), bf16), ((fresh, order + 128), f32)]
+    scratch = [pltpu.VMEM(*shape) for shape in scratch]
     if last:
-        shapes.append(jax.ShapeDtypeStruct((rows, nodes, width), jnp.float32))
+        shapes.append(shape_of((rows, nodes, width), f32))
         scratch = [pltpu.VMEM(shape.shape, bf16) for shape in held] + scratch
-        scratch += [pltpu.VMEM(array.shape, jnp.float32) for array in shapes]
+        scratch += [pltpu.VMEM(shape.shape, f32) for shape in shapes]
         scratch.append(pltpu.SemaphoreType.DMA((2 * nodes + 1,)))
     else:
-        shapes += [jax.ShapeDtypeStruct((order, order + 128), jnp.float32)] + held
+        shapes += [shape_of((rows, nodes * width), f32), shape_of((order, order + 128), f32)] + held
     results = kernel_call(
         kernel,
         "border" + ("_end" if last else "_begin" if begin else ""),
@@ -328,7 +352,7 @@
         in_specs=in_vmem(len(operands)),
         out_specs=at_home(len(shapes)) if last else in_vmem(len(shapes)),
         scratch_shapes=scratch,
-        limit=24 * 2**20 if last else 16 * 2**20,
+        limit=(24 if last else 16) * 2**20,
     )(*operands)
     return results[:2], results[2:]
 
@@ -346,9 +370,9 @@
         return [(shift, False, value), (shift, True, swap_bit(value, 0))]
 
     turned = anc_blocks[0].T
-    theirs = partner_rows(turned)
-    links = link_chain(after(anc_links, theirs), parent_links, pattern)
-    rows, own = whole_message(turned, swap_bit(theirs, PCOL.bit_length() - 1), links)
+    far_part = far_rows(turned)
+    links = link_chain(after(anc_links, far_part), parent_links, pattern)
+    own = message_of(turned, swap_bit(far_part, PCOL.bit_length() - 1), links)
     totals, state = inner_chain(after(parent_links, own), pivot_inverse), None
     arrivals, pair = both(0, own), [own] * 2
     for step in range(1, far):
@@ -359,7 +383,7 @@
     last, totals = lax.optimization_barrier((pick(pair), totals))
     totals, state = border(arrivals, state, *totals, chips)
     last, totals = lax.optimization_barrier((lax.ppermute(last, "row", across), totals))
-    totals, panels = border(both(far, last), state, *totals, chips, rows)
+    totals, panels = border(both(far, last), state, *totals, chips, True)
     return panels[0], *totals
 
 

time: 71.6 us -> 70.5 us (0.985)
  waiting for transfers between devices: 21.5 us -> 20.4 us
    ppermute x9, waiting for transfers between devices: 4.07 us -> 2.72 us  [swap_bit(): lax.ppermute(value, 'row', [(i, i ^ mask) for i in range(lax.axis_size('r...]
  transfers between devices with their start and end apart: 16 -> 16, of which waited for: 10 -> 10; matrix products, arithmetic and copies ran while one was open for 0% -> 0% of each run, Pallas kernels for 42% -> 43%
where the time goes in v10:
time: 70.5 us; the launch traced here: 70.3 us
  Pallas kernels  35.4 us (50%)
  waiting for transfers between devices  20.4 us (29%)
  starting transfers between devices  12.6 us (18%)
  between operations  0.94 us (1%)
  local copies, waits for them, and re-layouts  0.92 us (1%)
    pallas_call x5, Pallas kernels, border(): kernel_call(kernel, 'border' + ('_end' if last else '_begin' if begin els...  29 us
    ppermute x6, waiting for transfers between devices, move(): lax.ppermute(value, 'row', way)  17.3 us
    ppermute x6, starting transfers between devices, move(): lax.ppermute(value, 'row', way)  6.13 us
    ppermute x9, starting transfers between devices, swap_bit(): lax.ppermute(value, 'row', [(i, i ^ mask) for i in range(lax.axis_size('r...  4.7 us
    pallas_call x1, Pallas kernels, inner_chain(): kernel_call(kernel, 'inner_chain', out_shape=[jax.ShapeDtypeStruct(array....  4.18 us
    ppermute x9, waiting for transfers between devices, swap_bit(): lax.ppermute(value, 'row', [(i, i ^ mask) for i in range(lax.axis_size('r...  2.72 us
    pallas_call x1, Pallas kernels, link_chain(): kernel_call(kernel, 'link_chain', out_shape=jax.ShapeDtypeStruct((rows, n...  1.93 us
    ppermute x1, starting transfers between devices, gather_plan(): lax.ppermute(last, 'row', across)  1.8 us
  transfers between devices with their start and end apart: 16, of which 10 were waited for; matrix products, arithmetic and copies ran while one was open for 0% of the time, Pallas kernels for 43%

profile of v10, /device:TPU:0, one launch (start us, length us, event | category | flops | bytes accessed | tf_op | source)
XLA Modules:
  0.0 70.3 jit_solution(989214869702163327)
XLA Ops:
  0.6 0.9 %copy-done.3 = f32[1,384,96]{1,2,0:T(8,128)S(1)} copy-done((f32[1,384,96]{1,2,0:T(8,128)S(1)}, f32[1,384,96]{1,2,0:T(8,128)}, u32[]{:S(2)}) %copy-start.3) | copy-done | bytes 147480
  1.5 0.1 far_rows.1
  1.7 0.0 copy-start.1
  1.7 4.1 %collective-permute-start = (f32[48,192]{1,0:T(8,128)S(1)}, f32[48,192]{1,0:T(8,128)S(1)}, u32[]{:S(2)}, u32[]{:S(2)}) collective-permute-start(f32[48,192]{1,0:T(8,128)S(1)} %far_rows.1), channel_id=1, source_target_pairs={{0,8},{1,9},{2,10},{3,11},{4,12},{5,13},{6,14},{7,15},{8,0},{9,1},... | collective-permute-start | bytes 110600 | tf_op jit(solution)/shard_map/ppermute | solution.py:31
  5.8 1.9 %link_chain.1.links_ref = f32[48,2048]{1,0:T(8,128)S(1)} custom-call(f32[48,8,256]{2,1,0:T(8,128)S(1)} %copy-done.2, f32[7,256,256]{2,1,0:T(8,128)S(1)} %copy-done, s32[8,6]{1,0:T(8,128)S(1)} %copy-done.4), custom_call_target="tpu_custom_call" | custom-call | tf_op jit(solution)/shard_map/link_chain/pallas_call | solution.py:164
  7.7 0.7 collective-permute-done.far_ref
  8.4 0.1 message.1.refs_0_
  8.5 0.1 collective-permute-start.2
  8.6 1.4 %collective-permute-start.1 = (f32[48,2560]{1,0:T(8,128)S(1)}, f32[48,2560]{1,0:T(8,128)S(1)}, u32[]{:S(2)}, u32[]{:S(2)}) collective-permute-start(f32[48,2560]{1,0:T(8,128)S(1)} %message.1.refs_0_), channel_id=1, source_target_pairs={{0,4},{1,5},{4,8},{5,9},{8,12},{9,13},{12,14},{13,15},{14,10},{15,... | collective-permute-start | bytes 1474568 | tf_op jit(solution)/shard_map/ppermute | solution.py:367
  10.0 0.6 collective-permute-start.5
  10.6 4.2 %inner_chain.1 = (f32[7,256,256]{2,1,0:T(8,128)S(1)}, f32[8,256,256]{2,1,0:T(8,128)S(1)}) custom-call(f32[7,256,256]{2,1,0:T(8,128)S(1)} %copy-done, f32[8,256,256]{2,1,0:T(8,128)S(1)} %copy-done.1), custom_call_target="tpu_custom_call" | custom-call | tf_op jit(solution)/shard_map/inner_chain/pallas_call | solution.py:225
  14.8 4.0 %border_begin.1 = (f32[7,256,256]{2,1,0:T(8,128)S(1)}, f32[8,256,256]{2,1,0:T(8,128)S(1)}, f32[48,2048]{1,0:T(8,128)S(1)}, f32[768,896]{1,0:T(8,128)S(1)}, bf16[...) custom-call(f32[48,2560]{1,0:T(8,128)S(1)} %message.1.refs_0_, f32[48,2560]{1,0:T(8,128)S(1)} %collective-permute-done.2.refs_1_, ...), custom_call_target="tpu_custom_call" | custom-call | tf_op jit(solution)/shard_map/border_begin/pallas_call | solution.py:348
  18.8 3.4 %collective-permute-done.1.refs_0_ = f32[48,2560]{1,0:T(8,128)S(1)} collective-permute-done((f32[48,2560]{1,0:T(8,128)S(1)}, f32[48,2560]{1,0:T(8,128)S(1)}, u32[]{:S(2)}, u32[]{:S(2)}) %collective-permute-start.1) | collective-permute-done | bytes 491552 | tf_op jit(solution)/shard_map/ppermute | solution.py:367
  22.2 1.1 %collective-permute-done.5.refs_2_ = f32[48,2560]{1,0:T(8,128)S(1)} collective-permute-done((f32[48,2560]{1,0:T(8,128)S(1)}, f32[48,2560]{1,0:T(8,128)S(1)}, u32[]{:S(2)}, u32[]{:S(2)}) %collective-permute-start.5) | collective-permute-done | bytes 491552 | tf_op jit(solution)/shard_map/ppermute | solution.py:367
  23.3 1.8 %collective-permute-start.3 = (f32[48,2560]{1,0:T(8,128)S(1)}, f32[48,2560]{1,0:T(8,128)S(1)}, u32[]{:S(2)}, u32[]{:S(2)}) collective-permute-start(f32[48,2560]{1,0:T(8,128)S(1)} %collective-permute-done.1.refs_0_), channel_id=1, source_target_pairs={{0,4},{1,5},{4,8},{5,9},{8,12},{9,13},{12,14},{13,15},{14,10},{15,... | collective-permute-start | bytes 1474568 | tf_op jit(solution)/shard_map/ppermute | solution.py:367
  25.1 0.2 collective-permute-start.9
  25.3 6.7 %border.3 = (f32[7,256,256]{2,1,0:T(8,128)S(1)}, f32[8,256,256]{2,1,0:T(8,128)S(1)}, f32[48,2048]{1,0:T(8,128)S(1)}, f32[768,896]{1,0:T(8,128)S(1)}, bf16[768,20...) custom-call(f32[48,2560]{1,0:T(8,128)S(1)} %collective-permute-done.1.refs_0_, ...), custom_call_target="tpu_custom_call" | custom-call | tf_op jit(solution)/shard_map/border/pallas_call | solution.py:348
  32.0 4.9 %collective-permute-done.3.refs_0_ = f32[48,2560]{1,0:T(8,128)S(1)} collective-permute-done((f32[48,2560]{1,0:T(8,128)S(1)}, f32[48,2560]{1,0:T(8,128)S(1)}, u32[]{:S(2)}, u32[]{:S(2)}) %collective-permute-start.3) | collective-permute-done | bytes 491552 | tf_op jit(solution)/shard_map/ppermute | solution.py:367
  36.9 1.5 %collective-permute-done.9.refs_2_ = f32[48,2560]{1,0:T(8,128)S(1)} collective-permute-done((f32[48,2560]{1,0:T(8,128)S(1)}, f32[48,2560]{1,0:T(8,128)S(1)}, u32[]{:S(2)}, u32[]{:S(2)}) %collective-permute-start.9) | collective-permute-done | bytes 491552 | tf_op jit(solution)/shard_map/ppermute | solution.py:367
  38.5 1.7 %collective-permute-start.7 = (f32[48,2560]{1,0:T(8,128)S(1)}, f32[48,2560]{1,0:T(8,128)S(1)}, u32[]{:S(2)}, u32[]{:S(2)}) collective-permute-start(f32[48,2560]{1,0:T(8,128)S(1)} %collective-permute-done.3.refs_0_), channel_id=1, source_target_pairs={{0,4},{1,5},{4,8},{5,9},{8,12},{9,13},{12,14},{13,15},{14,10},{15,... | collective-permute-start | bytes 1474568 | tf_op jit(solution)/shard_map/ppermute | solution.py:367
  40.2 0.3 collective-permute-start.11
  40.5 6.7 %border.4 = (f32[7,256,256]{2,1,0:T(8,128)S(1)}, f32[8,256,256]{2,1,0:T(8,128)S(1)}, f32[48,2048]{1,0:T(8,128)S(1)}, f32[768,896]{1,0:T(8,128)S(1)}, bf16[768,20...) custom-call(f32[48,2560]{1,0:T(8,128)S(1)} %collective-permute-done.3.refs_0_, ...), custom_call_target="tpu_custom_call" | custom-call | tf_op jit(solution)/shard_map/border/pallas_call | solution.py:348
  47.2 4.9 %collective-permute-done.7.first_ref.refs_0_ = f32[48,2560]{1,0:T(8,128)S(1)} collective-permute-done((f32[48,2560]{1,0:T(8,128)S(1)}, f32[48,2560]{1,0:T(8,128)S(1)}, u32[]{:S(2)}, u32[]{:S(2)}) %collective-permute-start.7) | collective-permute-done | bytes 491552 | tf_op jit(solution)/shard_map/ppermute | solution.py:367
  52.1 1.5 %collective-permute-done.11.second_ref.refs_2_ = f32[48,2560]{1,0:T(8,128)S(1)} collective-permute-done((f32[48,2560]{1,0:T(8,128)S(1)}, f32[48,2560]{1,0:T(8,128)S(1)}, u32[]{:S(2)}, u32[]{:S(2)}) %collective-permute-start.11) | collective-permute-done | bytes 491552 | tf_op jit(solution)/shard_map/ppermute | solution.py:367
  53.6 0.5 collective-permute-start.14
  54.1 0.1 pick.1
  54.1 1.8 %collective-permute-start.12 = (f32[48,2560]{1,0:T(8,128)S(1)}, f32[48,2560]{1,0:T(8,128)S(1)}, u32[]{:S(2)}, u32[]{:S(2)}) collective-permute-start(f32[48,2560]{1,0:T(8,128)S(1)} %pick.1), channel_id=1, source_target_pairs={{0,4},{4,8},{8,12},{12,14},{14,10},{10,6},{6,2},{2,0},{1,3},{5,1},... | collective-permute-start | bytes 1474568 | tf_op jit(solution)/shard_map/ppermute | solution.py:385
  56.0 0.2 collective-permute-done.14.refs_3_
  56.1 6.7 %border.5 = (f32[7,256,256]{2,1,0:T(8,128)S(1)}, f32[8,256,256]{2,1,0:T(8,128)S(1)}, f32[48,2048]{1,0:T(8,128)S(1)}, f32[768,896]{1,0:T(8,128)S(1)}, bf16[768,20...) custom-call(f32[48,2560]{1,0:T(8,128)S(1)} %collective-permute-done.7.first_ref.refs_0_, ...), custom_call_target="tpu_custom_call" | custom-call | tf_op jit(solution)/shard_map/border/pallas_call | solution.py:348
  62.8 0.4 collective-permute-done.12.refs_0_
  63.3 1.9 %collective-permute-done.15.refs_1_ = f32[48,2560]{1,0:T(8,128)S(1)} collective-permute-done((f32[48,2560]{1,0:T(8,128)S(1)}, f32[48,2560]{1,0:T(8,128)S(1)}, u32[]{:S(2)}, u32[]{:S(2)}) %collective-permute-start.15) | collective-permute-done | bytes 491552 | tf_op jit(solution)/shard_map/ppermute | solution.py:31
  65.2 5.0 %border_end.1 = (f32[7,256,256]{2,1,0:T(8,128)}, f32[8,256,256]{2,1,0:T(8,128)}, f32[48,8,256]{2,1,0:T(8,128)}) custom-call(f32[48,2560]{1,0:T(8,128)S(1)} %collective-permute-done.12.refs_0_, f32[48,2560]{1,0:T(8,128)S(1)} %collective-permute-done.15.refs_1_, f32[48,2048]{1,0:T(8,128)S(1)} %get-tuple-element.80.refs_2_, ...), custom_call_target="tpu_custom_call" | custom-call | tf_op jit(solution)/shard_map/border_end/pallas_call | solution.py:348
  (20 shorter events, 0.0 us)
Async XLA Ops:
  0.6 0.9 %copy-start.3 = (f32[1,384,96]{1,2,0:T(8,128)S(1)}, f32[1,384,96]{1,2,0:T(8,128)}, u32[]{:S(2)}) copy-start(f32[1,384,96]{1,2,0:T(8,128)} %param.5) | copy-start | bytes 442372
  1.5 4.2 %copy-start = (f32[7,256,256]{2,1,0:T(8,128)S(1)}, f32[7,256,256]{2,1,0:T(8,128)}, u32[]{:S(2)}) copy-start(f32[7,256,256]{2,1,0:T(8,128)} %parent_ref.2) | copy-start | bytes 5505028
  1.5 4.2 %copy-start.2 = (f32[48,8,256]{2,1,0:T(8,128)S(1)}, f32[48,8,256]{2,1,0:T(8,128)}, u32[]{:S(2)}) copy-start(f32[48,8,256]{2,1,0:T(8,128)} %links_ref) | copy-start | bytes 1179652
  1.5 4.2 %copy-start.4 = (s32[8,6]{1,0:T(8,128)S(1)}, s32[8,6]{1,0:T(8,128)}, u32[]{:S(2)}) copy-start(s32[8,6]{1,0:T(8,128)} %pattern_ref.1) | copy-start | bytes 580
  1.7 9.0 %copy-start.1 = (f32[8,256,256]{2,1,0:T(8,128)S(1)}, f32[8,256,256]{2,1,0:T(8,128)}, u32[]{:S(2)}) copy-start(f32[8,256,256]{2,1,0:T(8,128)} %pivot_ref.1) | copy-start | bytes 6291460
  1.7 6.7 %collective-permute-start = (f32[48,192]{1,0:T(8,128)S(1)}, f32[48,192]{1,0:T(8,128)S(1)}, u32[]{:S(2)}, u32[]{:S(2)}) collective-permute-start(f32[48,192]{1,0:T(8,128)S(1)} %far_rows.1), channel_id=1, source_target_pairs={{0,8},{1,9},{2,10},{3,11},{4,12},{5,13},{6,14},{7,15},{8,0},{9,1},... | collective-permute-start | bytes 110600 | tf_op jit(solution)/shard_map/ppermute | solution.py:31
  8.5 6.3 %collective-permute-start.2 = (f32[48,2560]{1,0:T(8,128)S(1)}, f32[48,2560]{1,0:T(8,128)S(1)}, u32[]{:S(2)}, u32[]{:S(2)}) collective-permute-start(f32[48,2560]{1,0:T(8,128)S(1)} %message.1.refs_0_), channel_id=1, source_target_pairs={{0,1},{1,0},{2,3},{3,2},{4,5},{5,4},{6,7},{7,6},{8,9},{9,8},{10,11... | collective-permute-start | bytes 1474568 | tf_op jit(solution)/shard_map/ppermute | solution.py:31
  8.6 13.6 %collective-permute-start.1 = (f32[48,2560]{1,0:T(8,128)S(1)}, f32[48,2560]{1,0:T(8,128)S(1)}, u32[]{:S(2)}, u32[]{:S(2)}) collective-permute-start(f32[48,2560]{1,0:T(8,128)S(1)} %message.1.refs_0_), channel_id=1, source_target_pairs={{0,4},{1,5},{4,8},{5,9},{8,12},{9,13},{12,14},{13,15},{14,10},{15,... | collective-permute-start | bytes 1474568 | tf_op jit(solution)/shard_map/ppermute | solution.py:367
  10.0 13.3 %collective-permute-start.5 = (f32[48,2560]{1,0:T(8,128)S(1)}, f32[48,2560]{1,0:T(8,128)S(1)}, u32[]{:S(2)}, u32[]{:S(2)}) collective-permute-start(f32[48,2560]{1,0:T(8,128)S(1)} %message.1.refs_0_), channel_id=1, source_target_pairs={{0,2},{1,3},{4,0},{5,1},{8,4},{9,5},{12,8},{13,9},{14,12},{15,13},... | collective-permute-start | bytes 1474568 | tf_op jit(solution)/shard_map/ppermute | solution.py:367
  22.2 3.1 %collective-permute-start.4 = (f32[48,2560]{1,0:T(8,128)S(1)}, f32[48,2560]{1,0:T(8,128)S(1)}, u32[]{:S(2)}, u32[]{:S(2)}) collective-permute-start(f32[48,2560]{1,0:T(8,128)S(1)} %collective-permute-done.1.refs_0_), channel_id=1, source_target_pairs={{0,1},{1,0},{2,3},{3,2},{4,5},{5,4},{6,7},{7,6},{8,9},{9,8},{10,11... | collective-permute-start | bytes 1474568 | tf_op jit(solution)/shard_map/ppermute | solution.py:31
  23.3 2.0 %collective-permute-start.6 = (f32[48,2560]{1,0:T(8,128)S(1)}, f32[48,2560]{1,0:T(8,128)S(1)}, u32[]{:S(2)}, u32[]{:S(2)}) collective-permute-start(f32[48,2560]{1,0:T(8,128)S(1)} %collective-permute-done.5.refs_2_), channel_id=1, source_target_pairs={{0,1},{1,0},{2,3},{3,2},{4,5},{5,4},{6,7},{7,6},{8,9},{9,8},{10,11... | collective-permute-start | bytes 1474568 | tf_op jit(solution)/shard_map/ppermute | solution.py:31
  23.3 13.6 %collective-permute-start.3 = (f32[48,2560]{1,0:T(8,128)S(1)}, f32[48,2560]{1,0:T(8,128)S(1)}, u32[]{:S(2)}, u32[]{:S(2)}) collective-permute-start(f32[48,2560]{1,0:T(8,128)S(1)} %collective-permute-done.1.refs_0_), channel_id=1, source_target_pairs={{0,4},{1,5},{4,8},{5,9},{8,12},{9,13},{12,14},{13,15},{14,10},{15,... | collective-permute-start | bytes 1474568 | tf_op jit(solution)/shard_map/ppermute | solution.py:367
  25.1 13.4 %collective-permute-start.9 = (f32[48,2560]{1,0:T(8,128)S(1)}, f32[48,2560]{1,0:T(8,128)S(1)}, u32[]{:S(2)}, u32[]{:S(2)}) collective-permute-start(f32[48,2560]{1,0:T(8,128)S(1)} %collective-permute-done.5.refs_2_), channel_id=1, source_target_pairs={{0,2},{1,3},{4,0},{5,1},{8,4},{9,5},{12,8},{13,9},{14,12},{15,13},... | collective-permute-start | bytes 1474568 | tf_op jit(solution)/shard_map/ppermute | solution.py:367
  36.9 3.6 %collective-permute-start.8 = (f32[48,2560]{1,0:T(8,128)S(1)}, f32[48,2560]{1,0:T(8,128)S(1)}, u32[]{:S(2)}, u32[]{:S(2)}) collective-permute-start(f32[48,2560]{1,0:T(8,128)S(1)} %collective-permute-done.3.refs_0_), channel_id=1, source_target_pairs={{0,1},{1,0},{2,3},{3,2},{4,5},{5,4},{6,7},{7,6},{8,9},{9,8},{10,11... | collective-permute-start | bytes 1474568 | tf_op jit(solution)/shard_map/ppermute | solution.py:31
  38.5 2.0 %collective-permute-start.10 = (f32[48,2560]{1,0:T(8,128)S(1)}, f32[48,2560]{1,0:T(8,128)S(1)}, u32[]{:S(2)}, u32[]{:S(2)}) collective-permute-start(f32[48,2560]{1,0:T(8,128)S(1)} %collective-permute-done.9.refs_2_), channel_id=1, source_target_pairs={{0,1},{1,0},{2,3},{3,2},{4,5},{5,4},{6,7},{7,6},{8,9},{9,8},{10,11... | collective-permute-start | bytes 1474568 | tf_op jit(solution)/shard_map/ppermute | solution.py:31
  38.5 13.6 %collective-permute-start.7 = (f32[48,2560]{1,0:T(8,128)S(1)}, f32[48,2560]{1,0:T(8,128)S(1)}, u32[]{:S(2)}, u32[]{:S(2)}) collective-permute-start(f32[48,2560]{1,0:T(8,128)S(1)} %collective-permute-done.3.refs_0_), channel_id=1, source_target_pairs={{0,4},{1,5},{4,8},{5,9},{8,12},{9,13},{12,14},{13,15},{14,10},{15,... | collective-permute-start | bytes 1474568 | tf_op jit(solution)/shard_map/ppermute | solution.py:367
  40.2 13.4 %collective-permute-start.11 = (f32[48,2560]{1,0:T(8,128)S(1)}, f32[48,2560]{1,0:T(8,128)S(1)}, u32[]{:S(2)}, u32[]{:S(2)}) collective-permute-start(f32[48,2560]{1,0:T(8,128)S(1)} %collective-permute-done.9.refs_2_), channel_id=1, source_target_pairs={{0,2},{1,3},{4,0},{5,1},{8,4},{9,5},{12,8},{13,9},{14,12},{15,13},... | collective-permute-start | bytes 1474568 | tf_op jit(solution)/shard_map/ppermute | solution.py:367
  53.6 2.4 %collective-permute-start.13 = (f32[48,2560]{1,0:T(8,128)S(1)}, f32[48,2560]{1,0:T(8,128)S(1)}, u32[]{:S(2)}, u32[]{:S(2)}) collective-permute-start(f32[48,2560]{1,0:T(8,128)S(1)} %collective-permute-done.7.first_ref.refs_0_), channel_id=1, source_target_pairs={{0,1},{1,0},{2,3},{3,2},{4,5},{5,4},{6,7},{7,6},{8,9},{9,8},{10,11... | collective-permute-start | bytes 1474568 | tf_op jit(solution)/shard_map/ppermute | solution.py:31
  53.6 2.6 %collective-permute-start.14 = (f32[48,2560]{1,0:T(8,128)S(1)}, f32[48,2560]{1,0:T(8,128)S(1)}, u32[]{:S(2)}, u32[]{:S(2)}) collective-permute-start(f32[48,2560]{1,0:T(8,128)S(1)} %collective-permute-done.11.second_ref.refs_2_), channel_id=1, source_target_pairs={{0,1},{1,0},{2,3},{3,2},{4,5},{5,4},{6,7},{7,6},{8,9},{9,8},{10,11... | collective-permute-start | bytes 1474568 | tf_op jit(solution)/shard_map/ppermute | solution.py:31
  54.1 9.1 %collective-permute-start.12 = (f32[48,2560]{1,0:T(8,128)S(1)}, f32[48,2560]{1,0:T(8,128)S(1)}, u32[]{:S(2)}, u32[]{:S(2)}) collective-permute-start(f32[48,2560]{1,0:T(8,128)S(1)} %pick.1), channel_id=1, source_target_pairs={{0,4},{4,8},{8,12},{12,14},{14,10},{10,6},{6,2},{2,0},{1,3},{5,1},... | collective-permute-start | bytes 1474568 | tf_op jit(solution)/shard_map/ppermute | solution.py:385
  63.3 1.9 %collective-permute-start.15 = (f32[48,2560]{1,0:T(8,128)S(1)}, f32[48,2560]{1,0:T(8,128)S(1)}, u32[]{:S(2)}, u32[]{:S(2)}) collective-permute-start(f32[48,2560]{1,0:T(8,128)S(1)} %collective-permute-done.12.refs_0_), channel_id=1, source_target_pairs={{0,1},{1,0},{2,3},{3,2},{4,5},{5,4},{6,7},{7,6},{8,9},{9,8},{10,11... | collective-permute-start | bytes 1474568 | tf_op jit(solution)/shard_map/ppermute | solution.py:31

commit v11 on v10

--- a/solution.py
+++ b/solution.py
@@ -127,6 +127,19 @@
         in_specs=in_vmem(1),
         out_specs=in_vmem(1)[0],
     )(turned)
+
+
+def split(pair):
+    rows, columns = pair[0].shape
+
+    def kernel(*refs):
+        for place, ref in enumerate(refs[:2]):
+            refs[2 + 2 * place][...] = ref[:, : columns // 2]
+            refs[3 + 2 * place][...] = ref[:, columns // 2 :]
+
+    shape = jax.ShapeDtypeStruct((rows, columns // 2), jnp.float32)
+    parts = kernel_call(kernel, "split", out_shape=[shape] * 4, in_specs=in_vmem(2), out_specs=in_vmem(4))(*pair)
+    return parts[:2], parts[2:]
 
 
 def pick(pair):
@@ -240,10 +253,27 @@
     return 2 * chip + (1 - core if other else core)
 
 
+class Parts:
+    def __init__(self, refs):
+        self.refs = refs
+
+    def columns(self, first, stop):
+        for ref in self.refs:
+            if first < ref.shape[1]:
+                return ref[:, first:stop]
+            first, stop = first - ref.shape[1], stop - ref.shape[1]
+
+    def pieces(self, skip):
+        first = -skip
+        for ref in self.refs:
+            yield max(first, 0), ref[:, max(-first, 0) :]
+            first += ref.shape[1]
+
+
 def border(arrivals, state, parents, diagonals, chips, last=False):
     begin = state is None
     nodes, width, _ = diagonals.shape
-    rows = arrivals[0][2].shape[0]
+    rows = arrivals[0][2][0].shape[0]
     lanes = 2 * SIDE
     order = 2 * chips * rows
     count = len(arrivals)
@@ -253,7 +283,7 @@
     def kernel(*refs):
         refs = list(refs)
         take = lambda number: [refs.pop(0) for _ in range(number)]
-        part_refs = take(count)
+        part_refs = [Parts(take(len(parts))) for _, _, parts in arrivals]
         panel_before, kept_before, *held_before = take(4) if not begin else [None] * 4
         parents_ref, diagonals_ref, parents_out, diagonals_out, panel_out = take(5)
         copies = []
@@ -277,9 +307,10 @@
         for part, whole in enumerate(held_now):
             whole[...] = jnp.zeros(whole.shape, bf16) if begin else held_before[part][...]
         for start, ref in zip(starts, part_refs):
-            for whole, part in zip(held_now, halves(ref[:, lanes:])):
-                whole[pl.ds(start, rows), :] = part
-        sent = [sent_rows(ref[:, :lanes], owner, rows) for owner, ref in zip(owners, part_refs)]
+            for first, part in ref.pieces(lanes):
+                for whole, half in zip(held_now, halves(part)):
+                    whole[pl.ds(start, rows), first : first + part.shape[1]] = half
+        sent = [sent_rows(ref.columns(0, lanes), owner, rows) for owner, ref in zip(owners, part_refs)]
         if not last:
             kept_now[...] = jnp.zeros(kept_now.shape, f32) if begin else kept_before[...]
             for start, part in zip(starts, sent):
@@ -302,8 +333,8 @@
         for node in range(nodes):
             columns = slice(node * width, (node + 1) * width)
             image = stacked_dot(left, [whole[:, columns] for whole in held_now])
-            there = slice(lanes + node * width, lanes + (node + 1) * width)
-            new = jnp.concatenate([ref[:, there] for ref in part_refs], axis=0)
+            first = lanes + node * width
+            new = jnp.concatenate([ref.columns(first, first + width) for ref in part_refs], axis=0)
             new_high, new_low = halves(new)
             image_high, image_low = halves(image)
             own = stacked_dot(across, [new_high, new_low])
@@ -332,7 +363,7 @@
         for copy in copies:
             copy.wait()
 
-    operands = [part for _, _, part in arrivals] + list(state or []) + [parents, diagonals]
+    operands = [part for _, _, parts in arrivals for part in parts] + list(state or []) + [parents, diagonals]
     shape_of = jax.ShapeDtypeStruct
     shapes = [shape_of(parents.shape, f32), shape_of(diagonals.shape, f32)]
     held = [shape_of((order, nodes * width), bf16)] * 2
@@ -366,8 +397,9 @@
     def move(pair):
         return [lax.ppermute(value, "row", way) for value, way in zip(pair, (ahead, behind))]
 
-    def both(shift, value):
-        return [(shift, False, value), (shift, True, swap_bit(value, 0))]
+    def both(shift, value, parts=None):
+        parts = [swap_bit(part, 0) for part in parts or [value]]
+        return [(shift, False, [value]), (shift, True, parts)]
 
     turned = anc_blocks[0].T
     far_part = far_rows(turned)
@@ -379,7 +411,8 @@
         pair = move(pair)
         totals, state = border(arrivals, state, *totals, chips)
         pair = [after(value, *totals) for value in pair]
-        arrivals = both(-step, pair[0]) + both(step, pair[1])
+        parts = split(pair)
+        arrivals = both(-step, pair[0], parts[0]) + both(step, pair[1], parts[1])
     last, totals = lax.optimization_barrier((pick(pair), totals))
     totals, state = border(arrivals, state, *totals, chips)
     last, totals = lax.optimization_barrier((lax.ppermute(last, "row", across), totals))

time: 70.5 us -> 72.3 us (1.026)
  starting transfers between devices: 12.6 us -> 14.7 us
    ppermute x9 -> x15, waiting for transfers between devices: 2.72 us -> 7.3 us  [swap_bit(): lax.ppermute(value, 'row', [(i, i ^ mask) for i in range(lax.axis_size('r...]
    ppermute x6, waiting for transfers between devices: 17.3 us -> 12.8 us  [move(): lax.ppermute(value, 'row', way)]
    ppermute x9 -> x15, starting transfers between devices: 4.7 us -> 6.65 us  [swap_bit(): lax.ppermute(value, 'row', [(i, i ^ mask) for i in range(lax.axis_size('r...]
  transfers between devices with their start and end apart: 16 -> 22, of which waited for: 10 -> 18; matrix products, arithmetic and copies ran while one was open for 0% -> 0% of each run, Pallas kernels for 43% -> 42%
where the time goes in v11:
time: 72.3 us; the launch traced here: 72.2 us
  Pallas kernels  35.5 us (49%)
  waiting for transfers between devices  20.1 us (28%)
  starting transfers between devices  14.7 us (20%)
  between operations  0.99 us (1%)
  local copies, waits for them, and re-layouts  0.92 us (1%)
    pallas_call x5, Pallas kernels, border(): kernel_call(kernel, 'border' + ('_end' if last else '_begin' if begin els...  29 us
    ppermute x6, waiting for transfers between devices, move(): lax.ppermute(value, 'row', way)  12.8 us
    ppermute x15, waiting for transfers between devices, swap_bit(): lax.ppermute(value, 'row', [(i, i ^ mask) for i in range(lax.axis_size('r...  7.3 us
    ppermute x15, starting transfers between devices, swap_bit(): lax.ppermute(value, 'row', [(i, i ^ mask) for i in range(lax.axis_size('r...  6.65 us
    ppermute x6, starting transfers between devices, move(): lax.ppermute(value, 'row', way)  6.23 us
    pallas_call x1, Pallas kernels, inner_chain(): kernel_call(kernel, 'inner_chain', out_shape=[jax.ShapeDtypeStruct(array....  4.18 us
    pallas_call x1, Pallas kernels, link_chain(): kernel_call(kernel, 'link_chain', out_shape=jax.ShapeDtypeStruct((rows, n...  1.93 us
    ppermute x1, starting transfers between devices, gather_plan(): lax.ppermute(last, 'row', across)  1.8 us
  transfers between devices with their start and end apart: 22, of which 18 were waited for; matrix products, arithmetic and copies ran while one was open for 0% of the time, Pallas kernels for 42%

profile of v11, /device:TPU:0, one launch (start us, length us, event | category | flops | bytes accessed | tf_op | source)
XLA Modules:
  0.0 72.2 jit_solution(3540468514449960582)
XLA Ops:
  0.6 0.9 %copy-done.3 = f32[1,384,96]{1,2,0:T(8,128)S(1)} copy-done((f32[1,384,96]{1,2,0:T(8,128)S(1)}, f32[1,384,96]{1,2,0:T(8,128)}, u32[]{:S(2)}) %copy-start.3) | copy-done | bytes 147480
  1.7 4.1 %collective-permute-start = (f32[48,192]{1,0:T(8,128)S(1)}, f32[48,192]{1,0:T(8,128)S(1)}, u32[]{:S(2)}, u32[]{:S(2)}) collective-permute-start(f32[48,192]{1,0:T(8,128)S(1)} %far_rows.1), channel_id=1, source_target_pairs={{0,8},{1,9},{2,10},{3,11},{4,12},{5,13},{6,14},{7,15},{8,0},{9,1},... | collective-permute-start | bytes 110600 | tf_op jit(solution)/shard_map/ppermute | solution.py:31
  5.8 1.9 %link_chain.1.links_ref = f32[48,2048]{1,0:T(8,128)S(1)} custom-call(f32[48,8,256]{2,1,0:T(8,128)S(1)} %copy-done.2, f32[7,256,256]{2,1,0:T(8,128)S(1)} %copy-done, s32[8,6]{1,0:T(8,128)S(1)} %copy-done.4), custom_call_target="tpu_custom_call" | custom-call | tf_op jit(solution)/shard_map/link_chain/pallas_call | solution.py:177
  7.7 0.7 collective-permute-done.far_ref
  8.6 1.4 %collective-permute-start.1 = (f32[48,2560]{1,0:T(8,128)S(1)}, f32[48,2560]{1,0:T(8,128)S(1)}, u32[]{:S(2)}, u32[]{:S(2)}) collective-permute-start(f32[48,2560]{1,0:T(8,128)S(1)} %message.1.refs_0_), channel_id=1, source_target_pairs={{0,4},{1,5},{4,8},{5,9},{8,12},{9,13},{12,14},{13,15},{14,10},{15,... | collective-permute-start | bytes 1474568 | tf_op jit(solution)/shard_map/ppermute | solution.py:398
  10.0 0.6 collective-permute-start.4
  10.6 4.2 %inner_chain.1 = (f32[7,256,256]{2,1,0:T(8,128)S(1)}, f32[8,256,256]{2,1,0:T(8,128)S(1)}) custom-call(f32[7,256,256]{2,1,0:T(8,128)S(1)} %copy-done, f32[8,256,256]{2,1,0:T(8,128)S(1)} %copy-done.1), custom_call_target="tpu_custom_call" | custom-call | tf_op jit(solution)/shard_map/inner_chain/pallas_call | solution.py:238
  14.8 4.0 %border_begin.1 = (f32[7,256,256]{2,1,0:T(8,128)S(1)}, f32[8,256,256]{2,1,0:T(8,128)S(1)}, f32[48,2048]{1,0:T(8,128)S(1)}, f32[768,896]{1,0:T(8,128)S(1)}, bf16[...) custom-call(f32[48,2560]{1,0:T(8,128)S(1)} %message.1.refs_0_, f32[48,2560]{1,0:T(8,128)S(1)} %collective-permute-done.2.refs_1_, ...), custom_call_target="tpu_custom_call" | custom-call | tf_op jit(solution)/shard_map/border_begin/pallas_call | solution.py:379
  18.8 3.4 %collective-permute-done.1.refs_0_ = f32[48,2560]{1,0:T(8,128)S(1)} collective-permute-done((f32[48,2560]{1,0:T(8,128)S(1)}, f32[48,2560]{1,0:T(8,128)S(1)}, u32[]{:S(2)}, u32[]{:S(2)}) %collective-permute-start.1) | collective-permute-done | bytes 491552 | tf_op jit(solution)/shard_map/ppermute | solution.py:398
  22.2 1.1 %collective-permute-done.4.refs_1_.refs_3_ = f32[48,2560]{1,0:T(8,128)S(1)} collective-permute-done((f32[48,2560]{1,0:T(8,128)S(1)}, f32[48,2560]{1,0:T(8,128)S(1)}, u32[]{:S(2)}, u32[]{:S(2)}) %collective-permute-start.4) | collective-permute-done | bytes 491552 | tf_op jit(solution)/shard_map/ppermute | solution.py:398
  23.4 1.9 %collective-permute-start.3 = (f32[48,2560]{1,0:T(8,128)S(1)}, f32[48,2560]{1,0:T(8,128)S(1)}, u32[]{:S(2)}, u32[]{:S(2)}) collective-permute-start(f32[48,2560]{1,0:T(8,128)S(1)} %collective-permute-done.1.refs_0_), channel_id=1, source_target_pairs={{0,4},{1,5},{4,8},{5,9},{8,12},{9,13},{12,14},{13,15},{14,10},{15,... | collective-permute-start | bytes 1474568 | tf_op jit(solution)/shard_map/ppermute | solution.py:398
  25.5 0.5 collective-permute-start.7
  26.0 1.0 %collective-permute-done.6.refs_2_ = f32[48,1280]{1,0:T(8,128)S(1)} collective-permute-done((f32[48,1280]{1,0:T(8,128)S(1)}, f32[48,1280]{1,0:T(8,128)S(1)}, u32[]{:S(2)}, u32[]{:S(2)}) %collective-permute-start.6) | collective-permute-done | bytes 245792 | tf_op jit(solution)/shard_map/ppermute | solution.py:31
  27.0 0.4 collective-permute-done.7.refs_4_
  27.4 0.4 collective-permute-done.8.refs_5_
  27.7 6.7 %border.3 = (f32[7,256,256]{2,1,0:T(8,128)S(1)}, f32[8,256,256]{2,1,0:T(8,128)S(1)}, f32[48,2048]{1,0:T(8,128)S(1)}, f32[768,896]{1,0:T(8,128)S(1)}, bf16[768,20...) custom-call(f32[48,2560]{1,0:T(8,128)S(1)} %collective-permute-done.1.refs_0_, ...), custom_call_target="tpu_custom_call" | custom-call | tf_op jit(solution)/shard_map/border/pallas_call | solution.py:379
  34.4 2.6 %collective-permute-done.3.refs_0_ = f32[48,2560]{1,0:T(8,128)S(1)} collective-permute-done((f32[48,2560]{1,0:T(8,128)S(1)}, f32[48,2560]{1,0:T(8,128)S(1)}, u32[]{:S(2)}, u32[]{:S(2)}) %collective-permute-start.3) | collective-permute-done | bytes 491552 | tf_op jit(solution)/shard_map/ppermute | solution.py:398
  37.1 1.5 %collective-permute-done.10.refs_1_.refs_3_ = f32[48,2560]{1,0:T(8,128)S(1)} collective-permute-done((f32[48,2560]{1,0:T(8,128)S(1)}, f32[48,2560]{1,0:T(8,128)S(1)}, u32[]{:S(2)}, u32[]{:S(2)}) %collective-permute-start.10) | collective-permute-done | bytes 491552 | tf_op jit(solution)/shard_map/ppermute | solution.py:398
  38.8 1.8 %collective-permute-start.9 = (f32[48,2560]{1,0:T(8,128)S(1)}, f32[48,2560]{1,0:T(8,128)S(1)}, u32[]{:S(2)}, u32[]{:S(2)}) collective-permute-start(f32[48,2560]{1,0:T(8,128)S(1)} %collective-permute-done.3.refs_0_), channel_id=1, source_target_pairs={{0,4},{1,5},{4,8},{5,9},{8,12},{9,13},{12,14},{13,15},{14,10},{15,... | collective-permute-start | bytes 1474568 | tf_op jit(solution)/shard_map/ppermute | solution.py:398
  40.8 0.5 collective-permute-start.13
  41.4 1.0 %collective-permute-done.12.refs_2_ = f32[48,1280]{1,0:T(8,128)S(1)} collective-permute-done((f32[48,1280]{1,0:T(8,128)S(1)}, f32[48,1280]{1,0:T(8,128)S(1)}, u32[]{:S(2)}, u32[]{:S(2)}) %collective-permute-start.12) | collective-permute-done | bytes 245792 | tf_op jit(solution)/shard_map/ppermute | solution.py:31
  42.3 0.4 collective-permute-done.13.refs_4_
  43.0 6.7 %border.4 = (f32[7,256,256]{2,1,0:T(8,128)S(1)}, f32[8,256,256]{2,1,0:T(8,128)S(1)}, f32[48,2048]{1,0:T(8,128)S(1)}, f32[768,896]{1,0:T(8,128)S(1)}, bf16[768,20...) custom-call(f32[48,2560]{1,0:T(8,128)S(1)} %collective-permute-done.3.refs_0_, ...), custom_call_target="tpu_custom_call" | custom-call | tf_op jit(solution)/shard_map/border/pallas_call | solution.py:379
  49.7 2.6 %collective-permute-done.9.first_ref.refs_0_ = f32[48,2560]{1,0:T(8,128)S(1)} collective-permute-done((f32[48,2560]{1,0:T(8,128)S(1)}, f32[48,2560]{1,0:T(8,128)S(1)}, u32[]{:S(2)}, u32[]{:S(2)}) %collective-permute-start.9) | collective-permute-done | bytes 491552 | tf_op jit(solution)/shard_map/ppermute | solution.py:398
  52.4 1.5 %collective-permute-done.15.second_ref.refs_1_.refs_3_ = f32[48,2560]{1,0:T(8,128)S(1)} collective-permute-done((f32[48,2560]{1,0:T(8,128)S(1)}, f32[48,2560]{1,0:T(8,128)S(1)}, u32[]{:S(2)}, u32[]{:S(2)}) %collective-permute-start.15) | collective-permute-done | bytes 491552 | tf_op jit(solution)/shard_map/ppermute | solution.py:398
  53.9 1.8 %collective-permute-start.16 = (f32[48,2560]{1,0:T(8,128)S(1)}, f32[48,2560]{1,0:T(8,128)S(1)}, u32[]{:S(2)}, u32[]{:S(2)}) collective-permute-start(f32[48,2560]{1,0:T(8,128)S(1)} %pick.1), channel_id=1, source_target_pairs={{0,4},{4,8},{8,12},{12,14},{14,10},{10,6},{6,2},{2,0},{1,3},{5,1},... | collective-permute-start | bytes 1474568 | tf_op jit(solution)/shard_map/ppermute | solution.py:418
  55.9 0.5 collective-permute-start.18
  56.4 0.4 collective-permute-start.20
  56.9 0.5 collective-permute-done.17.refs_1_
  58.4 6.7 %border.5 = (f32[7,256,256]{2,1,0:T(8,128)S(1)}, f32[8,256,256]{2,1,0:T(8,128)S(1)}, f32[48,2048]{1,0:T(8,128)S(1)}, f32[768,896]{1,0:T(8,128)S(1)}, bf16[768,20...) custom-call(f32[48,2560]{1,0:T(8,128)S(1)} %collective-permute-done.9.first_ref.refs_0_, ...), custom_call_target="tpu_custom_call" | custom-call | tf_op jit(solution)/shard_map/border/pallas_call | solution.py:379
  65.3 1.7 %collective-permute-done.21.refs_1_ = f32[48,2560]{1,0:T(8,128)S(1)} collective-permute-done((f32[48,2560]{1,0:T(8,128)S(1)}, f32[48,2560]{1,0:T(8,128)S(1)}, u32[]{:S(2)}, u32[]{:S(2)}) %collective-permute-start.21) | collective-permute-done | bytes 491552 | tf_op jit(solution)/shard_map/ppermute | solution.py:31
  67.0 5.0 %border_end.1 = (f32[7,256,256]{2,1,0:T(8,128)}, f32[8,256,256]{2,1,0:T(8,128)}, f32[48,8,256]{2,1,0:T(8,128)}) custom-call(f32[48,2560]{1,0:T(8,128)S(1)} %collective-permute-done.16.refs_0_, f32[48,2560]{1,0:T(8,128)S(1)} %collective-permute-done.21.refs_1_, f32[48,2048]{1,0:T(8,128)S(1)} %get-tuple-element.104.refs_2_, ...), custom_call_target="tpu_custom_call" | custom-call | tf_op jit(solution)/shard_map/border_end/pallas_call | solution.py:379
  (35 shorter events, 3.0 us)
Async XLA Ops:
  0.6 0.9 %copy-start.3 = (f32[1,384,96]{1,2,0:T(8,128)S(1)}, f32[1,384,96]{1,2,0:T(8,128)}, u32[]{:S(2)}) copy-start(f32[1,384,96]{1,2,0:T(8,128)} %param.5) | copy-start | bytes 442372
  1.5 4.2 %copy-start = (f32[7,256,256]{2,1,0:T(8,128)S(1)}, f32[7,256,256]{2,1,0:T(8,128)}, u32[]{:S(2)}) copy-start(f32[7,256,256]{2,1,0:T(8,128)} %parent_ref.2) | copy-start | bytes 5505028
  1.5 4.2 %copy-start.2 = (f32[48,8,256]{2,1,0:T(8,128)S(1)}, f32[48,8,256]{2,1,0:T(8,128)}, u32[]{:S(2)}) copy-start(f32[48,8,256]{2,1,0:T(8,128)} %links_ref) | copy-start | bytes 1179652
  1.5 4.2 %copy-start.4 = (s32[8,6]{1,0:T(8,128)S(1)}, s32[8,6]{1,0:T(8,128)}, u32[]{:S(2)}) copy-start(s32[8,6]{1,0:T(8,128)} %pattern_ref.1) | copy-start | bytes 580
  1.7 9.0 %copy-start.1 = (f32[8,256,256]{2,1,0:T(8,128)S(1)}, f32[8,256,256]{2,1,0:T(8,128)}, u32[]{:S(2)}) copy-start(f32[8,256,256]{2,1,0:T(8,128)} %pivot_ref.1) | copy-start | bytes 6291460
  1.7 6.7 %collective-permute-start = (f32[48,192]{1,0:T(8,128)S(1)}, f32[48,192]{1,0:T(8,128)S(1)}, u32[]{:S(2)}, u32[]{:S(2)}) collective-permute-start(f32[48,192]{1,0:T(8,128)S(1)} %far_rows.1), channel_id=1, source_target_pairs={{0,8},{1,9},{2,10},{3,11},{4,12},{5,13},{6,14},{7,15},{8,0},{9,1},... | collective-permute-start | bytes 110600 | tf_op jit(solution)/shard_map/ppermute | solution.py:31
  8.5 6.3 %collective-permute-start.2 = (f32[48,2560]{1,0:T(8,128)S(1)}, f32[48,2560]{1,0:T(8,128)S(1)}, u32[]{:S(2)}, u32[]{:S(2)}) collective-permute-start(f32[48,2560]{1,0:T(8,128)S(1)} %message.1.refs_0_), channel_id=1, source_target_pairs={{0,1},{1,0},{2,3},{3,2},{4,5},{5,4},{6,7},{7,6},{8,9},{9,8},{10,11... | collective-permute-start | bytes 1474568 | tf_op jit(solution)/shard_map/ppermute | solution.py:31
  8.6 13.6 %collective-permute-start.1 = (f32[48,2560]{1,0:T(8,128)S(1)}, f32[48,2560]{1,0:T(8,128)S(1)}, u32[]{:S(2)}, u32[]{:S(2)}) collective-permute-start(f32[48,2560]{1,0:T(8,128)S(1)} %message.1.refs_0_), channel_id=1, source_target_pairs={{0,4},{1,5},{4,8},{5,9},{8,12},{9,13},{12,14},{13,15},{14,10},{15,... | collective-permute-start | bytes 1474568 | tf_op jit(solution)/shard_map/ppermute | solution.py:398
  10.0 13.3 %collective-permute-start.4 = (f32[48,2560]{1,0:T(8,128)S(1)}, f32[48,2560]{1,0:T(8,128)S(1)}, u32[]{:S(2)}, u32[]{:S(2)}) collective-permute-start(f32[48,2560]{1,0:T(8,128)S(1)} %message.1.refs_0_), channel_id=1, source_target_pairs={{0,2},{1,3},{4,0},{5,1},{8,4},{9,5},{12,8},{13,9},{14,12},{15,13},... | collective-permute-start | bytes 1474568 | tf_op jit(solution)/shard_map/ppermute | solution.py:398
  23.4 2.7 %collective-permute-start.5 = (f32[48,1280]{1,0:T(8,128)S(1)}, f32[48,1280]{1,0:T(8,128)S(1)}, u32[]{:S(2)}, u32[]{:S(2)}) collective-permute-start(f32[48,1280]{1,0:T(8,128)S(1)} %get-tuple-element.66), channel_id=1, source_target_pairs={{0,1},{1,0},{2,3},{3,2},{4,5},{5,4},{6,7},{7,6},{8,9},{9,8},{10,11... | collective-permute-start | bytes 737288 | tf_op jit(solution)/shard_map/ppermute | solution.py:31
  23.4 13.6 %collective-permute-start.3 = (f32[48,2560]{1,0:T(8,128)S(1)}, f32[48,2560]{1,0:T(8,128)S(1)}, u32[]{:S(2)}, u32[]{:S(2)}) collective-permute-start(f32[48,2560]{1,0:T(8,128)S(1)} %collective-permute-done.1.refs_0_), channel_id=1, source_target_pairs={{0,4},{1,5},{4,8},{5,9},{8,12},{9,13},{12,14},{13,15},{14,10},{15,... | collective-permute-start | bytes 1474568 | tf_op jit(solution)/shard_map/ppermute | solution.py:398
  25.3 13.3 %collective-permute-start.10 = (f32[48,2560]{1,0:T(8,128)S(1)}, f32[48,2560]{1,0:T(8,128)S(1)}, u32[]{:S(2)}, u32[]{:S(2)}) collective-permute-start(f32[48,2560]{1,0:T(8,128)S(1)} %collective-permute-done.4.refs_1_.refs_3_), channel_id=1, source_target_pairs={{0,2},{1,3},{4,0},{5,1},{8,4},{9,5},{12,8},{13,9},{14,12},{15,13},... | collective-permute-start | bytes 1474568 | tf_op jit(solution)/shard_map/ppermute | solution.py:398
  25.5 1.5 %collective-permute-start.6 = (f32[48,1280]{1,0:T(8,128)S(1)}, f32[48,1280]{1,0:T(8,128)S(1)}, u32[]{:S(2)}, u32[]{:S(2)}) collective-permute-start(f32[48,1280]{1,0:T(8,128)S(1)} %get-tuple-element.67), channel_id=1, source_target_pairs={{0,1},{1,0},{2,3},{3,2},{4,5},{5,4},{6,7},{7,6},{8,9},{9,8},{10,11... | collective-permute-start | bytes 737288 | tf_op jit(solution)/shard_map/ppermute | solution.py:31
  25.5 1.9 %collective-permute-start.7 = (f32[48,1280]{1,0:T(8,128)S(1)}, f32[48,1280]{1,0:T(8,128)S(1)}, u32[]{:S(2)}, u32[]{:S(2)}) collective-permute-start(f32[48,1280]{1,0:T(8,128)S(1)} %get-tuple-element.68), channel_id=1, source_target_pairs={{0,1},{1,0},{2,3},{3,2},{4,5},{5,4},{6,7},{7,6},{8,9},{9,8},{10,11... | collective-permute-start | bytes 737288 | tf_op jit(solution)/shard_map/ppermute | solution.py:31
  26.0 1.7 %collective-permute-start.8 = (f32[48,1280]{1,0:T(8,128)S(1)}, f32[48,1280]{1,0:T(8,128)S(1)}, u32[]{:S(2)}, u32[]{:S(2)}) collective-permute-start(f32[48,1280]{1,0:T(8,128)S(1)} %get-tuple-element.69), channel_id=1, source_target_pairs={{0,1},{1,0},{2,3},{3,2},{4,5},{5,4},{6,7},{7,6},{8,9},{9,8},{10,11... | collective-permute-start | bytes 737288 | tf_op jit(solution)/shard_map/ppermute | solution.py:31
  38.7 2.7 %collective-permute-start.11 = (f32[48,1280]{1,0:T(8,128)S(1)}, f32[48,1280]{1,0:T(8,128)S(1)}, u32[]{:S(2)}, u32[]{:S(2)}) collective-permute-start(f32[48,1280]{1,0:T(8,128)S(1)} %get-tuple-element.78), channel_id=1, source_target_pairs={{0,1},{1,0},{2,3},{3,2},{4,5},{5,4},{6,7},{7,6},{8,9},{9,8},{10,11... | collective-permute-start | bytes 737288 | tf_op jit(solution)/shard_map/ppermute | solution.py:31
  38.8 13.6 %collective-permute-start.9 = (f32[48,2560]{1,0:T(8,128)S(1)}, f32[48,2560]{1,0:T(8,128)S(1)}, u32[]{:S(2)}, u32[]{:S(2)}) collective-permute-start(f32[48,2560]{1,0:T(8,128)S(1)} %collective-permute-done.3.refs_0_), channel_id=1, source_target_pairs={{0,4},{1,5},{4,8},{5,9},{8,12},{9,13},{12,14},{13,15},{14,10},{15,... | collective-permute-start | bytes 1474568 | tf_op jit(solution)/shard_map/ppermute | solution.py:398
  40.5 13.3 %collective-permute-start.15 = (f32[48,2560]{1,0:T(8,128)S(1)}, f32[48,2560]{1,0:T(8,128)S(1)}, u32[]{:S(2)}, u32[]{:S(2)}) collective-permute-start(f32[48,2560]{1,0:T(8,128)S(1)} %collective-permute-done.10.refs_1_.refs_3_), channel_id=1, source_target_pairs={{0,2},{1,3},{4,0},{5,1},{8,4},{9,5},{12,8},{13,9},{14,12},{15,13},... | collective-permute-start | bytes 1474568 | tf_op jit(solution)/shard_map/ppermute | solution.py:398
  40.8 1.5 %collective-permute-start.12 = (f32[48,1280]{1,0:T(8,128)S(1)}, f32[48,1280]{1,0:T(8,128)S(1)}, u32[]{:S(2)}, u32[]{:S(2)}) collective-permute-start(f32[48,1280]{1,0:T(8,128)S(1)} %get-tuple-element.79), channel_id=1, source_target_pairs={{0,1},{1,0},{2,3},{3,2},{4,5},{5,4},{6,7},{7,6},{8,9},{9,8},{10,11... | collective-permute-start | bytes 737288 | tf_op jit(solution)/shard_map/ppermute | solution.py:31
  40.8 1.9 %collective-permute-start.13 = (f32[48,1280]{1,0:T(8,128)S(1)}, f32[48,1280]{1,0:T(8,128)S(1)}, u32[]{:S(2)}, u32[]{:S(2)}) collective-permute-start(f32[48,1280]{1,0:T(8,128)S(1)} %get-tuple-element.80), channel_id=1, source_target_pairs={{0,1},{1,0},{2,3},{3,2},{4,5},{5,4},{6,7},{7,6},{8,9},{9,8},{10,11... | collective-permute-start | bytes 737288 | tf_op jit(solution)/shard_map/ppermute | solution.py:31
  41.3 1.7 %collective-permute-start.14 = (f32[48,1280]{1,0:T(8,128)S(1)}, f32[48,1280]{1,0:T(8,128)S(1)}, u32[]{:S(2)}, u32[]{:S(2)}) collective-permute-start(f32[48,1280]{1,0:T(8,128)S(1)} %get-tuple-element.81), channel_id=1, source_target_pairs={{0,1},{1,0},{2,3},{3,2},{4,5},{5,4},{6,7},{7,6},{8,9},{9,8},{10,11... | collective-permute-start | bytes 737288 | tf_op jit(solution)/shard_map/ppermute | solution.py:31
  53.9 11.2 %collective-permute-start.16 = (f32[48,2560]{1,0:T(8,128)S(1)}, f32[48,2560]{1,0:T(8,128)S(1)}, u32[]{:S(2)}, u32[]{:S(2)}) collective-permute-start(f32[48,2560]{1,0:T(8,128)S(1)} %pick.1), channel_id=1, source_target_pairs={{0,4},{4,8},{8,12},{12,14},{14,10},{10,6},{6,2},{2,0},{1,3},{5,1},... | collective-permute-start | bytes 1474568 | tf_op jit(solution)/shard_map/ppermute | solution.py:418
  55.8 1.6 %collective-permute-start.17 = (f32[48,1280]{1,0:T(8,128)S(1)}, f32[48,1280]{1,0:T(8,128)S(1)}, u32[]{:S(2)}, u32[]{:S(2)}) collective-permute-start(f32[48,1280]{1,0:T(8,128)S(1)} %get-tuple-element.91), channel_id=1, source_target_pairs={{0,1},{1,0},{2,3},{3,2},{4,5},{5,4},{6,7},{7,6},{8,9},{9,8},{10,11... | collective-permute-start | bytes 737288 | tf_op jit(solution)/shard_map/ppermute | solution.py:31
  55.9 1.9 %collective-permute-start.18 = (f32[48,1280]{1,0:T(8,128)S(1)}, f32[48,1280]{1,0:T(8,128)S(1)}, u32[]{:S(2)}, u32[]{:S(2)}) collective-permute-start(f32[48,1280]{1,0:T(8,128)S(1)} %get-tuple-element.92), channel_id=1, source_target_pairs={{0,1},{1,0},{2,3},{3,2},{4,5},{5,4},{6,7},{7,6},{8,9},{9,8},{10,11... | collective-permute-start | bytes 737288 | tf_op jit(solution)/shard_map/ppermute | solution.py:31
  56.3 1.7 %collective-permute-start.19 = (f32[48,1280]{1,0:T(8,128)S(1)}, f32[48,1280]{1,0:T(8,128)S(1)}, u32[]{:S(2)}, u32[]{:S(2)}) collective-permute-start(f32[48,1280]{1,0:T(8,128)S(1)} %get-tuple-element.93), channel_id=1, source_target_pairs={{0,1},{1,0},{2,3},{3,2},{4,5},{5,4},{6,7},{7,6},{8,9},{9,8},{10,11... | collective-permute-start | bytes 737288 | tf_op jit(solution)/shard_map/ppermute | solution.py:31
  56.4 2.0 %collective-permute-start.20 = (f32[48,1280]{1,0:T(8,128)S(1)}, f32[48,1280]{1,0:T(8,128)S(1)}, u32[]{:S(2)}, u32[]{:S(2)}) collective-permute-start(f32[48,1280]{1,0:T(8,128)S(1)} %get-tuple-element.94), channel_id=1, source_target_pairs={{0,1},{1,0},{2,3},{3,2},{4,5},{5,4},{6,7},{7,6},{8,9},{9,8},{10,11... | collective-permute-start | bytes 737288 | tf_op jit(solution)/shard_map/ppermute | solution.py:31
  65.1 1.9 %collective-permute-start.21 = (f32[48,2560]{1,0:T(8,128)S(1)}, f32[48,2560]{1,0:T(8,128)S(1)}, u32[]{:S(2)}, u32[]{:S(2)}) collective-permute-start(f32[48,2560]{1,0:T(8,128)S(1)} %collective-permute-done.16.refs_0_), channel_id=1, source_target_pairs={{0,1},{1,0},{2,3},{3,2},{4,5},{5,4},{6,7},{7,6},{8,9},{9,8},{10,11... | collective-permute-start | bytes 1474568 | tf_op jit(solution)/shard_map/ppermute | solution.py:31

commit v12 on v10

--- a/solution.py
+++ b/solution.py
@@ -274,22 +274,14 @@
         owners = [ring_owner(me, chips, shift, other) for shift, other, _ in arrivals]
         starts = [pl.multiple_of(owner * rows, 16) for owner in owners]
 
-        for part, whole in enumerate(held_now):
-            whole[...] = jnp.zeros(whole.shape, bf16) if begin else held_before[part][...]
-        for start, ref in zip(starts, part_refs):
-            for whole, part in zip(held_now, halves(ref[:, lanes:])):
-                whole[pl.ds(start, rows), :] = part
         sent = [sent_rows(ref[:, :lanes], owner, rows) for owner, ref in zip(owners, part_refs)]
-        if not last:
-            kept_now[...] = jnp.zeros(kept_now.shape, f32) if begin else kept_before[...]
-            for start, part in zip(starts, sent):
-                kept_now[pl.ds(start, rows), :order] = part
+        ahead = list(sent)
         if not begin:
             for pair in range(0, count, 2):
                 back = columns_at(kept_before, lax.div(owners[pair], 2) * (2 * rows), 2 * rows).T
                 first, second = back[:rows], back[rows : 2 * rows]
-                sent[pair] += jnp.where(core == 0, first, second)
-                sent[pair + 1] += jnp.where(core == 0, second, first)
+                sent[pair] = sent[pair] + jnp.where(core == 0, first, second)
+                sent[pair + 1] = sent[pair + 1] + jnp.where(core == 0, second, first)
         left = jnp.concatenate(sent, axis=0)
         aside[:, :order] = left
         aside[:, order:] = jnp.zeros((fresh, 128), f32)
@@ -301,10 +293,14 @@
         left, across = halves(left), halves(across)
         for node in range(nodes):
             columns = slice(node * width, (node + 1) * width)
-            image = stacked_dot(left, [whole[:, columns] for whole in held_now])
             there = slice(lanes + node * width, lanes + (node + 1) * width)
             new = jnp.concatenate([ref[:, there] for ref in part_refs], axis=0)
             new_high, new_low = halves(new)
+            for part, (whole, values) in enumerate(zip(held_now, (new_high, new_low))):
+                whole[:, columns] = jnp.zeros((order, width), bf16) if begin else held_before[part][:, columns]
+                for place, start in enumerate(starts):
+                    whole[pl.ds(start, rows), columns] = values[place * rows : (place + 1) * rows]
+            image = stacked_dot(left, [whole[:, columns] for whole in held_now])
             image_high, image_low = halves(image)
             own = stacked_dot(across, [new_high, new_low])
             if not begin:
@@ -320,6 +316,10 @@
                 beside[fresh * place : fresh * (place + 1), columns] = part
         if last:
             finish(2 * nodes, panel_out, panel_end)
+        else:
+            kept_now[...] = jnp.zeros(kept_now.shape, f32) if begin else kept_before[...]
+            for start, part in zip(starts, ahead):
+                kept_now[pl.ds(start, rows), :order] = part
         for node in range(nodes):
             lower = max(node - 1, 0) * width
             columns = slice(node * width, (node + 1) * width)

time: 70.5 us -> 72.1 us (1.023)
  Pallas kernels: 35.4 us -> 39.8 us
  waiting for transfers between devices: 20.4 us -> 17.4 us
    pallas_call x5, Pallas kernels: 29 us -> 33.4 us  [border(): kernel_call(kernel, 'border' + ('_end' if last else '_begin' if begin els...]
    ppermute x6, waiting for transfers between devices: 17.3 us -> 14.8 us  [move(): lax.ppermute(value, 'row', way)]
  transfers between devices with their start and end apart: 16 -> 16, of which waited for: 10 -> 9; matrix products, arithmetic and copies ran while one was open for 0% -> 0% of each run, Pallas kernels for 43% -> 47%
where the time goes in v12:
time: 72.1 us; the launch traced here: 71.9 us
  Pallas kernels  39.8 us (55%)
  waiting for transfers between devices  17.4 us (24%)
  starting transfers between devices  12.8 us (18%)
  between operations  0.95 us (1%)
  local copies, waits for them, and re-layouts  0.92 us (1%)
    pallas_call x5, Pallas kernels, border(): kernel_call(kernel, 'border' + ('_end' if last else '_begin' if begin els...  33.4 us
    ppermute x6, waiting for transfers between devices, move(): lax.ppermute(value, 'row', way)  14.8 us
    ppermute x6, starting transfers between devices, move(): lax.ppermute(value, 'row', way)  6.13 us
    ppermute x9, starting transfers between devices, swap_bit(): lax.ppermute(value, 'row', [(i, i ^ mask) for i in range(lax.axis_size('r...  4.9 us
    pallas_call x1, Pallas kernels, inner_chain(): kernel_call(kernel, 'inner_chain', out_shape=[jax.ShapeDtypeStruct(array....  4.18 us
    ppermute x9, waiting for transfers between devices, swap_bit(): lax.ppermute(value, 'row', [(i, i ^ mask) for i in range(lax.axis_size('r...  2.58 us
    pallas_call x1, Pallas kernels, link_chain(): kernel_call(kernel, 'link_chain', out_shape=jax.ShapeDtypeStruct((rows, n...  1.93 us
    ppermute x1, starting transfers between devices, gather_plan(): lax.ppermute(last, 'row', across)  1.8 us
  transfers between devices with their start and end apart: 16, of which 9 were waited for; matrix products, arithmetic and copies ran while one was open for 0% of the time, Pallas kernels for 47%

profile of v12, /device:TPU:0, one launch (start us, length us, event | category | flops | bytes accessed | tf_op | source)
XLA Modules:
  0.0 71.9 jit_solution(17815610194397012649)
XLA Ops:
  0.6 0.9 %copy-done.3 = f32[1,384,96]{1,2,0:T(8,128)S(1)} copy-done((f32[1,384,96]{1,2,0:T(8,128)S(1)}, f32[1,384,96]{1,2,0:T(8,128)}, u32[]{:S(2)}) %copy-start.3) | copy-done | bytes 147480
  1.5 0.1 far_rows.1
  1.7 0.0 copy-start.1
  1.7 4.1 %collective-permute-start = (f32[48,192]{1,0:T(8,128)S(1)}, f32[48,192]{1,0:T(8,128)S(1)}, u32[]{:S(2)}, u32[]{:S(2)}) collective-permute-start(f32[48,192]{1,0:T(8,128)S(1)} %far_rows.1), channel_id=1, source_target_pairs={{0,8},{1,9},{2,10},{3,11},{4,12},{5,13},{6,14},{7,15},{8,0},{9,1},... | collective-permute-start | bytes 110600 | tf_op jit(solution)/shard_map/ppermute | solution.py:31
  5.8 1.9 %link_chain.1.links_ref = f32[48,2048]{1,0:T(8,128)S(1)} custom-call(f32[48,8,256]{2,1,0:T(8,128)S(1)} %copy-done.2, f32[7,256,256]{2,1,0:T(8,128)S(1)} %copy-done, s32[8,6]{1,0:T(8,128)S(1)} %copy-done.4), custom_call_target="tpu_custom_call" | custom-call | tf_op jit(solution)/shard_map/link_chain/pallas_call | solution.py:164
  7.7 0.7 collective-permute-done.far_ref
  8.4 0.1 message.1.refs_0_
  8.5 0.1 collective-permute-start.2
  8.6 1.4 %collective-permute-start.1 = (f32[48,2560]{1,0:T(8,128)S(1)}, f32[48,2560]{1,0:T(8,128)S(1)}, u32[]{:S(2)}, u32[]{:S(2)}) collective-permute-start(f32[48,2560]{1,0:T(8,128)S(1)} %message.1.refs_0_), channel_id=1, source_target_pairs={{0,4},{1,5},{4,8},{5,9},{8,12},{9,13},{12,14},{13,15},{14,10},{15,... | collective-permute-start | bytes 1474568 | tf_op jit(solution)/shard_map/ppermute | solution.py:367
  10.0 0.6 collective-permute-start.5
  10.6 4.2 %inner_chain.1 = (f32[7,256,256]{2,1,0:T(8,128)S(1)}, f32[8,256,256]{2,1,0:T(8,128)S(1)}) custom-call(f32[7,256,256]{2,1,0:T(8,128)S(1)} %copy-done, f32[8,256,256]{2,1,0:T(8,128)S(1)} %copy-done.1), custom_call_target="tpu_custom_call" | custom-call | tf_op jit(solution)/shard_map/inner_chain/pallas_call | solution.py:225
  14.8 4.5 %border_begin.1 = (f32[7,256,256]{2,1,0:T(8,128)S(1)}, f32[8,256,256]{2,1,0:T(8,128)S(1)}, f32[48,2048]{1,0:T(8,128)S(1)}, f32[768,896]{1,0:T(8,128)S(1)}, bf16[...) custom-call(f32[48,2560]{1,0:T(8,128)S(1)} %message.1.refs_0_, f32[48,2560]{1,0:T(8,128)S(1)} %collective-permute-done.2.refs_1_, ...), custom_call_target="tpu_custom_call" | custom-call | tf_op jit(solution)/shard_map/border_begin/pallas_call | solution.py:348
  19.4 2.8 %collective-permute-done.1.refs_0_ = f32[48,2560]{1,0:T(8,128)S(1)} collective-permute-done((f32[48,2560]{1,0:T(8,128)S(1)}, f32[48,2560]{1,0:T(8,128)S(1)}, u32[]{:S(2)}, u32[]{:S(2)}) %collective-permute-start.1) | collective-permute-done | bytes 491552 | tf_op jit(solution)/shard_map/ppermute | solution.py:367
  22.2 1.1 %collective-permute-done.5.refs_2_ = f32[48,2560]{1,0:T(8,128)S(1)} collective-permute-done((f32[48,2560]{1,0:T(8,128)S(1)}, f32[48,2560]{1,0:T(8,128)S(1)}, u32[]{:S(2)}, u32[]{:S(2)}) %collective-permute-start.5) | collective-permute-done | bytes 491552 | tf_op jit(solution)/shard_map/ppermute | solution.py:367
  23.3 1.8 %collective-permute-start.3 = (f32[48,2560]{1,0:T(8,128)S(1)}, f32[48,2560]{1,0:T(8,128)S(1)}, u32[]{:S(2)}, u32[]{:S(2)}) collective-permute-start(f32[48,2560]{1,0:T(8,128)S(1)} %collective-permute-done.1.refs_0_), channel_id=1, source_target_pairs={{0,4},{1,5},{4,8},{5,9},{8,12},{9,13},{12,14},{13,15},{14,10},{15,... | collective-permute-start | bytes 1474568 | tf_op jit(solution)/shard_map/ppermute | solution.py:367
  25.1 0.2 collective-permute-start.9
  25.3 7.6 %border.3 = (f32[7,256,256]{2,1,0:T(8,128)S(1)}, f32[8,256,256]{2,1,0:T(8,128)S(1)}, f32[48,2048]{1,0:T(8,128)S(1)}, f32[768,896]{1,0:T(8,128)S(1)}, bf16[768,20...) custom-call(f32[48,2560]{1,0:T(8,128)S(1)} %collective-permute-done.1.refs_0_, ...), custom_call_target="tpu_custom_call" | custom-call | tf_op jit(solution)/shard_map/border/pallas_call | solution.py:348
  33.0 3.9 %collective-permute-done.3.refs_0_ = f32[48,2560]{1,0:T(8,128)S(1)} collective-permute-done((f32[48,2560]{1,0:T(8,128)S(1)}, f32[48,2560]{1,0:T(8,128)S(1)}, u32[]{:S(2)}, u32[]{:S(2)}) %collective-permute-start.3) | collective-permute-done | bytes 491552 | tf_op jit(solution)/shard_map/ppermute | solution.py:367
  36.9 1.5 %collective-permute-done.9.refs_2_ = f32[48,2560]{1,0:T(8,128)S(1)} collective-permute-done((f32[48,2560]{1,0:T(8,128)S(1)}, f32[48,2560]{1,0:T(8,128)S(1)}, u32[]{:S(2)}, u32[]{:S(2)}) %collective-permute-start.9) | collective-permute-done | bytes 491552 | tf_op jit(solution)/shard_map/ppermute | solution.py:367
  38.5 1.7 %collective-permute-start.7 = (f32[48,2560]{1,0:T(8,128)S(1)}, f32[48,2560]{1,0:T(8,128)S(1)}, u32[]{:S(2)}, u32[]{:S(2)}) collective-permute-start(f32[48,2560]{1,0:T(8,128)S(1)} %collective-permute-done.3.refs_0_), channel_id=1, source_target_pairs={{0,4},{1,5},{4,8},{5,9},{8,12},{9,13},{12,14},{13,15},{14,10},{15,... | collective-permute-start | bytes 1474568 | tf_op jit(solution)/shard_map/ppermute | solution.py:367
  40.2 0.3 collective-permute-start.11
  40.5 7.6 %border.4 = (f32[7,256,256]{2,1,0:T(8,128)S(1)}, f32[8,256,256]{2,1,0:T(8,128)S(1)}, f32[48,2048]{1,0:T(8,128)S(1)}, f32[768,896]{1,0:T(8,128)S(1)}, bf16[768,20...) custom-call(f32[48,2560]{1,0:T(8,128)S(1)} %collective-permute-done.3.refs_0_, ...), custom_call_target="tpu_custom_call" | custom-call | tf_op jit(solution)/shard_map/border/pallas_call | solution.py:348
  48.2 3.9 %collective-permute-done.7.first_ref.refs_0_ = f32[48,2560]{1,0:T(8,128)S(1)} collective-permute-done((f32[48,2560]{1,0:T(8,128)S(1)}, f32[48,2560]{1,0:T(8,128)S(1)}, u32[]{:S(2)}, u32[]{:S(2)}) %collective-permute-start.7) | collective-permute-done | bytes 491552 | tf_op jit(solution)/shard_map/ppermute | solution.py:367
  52.1 1.5 %collective-permute-done.11.second_ref.refs_2_ = f32[48,2560]{1,0:T(8,128)S(1)} collective-permute-done((f32[48,2560]{1,0:T(8,128)S(1)}, f32[48,2560]{1,0:T(8,128)S(1)}, u32[]{:S(2)}, u32[]{:S(2)}) %collective-permute-start.11) | collective-permute-done | bytes 491552 | tf_op jit(solution)/shard_map/ppermute | solution.py:367
  53.6 0.5 collective-permute-start.14
  54.1 0.1 pick.1
  54.1 1.8 %collective-permute-start.12 = (f32[48,2560]{1,0:T(8,128)S(1)}, f32[48,2560]{1,0:T(8,128)S(1)}, u32[]{:S(2)}, u32[]{:S(2)}) collective-permute-start(f32[48,2560]{1,0:T(8,128)S(1)} %pick.1), channel_id=1, source_target_pairs={{0,4},{4,8},{8,12},{12,14},{14,10},{10,6},{6,2},{2,0},{1,3},{5,1},... | collective-permute-start | bytes 1474568 | tf_op jit(solution)/shard_map/ppermute | solution.py:385
  56.0 0.2 collective-permute-done.14.refs_3_
  56.1 7.6 %border.5 = (f32[7,256,256]{2,1,0:T(8,128)S(1)}, f32[8,256,256]{2,1,0:T(8,128)S(1)}, f32[48,2048]{1,0:T(8,128)S(1)}, f32[768,896]{1,0:T(8,128)S(1)}, bf16[768,20...) custom-call(f32[48,2560]{1,0:T(8,128)S(1)} %collective-permute-done.7.first_ref.refs_0_, ...), custom_call_target="tpu_custom_call" | custom-call | tf_op jit(solution)/shard_map/border/pallas_call | solution.py:348
  63.8 0.2 collective-permute-start.15
  64.0 1.7 %collective-permute-done.15.refs_1_ = f32[48,2560]{1,0:T(8,128)S(1)} collective-permute-done((f32[48,2560]{1,0:T(8,128)S(1)}, f32[48,2560]{1,0:T(8,128)S(1)}, u32[]{:S(2)}, u32[]{:S(2)}) %collective-permute-start.15) | collective-permute-done | bytes 491552 | tf_op jit(solution)/shard_map/ppermute | solution.py:31
  65.7 6.0 %border_end.1 = (f32[7,256,256]{2,1,0:T(8,128)}, f32[8,256,256]{2,1,0:T(8,128)}, f32[48,8,256]{2,1,0:T(8,128)}) custom-call(f32[48,2560]{1,0:T(8,128)S(1)} %collective-permute-done.12.refs_0_, f32[48,2560]{1,0:T(8,128)S(1)} %collective-permute-done.15.refs_1_, f32[48,2048]{1,0:T(8,128)S(1)} %get-tuple-element.80.refs_2_, ...), custom_call_target="tpu_custom_call" | custom-call | tf_op jit(solution)/shard_map/border_end/pallas_call | solution.py:348
  (20 shorter events, 0.0 us)
Async XLA Ops:
  0.6 0.9 %copy-start.3 = (f32[1,384,96]{1,2,0:T(8,128)S(1)}, f32[1,384,96]{1,2,0:T(8,128)}, u32[]{:S(2)}) copy-start(f32[1,384,96]{1,2,0:T(8,128)} %param.5) | copy-start | bytes 442372
  1.5 4.2 %copy-start = (f32[7,256,256]{2,1,0:T(8,128)S(1)}, f32[7,256,256]{2,1,0:T(8,128)}, u32[]{:S(2)}) copy-start(f32[7,256,256]{2,1,0:T(8,128)} %parent_ref.2) | copy-start | bytes 5505028
  1.5 4.2 %copy-start.2 = (f32[48,8,256]{2,1,0:T(8,128)S(1)}, f32[48,8,256]{2,1,0:T(8,128)}, u32[]{:S(2)}) copy-start(f32[48,8,256]{2,1,0:T(8,128)} %links_ref) | copy-start | bytes 1179652
  1.5 4.2 %copy-start.4 = (s32[8,6]{1,0:T(8,128)S(1)}, s32[8,6]{1,0:T(8,128)}, u32[]{:S(2)}) copy-start(s32[8,6]{1,0:T(8,128)} %pattern_ref.1) | copy-start | bytes 580
  1.7 9.0 %copy-start.1 = (f32[8,256,256]{2,1,0:T(8,128)S(1)}, f32[8,256,256]{2,1,0:T(8,128)}, u32[]{:S(2)}) copy-start(f32[8,256,256]{2,1,0:T(8,128)} %pivot_ref.1) | copy-start | bytes 6291460
  1.7 6.7 %collective-permute-start = (f32[48,192]{1,0:T(8,128)S(1)}, f32[48,192]{1,0:T(8,128)S(1)}, u32[]{:S(2)}, u32[]{:S(2)}) collective-permute-start(f32[48,192]{1,0:T(8,128)S(1)} %far_rows.1), channel_id=1, source_target_pairs={{0,8},{1,9},{2,10},{3,11},{4,12},{5,13},{6,14},{7,15},{8,0},{9,1},... | collective-permute-start | bytes 110600 | tf_op jit(solution)/shard_map/ppermute | solution.py:31
  8.5 6.3 %collective-permute-start.2 = (f32[48,2560]{1,0:T(8,128)S(1)}, f32[48,2560]{1,0:T(8,128)S(1)}, u32[]{:S(2)}, u32[]{:S(2)}) collective-permute-start(f32[48,2560]{1,0:T(8,128)S(1)} %message.1.refs_0_), channel_id=1, source_target_pairs={{0,1},{1,0},{2,3},{3,2},{4,5},{5,4},{6,7},{7,6},{8,9},{9,8},{10,11... | collective-permute-start | bytes 1474568 | tf_op jit(solution)/shard_map/ppermute | solution.py:31
  8.6 13.6 %collective-permute-start.1 = (f32[48,2560]{1,0:T(8,128)S(1)}, f32[48,2560]{1,0:T(8,128)S(1)}, u32[]{:S(2)}, u32[]{:S(2)}) collective-permute-start(f32[48,2560]{1,0:T(8,128)S(1)} %message.1.refs_0_), channel_id=1, source_target_pairs={{0,4},{1,5},{4,8},{5,9},{8,12},{9,13},{12,14},{13,15},{14,10},{15,... | collective-permute-start | bytes 1474568 | tf_op jit(solution)/shard_map/ppermute | solution.py:367
  10.0 13.3 %collective-permute-start.5 = (f32[48,2560]{1,0:T(8,128)S(1)}, f32[48,2560]{1,0:T(8,128)S(1)}, u32[]{:S(2)}, u32[]{:S(2)}) collective-permute-start(f32[48,2560]{1,0:T(8,128)S(1)} %message.1.refs_0_), channel_id=1, source_target_pairs={{0,2},{1,3},{4,0},{5,1},{8,4},{9,5},{12,8},{13,9},{14,12},{15,13},... | collective-permute-start | bytes 1474568 | tf_op jit(solution)/shard_map/ppermute | solution.py:367
  22.2 3.1 %collective-permute-start.4 = (f32[48,2560]{1,0:T(8,128)S(1)}, f32[48,2560]{1,0:T(8,128)S(1)}, u32[]{:S(2)}, u32[]{:S(2)}) collective-permute-start(f32[48,2560]{1,0:T(8,128)S(1)} %collective-permute-done.1.refs_0_), channel_id=1, source_target_pairs={{0,1},{1,0},{2,3},{3,2},{4,5},{5,4},{6,7},{7,6},{8,9},{9,8},{10,11... | collective-permute-start | bytes 1474568 | tf_op jit(solution)/shard_map/ppermute | solution.py:31
  23.3 2.0 %collective-permute-start.6 = (f32[48,2560]{1,0:T(8,128)S(1)}, f32[48,2560]{1,0:T(8,128)S(1)}, u32[]{:S(2)}, u32[]{:S(2)}) collective-permute-start(f32[48,2560]{1,0:T(8,128)S(1)} %collective-permute-done.5.refs_2_), channel_id=1, source_target_pairs={{0,1},{1,0},{2,3},{3,2},{4,5},{5,4},{6,7},{7,6},{8,9},{9,8},{10,11... | collective-permute-start | bytes 1474568 | tf_op jit(solution)/shard_map/ppermute | solution.py:31
  23.3 13.6 %collective-permute-start.3 = (f32[48,2560]{1,0:T(8,128)S(1)}, f32[48,2560]{1,0:T(8,128)S(1)}, u32[]{:S(2)}, u32[]{:S(2)}) collective-permute-start(f32[48,2560]{1,0:T(8,128)S(1)} %collective-permute-done.1.refs_0_), channel_id=1, source_target_pairs={{0,4},{1,5},{4,8},{5,9},{8,12},{9,13},{12,14},{13,15},{14,10},{15,... | collective-permute-start | bytes 1474568 | tf_op jit(solution)/shard_map/ppermute | solution.py:367
  25.1 13.4 %collective-permute-start.9 = (f32[48,2560]{1,0:T(8,128)S(1)}, f32[48,2560]{1,0:T(8,128)S(1)}, u32[]{:S(2)}, u32[]{:S(2)}) collective-permute-start(f32[48,2560]{1,0:T(8,128)S(1)} %collective-permute-done.5.refs_2_), channel_id=1, source_target_pairs={{0,2},{1,3},{4,0},{5,1},{8,4},{9,5},{12,8},{13,9},{14,12},{15,13},... | collective-permute-start | bytes 1474568 | tf_op jit(solution)/shard_map/ppermute | solution.py:367
  36.9 3.6 %collective-permute-start.8 = (f32[48,2560]{1,0:T(8,128)S(1)}, f32[48,2560]{1,0:T(8,128)S(1)}, u32[]{:S(2)}, u32[]{:S(2)}) collective-permute-start(f32[48,2560]{1,0:T(8,128)S(1)} %collective-permute-done.3.refs_0_), channel_id=1, source_target_pairs={{0,1},{1,0},{2,3},{3,2},{4,5},{5,4},{6,7},{7,6},{8,9},{9,8},{10,11... | collective-permute-start | bytes 1474568 | tf_op jit(solution)/shard_map/ppermute | solution.py:31
  38.5 2.0 %collective-permute-start.10 = (f32[48,2560]{1,0:T(8,128)S(1)}, f32[48,2560]{1,0:T(8,128)S(1)}, u32[]{:S(2)}, u32[]{:S(2)}) collective-permute-start(f32[48,2560]{1,0:T(8,128)S(1)} %collective-permute-done.9.refs_2_), channel_id=1, source_target_pairs={{0,1},{1,0},{2,3},{3,2},{4,5},{5,4},{6,7},{7,6},{8,9},{9,8},{10,11... | collective-permute-start | bytes 1474568 | tf_op jit(solution)/shard_map/ppermute | solution.py:31
  38.5 13.6 %collective-permute-start.7 = (f32[48,2560]{1,0:T(8,128)S(1)}, f32[48,2560]{1,0:T(8,128)S(1)}, u32[]{:S(2)}, u32[]{:S(2)}) collective-permute-start(f32[48,2560]{1,0:T(8,128)S(1)} %collective-permute-done.3.refs_0_), channel_id=1, source_target_pairs={{0,4},{1,5},{4,8},{5,9},{8,12},{9,13},{12,14},{13,15},{14,10},{15,... | collective-permute-start | bytes 1474568 | tf_op jit(solution)/shard_map/ppermute | solution.py:367
  40.2 13.4 %collective-permute-start.11 = (f32[48,2560]{1,0:T(8,128)S(1)}, f32[48,2560]{1,0:T(8,128)S(1)}, u32[]{:S(2)}, u32[]{:S(2)}) collective-permute-start(f32[48,2560]{1,0:T(8,128)S(1)} %collective-permute-done.9.refs_2_), channel_id=1, source_target_pairs={{0,2},{1,3},{4,0},{5,1},{8,4},{9,5},{12,8},{13,9},{14,12},{15,13},... | collective-permute-start | bytes 1474568 | tf_op jit(solution)/shard_map/ppermute | solution.py:367
  53.6 2.4 %collective-permute-start.13 = (f32[48,2560]{1,0:T(8,128)S(1)}, f32[48,2560]{1,0:T(8,128)S(1)}, u32[]{:S(2)}, u32[]{:S(2)}) collective-permute-start(f32[48,2560]{1,0:T(8,128)S(1)} %collective-permute-done.7.first_ref.refs_0_), channel_id=1, source_target_pairs={{0,1},{1,0},{2,3},{3,2},{4,5},{5,4},{6,7},{7,6},{8,9},{9,8},{10,11... | collective-permute-start | bytes 1474568 | tf_op jit(solution)/shard_map/ppermute | solution.py:31
  53.6 2.6 %collective-permute-start.14 = (f32[48,2560]{1,0:T(8,128)S(1)}, f32[48,2560]{1,0:T(8,128)S(1)}, u32[]{:S(2)}, u32[]{:S(2)}) collective-permute-start(f32[48,2560]{1,0:T(8,128)S(1)} %collective-permute-done.11.second_ref.refs_2_), channel_id=1, source_target_pairs={{0,1},{1,0},{2,3},{3,2},{4,5},{5,4},{6,7},{7,6},{8,9},{9,8},{10,11... | collective-permute-start | bytes 1474568 | tf_op jit(solution)/shard_map/ppermute | solution.py:31
  54.1 9.7 %collective-permute-start.12 = (f32[48,2560]{1,0:T(8,128)S(1)}, f32[48,2560]{1,0:T(8,128)S(1)}, u32[]{:S(2)}, u32[]{:S(2)}) collective-permute-start(f32[48,2560]{1,0:T(8,128)S(1)} %pick.1), channel_id=1, source_target_pairs={{0,4},{4,8},{8,12},{12,14},{14,10},{10,6},{6,2},{2,0},{1,3},{5,1},... | collective-permute-start | bytes 1474568 | tf_op jit(solution)/shard_map/ppermute | solution.py:385
  63.8 1.9 %collective-permute-start.15 = (f32[48,2560]{1,0:T(8,128)S(1)}, f32[48,2560]{1,0:T(8,128)S(1)}, u32[]{:S(2)}, u32[]{:S(2)}) collective-permute-start(f32[48,2560]{1,0:T(8,128)S(1)} %collective-permute-done.12.refs_0_), channel_id=1, source_target_pairs={{0,1},{1,0},{2,3},{3,2},{4,5},{5,4},{6,7},{7,6},{8,9},{9,8},{10,11... | collective-permute-start | bytes 1474568 | tf_op jit(solution)/shard_map/ppermute | solution.py:31

commit v13 on v10

--- a/solution.py
+++ b/solution.py
@@ -9,6 +9,7 @@
 TILE = 128
 GATHER_LIMIT = 16 * 2**20
 SIDE = 256
+BORDER_LIMIT = 20 * 2**20
 FIRST_FLOPS = 4_000_000_000
 
 
@@ -299,25 +300,23 @@
             swapped = jnp.concatenate([pair[:, rows : 2 * rows], pair[:, :rows]], axis=1)
             across += jnp.where(core == 0, pair[:, : 2 * rows], swapped)
         left, across = halves(left), halves(across)
-        for node in range(nodes):
-            columns = slice(node * width, (node + 1) * width)
-            image = stacked_dot(left, [whole[:, columns] for whole in held_now])
-            there = slice(lanes + node * width, lanes + (node + 1) * width)
-            new = jnp.concatenate([ref[:, there] for ref in part_refs], axis=0)
-            new_high, new_low = halves(new)
-            image_high, image_low = halves(image)
-            own = stacked_dot(across, [new_high, new_low])
-            if not begin:
-                own += panel_before[:, columns]
-            if last:
-                panel_out[:, node, :] = -own
-            else:
-                panel_out[:, columns] = own
-            high, low = halves(jnp.concatenate([new, image], axis=0).T)
-            for place, part in enumerate((high, low, high)):
-                turned[columns, 2 * fresh * place : 2 * fresh * (place + 1)] = part
-            for place, part in enumerate((image_high, new_high, image_high, new_high, image_low, new_low)):
-                beside[fresh * place : fresh * (place + 1), columns] = part
+        new = jnp.concatenate([ref[:, lanes:] for ref in part_refs], axis=0)
+        new_high, new_low = halves(new)
+        image = stacked_dot(left, [whole[...] for whole in held_now])
+        image_high, image_low = halves(image)
+        own = stacked_dot(across, [new_high, new_low])
+        if not begin:
+            own = own + panel_before[...]
+        if last:
+            for node in range(nodes):
+                panel_out[:, node, :] = -own[:, node * width : (node + 1) * width]
+        else:
+            panel_out[...] = own
+        high, low = halves(jnp.concatenate([new, image], axis=0).T)
+        for place, part in enumerate((high, low, high)):
+            turned[:, 2 * fresh * place : 2 * fresh * (place + 1)] = part
+        for place, part in enumerate((image_high, new_high, image_high, new_high, image_low, new_low)):
+            beside[fresh * place : fresh * (place + 1), :] = part
         if last:
             finish(2 * nodes, panel_out, panel_end)
         for node in range(nodes):
@@ -352,7 +351,7 @@
         in_specs=in_vmem(len(operands)),
         out_specs=at_home(len(shapes)) if last else in_vmem(len(shapes)),
         scratch_shapes=scratch,
-        limit=(24 if last else 16) * 2**20,
+        limit=24 * 2**20 if last else BORDER_LIMIT,
     )(*operands)
     return results[:2], results[2:]
 

time: 70.5 us -> 70.8 us (level)
  waiting for transfers between devices: 20.4 us -> 21.2 us
  transfers between devices with their start and end apart: 16 -> 16, of which waited for: 10 -> 10; matrix products, arithmetic and copies ran while one was open for 0% -> 0% of each run, Pallas kernels for 43% -> 42%
where the time goes in v13:
time: 70.8 us; the launch traced here: 70.7 us
  Pallas kernels  35 us (49%)
  waiting for transfers between devices  21.2 us (30%)
  starting transfers between devices  12.6 us (18%)
  local copies, waits for them, and re-layouts  0.92 us (1%)
  between operations  0.92 us (1%)
    pallas_call x5, Pallas kernels, border(): kernel_call(kernel, 'border' + ('_end' if last else '_begin' if begin els...  28.6 us
    ppermute x6, waiting for transfers between devices, move(): lax.ppermute(value, 'row', way)  17.8 us
    ppermute x6, starting transfers between devices, move(): lax.ppermute(value, 'row', way)  6.13 us
    ppermute x9, starting transfers between devices, swap_bit(): lax.ppermute(value, 'row', [(i, i ^ mask) for i in range(lax.axis_size('r...  4.7 us
    pallas_call x1, Pallas kernels, inner_chain(): kernel_call(kernel, 'inner_chain', out_shape=[jax.ShapeDtypeStruct(array....  4.18 us
    ppermute x9, waiting for transfers between devices, swap_bit(): lax.ppermute(value, 'row', [(i, i ^ mask) for i in range(lax.axis_size('r...  2.76 us
    pallas_call x1, Pallas kernels, link_chain(): kernel_call(kernel, 'link_chain', out_shape=jax.ShapeDtypeStruct((rows, n...  1.93 us
    ppermute x1, starting transfers between devices, gather_plan(): lax.ppermute(last, 'row', across)  1.76 us
  transfers between devices with their start and end apart: 16, of which 10 were waited for; matrix products, arithmetic and copies ran while one was open for 0% of the time, Pallas kernels for 42%

profile of v13, /device:TPU:0, one launch (start us, length us, event | category | flops | bytes accessed | tf_op | source)
XLA Modules:
  0.0 70.7 jit_solution(2476844913960401593)
XLA Ops:
  0.6 0.9 %copy-done.3 = f32[1,384,96]{1,2,0:T(8,128)S(1)} copy-done((f32[1,384,96]{1,2,0:T(8,128)S(1)}, f32[1,384,96]{1,2,0:T(8,128)}, u32[]{:S(2)}) %copy-start.3) | copy-done | bytes 147480
  1.5 0.1 far_rows.1
  1.7 0.0 copy-start.1
  1.7 4.1 %collective-permute-start = (f32[48,192]{1,0:T(8,128)S(1)}, f32[48,192]{1,0:T(8,128)S(1)}, u32[]{:S(2)}, u32[]{:S(2)}) collective-permute-start(f32[48,192]{1,0:T(8,128)S(1)} %far_rows.1), channel_id=1, source_target_pairs={{0,8},{1,9},{2,10},{3,11},{4,12},{5,13},{6,14},{7,15},{8,0},{9,1},... | collective-permute-start | bytes 110600 | tf_op jit(solution)/shard_map/ppermute | solution.py:32
  5.8 1.9 %link_chain.1.links_ref = f32[48,2048]{1,0:T(8,128)S(1)} custom-call(f32[48,8,256]{2,1,0:T(8,128)S(1)} %copy-done.2, f32[7,256,256]{2,1,0:T(8,128)S(1)} %copy-done, s32[8,6]{1,0:T(8,128)S(1)} %copy-done.4), custom_call_target="tpu_custom_call" | custom-call | tf_op jit(solution)/shard_map/link_chain/pallas_call | solution.py:165
  7.7 0.7 collective-permute-done.far_ref
  8.4 0.1 message.1.refs_0_
  8.5 0.1 collective-permute-start.2
  8.6 1.4 %collective-permute-start.1 = (f32[48,2560]{1,0:T(8,128)S(1)}, f32[48,2560]{1,0:T(8,128)S(1)}, u32[]{:S(2)}, u32[]{:S(2)}) collective-permute-start(f32[48,2560]{1,0:T(8,128)S(1)} %message.1.refs_0_), channel_id=1, source_target_pairs={{0,4},{1,5},{4,8},{5,9},{8,12},{9,13},{12,14},{13,15},{14,10},{15,... | collective-permute-start | bytes 1474568 | tf_op jit(solution)/shard_map/ppermute | solution.py:366
  10.0 0.6 collective-permute-start.5
  10.6 4.2 %inner_chain.1 = (f32[7,256,256]{2,1,0:T(8,128)S(1)}, f32[8,256,256]{2,1,0:T(8,128)S(1)}) custom-call(f32[7,256,256]{2,1,0:T(8,128)S(1)} %copy-done, f32[8,256,256]{2,1,0:T(8,128)S(1)} %copy-done.1), custom_call_target="tpu_custom_call" | custom-call | tf_op jit(solution)/shard_map/inner_chain/pallas_call | solution.py:226
  14.8 3.9 %border_begin.1 = (f32[7,256,256]{2,1,0:T(8,128)S(1)}, f32[8,256,256]{2,1,0:T(8,128)S(1)}, f32[48,2048]{1,0:T(8,128)S(1)}, f32[768,896]{1,0:T(8,128)S(1)}, bf16[...) custom-call(f32[48,2560]{1,0:T(8,128)S(1)} %message.1.refs_0_, f32[48,2560]{1,0:T(8,128)S(1)} %collective-permute-done.2.refs_1_, ...), custom_call_target="tpu_custom_call" | custom-call | tf_op jit(solution)/shard_map/border_begin/pallas_call | solution.py:347
  18.7 3.5 %collective-permute-done.1.refs_0_ = f32[48,2560]{1,0:T(8,128)S(1)} collective-permute-done((f32[48,2560]{1,0:T(8,128)S(1)}, f32[48,2560]{1,0:T(8,128)S(1)}, u32[]{:S(2)}, u32[]{:S(2)}) %collective-permute-start.1) | collective-permute-done | bytes 491552 | tf_op jit(solution)/shard_map/ppermute | solution.py:366
  22.2 1.1 %collective-permute-done.5.refs_2_ = f32[48,2560]{1,0:T(8,128)S(1)} collective-permute-done((f32[48,2560]{1,0:T(8,128)S(1)}, f32[48,2560]{1,0:T(8,128)S(1)}, u32[]{:S(2)}, u32[]{:S(2)}) %collective-permute-start.5) | collective-permute-done | bytes 491552 | tf_op jit(solution)/shard_map/ppermute | solution.py:366
  23.3 1.8 %collective-permute-start.3 = (f32[48,2560]{1,0:T(8,128)S(1)}, f32[48,2560]{1,0:T(8,128)S(1)}, u32[]{:S(2)}, u32[]{:S(2)}) collective-permute-start(f32[48,2560]{1,0:T(8,128)S(1)} %collective-permute-done.1.refs_0_), channel_id=1, source_target_pairs={{0,4},{1,5},{4,8},{5,9},{8,12},{9,13},{12,14},{13,15},{14,10},{15,... | collective-permute-start | bytes 1474568 | tf_op jit(solution)/shard_map/ppermute | solution.py:366
  25.1 0.2 collective-permute-start.9
  25.3 6.5 %border.3 = (f32[7,256,256]{2,1,0:T(8,128)S(1)}, f32[8,256,256]{2,1,0:T(8,128)S(1)}, f32[48,2048]{1,0:T(8,128)S(1)}, f32[768,896]{1,0:T(8,128)S(1)}, bf16[768,20...) custom-call(f32[48,2560]{1,0:T(8,128)S(1)} %collective-permute-done.1.refs_0_, ...), custom_call_target="tpu_custom_call" | custom-call | tf_op jit(solution)/shard_map/border/pallas_call | solution.py:347
  31.8 5.1 %collective-permute-done.3.refs_0_ = f32[48,2560]{1,0:T(8,128)S(1)} collective-permute-done((f32[48,2560]{1,0:T(8,128)S(1)}, f32[48,2560]{1,0:T(8,128)S(1)}, u32[]{:S(2)}, u32[]{:S(2)}) %collective-permute-start.3) | collective-permute-done | bytes 491552 | tf_op jit(solution)/shard_map/ppermute | solution.py:366
  36.9 1.5 %collective-permute-done.9.refs_2_ = f32[48,2560]{1,0:T(8,128)S(1)} collective-permute-done((f32[48,2560]{1,0:T(8,128)S(1)}, f32[48,2560]{1,0:T(8,128)S(1)}, u32[]{:S(2)}, u32[]{:S(2)}) %collective-permute-start.9) | collective-permute-done | bytes 491552 | tf_op jit(solution)/shard_map/ppermute | solution.py:366
  38.5 1.7 %collective-permute-start.7 = (f32[48,2560]{1,0:T(8,128)S(1)}, f32[48,2560]{1,0:T(8,128)S(1)}, u32[]{:S(2)}, u32[]{:S(2)}) collective-permute-start(f32[48,2560]{1,0:T(8,128)S(1)} %collective-permute-done.3.refs_0_), channel_id=1, source_target_pairs={{0,4},{1,5},{4,8},{5,9},{8,12},{9,13},{12,14},{13,15},{14,10},{15,... | collective-permute-start | bytes 1474568 | tf_op jit(solution)/shard_map/ppermute | solution.py:366
  40.2 0.3 collective-permute-start.11
  40.5 6.5 %border.4 = (f32[7,256,256]{2,1,0:T(8,128)S(1)}, f32[8,256,256]{2,1,0:T(8,128)S(1)}, f32[48,2048]{1,0:T(8,128)S(1)}, f32[768,896]{1,0:T(8,128)S(1)}, bf16[768,20...) custom-call(f32[48,2560]{1,0:T(8,128)S(1)} %collective-permute-done.3.refs_0_, ...), custom_call_target="tpu_custom_call" | custom-call | tf_op jit(solution)/shard_map/border/pallas_call | solution.py:347
  47.0 5.1 %collective-permute-done.7.first_ref.refs_0_ = f32[48,2560]{1,0:T(8,128)S(1)} collective-permute-done((f32[48,2560]{1,0:T(8,128)S(1)}, f32[48,2560]{1,0:T(8,128)S(1)}, u32[]{:S(2)}, u32[]{:S(2)}) %collective-permute-start.7) | collective-permute-done | bytes 491552 | tf_op jit(solution)/shard_map/ppermute | solution.py:366
  52.1 1.5 %collective-permute-done.11.second_ref.refs_2_ = f32[48,2560]{1,0:T(8,128)S(1)} collective-permute-done((f32[48,2560]{1,0:T(8,128)S(1)}, f32[48,2560]{1,0:T(8,128)S(1)}, u32[]{:S(2)}, u32[]{:S(2)}) %collective-permute-start.11) | collective-permute-done | bytes 491552 | tf_op jit(solution)/shard_map/ppermute | solution.py:366
  53.6 0.5 collective-permute-start.14
  54.1 0.1 pick.1
  54.1 1.8 %collective-permute-start.12 = (f32[48,2560]{1,0:T(8,128)S(1)}, f32[48,2560]{1,0:T(8,128)S(1)}, u32[]{:S(2)}, u32[]{:S(2)}) collective-permute-start(f32[48,2560]{1,0:T(8,128)S(1)} %pick.1), channel_id=1, source_target_pairs={{0,4},{4,8},{8,12},{12,14},{14,10},{10,6},{6,2},{2,0},{1,3},{5,1},... | collective-permute-start | bytes 1474568 | tf_op jit(solution)/shard_map/ppermute | solution.py:384
  55.9 0.2 collective-permute-done.14.refs_3_
  56.1 6.5 %border.5 = (f32[7,256,256]{2,1,0:T(8,128)S(1)}, f32[8,256,256]{2,1,0:T(8,128)S(1)}, f32[48,2048]{1,0:T(8,128)S(1)}, f32[768,896]{1,0:T(8,128)S(1)}, bf16[768,20...) custom-call(f32[48,2560]{1,0:T(8,128)S(1)} %collective-permute-done.7.first_ref.refs_0_, ...), custom_call_target="tpu_custom_call" | custom-call | tf_op jit(solution)/shard_map/border/pallas_call | solution.py:347
  62.6 0.6 collective-permute-done.12.refs_0_
  63.2 1.9 %collective-permute-done.15.refs_1_ = f32[48,2560]{1,0:T(8,128)S(1)} collective-permute-done((f32[48,2560]{1,0:T(8,128)S(1)}, f32[48,2560]{1,0:T(8,128)S(1)}, u32[]{:S(2)}, u32[]{:S(2)}) %collective-permute-start.15) | collective-permute-done | bytes 491552 | tf_op jit(solution)/shard_map/ppermute | solution.py:32
  65.1 5.4 %border_end.1 = (f32[7,256,256]{2,1,0:T(8,128)}, f32[8,256,256]{2,1,0:T(8,128)}, f32[48,8,256]{2,1,0:T(8,128)}) custom-call(f32[48,2560]{1,0:T(8,128)S(1)} %collective-permute-done.12.refs_0_, f32[48,2560]{1,0:T(8,128)S(1)} %collective-permute-done.15.refs_1_, f32[48,2048]{1,0:T(8,128)S(1)} %get-tuple-element.80.refs_2_, ...), custom_call_target="tpu_custom_call" | custom-call | tf_op jit(solution)/shard_map/border_end/pallas_call | solution.py:347
  (20 shorter events, 0.0 us)
Async XLA Ops:
  0.6 0.9 %copy-start.3 = (f32[1,384,96]{1,2,0:T(8,128)S(1)}, f32[1,384,96]{1,2,0:T(8,128)}, u32[]{:S(2)}) copy-start(f32[1,384,96]{1,2,0:T(8,128)} %param.5) | copy-start | bytes 442372
  1.5 4.2 %copy-start = (f32[7,256,256]{2,1,0:T(8,128)S(1)}, f32[7,256,256]{2,1,0:T(8,128)}, u32[]{:S(2)}) copy-start(f32[7,256,256]{2,1,0:T(8,128)} %parent_ref.2) | copy-start | bytes 5505028
  1.5 4.2 %copy-start.2 = (f32[48,8,256]{2,1,0:T(8,128)S(1)}, f32[48,8,256]{2,1,0:T(8,128)}, u32[]{:S(2)}) copy-start(f32[48,8,256]{2,1,0:T(8,128)} %links_ref) | copy-start | bytes 1179652
  1.5 4.2 %copy-start.4 = (s32[8,6]{1,0:T(8,128)S(1)}, s32[8,6]{1,0:T(8,128)}, u32[]{:S(2)}) copy-start(s32[8,6]{1,0:T(8,128)} %pattern_ref.1) | copy-start | bytes 580
  1.7 9.0 %copy-start.1 = (f32[8,256,256]{2,1,0:T(8,128)S(1)}, f32[8,256,256]{2,1,0:T(8,128)}, u32[]{:S(2)}) copy-start(f32[8,256,256]{2,1,0:T(8,128)} %pivot_ref.1) | copy-start | bytes 6291460
  1.7 6.7 %collective-permute-start = (f32[48,192]{1,0:T(8,128)S(1)}, f32[48,192]{1,0:T(8,128)S(1)}, u32[]{:S(2)}, u32[]{:S(2)}) collective-permute-start(f32[48,192]{1,0:T(8,128)S(1)} %far_rows.1), channel_id=1, source_target_pairs={{0,8},{1,9},{2,10},{3,11},{4,12},{5,13},{6,14},{7,15},{8,0},{9,1},... | collective-permute-start | bytes 110600 | tf_op jit(solution)/shard_map/ppermute | solution.py:32
  8.5 6.3 %collective-permute-start.2 = (f32[48,2560]{1,0:T(8,128)S(1)}, f32[48,2560]{1,0:T(8,128)S(1)}, u32[]{:S(2)}, u32[]{:S(2)}) collective-permute-start(f32[48,2560]{1,0:T(8,128)S(1)} %message.1.refs_0_), channel_id=1, source_target_pairs={{0,1},{1,0},{2,3},{3,2},{4,5},{5,4},{6,7},{7,6},{8,9},{9,8},{10,11... | collective-permute-start | bytes 1474568 | tf_op jit(solution)/shard_map/ppermute | solution.py:32
  8.6 13.6 %collective-permute-start.1 = (f32[48,2560]{1,0:T(8,128)S(1)}, f32[48,2560]{1,0:T(8,128)S(1)}, u32[]{:S(2)}, u32[]{:S(2)}) collective-permute-start(f32[48,2560]{1,0:T(8,128)S(1)} %message.1.refs_0_), channel_id=1, source_target_pairs={{0,4},{1,5},{4,8},{5,9},{8,12},{9,13},{12,14},{13,15},{14,10},{15,... | collective-permute-start | bytes 1474568 | tf_op jit(solution)/shard_map/ppermute | solution.py:366
  10.0 13.3 %collective-permute-start.5 = (f32[48,2560]{1,0:T(8,128)S(1)}, f32[48,2560]{1,0:T(8,128)S(1)}, u32[]{:S(2)}, u32[]{:S(2)}) collective-permute-start(f32[48,2560]{1,0:T(8,128)S(1)} %message.1.refs_0_), channel_id=1, source_target_pairs={{0,2},{1,3},{4,0},{5,1},{8,4},{9,5},{12,8},{13,9},{14,12},{15,13},... | collective-permute-start | bytes 1474568 | tf_op jit(solution)/shard_map/ppermute | solution.py:366
  22.2 3.1 %collective-permute-start.4 = (f32[48,2560]{1,0:T(8,128)S(1)}, f32[48,2560]{1,0:T(8,128)S(1)}, u32[]{:S(2)}, u32[]{:S(2)}) collective-permute-start(f32[48,2560]{1,0:T(8,128)S(1)} %collective-permute-done.1.refs_0_), channel_id=1, source_target_pairs={{0,1},{1,0},{2,3},{3,2},{4,5},{5,4},{6,7},{7,6},{8,9},{9,8},{10,11... | collective-permute-start | bytes 1474568 | tf_op jit(solution)/shard_map/ppermute | solution.py:32
  23.3 2.0 %collective-permute-start.6 = (f32[48,2560]{1,0:T(8,128)S(1)}, f32[48,2560]{1,0:T(8,128)S(1)}, u32[]{:S(2)}, u32[]{:S(2)}) collective-permute-start(f32[48,2560]{1,0:T(8,128)S(1)} %collective-permute-done.5.refs_2_), channel_id=1, source_target_pairs={{0,1},{1,0},{2,3},{3,2},{4,5},{5,4},{6,7},{7,6},{8,9},{9,8},{10,11... | collective-permute-start | bytes 1474568 | tf_op jit(solution)/shard_map/ppermute | solution.py:32
  23.3 13.6 %collective-permute-start.3 = (f32[48,2560]{1,0:T(8,128)S(1)}, f32[48,2560]{1,0:T(8,128)S(1)}, u32[]{:S(2)}, u32[]{:S(2)}) collective-permute-start(f32[48,2560]{1,0:T(8,128)S(1)} %collective-permute-done.1.refs_0_), channel_id=1, source_target_pairs={{0,4},{1,5},{4,8},{5,9},{8,12},{9,13},{12,14},{13,15},{14,10},{15,... | collective-permute-start | bytes 1474568 | tf_op jit(solution)/shard_map/ppermute | solution.py:366
  25.1 13.4 %collective-permute-start.9 = (f32[48,2560]{1,0:T(8,128)S(1)}, f32[48,2560]{1,0:T(8,128)S(1)}, u32[]{:S(2)}, u32[]{:S(2)}) collective-permute-start(f32[48,2560]{1,0:T(8,128)S(1)} %collective-permute-done.5.refs_2_), channel_id=1, source_target_pairs={{0,2},{1,3},{4,0},{5,1},{8,4},{9,5},{12,8},{13,9},{14,12},{15,13},... | collective-permute-start | bytes 1474568 | tf_op jit(solution)/shard_map/ppermute | solution.py:366
  36.9 3.6 %collective-permute-start.8 = (f32[48,2560]{1,0:T(8,128)S(1)}, f32[48,2560]{1,0:T(8,128)S(1)}, u32[]{:S(2)}, u32[]{:S(2)}) collective-permute-start(f32[48,2560]{1,0:T(8,128)S(1)} %collective-permute-done.3.refs_0_), channel_id=1, source_target_pairs={{0,1},{1,0},{2,3},{3,2},{4,5},{5,4},{6,7},{7,6},{8,9},{9,8},{10,11... | collective-permute-start | bytes 1474568 | tf_op jit(solution)/shard_map/ppermute | solution.py:32
  38.5 2.0 %collective-permute-start.10 = (f32[48,2560]{1,0:T(8,128)S(1)}, f32[48,2560]{1,0:T(8,128)S(1)}, u32[]{:S(2)}, u32[]{:S(2)}) collective-permute-start(f32[48,2560]{1,0:T(8,128)S(1)} %collective-permute-done.9.refs_2_), channel_id=1, source_target_pairs={{0,1},{1,0},{2,3},{3,2},{4,5},{5,4},{6,7},{7,6},{8,9},{9,8},{10,11... | collective-permute-start | bytes 1474568 | tf_op jit(solution)/shard_map/ppermute | solution.py:32
  38.5 13.6 %collective-permute-start.7 = (f32[48,2560]{1,0:T(8,128)S(1)}, f32[48,2560]{1,0:T(8,128)S(1)}, u32[]{:S(2)}, u32[]{:S(2)}) collective-permute-start(f32[48,2560]{1,0:T(8,128)S(1)} %collective-permute-done.3.refs_0_), channel_id=1, source_target_pairs={{0,4},{1,5},{4,8},{5,9},{8,12},{9,13},{12,14},{13,15},{14,10},{15,... | collective-permute-start | bytes 1474568 | tf_op jit(solution)/shard_map/ppermute | solution.py:366
  40.2 13.4 %collective-permute-start.11 = (f32[48,2560]{1,0:T(8,128)S(1)}, f32[48,2560]{1,0:T(8,128)S(1)}, u32[]{:S(2)}, u32[]{:S(2)}) collective-permute-start(f32[48,2560]{1,0:T(8,128)S(1)} %collective-permute-done.9.refs_2_), channel_id=1, source_target_pairs={{0,2},{1,3},{4,0},{5,1},{8,4},{9,5},{12,8},{13,9},{14,12},{15,13},... | collective-permute-start | bytes 1474568 | tf_op jit(solution)/shard_map/ppermute | solution.py:366
  53.6 2.3 %collective-permute-start.13 = (f32[48,2560]{1,0:T(8,128)S(1)}, f32[48,2560]{1,0:T(8,128)S(1)}, u32[]{:S(2)}, u32[]{:S(2)}) collective-permute-start(f32[48,2560]{1,0:T(8,128)S(1)} %collective-permute-done.7.first_ref.refs_0_), channel_id=1, source_target_pairs={{0,1},{1,0},{2,3},{3,2},{4,5},{5,4},{6,7},{7,6},{8,9},{9,8},{10,11... | collective-permute-start | bytes 1474568 | tf_op jit(solution)/shard_map/ppermute | solution.py:32
  53.6 2.6 %collective-permute-start.14 = (f32[48,2560]{1,0:T(8,128)S(1)}, f32[48,2560]{1,0:T(8,128)S(1)}, u32[]{:S(2)}, u32[]{:S(2)}) collective-permute-start(f32[48,2560]{1,0:T(8,128)S(1)} %collective-permute-done.11.second_ref.refs_2_), channel_id=1, source_target_pairs={{0,1},{1,0},{2,3},{3,2},{4,5},{5,4},{6,7},{7,6},{8,9},{9,8},{10,11... | collective-permute-start | bytes 1474568 | tf_op jit(solution)/shard_map/ppermute | solution.py:32
  54.1 9.1 %collective-permute-start.12 = (f32[48,2560]{1,0:T(8,128)S(1)}, f32[48,2560]{1,0:T(8,128)S(1)}, u32[]{:S(2)}, u32[]{:S(2)}) collective-permute-start(f32[48,2560]{1,0:T(8,128)S(1)} %pick.1), channel_id=1, source_target_pairs={{0,4},{4,8},{8,12},{12,14},{14,10},{10,6},{6,2},{2,0},{1,3},{5,1},... | collective-permute-start | bytes 1474568 | tf_op jit(solution)/shard_map/ppermute | solution.py:384
  63.2 1.9 %collective-permute-start.15 = (f32[48,2560]{1,0:T(8,128)S(1)}, f32[48,2560]{1,0:T(8,128)S(1)}, u32[]{:S(2)}, u32[]{:S(2)}) collective-permute-start(f32[48,2560]{1,0:T(8,128)S(1)} %collective-permute-done.12.refs_0_), channel_id=1, source_target_pairs={{0,1},{1,0},{2,3},{3,2},{4,5},{5,4},{6,7},{7,6},{8,9},{9,8},{10,11... | collective-permute-start | bytes 1474568 | tf_op jit(solution)/shard_map/ppermute | solution.py:32

commit v14 on v10

--- a/solution.py
+++ b/solution.py
@@ -9,6 +9,7 @@
 TILE = 128
 GATHER_LIMIT = 16 * 2**20
 SIDE = 256
+LATE_PANELS = 3
 FIRST_FLOPS = 4_000_000_000
 
 
@@ -240,7 +241,7 @@
     return 2 * chip + (1 - core if other else core)
 
 
-def border(arrivals, state, parents, diagonals, chips, last=False):
+def border(arrivals, state, parents, diagonals, chips, last=False, late=None, defer=0):
     begin = state is None
     nodes, width, _ = diagonals.shape
     rows = arrivals[0][2].shape[0]
@@ -255,7 +256,9 @@
         take = lambda number: [refs.pop(0) for _ in range(number)]
         part_refs = take(count)
         panel_before, kept_before, *held_before = take(4) if not begin else [None] * 4
-        parents_ref, diagonals_ref, parents_out, diagonals_out, panel_out = take(5)
+        parents_ref, diagonals_ref = take(2)
+        late_parents, late_diagonals = take(2) if late else [None] * 2
+        parents_out, diagonals_out, panel_out = take(3)
         copies = []
 
         def finish(place, source, target):
@@ -266,6 +269,7 @@
         parents_end, diagonals_end, panel_end = parents_out, diagonals_out, panel_out
         kept_now = None if last else take(1)[0]
         held_now = take(2)
+        tails = take(2 if defer else 0)
         turned, beside, aside = take(3)
         if last:
             parents_out, diagonals_out, panel_out, sems = take(4)
@@ -320,19 +324,31 @@
                 beside[fresh * place : fresh * (place + 1), columns] = part
         if last:
             finish(2 * nodes, panel_out, panel_end)
-        for node in range(nodes):
+        rest = nodes - defer
+        if defer:
+            tails[0][...] = turned[(rest - 1) * width :, :]
+            tails[1][...] = beside[:, rest * width :]
+            diagonals_out[rest:] = diagonals_ref[rest:]
+            parents_out[rest - 1 :] = parents_ref[rest - 1 :]
+        for node in range(rest):
             lower = max(node - 1, 0) * width
             columns = slice(node * width, (node + 1) * width)
             total = jnp.dot(turned[lower : columns.stop, :], beside[:, columns], preferred_element_type=f32)
-            diagonals_out[node] = diagonals_ref[node] + total[-width:]
+            total_below, total_here = total[:width], total[-width:]
+            if late and node >= nodes - late[0].shape[0]:
+                place = node - nodes + late[0].shape[0]
+                total_below = total_below + late_parents[place]
+                total_here = total_here + late_diagonals[place]
+            diagonals_out[node] = diagonals_ref[node] + total_here
             finish(node, diagonals_out.at[node], diagonals_end.at[node])
             if node > 0:
-                parents_out[node - 1] = parents_ref[node - 1] + total[:width]
+                parents_out[node - 1] = parents_ref[node - 1] + total_below
                 finish(nodes + node, parents_out.at[node - 1], parents_end.at[node - 1])
         for copy in copies:
             copy.wait()
 
-    operands = [part for _, _, part in arrivals] + list(state or []) + [parents, diagonals]
+    operands = [part for _, _, part in arrivals] + list(state or [])
+    operands += [parents, diagonals] + list(late or [])
     shape_of = jax.ShapeDtypeStruct
     shapes = [shape_of(parents.shape, f32), shape_of(diagonals.shape, f32)]
     held = [shape_of((order, nodes * width), bf16)] * 2
@@ -345,6 +361,9 @@
         scratch.append(pltpu.SemaphoreType.DMA((2 * nodes + 1,)))
     else:
         shapes += [shape_of((rows, nodes * width), f32), shape_of((order, order + 128), f32)] + held
+    if defer:
+        shapes.append(shape_of(((defer + 1) * width, 6 * fresh), bf16))
+        shapes.append(shape_of((6 * fresh, defer * width), bf16))
     results = kernel_call(
         kernel,
         "border" + ("_end" if last else "_begin" if begin else ""),
@@ -354,7 +373,27 @@
         scratch_shapes=scratch,
         limit=(24 if last else 16) * 2**20,
     )(*operands)
-    return results[:2], results[2:]
+    return (results[:2], results[2:6], results[6:]) if defer else (results[:2], results[2:])
+
+
+def late_products(turned, beside, width):
+    count = beside.shape[1] // width
+
+    def kernel(turned_ref, beside_ref, parents_ref, diagonals_ref):
+        for place in range(count):
+            left = turned_ref[place * width : (place + 2) * width, :]
+            right = beside_ref[:, place * width : (place + 1) * width]
+            total = jnp.dot(left, right, preferred_element_type=jnp.float32)
+            parents_ref[place] = total[:width]
+            diagonals_ref[place] = total[width:]
+
+    return kernel_call(
+        kernel,
+        "late_products",
+        out_shape=[jax.ShapeDtypeStruct((count, width, width), jnp.float32)] * 2,
+        in_specs=in_vmem(2),
+        out_specs=in_vmem(2),
+    )(turned, beside)
 
 
 def gather_plan(anc_blocks, anc_links, parent_links, pivot_inverse, pattern):
@@ -381,9 +420,10 @@
         pair = [after(value, *totals) for value in pair]
         arrivals = both(-step, pair[0]) + both(step, pair[1])
     last, totals = lax.optimization_barrier((pick(pair), totals))
-    totals, state = border(arrivals, state, *totals, chips)
-    last, totals = lax.optimization_barrier((lax.ppermute(last, "row", across), totals))
-    totals, panels = border(both(far, last), state, *totals, chips, True)
+    totals, state, tails = border(arrivals, state, *totals, chips, defer=LATE_PANELS)
+    last, totals, tails = lax.optimization_barrier((lax.ppermute(last, "row", across), totals, tails))
+    late = late_products(*tails, anc_links.shape[2])
+    totals, panels = border(both(far, last), state, *totals, chips, True, late)
     return panels[0], *totals
 
 

time: 70.5 us -> 70.2 us (level)
    ppermute x6, waiting for transfers between devices: 17.3 us -> 16 us  [move(): lax.ppermute(value, 'row', way)]
    ppermute x1, starting transfers between devices: 1.8 us -> 0.6 us  [gather_plan(): lax.ppermute(last, 'row', across)]
    pallas_call x0 -> x1, Pallas kernels: none -> 1.18 us  [late_products(): kernel_call(kernel, 'late_products', out_shape=[jax.ShapeDtypeStruct((cou...]
    ppermute x9, starting transfers between devices: 4.7 us -> 5.71 us  [swap_bit(): lax.ppermute(value, 'row', [(i, i ^ mask) for i in range(lax.axis_size('r...]
    pallas_call x5, Pallas kernels: 29 us -> 28.2 us  [border(): kernel_call(kernel, 'border' + ('_end' if last else '_begin' if begin els...]
    ppermute x1, waiting for transfers between devices: 0.44 us -> 1.27 us  [gather_plan(): lax.ppermute(last, 'row', across)]
  transfers between devices with their start and end apart: 16 -> 16, of which waited for: 10 -> 11; matrix products, arithmetic and copies ran while one was open for 0% -> 0% of each run, Pallas kernels for 43% -> 44%
where the time goes in v14:
time: 70.2 us; the launch traced here: 70.1 us
  Pallas kernels  35.7 us (51%)
  waiting for transfers between devices  20 us (28%)
  starting transfers between devices  12.4 us (18%)
  between operations  0.94 us (1%)
  local copies, waits for them, and re-layouts  0.92 us (1%)
    pallas_call x5, Pallas kernels, border(): kernel_call(kernel, 'border' + ('_end' if last else '_begin' if begin els...  28.2 us
    ppermute x6, waiting for transfers between devices, move(): lax.ppermute(value, 'row', way)  16 us
    ppermute x6, starting transfers between devices, move(): lax.ppermute(value, 'row', way)  6.13 us
    ppermute x9, starting transfers between devices, swap_bit(): lax.ppermute(value, 'row', [(i, i ^ mask) for i in range(lax.axis_size('r...  5.71 us
    pallas_call x1, Pallas kernels, inner_chain(): kernel_call(kernel, 'inner_chain', out_shape=[jax.ShapeDtypeStruct(array....  4.18 us
    ppermute x9, waiting for transfers between devices, swap_bit(): lax.ppermute(value, 'row', [(i, i ^ mask) for i in range(lax.axis_size('r...  2.79 us
    pallas_call x1, Pallas kernels, link_chain(): kernel_call(kernel, 'link_chain', out_shape=jax.ShapeDtypeStruct((rows, n...  1.93 us
  transfers between devices with their start and end apart: 16, of which 11 were waited for; matrix products, arithmetic and copies ran while one was open for 0% of the time, Pallas kernels for 44%

profile of v14, /device:TPU:0, one launch (start us, length us, event | category | flops | bytes accessed | tf_op | source)
XLA Modules:
  0.0 70.1 jit_solution(8383066281868290251)
XLA Ops:
  0.6 0.9 %copy-done.3 = f32[1,384,96]{1,2,0:T(8,128)S(1)} copy-done((f32[1,384,96]{1,2,0:T(8,128)S(1)}, f32[1,384,96]{1,2,0:T(8,128)}, u32[]{:S(2)}) %copy-start.3) | copy-done | bytes 147480
  1.7 4.1 %collective-permute-start = (f32[48,192]{1,0:T(8,128)S(1)}, f32[48,192]{1,0:T(8,128)S(1)}, u32[]{:S(2)}, u32[]{:S(2)}) collective-permute-start(f32[48,192]{1,0:T(8,128)S(1)} %far_rows.1), channel_id=1, source_target_pairs={{0,8},{1,9},{2,10},{3,11},{4,12},{5,13},{6,14},{7,15},{8,0},{9,1},... | collective-permute-start | bytes 110600 | tf_op jit(solution)/shard_map/ppermute | solution.py:32
  5.8 1.9 %link_chain.1.links_ref = f32[48,2048]{1,0:T(8,128)S(1)} custom-call(f32[48,8,256]{2,1,0:T(8,128)S(1)} %copy-done.2, f32[7,256,256]{2,1,0:T(8,128)S(1)} %copy-done, s32[8,6]{1,0:T(8,128)S(1)} %copy-done.4), custom_call_target="tpu_custom_call" | custom-call | tf_op jit(solution)/shard_map/link_chain/pallas_call | solution.py:165
  7.7 0.7 collective-permute-done.far_ref
  8.4 0.1 message.1.refs_0_
  8.6 1.8 %collective-permute-start.5 = (f32[48,2560]{1,0:T(8,128)S(1)}, f32[48,2560]{1,0:T(8,128)S(1)}, u32[]{:S(2)}, u32[]{:S(2)}) collective-permute-start(f32[48,2560]{1,0:T(8,128)S(1)} %message.1.refs_0_), channel_id=1, source_target_pairs={{0,2},{1,3},{4,0},{5,1},{8,4},{9,5},{12,8},{13,9},{14,12},{15,13},... | collective-permute-start | bytes 1474568 | tf_op jit(solution)/shard_map/ppermute | solution.py:406
  10.3 0.3 collective-permute-start.1
  10.6 4.2 %inner_chain.1 = (f32[7,256,256]{2,1,0:T(8,128)S(1)}, f32[8,256,256]{2,1,0:T(8,128)S(1)}) custom-call(f32[7,256,256]{2,1,0:T(8,128)S(1)} %copy-done, f32[8,256,256]{2,1,0:T(8,128)S(1)} %copy-done.1), custom_call_target="tpu_custom_call" | custom-call | tf_op jit(solution)/shard_map/inner_chain/pallas_call | solution.py:226
  14.8 4.0 %border_begin.1 = (f32[7,256,256]{2,1,0:T(8,128)S(1)}, f32[8,256,256]{2,1,0:T(8,128)S(1)}, f32[48,2048]{1,0:T(8,128)S(1)}, f32[768,896]{1,0:T(8,128)S(1)}, bf16[...) custom-call(f32[48,2560]{1,0:T(8,128)S(1)} %message.1.refs_0_, f32[48,2560]{1,0:T(8,128)S(1)} %collective-permute-done.2.refs_1_, ...), custom_call_target="tpu_custom_call" | custom-call | tf_op jit(solution)/shard_map/border_begin/pallas_call | solution.py:367
  18.8 3.4 %collective-permute-done.5.refs_2_ = f32[48,2560]{1,0:T(8,128)S(1)} collective-permute-done((f32[48,2560]{1,0:T(8,128)S(1)}, f32[48,2560]{1,0:T(8,128)S(1)}, u32[]{:S(2)}, u32[]{:S(2)}) %collective-permute-start.5) | collective-permute-done | bytes 491552 | tf_op jit(solution)/shard_map/ppermute | solution.py:406
  22.2 1.4 %collective-permute-done.1.refs_0_ = f32[48,2560]{1,0:T(8,128)S(1)} collective-permute-done((f32[48,2560]{1,0:T(8,128)S(1)}, f32[48,2560]{1,0:T(8,128)S(1)}, u32[]{:S(2)}, u32[]{:S(2)}) %collective-permute-start.1) | collective-permute-done | bytes 491552 | tf_op jit(solution)/shard_map/ppermute | solution.py:406
  23.6 0.5 collective-permute-start.6
  24.1 1.2 %collective-permute-start.9 = (f32[48,2560]{1,0:T(8,128)S(1)}, f32[48,2560]{1,0:T(8,128)S(1)}, u32[]{:S(2)}, u32[]{:S(2)}) collective-permute-start(f32[48,2560]{1,0:T(8,128)S(1)} %collective-permute-done.5.refs_2_), channel_id=1, source_target_pairs={{0,2},{1,3},{4,0},{5,1},{8,4},{9,5},{12,8},{13,9},{14,12},{15,13},... | collective-permute-start | bytes 1474568 | tf_op jit(solution)/shard_map/ppermute | solution.py:406
  25.3 0.9 %collective-permute-start.3 = (f32[48,2560]{1,0:T(8,128)S(1)}, f32[48,2560]{1,0:T(8,128)S(1)}, u32[]{:S(2)}, u32[]{:S(2)}) collective-permute-start(f32[48,2560]{1,0:T(8,128)S(1)} %collective-permute-done.1.refs_0_), channel_id=1, source_target_pairs={{0,4},{1,5},{4,8},{5,9},{8,12},{9,13},{12,14},{13,15},{14,10},{15,... | collective-permute-start | bytes 1474568 | tf_op jit(solution)/shard_map/ppermute | solution.py:406
  26.2 6.7 %border.3 = (f32[7,256,256]{2,1,0:T(8,128)S(1)}, f32[8,256,256]{2,1,0:T(8,128)S(1)}, f32[48,2048]{1,0:T(8,128)S(1)}, f32[768,896]{1,0:T(8,128)S(1)}, bf16[768,20...) custom-call(f32[48,2560]{1,0:T(8,128)S(1)} %collective-permute-done.1.refs_0_, ...), custom_call_target="tpu_custom_call" | custom-call | tf_op jit(solution)/shard_map/border/pallas_call | solution.py:367
  32.9 4.4 %collective-permute-done.9.refs_2_ = f32[48,2560]{1,0:T(8,128)S(1)} collective-permute-done((f32[48,2560]{1,0:T(8,128)S(1)}, f32[48,2560]{1,0:T(8,128)S(1)}, u32[]{:S(2)}, u32[]{:S(2)}) %collective-permute-start.9) | collective-permute-done | bytes 491552 | tf_op jit(solution)/shard_map/ppermute | solution.py:406
  37.3 1.0 %collective-permute-done.3.refs_0_ = f32[48,2560]{1,0:T(8,128)S(1)} collective-permute-done((f32[48,2560]{1,0:T(8,128)S(1)}, f32[48,2560]{1,0:T(8,128)S(1)}, u32[]{:S(2)}, u32[]{:S(2)}) %collective-permute-start.3) | collective-permute-done | bytes 491552 | tf_op jit(solution)/shard_map/ppermute | solution.py:406
  38.2 0.5 collective-permute-start.10
  38.7 1.7 %collective-permute-start.11 = (f32[48,2560]{1,0:T(8,128)S(1)}, f32[48,2560]{1,0:T(8,128)S(1)}, u32[]{:S(2)}, u32[]{:S(2)}) collective-permute-start(f32[48,2560]{1,0:T(8,128)S(1)} %collective-permute-done.9.refs_2_), channel_id=1, source_target_pairs={{0,2},{1,3},{4,0},{5,1},{8,4},{9,5},{12,8},{13,9},{14,12},{15,13},... | collective-permute-start | bytes 1474568 | tf_op jit(solution)/shard_map/ppermute | solution.py:406
  40.5 0.3 collective-permute-start.7
  40.8 6.7 %border.4 = (f32[7,256,256]{2,1,0:T(8,128)S(1)}, f32[8,256,256]{2,1,0:T(8,128)S(1)}, f32[48,2048]{1,0:T(8,128)S(1)}, f32[768,896]{1,0:T(8,128)S(1)}, bf16[768,20...) custom-call(f32[48,2560]{1,0:T(8,128)S(1)} %collective-permute-done.3.refs_0_, ...), custom_call_target="tpu_custom_call" | custom-call | tf_op jit(solution)/shard_map/border/pallas_call | solution.py:367
  47.5 4.4 %collective-permute-done.11.second_ref.refs_2_ = f32[48,2560]{1,0:T(8,128)S(1)} collective-permute-done((f32[48,2560]{1,0:T(8,128)S(1)}, f32[48,2560]{1,0:T(8,128)S(1)}, u32[]{:S(2)}, u32[]{:S(2)}) %collective-permute-start.11) | collective-permute-done | bytes 491552 | tf_op jit(solution)/shard_map/ppermute | solution.py:406
  51.9 1.5 %collective-permute-done.7.first_ref.refs_0_ = f32[48,2560]{1,0:T(8,128)S(1)} collective-permute-done((f32[48,2560]{1,0:T(8,128)S(1)}, f32[48,2560]{1,0:T(8,128)S(1)}, u32[]{:S(2)}, u32[]{:S(2)}) %collective-permute-start.7) | collective-permute-done | bytes 491552 | tf_op jit(solution)/shard_map/ppermute | solution.py:406
  53.3 0.5 collective-permute-start.14
  53.9 0.6 collective-permute-start.12
  54.5 0.7 collective-permute-done.13.refs_1_
  55.2 0.7 %collective-permute-done.14.refs_3_ = f32[48,2560]{1,0:T(8,128)S(1)} collective-permute-done((f32[48,2560]{1,0:T(8,128)S(1)}, f32[48,2560]{1,0:T(8,128)S(1)}, u32[]{:S(2)}, u32[]{:S(2)}) %collective-permute-start.14) | collective-permute-done | bytes 491552 | tf_op jit(solution)/shard_map/ppermute | solution.py:32
  55.9 5.9 %border.5 = (f32[7,256,256]{2,1,0:T(8,128)S(1)}, f32[8,256,256]{2,1,0:T(8,128)S(1)}, f32[48,2048]{1,0:T(8,128)S(1)}, f32[768,896]{1,0:T(8,128)S(1)}, bf16[768,20...) custom-call(f32[48,2560]{1,0:T(8,128)S(1)} %collective-permute-done., ...), custom_call_target="tpu_custom_call" | custom-call | tf_op jit(solution)/shard_map/border/pallas_call | solution.py:367
  61.8 1.3 %collective-permute-done.12.refs_0_ = f32[48,2560]{1,0:T(8,128)S(1)} collective-permute-done((f32[48,2560]{1,0:T(8,128)S(1)}, f32[48,2560]{1,0:T(8,128)S(1)}, u32[]{:S(2)}, u32[]{:S(2)}) %collective-permute-start.12) | collective-permute-done | bytes 491552 | tf_op jit(solution)/shard_map/ppermute | solution.py:424
  63.0 1.2 %late_products.1 = (f32[3,256,256]{2,1,0:T(8,128)S(1)}, f32[3,256,256]{2,1,0:T(8,128)S(1)}) custom-call(bf16[1024,1152]{1,0:T(8,128)(2,1)S(1)} %get-tuple-element.94.turned_ref, bf16[1152,768]{1,0:T(8,128)(2,1)S(1)} %get-tuple-element.95.beside_ref), custom_call_target="tpu_custom_call" | custom-call | tf_op jit(solution)/shard_map/late_products/pallas_call | solution.py:390
  64.2 0.7 collective-permute-done.15.refs_1_
  64.9 5.0 %border_end.1 = (f32[7,256,256]{2,1,0:T(8,128)}, f32[8,256,256]{2,1,0:T(8,128)}, f32[48,8,256]{2,1,0:T(8,128)}) custom-call(f32[48,2560]{1,0:T(8,128)S(1)} %collective-permute-done.12.refs_0_, f32[48,2560]{1,0:T(8,128)S(1)} %collective-permute-done.15.refs_1_, f32[48,2048]{1,0:T(8,128)S(1)} %get-tuple-element.88.refs_2_, ...), custom_call_target="tpu_custom_call" | custom-call | tf_op jit(solution)/shard_map/border_end/pallas_call | solution.py:367
  (21 shorter events, 0.3 us)
Async XLA Ops:
  0.6 0.9 %copy-start.3 = (f32[1,384,96]{1,2,0:T(8,128)S(1)}, f32[1,384,96]{1,2,0:T(8,128)}, u32[]{:S(2)}) copy-start(f32[1,384,96]{1,2,0:T(8,128)} %param.5) | copy-start | bytes 442372
  1.5 4.2 %copy-start = (f32[7,256,256]{2,1,0:T(8,128)S(1)}, f32[7,256,256]{2,1,0:T(8,128)}, u32[]{:S(2)}) copy-start(f32[7,256,256]{2,1,0:T(8,128)} %parent_ref.2) | copy-start | bytes 5505028
  1.5 4.2 %copy-start.2 = (f32[48,8,256]{2,1,0:T(8,128)S(1)}, f32[48,8,256]{2,1,0:T(8,128)}, u32[]{:S(2)}) copy-start(f32[48,8,256]{2,1,0:T(8,128)} %links_ref) | copy-start | bytes 1179652
  1.5 4.2 %copy-start.4 = (s32[8,6]{1,0:T(8,128)S(1)}, s32[8,6]{1,0:T(8,128)}, u32[]{:S(2)}) copy-start(s32[8,6]{1,0:T(8,128)} %pattern_ref.1) | copy-start | bytes 580
  1.7 9.0 %copy-start.1 = (f32[8,256,256]{2,1,0:T(8,128)S(1)}, f32[8,256,256]{2,1,0:T(8,128)}, u32[]{:S(2)}) copy-start(f32[8,256,256]{2,1,0:T(8,128)} %pivot_ref.1) | copy-start | bytes 6291460
  1.7 6.7 %collective-permute-start = (f32[48,192]{1,0:T(8,128)S(1)}, f32[48,192]{1,0:T(8,128)S(1)}, u32[]{:S(2)}, u32[]{:S(2)}) collective-permute-start(f32[48,192]{1,0:T(8,128)S(1)} %far_rows.1), channel_id=1, source_target_pairs={{0,8},{1,9},{2,10},{3,11},{4,12},{5,13},{6,14},{7,15},{8,0},{9,1},... | collective-permute-start | bytes 110600 | tf_op jit(solution)/shard_map/ppermute | solution.py:32
  8.5 6.3 %collective-permute-start.2 = (f32[48,2560]{1,0:T(8,128)S(1)}, f32[48,2560]{1,0:T(8,128)S(1)}, u32[]{:S(2)}, u32[]{:S(2)}) collective-permute-start(f32[48,2560]{1,0:T(8,128)S(1)} %message.1.refs_0_), channel_id=1, source_target_pairs={{0,1},{1,0},{2,3},{3,2},{4,5},{5,4},{6,7},{7,6},{8,9},{9,8},{10,11... | collective-permute-start | bytes 1474568 | tf_op jit(solution)/shard_map/ppermute | solution.py:32
  8.6 13.6 %collective-permute-start.5 = (f32[48,2560]{1,0:T(8,128)S(1)}, f32[48,2560]{1,0:T(8,128)S(1)}, u32[]{:S(2)}, u32[]{:S(2)}) collective-permute-start(f32[48,2560]{1,0:T(8,128)S(1)} %message.1.refs_0_), channel_id=1, source_target_pairs={{0,2},{1,3},{4,0},{5,1},{8,4},{9,5},{12,8},{13,9},{14,12},{15,13},... | collective-permute-start | bytes 1474568 | tf_op jit(solution)/shard_map/ppermute | solution.py:406
  10.3 13.3 %collective-permute-start.1 = (f32[48,2560]{1,0:T(8,128)S(1)}, f32[48,2560]{1,0:T(8,128)S(1)}, u32[]{:S(2)}, u32[]{:S(2)}) collective-permute-start(f32[48,2560]{1,0:T(8,128)S(1)} %message.1.refs_0_), channel_id=1, source_target_pairs={{0,4},{1,5},{4,8},{5,9},{8,12},{9,13},{12,14},{13,15},{14,10},{15,... | collective-permute-start | bytes 1474568 | tf_op jit(solution)/shard_map/ppermute | solution.py:406
  23.6 2.5 %collective-permute-start.4 = (f32[48,2560]{1,0:T(8,128)S(1)}, f32[48,2560]{1,0:T(8,128)S(1)}, u32[]{:S(2)}, u32[]{:S(2)}) collective-permute-start(f32[48,2560]{1,0:T(8,128)S(1)} %collective-permute-done.1.refs_0_), channel_id=1, source_target_pairs={{0,1},{1,0},{2,3},{3,2},{4,5},{5,4},{6,7},{7,6},{8,9},{9,8},{10,11... | collective-permute-start | bytes 1474568 | tf_op jit(solution)/shard_map/ppermute | solution.py:32
  23.6 2.6 %collective-permute-start.6 = (f32[48,2560]{1,0:T(8,128)S(1)}, f32[48,2560]{1,0:T(8,128)S(1)}, u32[]{:S(2)}, u32[]{:S(2)}) collective-permute-start(f32[48,2560]{1,0:T(8,128)S(1)} %collective-permute-done.5.refs_2_), channel_id=1, source_target_pairs={{0,1},{1,0},{2,3},{3,2},{4,5},{5,4},{6,7},{7,6},{8,9},{9,8},{10,11... | collective-permute-start | bytes 1474568 | tf_op jit(solution)/shard_map/ppermute | solution.py:32
  24.1 13.1 %collective-permute-start.9 = (f32[48,2560]{1,0:T(8,128)S(1)}, f32[48,2560]{1,0:T(8,128)S(1)}, u32[]{:S(2)}, u32[]{:S(2)}) collective-permute-start(f32[48,2560]{1,0:T(8,128)S(1)} %collective-permute-done.5.refs_2_), channel_id=1, source_target_pairs={{0,2},{1,3},{4,0},{5,1},{8,4},{9,5},{12,8},{13,9},{14,12},{15,13},... | collective-permute-start | bytes 1474568 | tf_op jit(solution)/shard_map/ppermute | solution.py:406
  25.3 12.9 %collective-permute-start.3 = (f32[48,2560]{1,0:T(8,128)S(1)}, f32[48,2560]{1,0:T(8,128)S(1)}, u32[]{:S(2)}, u32[]{:S(2)}) collective-permute-start(f32[48,2560]{1,0:T(8,128)S(1)} %collective-permute-done.1.refs_0_), channel_id=1, source_target_pairs={{0,4},{1,5},{4,8},{5,9},{8,12},{9,13},{12,14},{13,15},{14,10},{15,... | collective-permute-start | bytes 1474568 | tf_op jit(solution)/shard_map/ppermute | solution.py:406
  38.2 2.5 %collective-permute-start.8 = (f32[48,2560]{1,0:T(8,128)S(1)}, f32[48,2560]{1,0:T(8,128)S(1)}, u32[]{:S(2)}, u32[]{:S(2)}) collective-permute-start(f32[48,2560]{1,0:T(8,128)S(1)} %collective-permute-done.3.refs_0_), channel_id=1, source_target_pairs={{0,1},{1,0},{2,3},{3,2},{4,5},{5,4},{6,7},{7,6},{8,9},{9,8},{10,11... | collective-permute-start | bytes 1474568 | tf_op jit(solution)/shard_map/ppermute | solution.py:32
  38.2 2.6 %collective-permute-start.10 = (f32[48,2560]{1,0:T(8,128)S(1)}, f32[48,2560]{1,0:T(8,128)S(1)}, u32[]{:S(2)}, u32[]{:S(2)}) collective-permute-start(f32[48,2560]{1,0:T(8,128)S(1)} %collective-permute-done.9.refs_2_), channel_id=1, source_target_pairs={{0,1},{1,0},{2,3},{3,2},{4,5},{5,4},{6,7},{7,6},{8,9},{9,8},{10,11... | collective-permute-start | bytes 1474568 | tf_op jit(solution)/shard_map/ppermute | solution.py:32
  38.7 13.1 %collective-permute-start.11 = (f32[48,2560]{1,0:T(8,128)S(1)}, f32[48,2560]{1,0:T(8,128)S(1)}, u32[]{:S(2)}, u32[]{:S(2)}) collective-permute-start(f32[48,2560]{1,0:T(8,128)S(1)} %collective-permute-done.9.refs_2_), channel_id=1, source_target_pairs={{0,2},{1,3},{4,0},{5,1},{8,4},{9,5},{12,8},{13,9},{14,12},{15,13},... | collective-permute-start | bytes 1474568 | tf_op jit(solution)/shard_map/ppermute | solution.py:406
  40.5 12.9 %collective-permute-start.7 = (f32[48,2560]{1,0:T(8,128)S(1)}, f32[48,2560]{1,0:T(8,128)S(1)}, u32[]{:S(2)}, u32[]{:S(2)}) collective-permute-start(f32[48,2560]{1,0:T(8,128)S(1)} %collective-permute-done.3.refs_0_), channel_id=1, source_target_pairs={{0,4},{1,5},{4,8},{5,9},{8,12},{9,13},{12,14},{13,15},{14,10},{15,... | collective-permute-start | bytes 1474568 | tf_op jit(solution)/shard_map/ppermute | solution.py:406
  53.3 1.9 %collective-permute-start.13 = (f32[48,2560]{1,0:T(8,128)S(1)}, f32[48,2560]{1,0:T(8,128)S(1)}, u32[]{:S(2)}, u32[]{:S(2)}) collective-permute-start(f32[48,2560]{1,0:T(8,128)S(1)} %collective-permute-done.7.first_ref.refs_0_), channel_id=1, source_target_pairs={{0,1},{1,0},{2,3},{3,2},{4,5},{5,4},{6,7},{7,6},{8,9},{9,8},{10,11... | collective-permute-start | bytes 1474568 | tf_op jit(solution)/shard_map/ppermute | solution.py:32
  53.3 2.6 %collective-permute-start.14 = (f32[48,2560]{1,0:T(8,128)S(1)}, f32[48,2560]{1,0:T(8,128)S(1)}, u32[]{:S(2)}, u32[]{:S(2)}) collective-permute-start(f32[48,2560]{1,0:T(8,128)S(1)} %collective-permute-done.11.second_ref.refs_2_), channel_id=1, source_target_pairs={{0,1},{1,0},{2,3},{3,2},{4,5},{5,4},{6,7},{7,6},{8,9},{9,8},{10,11... | collective-permute-start | bytes 1474568 | tf_op jit(solution)/shard_map/ppermute | solution.py:32
  53.9 9.1 %collective-permute-start.12 = (f32[48,2560]{1,0:T(8,128)S(1)}, f32[48,2560]{1,0:T(8,128)S(1)}, u32[]{:S(2)}, u32[]{:S(2)}) collective-permute-start(f32[48,2560]{1,0:T(8,128)S(1)} %pick.1), channel_id=1, source_target_pairs={{0,4},{4,8},{8,12},{12,14},{14,10},{10,6},{6,2},{2,0},{1,3},{5,1},... | collective-permute-start | bytes 1474568 | tf_op jit(solution)/shard_map/ppermute | solution.py:424
  63.0 1.9 %collective-permute-start.15 = (f32[48,2560]{1,0:T(8,128)S(1)}, f32[48,2560]{1,0:T(8,128)S(1)}, u32[]{:S(2)}, u32[]{:S(2)}) collective-permute-start(f32[48,2560]{1,0:T(8,128)S(1)} %collective-permute-done.12.refs_0_), channel_id=1, source_target_pairs={{0,1},{1,0},{2,3},{3,2},{4,5},{5,4},{6,7},{7,6},{8,9},{9,8},{10,11... | collective-permute-start | bytes 1474568 | tf_op jit(solution)/shard_map/ppermute | solution.py:32

commit v15 on v14

--- a/solution.py
+++ b/solution.py
@@ -118,13 +118,14 @@
         low = me < PCOL
         theirs = jnp.where(low, turned_ref[rows:], turned_ref[:rows])
         first = lax.rem(me, PCOL) + jnp.where(low, 1, 0)
-        out_ref[...] = pltpu.roll(theirs, lax.rem(columns - lax.rem(first, PCOL) * rows, columns), 1)[:, : columns // 2]
+        theirs = pltpu.roll(theirs, lax.rem(columns - lax.rem(first, PCOL) * rows, columns), 1)[:, : columns // 2]
+        out_ref[...] = jnp.concatenate([theirs[: rows // 2], theirs[rows // 2 :]], axis=1)
 
     return kernel_call(
         kernel,
         "far_rows",
         flops=FIRST_FLOPS,
-        out_shape=jax.ShapeDtypeStruct((rows, columns // 2), jnp.float32),
+        out_shape=jax.ShapeDtypeStruct((rows // 2, columns), jnp.float32),
         in_specs=in_vmem(1),
         out_specs=in_vmem(1)[0],
     )(turned)
@@ -183,7 +184,8 @@
         weight = jnp.where((lane < rows) | (lane >= near - rows), 0.5, 1.0)
         out_ref[:, :SIDE] = mine * jnp.where(lane < near, weight, 0.0)
         out_ref[:, SIDE : 2 * SIDE] = jnp.zeros((rows, SIDE), jnp.float32)
-        out_ref[:, SIDE : SIDE + columns // 2] = far_ref[...]
+        out_ref[: rows // 2, SIDE : SIDE + columns // 2] = far_ref[:, : columns // 2]
+        out_ref[rows // 2 :, SIDE : SIDE + columns // 2] = far_ref[:, columns // 2 :]
         out_ref[:, 2 * SIDE :] = links_ref[...]
 
     return kernel_call(
@@ -268,7 +270,7 @@
 
         parents_end, diagonals_end, panel_end = parents_out, diagonals_out, panel_out
         kept_now = None if last else take(1)[0]
-        held_now = take(2)
+        held_now = take(0 if last else 2)
         tails = take(2 if defer else 0)
         turned, beside, aside = take(3)
         if last:
@@ -280,6 +282,7 @@
 
         for part, whole in enumerate(held_now):
             whole[...] = jnp.zeros(whole.shape, bf16) if begin else held_before[part][...]
+        held = held_before if last else held_now
         for start, ref in zip(starts, part_refs):
             for whole, part in zip(held_now, halves(ref[:, lanes:])):
                 whole[pl.ds(start, rows), :] = part
@@ -302,13 +305,19 @@
             pair = columns_at(aside, lax.div(me, 2) * (2 * rows), 2 * rows)[:rows]
             swapped = jnp.concatenate([pair[:, rows : 2 * rows], pair[:, :rows]], axis=1)
             across += jnp.where(core == 0, pair[:, : 2 * rows], swapped)
+        if last:
+            pair = columns_at(aside, lax.div(owners[0], 2) * (2 * rows), 2 * rows)
+            swapped = jnp.concatenate([pair[:, rows : 2 * rows], pair[:, :rows]], axis=1)
+            between = halves(jnp.where(core == 0, pair[:, : 2 * rows], swapped))
         left, across = halves(left), halves(across)
         for node in range(nodes):
             columns = slice(node * width, (node + 1) * width)
-            image = stacked_dot(left, [whole[:, columns] for whole in held_now])
+            image = stacked_dot(left, [whole[:, columns] for whole in held])
             there = slice(lanes + node * width, lanes + (node + 1) * width)
             new = jnp.concatenate([ref[:, there] for ref in part_refs], axis=0)
             new_high, new_low = halves(new)
+            if last:
+                image = image + stacked_dot(between, [new_high, new_low])
             image_high, image_low = halves(image)
             own = stacked_dot(across, [new_high, new_low])
             if not begin:
@@ -356,7 +365,6 @@
     scratch = [pltpu.VMEM(*shape) for shape in scratch]
     if last:
         shapes.append(shape_of((rows, nodes, width), f32))
-        scratch = [pltpu.VMEM(shape.shape, bf16) for shape in held] + scratch
         scratch += [pltpu.VMEM(shape.shape, f32) for shape in shapes]
         scratch.append(pltpu.SemaphoreType.DMA((2 * nodes + 1,)))
     else:

time: 70.2 us -> 69.8 us (level)
  no operation moved by 1% of the time
where the time goes in v15:
time: 69.8 us; the launch traced here: 69.6 us
  Pallas kernels  35.6 us (51%)
  waiting for transfers between devices  19.7 us (28%)
  starting transfers between devices  12.4 us (18%)
  between operations  0.93 us (1%)
  local copies, waits for them, and re-layouts  0.92 us (1%)
    pallas_call x5, Pallas kernels, border(): kernel_call(kernel, 'border' + ('_end' if last else '_begin' if begin els...  28 us
    ppermute x6, waiting for transfers between devices, move(): lax.ppermute(value, 'row', way)  16 us
    ppermute x6, starting transfers between devices, move(): lax.ppermute(value, 'row', way)  6.13 us
    ppermute x9, starting transfers between devices, swap_bit(): lax.ppermute(value, 'row', [(i, i ^ mask) for i in range(lax.axis_size('r...  5.67 us
    pallas_call x1, Pallas kernels, inner_chain(): kernel_call(kernel, 'inner_chain', out_shape=[jax.ShapeDtypeStruct(array....  4.18 us
    ppermute x9, waiting for transfers between devices, swap_bit(): lax.ppermute(value, 'row', [(i, i ^ mask) for i in range(lax.axis_size('r...  2.47 us
    pallas_call x1, Pallas kernels, link_chain(): kernel_call(kernel, 'link_chain', out_shape=jax.ShapeDtypeStruct((rows, n...  1.94 us
  transfers between devices with their start and end apart: 16, of which 11 were waited for; matrix products, arithmetic and copies ran while one was open for 0% of the time, Pallas kernels for 44%

profile of v15, /device:TPU:0, one launch (start us, length us, event | category | flops | bytes accessed | tf_op | source)
XLA Modules:
  0.0 69.6 jit_solution(17617066227522294220)
XLA Ops:
  0.6 0.9 %copy-done.3 = f32[1,384,96]{1,2,0:T(8,128)S(1)} copy-done((f32[1,384,96]{1,2,0:T(8,128)S(1)}, f32[1,384,96]{1,2,0:T(8,128)}, u32[]{:S(2)}) %copy-start.3) | copy-done | bytes 147480
  1.5 0.2 far_rows.1
  1.7 4.1 %collective-permute-start = (f32[24,384]{1,0:T(8,128)S(1)}, f32[24,384]{1,0:T(8,128)S(1)}, u32[]{:S(2)}, u32[]{:S(2)}) collective-permute-start(f32[24,384]{1,0:T(8,128)S(1)} %far_rows.1), channel_id=1, source_target_pairs={{0,8},{1,9},{2,10},{3,11},{4,12},{5,13},{6,14},{7,15},{8,0},{9,1},... | collective-permute-start | bytes 110600 | tf_op jit(solution)/shard_map/ppermute | solution.py:32
  5.8 1.9 %link_chain.1.links_ref = f32[48,2048]{1,0:T(8,128)S(1)} custom-call(f32[48,8,256]{2,1,0:T(8,128)S(1)} %copy-done.2, f32[7,256,256]{2,1,0:T(8,128)S(1)} %copy-done, s32[8,6]{1,0:T(8,128)S(1)} %copy-done.4), custom_call_target="tpu_custom_call" | custom-call | tf_op jit(solution)/shard_map/link_chain/pallas_call | solution.py:166
  7.7 0.4 collective-permute-done.far_ref
  8.3 1.8 %collective-permute-start.5 = (f32[48,2560]{1,0:T(8,128)S(1)}, f32[48,2560]{1,0:T(8,128)S(1)}, u32[]{:S(2)}, u32[]{:S(2)}) collective-permute-start(f32[48,2560]{1,0:T(8,128)S(1)} %message.1.refs_0_), channel_id=1, source_target_pairs={{0,2},{1,3},{4,0},{5,1},{8,4},{9,5},{12,8},{13,9},{14,12},{15,13},... | collective-permute-start | bytes 1474568 | tf_op jit(solution)/shard_map/ppermute | solution.py:414
  10.1 0.3 collective-permute-start.1
  10.4 4.2 %inner_chain.1 = (f32[7,256,256]{2,1,0:T(8,128)S(1)}, f32[8,256,256]{2,1,0:T(8,128)S(1)}) custom-call(f32[7,256,256]{2,1,0:T(8,128)S(1)} %copy-done, f32[8,256,256]{2,1,0:T(8,128)S(1)} %copy-done.1), custom_call_target="tpu_custom_call" | custom-call | tf_op jit(solution)/shard_map/inner_chain/pallas_call | solution.py:228
  14.6 4.0 %border_begin.1 = (f32[7,256,256]{2,1,0:T(8,128)S(1)}, f32[8,256,256]{2,1,0:T(8,128)S(1)}, f32[48,2048]{1,0:T(8,128)S(1)}, f32[768,896]{1,0:T(8,128)S(1)}, bf16[...) custom-call(f32[48,2560]{1,0:T(8,128)S(1)} %message.1.refs_0_, f32[48,2560]{1,0:T(8,128)S(1)} %collective-permute-done.2.refs_1_, ...), custom_call_target="tpu_custom_call" | custom-call | tf_op jit(solution)/shard_map/border_begin/pallas_call | solution.py:375
  18.5 3.4 %collective-permute-done.5.refs_2_ = f32[48,2560]{1,0:T(8,128)S(1)} collective-permute-done((f32[48,2560]{1,0:T(8,128)S(1)}, f32[48,2560]{1,0:T(8,128)S(1)}, u32[]{:S(2)}, u32[]{:S(2)}) %collective-permute-start.5) | collective-permute-done | bytes 491552 | tf_op jit(solution)/shard_map/ppermute | solution.py:414
  21.9 1.4 %collective-permute-done.1.refs_0_ = f32[48,2560]{1,0:T(8,128)S(1)} collective-permute-done((f32[48,2560]{1,0:T(8,128)S(1)}, f32[48,2560]{1,0:T(8,128)S(1)}, u32[]{:S(2)}, u32[]{:S(2)}) %collective-permute-start.1) | collective-permute-done | bytes 491552 | tf_op jit(solution)/shard_map/ppermute | solution.py:414
  23.4 0.5 collective-permute-start.6
  23.9 1.3 %collective-permute-start.9 = (f32[48,2560]{1,0:T(8,128)S(1)}, f32[48,2560]{1,0:T(8,128)S(1)}, u32[]{:S(2)}, u32[]{:S(2)}) collective-permute-start(f32[48,2560]{1,0:T(8,128)S(1)} %collective-permute-done.5.refs_2_), channel_id=1, source_target_pairs={{0,2},{1,3},{4,0},{5,1},{8,4},{9,5},{12,8},{13,9},{14,12},{15,13},... | collective-permute-start | bytes 1474568 | tf_op jit(solution)/shard_map/ppermute | solution.py:414
  25.2 0.7 %collective-permute-start.3 = (f32[48,2560]{1,0:T(8,128)S(1)}, f32[48,2560]{1,0:T(8,128)S(1)}, u32[]{:S(2)}, u32[]{:S(2)}) collective-permute-start(f32[48,2560]{1,0:T(8,128)S(1)} %collective-permute-done.1.refs_0_), channel_id=1, source_target_pairs={{0,4},{1,5},{4,8},{5,9},{8,12},{9,13},{12,14},{13,15},{14,10},{15,... | collective-permute-start | bytes 1474568 | tf_op jit(solution)/shard_map/ppermute | solution.py:414
  25.9 6.7 %border.3 = (f32[7,256,256]{2,1,0:T(8,128)S(1)}, f32[8,256,256]{2,1,0:T(8,128)S(1)}, f32[48,2048]{1,0:T(8,128)S(1)}, f32[768,896]{1,0:T(8,128)S(1)}, bf16[768,20...) custom-call(f32[48,2560]{1,0:T(8,128)S(1)} %collective-permute-done.1.refs_0_, ...), custom_call_target="tpu_custom_call" | custom-call | tf_op jit(solution)/shard_map/border/pallas_call | solution.py:375
  32.6 4.4 %collective-permute-done.9.refs_2_ = f32[48,2560]{1,0:T(8,128)S(1)} collective-permute-done((f32[48,2560]{1,0:T(8,128)S(1)}, f32[48,2560]{1,0:T(8,128)S(1)}, u32[]{:S(2)}, u32[]{:S(2)}) %collective-permute-start.9) | collective-permute-done | bytes 491552 | tf_op jit(solution)/shard_map/ppermute | solution.py:414
  37.0 1.0 %collective-permute-done.3.refs_0_ = f32[48,2560]{1,0:T(8,128)S(1)} collective-permute-done((f32[48,2560]{1,0:T(8,128)S(1)}, f32[48,2560]{1,0:T(8,128)S(1)}, u32[]{:S(2)}, u32[]{:S(2)}) %collective-permute-start.3) | collective-permute-done | bytes 491552 | tf_op jit(solution)/shard_map/ppermute | solution.py:414
  38.0 0.5 collective-permute-start.10
  38.5 1.7 %collective-permute-start.11 = (f32[48,2560]{1,0:T(8,128)S(1)}, f32[48,2560]{1,0:T(8,128)S(1)}, u32[]{:S(2)}, u32[]{:S(2)}) collective-permute-start(f32[48,2560]{1,0:T(8,128)S(1)} %collective-permute-done.9.refs_2_), channel_id=1, source_target_pairs={{0,2},{1,3},{4,0},{5,1},{8,4},{9,5},{12,8},{13,9},{14,12},{15,13},... | collective-permute-start | bytes 1474568 | tf_op jit(solution)/shard_map/ppermute | solution.py:414
  40.2 0.3 collective-permute-start.7
  40.6 6.7 %border.4 = (f32[7,256,256]{2,1,0:T(8,128)S(1)}, f32[8,256,256]{2,1,0:T(8,128)S(1)}, f32[48,2048]{1,0:T(8,128)S(1)}, f32[768,896]{1,0:T(8,128)S(1)}, bf16[768,20...) custom-call(f32[48,2560]{1,0:T(8,128)S(1)} %collective-permute-done.3.refs_0_, ...), custom_call_target="tpu_custom_call" | custom-call | tf_op jit(solution)/shard_map/border/pallas_call | solution.py:375
  47.3 4.4 %collective-permute-done.11.second_ref.refs_2_ = f32[48,2560]{1,0:T(8,128)S(1)} collective-permute-done((f32[48,2560]{1,0:T(8,128)S(1)}, f32[48,2560]{1,0:T(8,128)S(1)}, u32[]{:S(2)}, u32[]{:S(2)}) %collective-permute-start.11) | collective-permute-done | bytes 491552 | tf_op jit(solution)/shard_map/ppermute | solution.py:414
  51.7 1.4 %collective-permute-done.7.first_ref.refs_0_ = f32[48,2560]{1,0:T(8,128)S(1)} collective-permute-done((f32[48,2560]{1,0:T(8,128)S(1)}, f32[48,2560]{1,0:T(8,128)S(1)}, u32[]{:S(2)}, u32[]{:S(2)}) %collective-permute-start.7) | collective-permute-done | bytes 491552 | tf_op jit(solution)/shard_map/ppermute | solution.py:414
  53.1 0.5 collective-permute-start.14
  53.6 0.6 collective-permute-start.12
  54.3 0.6 collective-permute-done.13.refs_1_
  54.9 0.7 %collective-permute-done.14.refs_3_ = f32[48,2560]{1,0:T(8,128)S(1)} collective-permute-done((f32[48,2560]{1,0:T(8,128)S(1)}, f32[48,2560]{1,0:T(8,128)S(1)}, u32[]{:S(2)}, u32[]{:S(2)}) %collective-permute-start.14) | collective-permute-done | bytes 491552 | tf_op jit(solution)/shard_map/ppermute | solution.py:32
  55.6 5.9 %border.5 = (f32[7,256,256]{2,1,0:T(8,128)S(1)}, f32[8,256,256]{2,1,0:T(8,128)S(1)}, f32[48,2048]{1,0:T(8,128)S(1)}, f32[768,896]{1,0:T(8,128)S(1)}, bf16[768,20...) custom-call(f32[48,2560]{1,0:T(8,128)S(1)} %collective-permute-done., ...), custom_call_target="tpu_custom_call" | custom-call | tf_op jit(solution)/shard_map/border/pallas_call | solution.py:375
  61.5 1.3 %collective-permute-done.12.refs_0_ = f32[48,2560]{1,0:T(8,128)S(1)} collective-permute-done((f32[48,2560]{1,0:T(8,128)S(1)}, f32[48,2560]{1,0:T(8,128)S(1)}, u32[]{:S(2)}, u32[]{:S(2)}) %collective-permute-start.12) | collective-permute-done | bytes 491552 | tf_op jit(solution)/shard_map/ppermute | solution.py:432
  62.8 1.2 %late_products.1 = (f32[3,256,256]{2,1,0:T(8,128)S(1)}, f32[3,256,256]{2,1,0:T(8,128)S(1)}) custom-call(bf16[1024,1152]{1,0:T(8,128)(2,1)S(1)} %get-tuple-element.94.turned_ref, bf16[1152,768]{1,0:T(8,128)(2,1)S(1)} %get-tuple-element.95.beside_ref), custom_call_target="tpu_custom_call" | custom-call | tf_op jit(solution)/shard_map/late_products/pallas_call | solution.py:398
  64.0 0.7 collective-permute-done.15.refs_1_
  64.7 4.8 %border_end.1 = (f32[7,256,256]{2,1,0:T(8,128)}, f32[8,256,256]{2,1,0:T(8,128)}, f32[48,8,256]{2,1,0:T(8,128)}) custom-call(f32[48,2560]{1,0:T(8,128)S(1)} %collective-permute-done.12.refs_0_, f32[48,2560]{1,0:T(8,128)S(1)} %collective-permute-done.15.refs_1_, f32[48,2048]{1,0:T(8,128)S(1)} %get-tuple-element.88.refs_2_, ...), custom_call_target="tpu_custom_call" | custom-call | tf_op jit(solution)/shard_map/border_end/pallas_call | solution.py:375
  (21 shorter events, 0.3 us)
Async XLA Ops:
  0.6 0.9 %copy-start.3 = (f32[1,384,96]{1,2,0:T(8,128)S(1)}, f32[1,384,96]{1,2,0:T(8,128)}, u32[]{:S(2)}) copy-start(f32[1,384,96]{1,2,0:T(8,128)} %param.5) | copy-start | bytes 442372
  1.5 4.2 %copy-start = (f32[7,256,256]{2,1,0:T(8,128)S(1)}, f32[7,256,256]{2,1,0:T(8,128)}, u32[]{:S(2)}) copy-start(f32[7,256,256]{2,1,0:T(8,128)} %parent_ref.2) | copy-start | bytes 5505028
  1.5 4.2 %copy-start.2 = (f32[48,8,256]{2,1,0:T(8,128)S(1)}, f32[48,8,256]{2,1,0:T(8,128)}, u32[]{:S(2)}) copy-start(f32[48,8,256]{2,1,0:T(8,128)} %links_ref) | copy-start | bytes 1179652
  1.5 4.2 %copy-start.4 = (s32[8,6]{1,0:T(8,128)S(1)}, s32[8,6]{1,0:T(8,128)}, u32[]{:S(2)}) copy-start(s32[8,6]{1,0:T(8,128)} %pattern_ref.1) | copy-start | bytes 580
  1.7 8.7 %copy-start.1 = (f32[8,256,256]{2,1,0:T(8,128)S(1)}, f32[8,256,256]{2,1,0:T(8,128)}, u32[]{:S(2)}) copy-start(f32[8,256,256]{2,1,0:T(8,128)} %pivot_ref.1) | copy-start | bytes 6291460
  1.7 6.4 %collective-permute-start = (f32[24,384]{1,0:T(8,128)S(1)}, f32[24,384]{1,0:T(8,128)S(1)}, u32[]{:S(2)}, u32[]{:S(2)}) collective-permute-start(f32[24,384]{1,0:T(8,128)S(1)} %far_rows.1), channel_id=1, source_target_pairs={{0,8},{1,9},{2,10},{3,11},{4,12},{5,13},{6,14},{7,15},{8,0},{9,1},... | collective-permute-start | bytes 110600 | tf_op jit(solution)/shard_map/ppermute | solution.py:32
  8.2 6.3 %collective-permute-start.2 = (f32[48,2560]{1,0:T(8,128)S(1)}, f32[48,2560]{1,0:T(8,128)S(1)}, u32[]{:S(2)}, u32[]{:S(2)}) collective-permute-start(f32[48,2560]{1,0:T(8,128)S(1)} %message.1.refs_0_), channel_id=1, source_target_pairs={{0,1},{1,0},{2,3},{3,2},{4,5},{5,4},{6,7},{7,6},{8,9},{9,8},{10,11... | collective-permute-start | bytes 1474568 | tf_op jit(solution)/shard_map/ppermute | solution.py:32
  8.3 13.6 %collective-permute-start.5 = (f32[48,2560]{1,0:T(8,128)S(1)}, f32[48,2560]{1,0:T(8,128)S(1)}, u32[]{:S(2)}, u32[]{:S(2)}) collective-permute-start(f32[48,2560]{1,0:T(8,128)S(1)} %message.1.refs_0_), channel_id=1, source_target_pairs={{0,2},{1,3},{4,0},{5,1},{8,4},{9,5},{12,8},{13,9},{14,12},{15,13},... | collective-permute-start | bytes 1474568 | tf_op jit(solution)/shard_map/ppermute | solution.py:414
  10.1 13.3 %collective-permute-start.1 = (f32[48,2560]{1,0:T(8,128)S(1)}, f32[48,2560]{1,0:T(8,128)S(1)}, u32[]{:S(2)}, u32[]{:S(2)}) collective-permute-start(f32[48,2560]{1,0:T(8,128)S(1)} %message.1.refs_0_), channel_id=1, source_target_pairs={{0,4},{1,5},{4,8},{5,9},{8,12},{9,13},{12,14},{13,15},{14,10},{15,... | collective-permute-start | bytes 1474568 | tf_op jit(solution)/shard_map/ppermute | solution.py:414
  23.4 2.5 %collective-permute-start.4 = (f32[48,2560]{1,0:T(8,128)S(1)}, f32[48,2560]{1,0:T(8,128)S(1)}, u32[]{:S(2)}, u32[]{:S(2)}) collective-permute-start(f32[48,2560]{1,0:T(8,128)S(1)} %collective-permute-done.1.refs_0_), channel_id=1, source_target_pairs={{0,1},{1,0},{2,3},{3,2},{4,5},{5,4},{6,7},{7,6},{8,9},{9,8},{10,11... | collective-permute-start | bytes 1474568 | tf_op jit(solution)/shard_map/ppermute | solution.py:32
  23.4 2.6 %collective-permute-start.6 = (f32[48,2560]{1,0:T(8,128)S(1)}, f32[48,2560]{1,0:T(8,128)S(1)}, u32[]{:S(2)}, u32[]{:S(2)}) collective-permute-start(f32[48,2560]{1,0:T(8,128)S(1)} %collective-permute-done.5.refs_2_), channel_id=1, source_target_pairs={{0,1},{1,0},{2,3},{3,2},{4,5},{5,4},{6,7},{7,6},{8,9},{9,8},{10,11... | collective-permute-start | bytes 1474568 | tf_op jit(solution)/shard_map/ppermute | solution.py:32
  23.9 13.1 %collective-permute-start.9 = (f32[48,2560]{1,0:T(8,128)S(1)}, f32[48,2560]{1,0:T(8,128)S(1)}, u32[]{:S(2)}, u32[]{:S(2)}) collective-permute-start(f32[48,2560]{1,0:T(8,128)S(1)} %collective-permute-done.5.refs_2_), channel_id=1, source_target_pairs={{0,2},{1,3},{4,0},{5,1},{8,4},{9,5},{12,8},{13,9},{14,12},{15,13},... | collective-permute-start | bytes 1474568 | tf_op jit(solution)/shard_map/ppermute | solution.py:414
  25.2 12.9 %collective-permute-start.3 = (f32[48,2560]{1,0:T(8,128)S(1)}, f32[48,2560]{1,0:T(8,128)S(1)}, u32[]{:S(2)}, u32[]{:S(2)}) collective-permute-start(f32[48,2560]{1,0:T(8,128)S(1)} %collective-permute-done.1.refs_0_), channel_id=1, source_target_pairs={{0,4},{1,5},{4,8},{5,9},{8,12},{9,13},{12,14},{13,15},{14,10},{15,... | collective-permute-start | bytes 1474568 | tf_op jit(solution)/shard_map/ppermute | solution.py:414
  38.0 2.5 %collective-permute-start.8 = (f32[48,2560]{1,0:T(8,128)S(1)}, f32[48,2560]{1,0:T(8,128)S(1)}, u32[]{:S(2)}, u32[]{:S(2)}) collective-permute-start(f32[48,2560]{1,0:T(8,128)S(1)} %collective-permute-done.3.refs_0_), channel_id=1, source_target_pairs={{0,1},{1,0},{2,3},{3,2},{4,5},{5,4},{6,7},{7,6},{8,9},{9,8},{10,11... | collective-permute-start | bytes 1474568 | tf_op jit(solution)/shard_map/ppermute | solution.py:32
  38.0 2.6 %collective-permute-start.10 = (f32[48,2560]{1,0:T(8,128)S(1)}, f32[48,2560]{1,0:T(8,128)S(1)}, u32[]{:S(2)}, u32[]{:S(2)}) collective-permute-start(f32[48,2560]{1,0:T(8,128)S(1)} %collective-permute-done.9.refs_2_), channel_id=1, source_target_pairs={{0,1},{1,0},{2,3},{3,2},{4,5},{5,4},{6,7},{7,6},{8,9},{9,8},{10,11... | collective-permute-start | bytes 1474568 | tf_op jit(solution)/shard_map/ppermute | solution.py:32
  38.5 13.1 %collective-permute-start.11 = (f32[48,2560]{1,0:T(8,128)S(1)}, f32[48,2560]{1,0:T(8,128)S(1)}, u32[]{:S(2)}, u32[]{:S(2)}) collective-permute-start(f32[48,2560]{1,0:T(8,128)S(1)} %collective-permute-done.9.refs_2_), channel_id=1, source_target_pairs={{0,2},{1,3},{4,0},{5,1},{8,4},{9,5},{12,8},{13,9},{14,12},{15,13},... | collective-permute-start | bytes 1474568 | tf_op jit(solution)/shard_map/ppermute | solution.py:414
  40.2 12.9 %collective-permute-start.7 = (f32[48,2560]{1,0:T(8,128)S(1)}, f32[48,2560]{1,0:T(8,128)S(1)}, u32[]{:S(2)}, u32[]{:S(2)}) collective-permute-start(f32[48,2560]{1,0:T(8,128)S(1)} %collective-permute-done.3.refs_0_), channel_id=1, source_target_pairs={{0,4},{1,5},{4,8},{5,9},{8,12},{9,13},{12,14},{13,15},{14,10},{15,... | collective-permute-start | bytes 1474568 | tf_op jit(solution)/shard_map/ppermute | solution.py:414
  53.1 1.9 %collective-permute-start.13 = (f32[48,2560]{1,0:T(8,128)S(1)}, f32[48,2560]{1,0:T(8,128)S(1)}, u32[]{:S(2)}, u32[]{:S(2)}) collective-permute-start(f32[48,2560]{1,0:T(8,128)S(1)} %collective-permute-done.7.first_ref.refs_0_), channel_id=1, source_target_pairs={{0,1},{1,0},{2,3},{3,2},{4,5},{5,4},{6,7},{7,6},{8,9},{9,8},{10,11... | collective-permute-start | bytes 1474568 | tf_op jit(solution)/shard_map/ppermute | solution.py:32
  53.1 2.6 %collective-permute-start.14 = (f32[48,2560]{1,0:T(8,128)S(1)}, f32[48,2560]{1,0:T(8,128)S(1)}, u32[]{:S(2)}, u32[]{:S(2)}) collective-permute-start(f32[48,2560]{1,0:T(8,128)S(1)} %collective-permute-done.11.second_ref.refs_2_), channel_id=1, source_target_pairs={{0,1},{1,0},{2,3},{3,2},{4,5},{5,4},{6,7},{7,6},{8,9},{9,8},{10,11... | collective-permute-start | bytes 1474568 | tf_op jit(solution)/shard_map/ppermute | solution.py:32
  53.6 9.1 %collective-permute-start.12 = (f32[48,2560]{1,0:T(8,128)S(1)}, f32[48,2560]{1,0:T(8,128)S(1)}, u32[]{:S(2)}, u32[]{:S(2)}) collective-permute-start(f32[48,2560]{1,0:T(8,128)S(1)} %pick.1), channel_id=1, source_target_pairs={{0,4},{4,8},{8,12},{12,14},{14,10},{10,6},{6,2},{2,0},{1,3},{5,1},... | collective-permute-start | bytes 1474568 | tf_op jit(solution)/shard_map/ppermute | solution.py:432
  62.8 1.9 %collective-permute-start.15 = (f32[48,2560]{1,0:T(8,128)S(1)}, f32[48,2560]{1,0:T(8,128)S(1)}, u32[]{:S(2)}, u32[]{:S(2)}) collective-permute-start(f32[48,2560]{1,0:T(8,128)S(1)} %collective-permute-done.12.refs_0_), channel_id=1, source_target_pairs={{0,1},{1,0},{2,3},{3,2},{4,5},{5,4},{6,7},{7,6},{8,9},{9,8},{10,11... | collective-permute-start | bytes 1474568 | tf_op jit(solution)/shard_map/ppermute | solution.py:32

commit v16 on v15

--- a/solution.py
+++ b/solution.py
@@ -14,7 +14,7 @@
 
 
 def product(left, right):
-    return jnp.dot(left, right, precision=lax.Precision.HIGH, preferred_element_type=jnp.float32)
+    return jnp.dot(left, right, precision=lax.Precision.HIGHEST, preferred_element_type=jnp.float32)
 
 
 def inner_product(left, right):
@@ -22,7 +22,7 @@
         left,
         right,
         (((0,), (0,)), ((), ())),
-        precision=lax.Precision.HIGH,
+        precision=lax.Precision.HIGHEST,
         preferred_element_type=jnp.float32,
     )
 

time: 69.8 us -> 69.8 us (level)
  no operation moved by 1% of the time
where the time goes in v16:
time: 69.8 us; the launch traced here: 69.6 us
  Pallas kernels  35.6 us (51%)
  waiting for transfers between devices  19.7 us (28%)
  starting transfers between devices  12.4 us (18%)
  between operations  0.93 us (1%)
  local copies, waits for them, and re-layouts  0.92 us (1%)
    pallas_call x5, Pallas kernels, border(): kernel_call(kernel, 'border' + ('_end' if last else '_begin' if begin els...  28 us
    ppermute x6, waiting for transfers between devices, move(): lax.ppermute(value, 'row', way)  16 us
    ppermute x6, starting transfers between devices, move(): lax.ppermute(value, 'row', way)  6.13 us
    ppermute x9, starting transfers between devices, swap_bit(): lax.ppermute(value, 'row', [(i, i ^ mask) for i in range(lax.axis_size('r...  5.67 us
    pallas_call x1, Pallas kernels, inner_chain(): kernel_call(kernel, 'inner_chain', out_shape=[jax.ShapeDtypeStruct(array....  4.18 us
    ppermute x9, waiting for transfers between devices, swap_bit(): lax.ppermute(value, 'row', [(i, i ^ mask) for i in range(lax.axis_size('r...  2.47 us
    pallas_call x1, Pallas kernels, link_chain(): kernel_call(kernel, 'link_chain', out_shape=jax.ShapeDtypeStruct((rows, n...  1.94 us
  transfers between devices with their start and end apart: 16, of which 11 were waited for; matrix products, arithmetic and copies ran while one was open for 0% of the time, Pallas kernels for 44%

profile of v16, /device:TPU:0, one launch (start us, length us, event | category | flops | bytes accessed | tf_op | source)
XLA Modules:
  0.0 69.6 jit_solution(17617066227522294220)
XLA Ops:
  0.6 0.9 %copy-done.3 = f32[1,384,96]{1,2,0:T(8,128)S(1)} copy-done((f32[1,384,96]{1,2,0:T(8,128)S(1)}, f32[1,384,96]{1,2,0:T(8,128)}, u32[]{:S(2)}) %copy-start.3) | copy-done | bytes 147480
  1.5 0.2 far_rows.1
  1.7 4.1 %collective-permute-start = (f32[24,384]{1,0:T(8,128)S(1)}, f32[24,384]{1,0:T(8,128)S(1)}, u32[]{:S(2)}, u32[]{:S(2)}) collective-permute-start(f32[24,384]{1,0:T(8,128)S(1)} %far_rows.1), channel_id=1, source_target_pairs={{0,8},{1,9},{2,10},{3,11},{4,12},{5,13},{6,14},{7,15},{8,0},{9,1},... | collective-permute-start | bytes 110600 | tf_op jit(solution)/shard_map/ppermute | solution.py:32
  5.8 1.9 %link_chain.1.links_ref = f32[48,2048]{1,0:T(8,128)S(1)} custom-call(f32[48,8,256]{2,1,0:T(8,128)S(1)} %copy-done.2, f32[7,256,256]{2,1,0:T(8,128)S(1)} %copy-done, s32[8,6]{1,0:T(8,128)S(1)} %copy-done.4), custom_call_target="tpu_custom_call" | custom-call | tf_op jit(solution)/shard_map/link_chain/pallas_call | solution.py:166
  7.7 0.4 collective-permute-done.far_ref
  8.3 1.8 %collective-permute-start.5 = (f32[48,2560]{1,0:T(8,128)S(1)}, f32[48,2560]{1,0:T(8,128)S(1)}, u32[]{:S(2)}, u32[]{:S(2)}) collective-permute-start(f32[48,2560]{1,0:T(8,128)S(1)} %message.1.refs_0_), channel_id=1, source_target_pairs={{0,2},{1,3},{4,0},{5,1},{8,4},{9,5},{12,8},{13,9},{14,12},{15,13},... | collective-permute-start | bytes 1474568 | tf_op jit(solution)/shard_map/ppermute | solution.py:414
  10.1 0.3 collective-permute-start.1
  10.4 4.2 %inner_chain.1 = (f32[7,256,256]{2,1,0:T(8,128)S(1)}, f32[8,256,256]{2,1,0:T(8,128)S(1)}) custom-call(f32[7,256,256]{2,1,0:T(8,128)S(1)} %copy-done, f32[8,256,256]{2,1,0:T(8,128)S(1)} %copy-done.1), custom_call_target="tpu_custom_call" | custom-call | tf_op jit(solution)/shard_map/inner_chain/pallas_call | solution.py:228
  14.6 4.0 %border_begin.1 = (f32[7,256,256]{2,1,0:T(8,128)S(1)}, f32[8,256,256]{2,1,0:T(8,128)S(1)}, f32[48,2048]{1,0:T(8,128)S(1)}, f32[768,896]{1,0:T(8,128)S(1)}, bf16[...) custom-call(f32[48,2560]{1,0:T(8,128)S(1)} %message.1.refs_0_, f32[48,2560]{1,0:T(8,128)S(1)} %collective-permute-done.2.refs_1_, ...), custom_call_target="tpu_custom_call" | custom-call | tf_op jit(solution)/shard_map/border_begin/pallas_call | solution.py:375
  18.5 3.4 %collective-permute-done.5.refs_2_ = f32[48,2560]{1,0:T(8,128)S(1)} collective-permute-done((f32[48,2560]{1,0:T(8,128)S(1)}, f32[48,2560]{1,0:T(8,128)S(1)}, u32[]{:S(2)}, u32[]{:S(2)}) %collective-permute-start.5) | collective-permute-done | bytes 491552 | tf_op jit(solution)/shard_map/ppermute | solution.py:414
  21.9 1.4 %collective-permute-done.1.refs_0_ = f32[48,2560]{1,0:T(8,128)S(1)} collective-permute-done((f32[48,2560]{1,0:T(8,128)S(1)}, f32[48,2560]{1,0:T(8,128)S(1)}, u32[]{:S(2)}, u32[]{:S(2)}) %collective-permute-start.1) | collective-permute-done | bytes 491552 | tf_op jit(solution)/shard_map/ppermute | solution.py:414
  23.4 0.5 collective-permute-start.6
  23.9 1.3 %collective-permute-start.9 = (f32[48,2560]{1,0:T(8,128)S(1)}, f32[48,2560]{1,0:T(8,128)S(1)}, u32[]{:S(2)}, u32[]{:S(2)}) collective-permute-start(f32[48,2560]{1,0:T(8,128)S(1)} %collective-permute-done.5.refs_2_), channel_id=1, source_target_pairs={{0,2},{1,3},{4,0},{5,1},{8,4},{9,5},{12,8},{13,9},{14,12},{15,13},... | collective-permute-start | bytes 1474568 | tf_op jit(solution)/shard_map/ppermute | solution.py:414
  25.2 0.7 %collective-permute-start.3 = (f32[48,2560]{1,0:T(8,128)S(1)}, f32[48,2560]{1,0:T(8,128)S(1)}, u32[]{:S(2)}, u32[]{:S(2)}) collective-permute-start(f32[48,2560]{1,0:T(8,128)S(1)} %collective-permute-done.1.refs_0_), channel_id=1, source_target_pairs={{0,4},{1,5},{4,8},{5,9},{8,12},{9,13},{12,14},{13,15},{14,10},{15,... | collective-permute-start | bytes 1474568 | tf_op jit(solution)/shard_map/ppermute | solution.py:414
  25.9 6.7 %border.3 = (f32[7,256,256]{2,1,0:T(8,128)S(1)}, f32[8,256,256]{2,1,0:T(8,128)S(1)}, f32[48,2048]{1,0:T(8,128)S(1)}, f32[768,896]{1,0:T(8,128)S(1)}, bf16[768,20...) custom-call(f32[48,2560]{1,0:T(8,128)S(1)} %collective-permute-done.1.refs_0_, ...), custom_call_target="tpu_custom_call" | custom-call | tf_op jit(solution)/shard_map/border/pallas_call | solution.py:375
  32.6 4.4 %collective-permute-done.9.refs_2_ = f32[48,2560]{1,0:T(8,128)S(1)} collective-permute-done((f32[48,2560]{1,0:T(8,128)S(1)}, f32[48,2560]{1,0:T(8,128)S(1)}, u32[]{:S(2)}, u32[]{:S(2)}) %collective-permute-start.9) | collective-permute-done | bytes 491552 | tf_op jit(solution)/shard_map/ppermute | solution.py:414
  37.0 1.0 %collective-permute-done.3.refs_0_ = f32[48,2560]{1,0:T(8,128)S(1)} collective-permute-done((f32[48,2560]{1,0:T(8,128)S(1)}, f32[48,2560]{1,0:T(8,128)S(1)}, u32[]{:S(2)}, u32[]{:S(2)}) %collective-permute-start.3) | collective-permute-done | bytes 491552 | tf_op jit(solution)/shard_map/ppermute | solution.py:414
  38.0 0.5 collective-permute-start.10
  38.5 1.7 %collective-permute-start.11 = (f32[48,2560]{1,0:T(8,128)S(1)}, f32[48,2560]{1,0:T(8,128)S(1)}, u32[]{:S(2)}, u32[]{:S(2)}) collective-permute-start(f32[48,2560]{1,0:T(8,128)S(1)} %collective-permute-done.9.refs_2_), channel_id=1, source_target_pairs={{0,2},{1,3},{4,0},{5,1},{8,4},{9,5},{12,8},{13,9},{14,12},{15,13},... | collective-permute-start | bytes 1474568 | tf_op jit(solution)/shard_map/ppermute | solution.py:414
  40.2 0.3 collective-permute-start.7
  40.6 6.7 %border.4 = (f32[7,256,256]{2,1,0:T(8,128)S(1)}, f32[8,256,256]{2,1,0:T(8,128)S(1)}, f32[48,2048]{1,0:T(8,128)S(1)}, f32[768,896]{1,0:T(8,128)S(1)}, bf16[768,20...) custom-call(f32[48,2560]{1,0:T(8,128)S(1)} %collective-permute-done.3.refs_0_, ...), custom_call_target="tpu_custom_call" | custom-call | tf_op jit(solution)/shard_map/border/pallas_call | solution.py:375
  47.3 4.4 %collective-permute-done.11.second_ref.refs_2_ = f32[48,2560]{1,0:T(8,128)S(1)} collective-permute-done((f32[48,2560]{1,0:T(8,128)S(1)}, f32[48,2560]{1,0:T(8,128)S(1)}, u32[]{:S(2)}, u32[]{:S(2)}) %collective-permute-start.11) | collective-permute-done | bytes 491552 | tf_op jit(solution)/shard_map/ppermute | solution.py:414
  51.7 1.4 %collective-permute-done.7.first_ref.refs_0_ = f32[48,2560]{1,0:T(8,128)S(1)} collective-permute-done((f32[48,2560]{1,0:T(8,128)S(1)}, f32[48,2560]{1,0:T(8,128)S(1)}, u32[]{:S(2)}, u32[]{:S(2)}) %collective-permute-start.7) | collective-permute-done | bytes 491552 | tf_op jit(solution)/shard_map/ppermute | solution.py:414
  53.1 0.5 collective-permute-start.14
  53.6 0.6 collective-permute-start.12
  54.3 0.6 collective-permute-done.13.refs_1_
  54.9 0.7 %collective-permute-done.14.refs_3_ = f32[48,2560]{1,0:T(8,128)S(1)} collective-permute-done((f32[48,2560]{1,0:T(8,128)S(1)}, f32[48,2560]{1,0:T(8,128)S(1)}, u32[]{:S(2)}, u32[]{:S(2)}) %collective-permute-start.14) | collective-permute-done | bytes 491552 | tf_op jit(solution)/shard_map/ppermute | solution.py:32
  55.6 5.9 %border.5 = (f32[7,256,256]{2,1,0:T(8,128)S(1)}, f32[8,256,256]{2,1,0:T(8,128)S(1)}, f32[48,2048]{1,0:T(8,128)S(1)}, f32[768,896]{1,0:T(8,128)S(1)}, bf16[768,20...) custom-call(f32[48,2560]{1,0:T(8,128)S(1)} %collective-permute-done., ...), custom_call_target="tpu_custom_call" | custom-call | tf_op jit(solution)/shard_map/border/pallas_call | solution.py:375
  61.5 1.3 %collective-permute-done.12.refs_0_ = f32[48,2560]{1,0:T(8,128)S(1)} collective-permute-done((f32[48,2560]{1,0:T(8,128)S(1)}, f32[48,2560]{1,0:T(8,128)S(1)}, u32[]{:S(2)}, u32[]{:S(2)}) %collective-permute-start.12) | collective-permute-done | bytes 491552 | tf_op jit(solution)/shard_map/ppermute | solution.py:432
  62.8 1.2 %late_products.1 = (f32[3,256,256]{2,1,0:T(8,128)S(1)}, f32[3,256,256]{2,1,0:T(8,128)S(1)}) custom-call(bf16[1024,1152]{1,0:T(8,128)(2,1)S(1)} %get-tuple-element.94.turned_ref, bf16[1152,768]{1,0:T(8,128)(2,1)S(1)} %get-tuple-element.95.beside_ref), custom_call_target="tpu_custom_call" | custom-call | tf_op jit(solution)/shard_map/late_products/pallas_call | solution.py:398
  64.0 0.7 collective-permute-done.15.refs_1_
  64.7 4.8 %border_end.1 = (f32[7,256,256]{2,1,0:T(8,128)}, f32[8,256,256]{2,1,0:T(8,128)}, f32[48,8,256]{2,1,0:T(8,128)}) custom-call(f32[48,2560]{1,0:T(8,128)S(1)} %collective-permute-done.12.refs_0_, f32[48,2560]{1,0:T(8,128)S(1)} %collective-permute-done.15.refs_1_, f32[48,2048]{1,0:T(8,128)S(1)} %get-tuple-element.88.refs_2_, ...), custom_call_target="tpu_custom_call" | custom-call | tf_op jit(solution)/shard_map/border_end/pallas_call | solution.py:375
  (21 shorter events, 0.3 us)
Async XLA Ops:
  0.6 0.9 %copy-start.3 = (f32[1,384,96]{1,2,0:T(8,128)S(1)}, f32[1,384,96]{1,2,0:T(8,128)}, u32[]{:S(2)}) copy-start(f32[1,384,96]{1,2,0:T(8,128)} %param.5) | copy-start | bytes 442372
  1.5 4.2 %copy-start = (f32[7,256,256]{2,1,0:T(8,128)S(1)}, f32[7,256,256]{2,1,0:T(8,128)}, u32[]{:S(2)}) copy-start(f32[7,256,256]{2,1,0:T(8,128)} %parent_ref.2) | copy-start | bytes 5505028
  1.5 4.2 %copy-start.2 = (f32[48,8,256]{2,1,0:T(8,128)S(1)}, f32[48,8,256]{2,1,0:T(8,128)}, u32[]{:S(2)}) copy-start(f32[48,8,256]{2,1,0:T(8,128)} %links_ref) | copy-start | bytes 1179652
  1.5 4.2 %copy-start.4 = (s32[8,6]{1,0:T(8,128)S(1)}, s32[8,6]{1,0:T(8,128)}, u32[]{:S(2)}) copy-start(s32[8,6]{1,0:T(8,128)} %pattern_ref.1) | copy-start | bytes 580
  1.7 8.7 %copy-start.1 = (f32[8,256,256]{2,1,0:T(8,128)S(1)}, f32[8,256,256]{2,1,0:T(8,128)}, u32[]{:S(2)}) copy-start(f32[8,256,256]{2,1,0:T(8,128)} %pivot_ref.1) | copy-start | bytes 6291460
  1.7 6.4 %collective-permute-start = (f32[24,384]{1,0:T(8,128)S(1)}, f32[24,384]{1,0:T(8,128)S(1)}, u32[]{:S(2)}, u32[]{:S(2)}) collective-permute-start(f32[24,384]{1,0:T(8,128)S(1)} %far_rows.1), channel_id=1, source_target_pairs={{0,8},{1,9},{2,10},{3,11},{4,12},{5,13},{6,14},{7,15},{8,0},{9,1},... | collective-permute-start | bytes 110600 | tf_op jit(solution)/shard_map/ppermute | solution.py:32
  8.2 6.3 %collective-permute-start.2 = (f32[48,2560]{1,0:T(8,128)S(1)}, f32[48,2560]{1,0:T(8,128)S(1)}, u32[]{:S(2)}, u32[]{:S(2)}) collective-permute-start(f32[48,2560]{1,0:T(8,128)S(1)} %message.1.refs_0_), channel_id=1, source_target_pairs={{0,1},{1,0},{2,3},{3,2},{4,5},{5,4},{6,7},{7,6},{8,9},{9,8},{10,11... | collective-permute-start | bytes 1474568 | tf_op jit(solution)/shard_map/ppermute | solution.py:32
  8.3 13.6 %collective-permute-start.5 = (f32[48,2560]{1,0:T(8,128)S(1)}, f32[48,2560]{1,0:T(8,128)S(1)}, u32[]{:S(2)}, u32[]{:S(2)}) collective-permute-start(f32[48,2560]{1,0:T(8,128)S(1)} %message.1.refs_0_), channel_id=1, source_target_pairs={{0,2},{1,3},{4,0},{5,1},{8,4},{9,5},{12,8},{13,9},{14,12},{15,13},... | collective-permute-start | bytes 1474568 | tf_op jit(solution)/shard_map/ppermute | solution.py:414
  10.1 13.3 %collective-permute-start.1 = (f32[48,2560]{1,0:T(8,128)S(1)}, f32[48,2560]{1,0:T(8,128)S(1)}, u32[]{:S(2)}, u32[]{:S(2)}) collective-permute-start(f32[48,2560]{1,0:T(8,128)S(1)} %message.1.refs_0_), channel_id=1, source_target_pairs={{0,4},{1,5},{4,8},{5,9},{8,12},{9,13},{12,14},{13,15},{14,10},{15,... | collective-permute-start | bytes 1474568 | tf_op jit(solution)/shard_map/ppermute | solution.py:414
  23.4 2.5 %collective-permute-start.4 = (f32[48,2560]{1,0:T(8,128)S(1)}, f32[48,2560]{1,0:T(8,128)S(1)}, u32[]{:S(2)}, u32[]{:S(2)}) collective-permute-start(f32[48,2560]{1,0:T(8,128)S(1)} %collective-permute-done.1.refs_0_), channel_id=1, source_target_pairs={{0,1},{1,0},{2,3},{3,2},{4,5},{5,4},{6,7},{7,6},{8,9},{9,8},{10,11... | collective-permute-start | bytes 1474568 | tf_op jit(solution)/shard_map/ppermute | solution.py:32
  23.4 2.6 %collective-permute-start.6 = (f32[48,2560]{1,0:T(8,128)S(1)}, f32[48,2560]{1,0:T(8,128)S(1)}, u32[]{:S(2)}, u32[]{:S(2)}) collective-permute-start(f32[48,2560]{1,0:T(8,128)S(1)} %collective-permute-done.5.refs_2_), channel_id=1, source_target_pairs={{0,1},{1,0},{2,3},{3,2},{4,5},{5,4},{6,7},{7,6},{8,9},{9,8},{10,11... | collective-permute-start | bytes 1474568 | tf_op jit(solution)/shard_map/ppermute | solution.py:32
  23.9 13.1 %collective-permute-start.9 = (f32[48,2560]{1,0:T(8,128)S(1)}, f32[48,2560]{1,0:T(8,128)S(1)}, u32[]{:S(2)}, u32[]{:S(2)}) collective-permute-start(f32[48,2560]{1,0:T(8,128)S(1)} %collective-permute-done.5.refs_2_), channel_id=1, source_target_pairs={{0,2},{1,3},{4,0},{5,1},{8,4},{9,5},{12,8},{13,9},{14,12},{15,13},... | collective-permute-start | bytes 1474568 | tf_op jit(solution)/shard_map/ppermute | solution.py:414
  25.2 12.9 %collective-permute-start.3 = (f32[48,2560]{1,0:T(8,128)S(1)}, f32[48,2560]{1,0:T(8,128)S(1)}, u32[]{:S(2)}, u32[]{:S(2)}) collective-permute-start(f32[48,2560]{1,0:T(8,128)S(1)} %collective-permute-done.1.refs_0_), channel_id=1, source_target_pairs={{0,4},{1,5},{4,8},{5,9},{8,12},{9,13},{12,14},{13,15},{14,10},{15,... | collective-permute-start | bytes 1474568 | tf_op jit(solution)/shard_map/ppermute | solution.py:414
  38.0 2.5 %collective-permute-start.8 = (f32[48,2560]{1,0:T(8,128)S(1)}, f32[48,2560]{1,0:T(8,128)S(1)}, u32[]{:S(2)}, u32[]{:S(2)}) collective-permute-start(f32[48,2560]{1,0:T(8,128)S(1)} %collective-permute-done.3.refs_0_), channel_id=1, source_target_pairs={{0,1},{1,0},{2,3},{3,2},{4,5},{5,4},{6,7},{7,6},{8,9},{9,8},{10,11... | collective-permute-start | bytes 1474568 | tf_op jit(solution)/shard_map/ppermute | solution.py:32
  38.0 2.6 %collective-permute-start.10 = (f32[48,2560]{1,0:T(8,128)S(1)}, f32[48,2560]{1,0:T(8,128)S(1)}, u32[]{:S(2)}, u32[]{:S(2)}) collective-permute-start(f32[48,2560]{1,0:T(8,128)S(1)} %collective-permute-done.9.refs_2_), channel_id=1, source_target_pairs={{0,1},{1,0},{2,3},{3,2},{4,5},{5,4},{6,7},{7,6},{8,9},{9,8},{10,11... | collective-permute-start | bytes 1474568 | tf_op jit(solution)/shard_map/ppermute | solution.py:32
  38.5 13.1 %collective-permute-start.11 = (f32[48,2560]{1,0:T(8,128)S(1)}, f32[48,2560]{1,0:T(8,128)S(1)}, u32[]{:S(2)}, u32[]{:S(2)}) collective-permute-start(f32[48,2560]{1,0:T(8,128)S(1)} %collective-permute-done.9.refs_2_), channel_id=1, source_target_pairs={{0,2},{1,3},{4,0},{5,1},{8,4},{9,5},{12,8},{13,9},{14,12},{15,13},... | collective-permute-start | bytes 1474568 | tf_op jit(solution)/shard_map/ppermute | solution.py:414
  40.2 12.9 %collective-permute-start.7 = (f32[48,2560]{1,0:T(8,128)S(1)}, f32[48,2560]{1,0:T(8,128)S(1)}, u32[]{:S(2)}, u32[]{:S(2)}) collective-permute-start(f32[48,2560]{1,0:T(8,128)S(1)} %collective-permute-done.3.refs_0_), channel_id=1, source_target_pairs={{0,4},{1,5},{4,8},{5,9},{8,12},{9,13},{12,14},{13,15},{14,10},{15,... | collective-permute-start | bytes 1474568 | tf_op jit(solution)/shard_map/ppermute | solution.py:414
  53.1 1.9 %collective-permute-start.13 = (f32[48,2560]{1,0:T(8,128)S(1)}, f32[48,2560]{1,0:T(8,128)S(1)}, u32[]{:S(2)}, u32[]{:S(2)}) collective-permute-start(f32[48,2560]{1,0:T(8,128)S(1)} %collective-permute-done.7.first_ref.refs_0_), channel_id=1, source_target_pairs={{0,1},{1,0},{2,3},{3,2},{4,5},{5,4},{6,7},{7,6},{8,9},{9,8},{10,11... | collective-permute-start | bytes 1474568 | tf_op jit(solution)/shard_map/ppermute | solution.py:32
  53.1 2.6 %collective-permute-start.14 = (f32[48,2560]{1,0:T(8,128)S(1)}, f32[48,2560]{1,0:T(8,128)S(1)}, u32[]{:S(2)}, u32[]{:S(2)}) collective-permute-start(f32[48,2560]{1,0:T(8,128)S(1)} %collective-permute-done.11.second_ref.refs_2_), channel_id=1, source_target_pairs={{0,1},{1,0},{2,3},{3,2},{4,5},{5,4},{6,7},{7,6},{8,9},{9,8},{10,11... | collective-permute-start | bytes 1474568 | tf_op jit(solution)/shard_map/ppermute | solution.py:32
  53.6 9.1 %collective-permute-start.12 = (f32[48,2560]{1,0:T(8,128)S(1)}, f32[48,2560]{1,0:T(8,128)S(1)}, u32[]{:S(2)}, u32[]{:S(2)}) collective-permute-start(f32[48,2560]{1,0:T(8,128)S(1)} %pick.1), channel_id=1, source_target_pairs={{0,4},{4,8},{8,12},{12,14},{14,10},{10,6},{6,2},{2,0},{1,3},{5,1},... | collective-permute-start | bytes 1474568 | tf_op jit(solution)/shard_map/ppermute | solution.py:432
  62.8 1.9 %collective-permute-start.15 = (f32[48,2560]{1,0:T(8,128)S(1)}, f32[48,2560]{1,0:T(8,128)S(1)}, u32[]{:S(2)}, u32[]{:S(2)}) collective-permute-start(f32[48,2560]{1,0:T(8,128)S(1)} %collective-permute-done.12.refs_0_), channel_id=1, source_target_pairs={{0,1},{1,0},{2,3},{3,2},{4,5},{5,4},{6,7},{7,6},{8,9},{9,8},{10,11... | collective-permute-start | bytes 1474568 | tf_op jit(solution)/shard_map/ppermute | solution.py:32

commit v17 on v16

--- a/solution.py
+++ b/solution.py
@@ -131,17 +131,26 @@
     )(turned)
 
 
-def pick(pair):
-    def kernel(first_ref, second_ref, out_ref):
-        out_ref[...] = jnp.where(lax.rem(lax.axis_index("row"), 2) == 0, first_ref[...], second_ref[...])
-
-    return kernel_call(
-        kernel,
-        "pick",
-        out_shape=jax.ShapeDtypeStruct(pair[0].shape, jnp.float32),
-        in_specs=in_vmem(2),
-        out_specs=in_vmem(1)[0],
-    )(*pair)
+def upper_and_lower(pair):
+    rows, columns = pair[0].shape
+
+    def kernel(first_ref, second_ref, upper_ref, lower_ref):
+        upper_ref[...] = first_ref[: rows // 2]
+        lower_ref[...] = second_ref[rows // 2 :]
+
+    shape = jax.ShapeDtypeStruct((rows // 2, columns), jnp.float32)
+    return kernel_call(kernel, "upper_lower", out_shape=[shape] * 2, in_specs=in_vmem(2), out_specs=in_vmem(2))(*pair)
+
+
+def stacked(pair):
+    rows, columns = pair[0].shape
+
+    def kernel(upper_ref, lower_ref, out_ref):
+        out_ref[:rows] = upper_ref[...]
+        out_ref[rows:] = lower_ref[...]
+
+    shape = jax.ShapeDtypeStruct((2 * rows, columns), jnp.float32)
+    return kernel_call(kernel, "stacked", out_shape=shape, in_specs=in_vmem(2), out_specs=in_vmem(1)[0])(*pair)
 
 
 def link_chain(anc_links, parent_links, pattern):
@@ -408,7 +417,6 @@
     chips = lax.axis_size("row") // 2
     far = chips // 2
     ahead, behind = ring_pairs(chips, 1), ring_pairs(chips, -1)
-    across = [p for p in ahead if p[0] % 2 == 0] + [p for p in behind if p[0] % 2 == 1]
 
     def move(pair):
         return [lax.ppermute(value, "row", way) for value, way in zip(pair, (ahead, behind))]
@@ -427,9 +435,10 @@
         totals, state = border(arrivals, state, *totals, chips)
         pair = [after(value, *totals) for value in pair]
         arrivals = both(-step, pair[0]) + both(step, pair[1])
-    last, totals = lax.optimization_barrier((pick(pair), totals))
+    halves_on, totals = lax.optimization_barrier((upper_and_lower(pair), totals))
     totals, state, tails = border(arrivals, state, *totals, chips, defer=LATE_PANELS)
-    last, totals, tails = lax.optimization_barrier((lax.ppermute(last, "row", across), totals, tails))
+    halves_on, totals, tails = lax.optimization_barrier((move(halves_on), totals, tails))
+    last = stacked(halves_on)
     late = late_products(*tails, anc_links.shape[2])
     totals, panels = border(both(far, last), state, *totals, chips, True, late)
     return panels[0], *totals

time: 69.8 us -> 69 us (0.989)
  waiting for transfers between devices: 19.7 us -> 17.3 us
  starting transfers between devices: 12.4 us -> 14 us
    ppermute x6 -> x8, starting transfers between devices: 6.13 us -> 8.25 us  [move(): lax.ppermute(value, 'row', way)]
    ppermute x9, waiting for transfers between devices: 2.47 us -> 1.12 us  [swap_bit(): lax.ppermute(value, 'row', [(i, i ^ mask) for i in range(lax.axis_size('r...]
    ppermute x1 -> x0, waiting for transfers between devices: 1.27 us -> none  [gather_plan(): lax.ppermute(last, 'row', across)]
    ppermute x6 -> x8, waiting for transfers between devices: 16 us -> 16.2 us  [move(): lax.ppermute(value, 'row', way)]
  transfers between devices with their start and end apart: 16 -> 17, of which waited for: 11 -> 9; matrix products, arithmetic and copies ran while one was open for 0% -> 0% of each run, Pallas kernels for 44% -> 44%
where the time goes in v17:
time: 69 us; the launch traced here: 68.8 us
  Pallas kernels  35.6 us (52%)
  waiting for transfers between devices  17.3 us (25%)
  starting transfers between devices  14 us (20%)
  between operations  0.95 us (1%)
  local copies, waits for them, and re-layouts  0.92 us (1%)
    pallas_call x5, Pallas kernels, border(): kernel_call(kernel, 'border' + ('_end' if last else '_begin' if begin els...  28 us
    ppermute x8, waiting for transfers between devices, move(): lax.ppermute(value, 'row', way)  16.2 us
    ppermute x8, starting transfers between devices, move(): lax.ppermute(value, 'row', way)  8.25 us
    ppermute x9, starting transfers between devices, swap_bit(): lax.ppermute(value, 'row', [(i, i ^ mask) for i in range(lax.axis_size('r...  5.74 us
    pallas_call x1, Pallas kernels, inner_chain(): kernel_call(kernel, 'inner_chain', out_shape=[jax.ShapeDtypeStruct(array....  4.18 us
    pallas_call x1, Pallas kernels, link_chain(): kernel_call(kernel, 'link_chain', out_shape=jax.ShapeDtypeStruct((rows, n...  1.94 us
  transfers between devices with their start and end apart: 17, of which 9 were waited for; matrix products, arithmetic and copies ran while one was open for 0% of the time, Pallas kernels for 44%

profile of v17, /device:TPU:0, one launch (start us, length us, event | category | flops | bytes accessed | tf_op | source)
XLA Modules:
  0.0 68.8 jit_solution(10814079225994335864)
XLA Ops:
  0.6 0.9 %copy-done.3 = f32[1,384,96]{1,2,0:T(8,128)S(1)} copy-done((f32[1,384,96]{1,2,0:T(8,128)S(1)}, f32[1,384,96]{1,2,0:T(8,128)}, u32[]{:S(2)}) %copy-start.3) | copy-done | bytes 147480
  1.5 0.2 far_rows.1
  1.7 4.1 %collective-permute-start = (f32[24,384]{1,0:T(8,128)S(1)}, f32[24,384]{1,0:T(8,128)S(1)}, u32[]{:S(2)}, u32[]{:S(2)}) collective-permute-start(f32[24,384]{1,0:T(8,128)S(1)} %far_rows.1), channel_id=1, source_target_pairs={{0,8},{1,9},{2,10},{3,11},{4,12},{5,13},{6,14},{7,15},{8,0},{9,1},... | collective-permute-start | bytes 110600 | tf_op jit(solution)/shard_map/ppermute | solution.py:32
  5.8 1.9 %link_chain.1.links_ref = f32[48,2048]{1,0:T(8,128)S(1)} custom-call(f32[48,8,256]{2,1,0:T(8,128)S(1)} %copy-done.2, f32[7,256,256]{2,1,0:T(8,128)S(1)} %copy-done, s32[8,6]{1,0:T(8,128)S(1)} %copy-done.4), custom_call_target="tpu_custom_call" | custom-call | tf_op jit(solution)/shard_map/link_chain/pallas_call | solution.py:175
  7.7 0.4 collective-permute-done.far_ref
  8.1 0.1 message.1.refs_0_
  8.3 1.8 %collective-permute-start.5 = (f32[48,2560]{1,0:T(8,128)S(1)}, f32[48,2560]{1,0:T(8,128)S(1)}, u32[]{:S(2)}, u32[]{:S(2)}) collective-permute-start(f32[48,2560]{1,0:T(8,128)S(1)} %message.1.refs_0_), channel_id=1, source_target_pairs={{0,2},{1,3},{4,0},{5,1},{8,4},{9,5},{12,8},{13,9},{14,12},{15,13},... | collective-permute-start | bytes 1474568 | tf_op jit(solution)/shard_map/ppermute | solution.py:422
  10.1 0.3 collective-permute-start.1
  10.4 4.2 %inner_chain.1 = (f32[7,256,256]{2,1,0:T(8,128)S(1)}, f32[8,256,256]{2,1,0:T(8,128)S(1)}) custom-call(f32[7,256,256]{2,1,0:T(8,128)S(1)} %copy-done, f32[8,256,256]{2,1,0:T(8,128)S(1)} %copy-done.1), custom_call_target="tpu_custom_call" | custom-call | tf_op jit(solution)/shard_map/inner_chain/pallas_call | solution.py:237
  14.6 4.0 %border_begin.1 = (f32[7,256,256]{2,1,0:T(8,128)S(1)}, f32[8,256,256]{2,1,0:T(8,128)S(1)}, f32[48,2048]{1,0:T(8,128)S(1)}, f32[768,896]{1,0:T(8,128)S(1)}, bf16[...) custom-call(f32[48,2560]{1,0:T(8,128)S(1)} %message.1.refs_0_, f32[48,2560]{1,0:T(8,128)S(1)} %collective-permute-done.2.refs_1_, ...), custom_call_target="tpu_custom_call" | custom-call | tf_op jit(solution)/shard_map/border_begin/pallas_call | solution.py:384
  18.5 3.4 %collective-permute-done.5.refs_2_ = f32[48,2560]{1,0:T(8,128)S(1)} collective-permute-done((f32[48,2560]{1,0:T(8,128)S(1)}, f32[48,2560]{1,0:T(8,128)S(1)}, u32[]{:S(2)}, u32[]{:S(2)}) %collective-permute-start.5) | collective-permute-done | bytes 491552 | tf_op jit(solution)/shard_map/ppermute | solution.py:422
  21.9 1.4 %collective-permute-done.1.refs_0_ = f32[48,2560]{1,0:T(8,128)S(1)} collective-permute-done((f32[48,2560]{1,0:T(8,128)S(1)}, f32[48,2560]{1,0:T(8,128)S(1)}, u32[]{:S(2)}, u32[]{:S(2)}) %collective-permute-start.1) | collective-permute-done | bytes 491552 | tf_op jit(solution)/shard_map/ppermute | solution.py:422
  23.4 0.5 collective-permute-start.6
  23.9 1.3 %collective-permute-start.9 = (f32[48,2560]{1,0:T(8,128)S(1)}, f32[48,2560]{1,0:T(8,128)S(1)}, u32[]{:S(2)}, u32[]{:S(2)}) collective-permute-start(f32[48,2560]{1,0:T(8,128)S(1)} %collective-permute-done.5.refs_2_), channel_id=1, source_target_pairs={{0,2},{1,3},{4,0},{5,1},{8,4},{9,5},{12,8},{13,9},{14,12},{15,13},... | collective-permute-start | bytes 1474568 | tf_op jit(solution)/shard_map/ppermute | solution.py:422
  25.2 0.7 %collective-permute-start.3 = (f32[48,2560]{1,0:T(8,128)S(1)}, f32[48,2560]{1,0:T(8,128)S(1)}, u32[]{:S(2)}, u32[]{:S(2)}) collective-permute-start(f32[48,2560]{1,0:T(8,128)S(1)} %collective-permute-done.1.refs_0_), channel_id=1, source_target_pairs={{0,4},{1,5},{4,8},{5,9},{8,12},{9,13},{12,14},{13,15},{14,10},{15,... | collective-permute-start | bytes 1474568 | tf_op jit(solution)/shard_map/ppermute | solution.py:422
  25.9 6.7 %border.3 = (f32[7,256,256]{2,1,0:T(8,128)S(1)}, f32[8,256,256]{2,1,0:T(8,128)S(1)}, f32[48,2048]{1,0:T(8,128)S(1)}, f32[768,896]{1,0:T(8,128)S(1)}, bf16[768,20...) custom-call(f32[48,2560]{1,0:T(8,128)S(1)} %collective-permute-done.1.refs_0_, ...), custom_call_target="tpu_custom_call" | custom-call | tf_op jit(solution)/shard_map/border/pallas_call | solution.py:384
  32.6 4.4 %collective-permute-done.9.refs_2_ = f32[48,2560]{1,0:T(8,128)S(1)} collective-permute-done((f32[48,2560]{1,0:T(8,128)S(1)}, f32[48,2560]{1,0:T(8,128)S(1)}, u32[]{:S(2)}, u32[]{:S(2)}) %collective-permute-start.9) | collective-permute-done | bytes 491552 | tf_op jit(solution)/shard_map/ppermute | solution.py:422
  37.0 1.0 %collective-permute-done.3.refs_0_ = f32[48,2560]{1,0:T(8,128)S(1)} collective-permute-done((f32[48,2560]{1,0:T(8,128)S(1)}, f32[48,2560]{1,0:T(8,128)S(1)}, u32[]{:S(2)}, u32[]{:S(2)}) %collective-permute-start.3) | collective-permute-done | bytes 491552 | tf_op jit(solution)/shard_map/ppermute | solution.py:422
  38.0 0.5 collective-permute-start.10
  38.5 1.7 %collective-permute-start.11 = (f32[48,2560]{1,0:T(8,128)S(1)}, f32[48,2560]{1,0:T(8,128)S(1)}, u32[]{:S(2)}, u32[]{:S(2)}) collective-permute-start(f32[48,2560]{1,0:T(8,128)S(1)} %collective-permute-done.9.refs_2_), channel_id=1, source_target_pairs={{0,2},{1,3},{4,0},{5,1},{8,4},{9,5},{12,8},{13,9},{14,12},{15,13},... | collective-permute-start | bytes 1474568 | tf_op jit(solution)/shard_map/ppermute | solution.py:422
  40.2 0.3 collective-permute-start.7
  40.6 6.7 %border.4 = (f32[7,256,256]{2,1,0:T(8,128)S(1)}, f32[8,256,256]{2,1,0:T(8,128)S(1)}, f32[48,2048]{1,0:T(8,128)S(1)}, f32[768,896]{1,0:T(8,128)S(1)}, bf16[768,20...) custom-call(f32[48,2560]{1,0:T(8,128)S(1)} %collective-permute-done.3.refs_0_, ...), custom_call_target="tpu_custom_call" | custom-call | tf_op jit(solution)/shard_map/border/pallas_call | solution.py:384
  47.3 4.4 %collective-permute-done.11.second_ref.refs_2_ = f32[48,2560]{1,0:T(8,128)S(1)} collective-permute-done((f32[48,2560]{1,0:T(8,128)S(1)}, f32[48,2560]{1,0:T(8,128)S(1)}, u32[]{:S(2)}, u32[]{:S(2)}) %collective-permute-start.11) | collective-permute-done | bytes 491552 | tf_op jit(solution)/shard_map/ppermute | solution.py:422
  51.7 1.4 %collective-permute-done.7.first_ref.refs_0_ = f32[48,2560]{1,0:T(8,128)S(1)} collective-permute-done((f32[48,2560]{1,0:T(8,128)S(1)}, f32[48,2560]{1,0:T(8,128)S(1)}, u32[]{:S(2)}, u32[]{:S(2)}) %collective-permute-start.7) | collective-permute-done | bytes 491552 | tf_op jit(solution)/shard_map/ppermute | solution.py:422
  53.1 0.5 collective-permute-start.15
  53.6 0.4 collective-permute-start.12
  54.0 1.7 %collective-permute-start.13 = (f32[24,2560]{1,0:T(8,128)S(1)}, f32[24,2560]{1,0:T(8,128)S(1)}, u32[]{:S(2)}, u32[]{:S(2)}) collective-permute-start(f32[24,2560]{1,0:T(8,128)S(1)} %get-tuple-element.83), channel_id=1, source_target_pairs={{0,2},{1,3},{4,0},{5,1},{8,4},{9,5},{12,8},{13,9},{14,12},{15,13},... | collective-permute-start | bytes 737288 | tf_op jit(solution)/shard_map/ppermute | solution.py:422
  55.7 5.9 %border.5 = (f32[7,256,256]{2,1,0:T(8,128)S(1)}, f32[8,256,256]{2,1,0:T(8,128)S(1)}, f32[48,2048]{1,0:T(8,128)S(1)}, f32[768,896]{1,0:T(8,128)S(1)}, bf16[768,20...) custom-call(f32[48,2560]{1,0:T(8,128)S(1)} %collective-permute-done., ...), custom_call_target="tpu_custom_call" | custom-call | tf_op jit(solution)/shard_map/border/pallas_call | solution.py:384
  61.6 0.2 collective-permute-done.13.lower_ref
  62.0 1.2 %late_products.1 = (f32[3,256,256]{2,1,0:T(8,128)S(1)}, f32[3,256,256]{2,1,0:T(8,128)S(1)}) custom-call(bf16[1024,1152]{1,0:T(8,128)(2,1)S(1)} %get-tuple-element.102.turned_ref, bf16[1152,768]{1,0:T(8,128)(2,1)S(1)} %get-tuple-element.103.beside_ref), custom_call_target="tpu_custom_call" | custom-call | tf_op jit(solution)/shard_map/late_products/pallas_call | solution.py:407
  63.2 0.7 collective-permute-done.16.refs_1_
  63.8 4.8 %border_end.1 = (f32[7,256,256]{2,1,0:T(8,128)}, f32[8,256,256]{2,1,0:T(8,128)}, f32[48,8,256]{2,1,0:T(8,128)}) custom-call(f32[48,2560]{1,0:T(8,128)S(1)} %stacked.1.refs_0_, f32[48,2560]{1,0:T(8,128)S(1)} %collective-permute-done.16.refs_1_, f32[48,2048]{1,0:T(8,128)S(1)} %get-tuple-element.96.refs_2_, f32[768,896]{1,0:T(8,128)S(1)} %get-tuple-element.97.refs_3_, ...), custom_call_target="tpu_custom_call" | custom-call | tf_op jit(solution)/shard_map/border_end/pallas_call | solution.py:384
  (24 shorter events, 0.3 us)
Async XLA Ops:
  0.6 0.9 %copy-start.3 = (f32[1,384,96]{1,2,0:T(8,128)S(1)}, f32[1,384,96]{1,2,0:T(8,128)}, u32[]{:S(2)}) copy-start(f32[1,384,96]{1,2,0:T(8,128)} %param.5) | copy-start | bytes 442372
  1.5 4.2 %copy-start = (f32[7,256,256]{2,1,0:T(8,128)S(1)}, f32[7,256,256]{2,1,0:T(8,128)}, u32[]{:S(2)}) copy-start(f32[7,256,256]{2,1,0:T(8,128)} %parent_ref.2) | copy-start | bytes 5505028
  1.5 4.2 %copy-start.2 = (f32[48,8,256]{2,1,0:T(8,128)S(1)}, f32[48,8,256]{2,1,0:T(8,128)}, u32[]{:S(2)}) copy-start(f32[48,8,256]{2,1,0:T(8,128)} %links_ref) | copy-start | bytes 1179652
  1.5 4.2 %copy-start.4 = (s32[8,6]{1,0:T(8,128)S(1)}, s32[8,6]{1,0:T(8,128)}, u32[]{:S(2)}) copy-start(s32[8,6]{1,0:T(8,128)} %pattern_ref.1) | copy-start | bytes 580
  1.7 8.7 %copy-start.1 = (f32[8,256,256]{2,1,0:T(8,128)S(1)}, f32[8,256,256]{2,1,0:T(8,128)}, u32[]{:S(2)}) copy-start(f32[8,256,256]{2,1,0:T(8,128)} %pivot_ref.1) | copy-start | bytes 6291460
  1.7 6.4 %collective-permute-start = (f32[24,384]{1,0:T(8,128)S(1)}, f32[24,384]{1,0:T(8,128)S(1)}, u32[]{:S(2)}, u32[]{:S(2)}) collective-permute-start(f32[24,384]{1,0:T(8,128)S(1)} %far_rows.1), channel_id=1, source_target_pairs={{0,8},{1,9},{2,10},{3,11},{4,12},{5,13},{6,14},{7,15},{8,0},{9,1},... | collective-permute-start | bytes 110600 | tf_op jit(solution)/shard_map/ppermute | solution.py:32
  8.2 6.3 %collective-permute-start.2 = (f32[48,2560]{1,0:T(8,128)S(1)}, f32[48,2560]{1,0:T(8,128)S(1)}, u32[]{:S(2)}, u32[]{:S(2)}) collective-permute-start(f32[48,2560]{1,0:T(8,128)S(1)} %message.1.refs_0_), channel_id=1, source_target_pairs={{0,1},{1,0},{2,3},{3,2},{4,5},{5,4},{6,7},{7,6},{8,9},{9,8},{10,11... | collective-permute-start | bytes 1474568 | tf_op jit(solution)/shard_map/ppermute | solution.py:32
  8.3 13.6 %collective-permute-start.5 = (f32[48,2560]{1,0:T(8,128)S(1)}, f32[48,2560]{1,0:T(8,128)S(1)}, u32[]{:S(2)}, u32[]{:S(2)}) collective-permute-start(f32[48,2560]{1,0:T(8,128)S(1)} %message.1.refs_0_), channel_id=1, source_target_pairs={{0,2},{1,3},{4,0},{5,1},{8,4},{9,5},{12,8},{13,9},{14,12},{15,13},... | collective-permute-start | bytes 1474568 | tf_op jit(solution)/shard_map/ppermute | solution.py:422
  10.1 13.3 %collective-permute-start.1 = (f32[48,2560]{1,0:T(8,128)S(1)}, f32[48,2560]{1,0:T(8,128)S(1)}, u32[]{:S(2)}, u32[]{:S(2)}) collective-permute-start(f32[48,2560]{1,0:T(8,128)S(1)} %message.1.refs_0_), channel_id=1, source_target_pairs={{0,4},{1,5},{4,8},{5,9},{8,12},{9,13},{12,14},{13,15},{14,10},{15,... | collective-permute-start | bytes 1474568 | tf_op jit(solution)/shard_map/ppermute | solution.py:422
  23.4 2.5 %collective-permute-start.4 = (f32[48,2560]{1,0:T(8,128)S(1)}, f32[48,2560]{1,0:T(8,128)S(1)}, u32[]{:S(2)}, u32[]{:S(2)}) collective-permute-start(f32[48,2560]{1,0:T(8,128)S(1)} %collective-permute-done.1.refs_0_), channel_id=1, source_target_pairs={{0,1},{1,0},{2,3},{3,2},{4,5},{5,4},{6,7},{7,6},{8,9},{9,8},{10,11... | collective-permute-start | bytes 1474568 | tf_op jit(solution)/shard_map/ppermute | solution.py:32
  23.4 2.6 %collective-permute-start.6 = (f32[48,2560]{1,0:T(8,128)S(1)}, f32[48,2560]{1,0:T(8,128)S(1)}, u32[]{:S(2)}, u32[]{:S(2)}) collective-permute-start(f32[48,2560]{1,0:T(8,128)S(1)} %collective-permute-done.5.refs_2_), channel_id=1, source_target_pairs={{0,1},{1,0},{2,3},{3,2},{4,5},{5,4},{6,7},{7,6},{8,9},{9,8},{10,11... | collective-permute-start | bytes 1474568 | tf_op jit(solution)/shard_map/ppermute | solution.py:32
  23.9 13.1 %collective-permute-start.9 = (f32[48,2560]{1,0:T(8,128)S(1)}, f32[48,2560]{1,0:T(8,128)S(1)}, u32[]{:S(2)}, u32[]{:S(2)}) collective-permute-start(f32[48,2560]{1,0:T(8,128)S(1)} %collective-permute-done.5.refs_2_), channel_id=1, source_target_pairs={{0,2},{1,3},{4,0},{5,1},{8,4},{9,5},{12,8},{13,9},{14,12},{15,13},... | collective-permute-start | bytes 1474568 | tf_op jit(solution)/shard_map/ppermute | solution.py:422
  25.2 12.9 %collective-permute-start.3 = (f32[48,2560]{1,0:T(8,128)S(1)}, f32[48,2560]{1,0:T(8,128)S(1)}, u32[]{:S(2)}, u32[]{:S(2)}) collective-permute-start(f32[48,2560]{1,0:T(8,128)S(1)} %collective-permute-done.1.refs_0_), channel_id=1, source_target_pairs={{0,4},{1,5},{4,8},{5,9},{8,12},{9,13},{12,14},{13,15},{14,10},{15,... | collective-permute-start | bytes 1474568 | tf_op jit(solution)/shard_map/ppermute | solution.py:422
  38.0 2.5 %collective-permute-start.8 = (f32[48,2560]{1,0:T(8,128)S(1)}, f32[48,2560]{1,0:T(8,128)S(1)}, u32[]{:S(2)}, u32[]{:S(2)}) collective-permute-start(f32[48,2560]{1,0:T(8,128)S(1)} %collective-permute-done.3.refs_0_), channel_id=1, source_target_pairs={{0,1},{1,0},{2,3},{3,2},{4,5},{5,4},{6,7},{7,6},{8,9},{9,8},{10,11... | collective-permute-start | bytes 1474568 | tf_op jit(solution)/shard_map/ppermute | solution.py:32
  38.0 2.6 %collective-permute-start.10 = (f32[48,2560]{1,0:T(8,128)S(1)}, f32[48,2560]{1,0:T(8,128)S(1)}, u32[]{:S(2)}, u32[]{:S(2)}) collective-permute-start(f32[48,2560]{1,0:T(8,128)S(1)} %collective-permute-done.9.refs_2_), channel_id=1, source_target_pairs={{0,1},{1,0},{2,3},{3,2},{4,5},{5,4},{6,7},{7,6},{8,9},{9,8},{10,11... | collective-permute-start | bytes 1474568 | tf_op jit(solution)/shard_map/ppermute | solution.py:32
  38.5 13.1 %collective-permute-start.11 = (f32[48,2560]{1,0:T(8,128)S(1)}, f32[48,2560]{1,0:T(8,128)S(1)}, u32[]{:S(2)}, u32[]{:S(2)}) collective-permute-start(f32[48,2560]{1,0:T(8,128)S(1)} %collective-permute-done.9.refs_2_), channel_id=1, source_target_pairs={{0,2},{1,3},{4,0},{5,1},{8,4},{9,5},{12,8},{13,9},{14,12},{15,13},... | collective-permute-start | bytes 1474568 | tf_op jit(solution)/shard_map/ppermute | solution.py:422
  40.2 12.9 %collective-permute-start.7 = (f32[48,2560]{1,0:T(8,128)S(1)}, f32[48,2560]{1,0:T(8,128)S(1)}, u32[]{:S(2)}, u32[]{:S(2)}) collective-permute-start(f32[48,2560]{1,0:T(8,128)S(1)} %collective-permute-done.3.refs_0_), channel_id=1, source_target_pairs={{0,4},{1,5},{4,8},{5,9},{8,12},{9,13},{12,14},{13,15},{14,10},{15,... | collective-permute-start | bytes 1474568 | tf_op jit(solution)/shard_map/ppermute | solution.py:422
  53.1 2.7 %collective-permute-start.14 = (f32[48,2560]{1,0:T(8,128)S(1)}, f32[48,2560]{1,0:T(8,128)S(1)}, u32[]{:S(2)}, u32[]{:S(2)}) collective-permute-start(f32[48,2560]{1,0:T(8,128)S(1)} %collective-permute-done.7.first_ref.refs_0_), channel_id=1, source_target_pairs={{0,1},{1,0},{2,3},{3,2},{4,5},{5,4},{6,7},{7,6},{8,9},{9,8},{10,11... | collective-permute-start | bytes 1474568 | tf_op jit(solution)/shard_map/ppermute | solution.py:32
  53.1 2.7 %collective-permute-start.15 = (f32[48,2560]{1,0:T(8,128)S(1)}, f32[48,2560]{1,0:T(8,128)S(1)}, u32[]{:S(2)}, u32[]{:S(2)}) collective-permute-start(f32[48,2560]{1,0:T(8,128)S(1)} %collective-permute-done.11.second_ref.refs_2_), channel_id=1, source_target_pairs={{0,1},{1,0},{2,3},{3,2},{4,5},{5,4},{6,7},{7,6},{8,9},{9,8},{10,11... | collective-permute-start | bytes 1474568 | tf_op jit(solution)/shard_map/ppermute | solution.py:32
  53.6 8.0 %collective-permute-start.12 = (f32[24,2560]{1,0:T(8,128)S(1)}, f32[24,2560]{1,0:T(8,128)S(1)}, u32[]{:S(2)}, u32[]{:S(2)}) collective-permute-start(f32[24,2560]{1,0:T(8,128)S(1)} %get-tuple-element.82), channel_id=1, source_target_pairs={{0,4},{1,5},{4,8},{5,9},{8,12},{9,13},{12,14},{13,15},{14,10},{15,... | collective-permute-start | bytes 737288 | tf_op jit(solution)/shard_map/ppermute | solution.py:422
  54.0 7.9 %collective-permute-start.13 = (f32[24,2560]{1,0:T(8,128)S(1)}, f32[24,2560]{1,0:T(8,128)S(1)}, u32[]{:S(2)}, u32[]{:S(2)}) collective-permute-start(f32[24,2560]{1,0:T(8,128)S(1)} %get-tuple-element.83), channel_id=1, source_target_pairs={{0,2},{1,3},{4,0},{5,1},{8,4},{9,5},{12,8},{13,9},{14,12},{15,13},... | collective-permute-start | bytes 737288 | tf_op jit(solution)/shard_map/ppermute | solution.py:422
  61.9 1.9 %collective-permute-start.16 = (f32[48,2560]{1,0:T(8,128)S(1)}, f32[48,2560]{1,0:T(8,128)S(1)}, u32[]{:S(2)}, u32[]{:S(2)}) collective-permute-start(f32[48,2560]{1,0:T(8,128)S(1)} %stacked.1.refs_0_), channel_id=1, source_target_pairs={{0,1},{1,0},{2,3},{3,2},{4,5},{5,4},{6,7},{7,6},{8,9},{9,8},{10,11... | collective-permute-start | bytes 1474568 | tf_op jit(solution)/shard_map/ppermute | solution.py:32
